TPU v7x, 32 devices: a whole 2x2x4 slice. The times are simulated.
32 devices in a mesh: groups: 2 (over y), col: 4 (over x, core), row: 4 (over z).
Axes of the slice: x: 2, y: 2, z: 4, core: 2. Of those that a mesh axis runs over, the one named last changes fastest.
Arguments:
- momentum: float32 [7168, 18432], P(('groups', 'row'), 'col'), parts along dimension 0, may hold values from -300 to 300
Outputs:
- update: float32 [7168, 18432], P(('groups', 'row'), 'col'), parts along dimension 0
There are 2 independent parts, one for each index of `groups`. A program takes and returns all parts, laid end to end along the dimension named above; each array names one. Nothing has to cross between parts.
All inputs are finite; a program needn't handle non-finite values.
Results may differ from a plain program's by a relative error of at most 0.017.
Values may be sent and summed in bfloat16 or wider, within the bound.
No kernel may reach another device: no remote copies, remote signals or barrier semaphores. Data moves between devices by JAX's collectives and lax.ppermute only.
A program may use at most 192 MiB of HBM per device.

v0:
```python
import math

import jax
import jax.numpy as jnp
from jax import lax
from jax.sharding import PartitionSpec as P

M = 3584
N = 18432


coef_linear = 3.4445
coef_cubic = -4.775
coef_quintic = 2.0315


def per_device(momentum):
    norm_sum = lax.psum(jnp.sum(momentum * momentum), ("col", "row"))
    spectral_edge = 1.0 + math.sqrt(M / N)
    scaled = (momentum / (jnp.sqrt(norm_sum / M) * spectral_edge + 1e-07)).astype(jnp.bfloat16)
    columns = lax.all_gather(scaled, "row", axis=0, tiled=True)
    gram_tile = lax.psum_scatter(
        lax.dot_general(
            columns, scaled, (((1,), (1,)), ((), ())), preferred_element_type=jnp.float32
        ).astype(jnp.bfloat16),
        "col",
        scatter_dimension=0,
        tiled=True,
    )
    left_rows = lax.all_gather(gram_tile, "row", axis=1, tiled=True)
    squared = jnp.dot(
        left_rows,
        lax.all_gather(gram_tile, "col", axis=0, tiled=True),
        preferred_element_type=jnp.float32,
    )
    poly = (coef_cubic * gram_tile.astype(jnp.float32) + coef_quintic * squared).astype(
        jnp.bfloat16
    )
    product = lax.dot_general(
        lax.all_gather(poly, "col", axis=0, tiled=True),
        columns,
        (((0,), (0,)), ((), ())),
        preferred_element_type=jnp.float32,
    )
    newton = coef_linear * scaled.astype(jnp.float32) + product
    newton_sq = lax.psum(jnp.sum(newton * newton), ("col", "row"))
    update_rms = jnp.sqrt(newton_sq) / math.sqrt(M * N)
    return newton / (update_rms + 1e-07)


def solution(mesh):
    return jax.shard_map(
        per_device,
        mesh=mesh,
        in_specs=(P(("groups", "row"), "col"),),
        out_specs=P(("groups", "row"), "col"),
        check_vma=False,
    )
```

profile of v0, /device:TPU:0, one launch (start us, length us, event | category | flops | bytes accessed | tf_op | source)
XLA Modules:
  0.0 1035.2 jit_solution(1219075776046653555)
XLA Ops:
  6.5 0.0 all-gather.5.cloned.1.call-start
  6.5 10.5 %multiply_reduce_fusion.1 = f32[]{:T(128)} fusion(f32[896,4608]{1,0:T(8,128)} %param.1), kind=kLoop, calls=%fused_computation.3 | loop fusion | flops 8257535 | bytes 16515076 | tf_op jit(solution)/shard_map/reduce_sum | solution.py:18
  17.1 35.8 %psum.14 = f32[]{:T(128)} all-reduce(f32[]{:T(128)} %multiply_reduce_fusion.1), channel_id=1, replica_groups=mesh['groups'=2,'col'=4,'row'=4] {'col','row'}, use_global_device_ids=true, to_apply=%region_1.0 | all-reduce | flops 1 | bytes 8 | tf_op jit(solution)/shard_map/psum | solution.py:18
  53.5 8.8 divide_convert_fusion
  62.3 0.0 all-gather.5.cloned.1.call-update
  62.3 0.0 reduce-scatter.2.cloned.1.call-start
  62.4 550.2 %all-gather.5.cloned.1.call-done = bf16[3584,4608]{1,0:T(8,128)(2,1)} async-done(((bf16[896,4608]{1,0:T(8,128)(2,1)}), bf16[3584,4608]{1,0:T(8,128)(2,1)}) %all-gather.5.cloned.1.call-update) | async-done | bytes 33030160 | tf_op jit(solution)/shard_map/all_gather | solution.py:21
  612.6 41.5 %convolution_convert_fusion = bf16[3584,896]{1,0:T(8,128)(2,1)} fusion(bf16[3584,4608]{1,0:T(8,128)(2,1)} %all-gather.5.cloned.1.call-done, bf16[896,4608]{1,0:T(8,128)(2,1)} %divide_convert_fusion), kind=kOutput, calls=%fused_computation.5 | convolution fusion | flops 29598220288 | bytes 47710208 | tf_op jit(solution)/shard_map/dot_general | solution.py:23
  654.1 0.0 reduce-scatter.2.cloned.1.call-update
  654.1 0.0 all-gather.7.cloned.1.call-start
  654.1 57.5 %reduce-scatter.2.cloned.1.call-done = bf16[896,896]{1,0:T(8,128)(2,1)} async-done(((bf16[3584,896]{1,0:T(8,128)(2,1)}), bf16[896,896]{1,0:T(8,128)(2,1)}) %reduce-scatter.2.cloned.1.call-update) | async-done | bytes 1605648 | tf_op jit(solution)/shard_map/reduce_scatter | solution.py:22
  711.7 0.0 all-gather.7.cloned.1.call-update
  711.7 0.0 all-gather.9.cloned.1.call-start
  711.7 0.5 all-gather.9.cloned.1.call-update
  712.3 0.2 all-gather.11.cloned.1.call-start
  712.5 118.4 %all-gather.7.cloned.1.call-done = bf16[896,3584]{1,0:T(8,128)(2,1)} async-done(((bf16[896,896]{1,0:T(8,128)(2,1)}), bf16[896,3584]{1,0:T(8,128)(2,1)}) %all-gather.7.cloned.1.call-update) | async-done | bytes 6422544 | tf_op jit(solution)/shard_map/all_gather | solution.py:30
  830.9 46.8 %all-gather.9.cloned.1.call-done = bf16[3584,896]{1,0:T(8,128)(2,1)} async-done(((bf16[896,896]{1,0:T(8,128)(2,1)}), bf16[3584,896]{1,0:T(8,128)(2,1)}) %all-gather.9.cloned.1.call-update) | async-done | bytes 6422544 | tf_op jit(solution)/shard_map/all_gather | solution.py:33
  877.7 11.9 %add_convert_fusion = bf16[896,896]{1,0:T(8,128)(2,1)} fusion(bf16[896,896]{1,0:T(8,128)(2,1)} %reduce-scatter.2.cloned.1.call-done, bf16[896,3584]{1,0:T(8,128)(2,1)} %all-gather.7.cloned.1.call-done, bf16[3584,896]{1,0:T(8,128)(2,1)} %all-gather.9.cloned.1.call-done), kind=kOutput, calls=%fused_computation.6 | convolution fusion | flops 5758599168 | bytes 16056320 | tf_op jit(solution)/shard_map/dot_general | solution.py:31
  889.6 0.0 all-gather.11.cloned.1.call-update
  889.7 47.3 %all-gather.11.cloned.1.call-done = bf16[3584,896]{1,0:T(8,128)(2,1)} async-done(((bf16[896,896]{1,0:T(8,128)(2,1)}), bf16[3584,896]{1,0:T(8,128)(2,1)}) %all-gather.11.cloned.1.call-update) | async-done | bytes 6422544 | tf_op jit(solution)/shard_map/all_gather | solution.py:40
  937.0 40.0 %multiply_reduce_fusion = (f32[]{:T(128)}, f32[896,4608]{1,0:T(8,128)}) fusion(bf16[896,4608]{1,0:T(8,128)(2,1)} %divide_convert_fusion, bf16[3584,896]{1,0:T(8,128)(2,1)} %all-gather.11.cloned.1.call-done, bf16[3584,4608]{1,0:T(8,128)(2,1)} %all-gather.5.cloned.1.call-done), kind=kOutput, calls=%fused_computation | convolution fusion | flops 29615652864 | bytes 64225284 | tf_op jit(solution)/shard_map/dot_general | solution.py:39
  977.0 33.5 %psum.15 = f32[]{:T(128)} all-reduce(f32[]{:T(128)} %get-tuple-element.5), channel_id=1, replica_groups=mesh['groups'=2,'col'=4,'row'=4] {'col','row'}, use_global_device_ids=true, to_apply=%region_4.0 | all-reduce | flops 1 | bytes 8 | tf_op jit(solution)/shard_map/psum | solution.py:46
  1011.1 17.6 %fusion = f32[896,4608]{1,0:T(8,128)} fusion(f32[896,4608]{1,0:T(8,128)} %get-tuple-element.6, f32[]{:T(128)S(6)} %add.21, f32[896,4608]{1,0:T(8,128)} %param.1, f32[]{:T(128)S(6)} %add.18), kind=kLoop, calls=%fused_computation.4 | loop fusion | flops 24772608 | bytes 49545224 | tf_op jit(solution)/shard_map/div | solution.py:48
Async XLA Ops:
  6.5 606.1 %all-gather.5.cloned.1.call-start = ((), (), s32[]{:S(2)}) async-start(), calls=%async_computation.1 | async-start | bytes 41287680 | tf_op jit(solution)/shard_map/all_gather | solution.py:21
  62.3 649.3 %reduce-scatter.2.cloned.1.call-start = ((), (), s32[]{:S(2)}) async-start(), calls=%async_computation.2 | async-start | bytes 8028160 | tf_op jit(solution)/shard_map/reduce_scatter | solution.py:22
  654.1 176.8 %all-gather.7.cloned.1.call-start = ((), (), s32[]{:S(2)}) async-start(), calls=%async_computation.3 | async-start | bytes 8028160 | tf_op jit(solution)/shard_map/all_gather | solution.py:30
  711.7 166.1 %all-gather.9.cloned.1.call-start = ((), (), s32[]{:S(2)}) async-start(), calls=%async_computation.4 | async-start | bytes 8028160 | tf_op jit(solution)/shard_map/all_gather | solution.py:33
  712.3 224.7 %all-gather.11.cloned.1.call-start = ((), (), s32[]{:S(2)}) async-start(), calls=%async_computation.5 | async-start | bytes 8028160 | tf_op jit(solution)/shard_map/all_gather | solution.py:40
Sparse Core Ops, SparseCore 0:
  62.5 550.0 all-gather.4
  654.2 57.3 reduce-scatter.1
  713.3 117.5 all-gather.6
  832.4 45.2 all-gather.8
  889.8 47.1 all-gather.10
where the time goes:
time: 1040 us
  waiting for transfers between devices  821 us (79%)
  matrix products  93.4 us (9%)
  blocking collectives  69.2 us (7%)
  other arithmetic  36.9 us (4%)
  between operations  14.5 us (1%)
    all_gather x1, waiting for transfers between devices, per_device(): columns = lax.all_gather(scaled, 'row', axis=0, tiled=True)  550 us
    all_gather x1, waiting for transfers between devices, per_device(): left_rows = lax.all_gather(gram_tile, 'row', axis=1, tiled=True)  118 us
    reduce_scatter x1, waiting for transfers between devices, per_device(): lax.psum_scatter(lax.dot_general(columns, scaled, (((1,), (1,)), ((), ())...  57.5 us
    all_gather x1, waiting for transfers between devices, per_device(): lax.all_gather(poly, 'col', axis=0, tiled=True)  47.3 us
    all_gather x1, waiting for transfers between devices, per_device(): lax.all_gather(gram_tile, 'col', axis=0, tiled=True)  46.8 us
    dot_general x1, matrix products, per_device(): lax.dot_general(columns, scaled, (((1,), (1,)), ((), ())), preferred_elem...  41.5 us
    dot_general x1, matrix products, per_device(): lax.dot_general(lax.all_gather(poly, 'col', axis=0, tiled=True), columns,...  40 us
    psum x1, blocking collectives, per_device(): norm_sum = lax.psum(jnp.sum(momentum * momentum), ('col', 'row'))  35.8 us
  transfers between devices with their start and end apart: 5, of which 5 were waited for; matrix products, arithmetic and copies ran while one was open for 0% of the time, Pallas kernels for 0%

commit v1 on v0

v1 whole, which is shorter than its diff:
```python
import math

import jax
import jax.numpy as jnp
from jax import lax
from jax.sharding import PartitionSpec as P

M = 3584
N = 18432

coef_linear = 3.4445
coef_cubic = -4.775
coef_quintic = 2.0315


def orientation(i, j, n):
    low, high = min(i, j), max(i, j)
    return (low, high) if i + j <= n - 1 else (high, low)


def per_device(momentum):
    n_row = lax.axis_size("row")
    n_col = lax.axis_size("col")
    rows, cols = momentum.shape
    half = n_row // 2
    width = cols // 2
    z = lax.axis_index("row")
    left = z < half
    is_hub = (z == half) | (z == half - 1)

    near_at = jnp.where(left, width, 0)
    far_at = width - near_at
    far = lax.dynamic_slice(momentum, (0, far_at), (rows, width)).astype(jnp.bfloat16)
    near = lax.dynamic_slice(momentum, (0, near_at), (rows, width)).astype(jnp.bfloat16)

    def to_hub(block, r):
        return lax.ppermute(block, "row", [(r, half), (n_row - 1 - r, half - 1)])

    def from_hub(block, r):
        return lax.ppermute(block, "row", [(half, r), (half - 1, n_row - 1 - r)])

    early = list(range(half - 1, n_row))
    late = list(range(half - 1))
    blocks = {half: near}
    for r in early:
        if r != half:
            blocks[r] = to_hub(far if r < half else near, r)
    far_later, blocks[half - 1] = lax.optimization_barrier((far, blocks[half - 1]))
    for r in late:
        blocks[r] = to_hub(far_later, r)

    norm_sum = lax.psum(jnp.sum(momentum * momentum), ("col", "row"))
    spectral_edge = 1.0 + math.sqrt(M / N)
    inverse = 1.0 / (jnp.sqrt(norm_sum / M) * spectral_edge + 1e-07)

    def partial_gram(i, j):
        value = lax.dot_general(
            blocks[i], blocks[j], (((1,), (1,)), ((), ())), preferred_element_type=jnp.float32
        ).astype(jnp.bfloat16)
        if i != j and i + j == n_row - 1:
            value = jnp.where(left, value.T, value)
        return value

    def scattered(pairs):
        stack = jnp.stack(
            [partial_gram(i, j).reshape(n_col, rows // n_col, rows) for i, j in pairs], axis=1
        )
        summed = lax.psum_scatter(stack, "col", scatter_dimension=0, tiled=False)
        other = lax.ppermute(summed, "row", [(half, half - 1), (half - 1, half)])
        return summed, other

    pairs_early = [orientation(i, j, n_row) for i in early for j in early if i <= j]
    pairs_late = [
        orientation(i, j, n_row) for i in range(n_row) for j in range(i, n_row) if min(i, j) < half - 1
    ]
    pairs = pairs_early + pairs_late
    mine_early, other_early = scattered(pairs_early)
    mine, other = mine_early, other_early
    if pairs_late:
        mine_late, other_late = scattered(pairs_late)
        mine = jnp.concatenate([mine_early, mine_late])
        other = jnp.concatenate([other_early, other_late])
    place = {pair: k for k, pair in enumerate(pairs)}

    def mirror(pair):
        i, j = pair
        if i + j == n_row - 1:
            return pair
        return (n_row - 1 - i, n_row - 1 - j)

    gram_sum = jnp.stack(
        [
            mine[k].astype(jnp.float32) + other[place[mirror(pair)]].astype(jnp.float32)
            for k, pair in enumerate(pairs)
        ]
    )
    gram_part = (gram_sum * (inverse * inverse)).astype(jnp.bfloat16)
    gram_blocks = lax.all_gather(gram_part, "col", axis=0, tiled=False)

    def gram_block(i, j):
        pair = orientation(i, j, n_row)
        value = gram_blocks[:, place[pair]].reshape(rows, rows)
        if i != j and i + j == n_row - 1:
            return jnp.where(left, value.T, value) if (i, j) == pair else jnp.where(left, value, value.T)
        return value if (i, j) == pair else value.T

    gram = jnp.concatenate(
        [jnp.concatenate([gram_block(i, j) for j in range(n_row)], axis=1) for i in range(n_row)], axis=0
    )

    share = gram.shape[0] // 2
    core = lax.axis_index("col") % 2
    gram_rows = lax.dynamic_slice(gram, (core * share, 0), (share, gram.shape[1]))
    squared = jnp.dot(gram_rows, gram, preferred_element_type=jnp.float32)
    poly_rows = (coef_cubic * gram_rows.astype(jnp.float32) + coef_quintic * squared).astype(jnp.bfloat16)
    poly_pair = lax.ppermute(poly_rows, "col", [(c, c ^ 1) for c in range(n_col)])
    first = jnp.where(core == 0, poly_rows, poly_pair)
    second = jnp.where(core == 0, poly_pair, poly_rows)
    poly = jnp.concatenate([first, second], axis=0)

    chunks = 3
    step = width // chunks
    near_parts, far_parts = [], []
    newton_sq = jnp.float32(0.0)
    for k in range(chunks):
        raw = jnp.concatenate([blocks[r][:, k * step : (k + 1) * step] for r in range(n_row)], axis=0)
        product = jnp.dot(poly, raw, preferred_element_type=jnp.float32)
        newton = inverse * (coef_linear * raw.astype(jnp.float32) + product)
        newton_sq += jnp.sum(newton * newton)
        newton = newton.astype(jnp.bfloat16).reshape(n_row, rows, step)
        near_part, far_part = jnp.where(is_hub, newton[half], 0), 0
        for r in range(n_row):
            if r > half:
                near_part = near_part + from_hub(newton[r], r)
            if r < half:
                far_part = far_part + from_hub(newton[r], r)
        near_parts.append(near_part)
        far_parts.append(far_part)
    newton_sq = lax.psum(jnp.where(is_hub, newton_sq, 0.0), ("col", "row"))
    factor = 1.0 / (jnp.sqrt(newton_sq) / math.sqrt(M * N) + 1e-07)
    near_all = jnp.concatenate(near_parts, axis=1)
    far_all = jnp.concatenate(far_parts, axis=1)
    update = jnp.concatenate(
        [jnp.where(left, far_all, near_all), jnp.where(left, near_all, far_all)], axis=1
    )
    return update.astype(jnp.float32) * factor


def solution(mesh):
    return jax.shard_map(
        per_device,
        mesh=mesh,
        in_specs=(P(("groups", "row"), "col"),),
        out_specs=P(("groups", "row"), "col"),
        check_vma=False,
    )
```

time: 1040 us -> 1130 us (1.087)
  waiting for transfers between devices: 821 us -> 322 us
  other arithmetic: 36.9 us -> 222 us
  matrix products: 93.4 us -> 231 us
  local copies, waits for them, and re-layouts: 0 us -> 108 us
  blocking collectives: 69.2 us -> 176 us
  starting transfers between devices: 0.34 us -> 42.5 us
    all_gather x4 -> x1, waiting for transfers between devices: 763 us -> 99.2 us  [per_device(): gram_blocks = lax.all_gather(gram_part, 'col', axis=0, tiled=False)]
    ppermute x0 -> x15, waiting for transfers between devices: none -> 165 us  [the longest x3 146 us: to_hub(): return lax.ppermute(block, 'row', [(r, half), (n_row - 1 - r, half - 1)])]
    concatenate x0 -> x1, other arithmetic: none -> 142 us  [per_device(): jnp.concatenate([jnp.concatenate([gram_block(i, j) for j in range(n_row)]...]
    dot_general x3 -> x14, matrix products: 93.4 us -> 231 us  [the longest x3 103 us: per_device(): product = jnp.dot(poly, raw, preferred_element_type=jnp.float32)]
    psum x1, blocking collectives: 33.5 us -> 124 us  [per_device(): newton_sq = lax.psum(jnp.where(is_hub, newton_sq, 0.0), ('col', 'row'))]
    ppermute x0 -> x15, starting transfers between devices: none -> 42.4 us  [the longest x3 25.6 us: to_hub(): return lax.ppermute(block, 'row', [(r, half), (n_row - 1 - r, half - 1)])]
    slice x0 -> x7, local copies, waits for them, and re-layouts: none -> 35.1 us  [the longest x3 12.9 us: per_device(): far_part = far_part + from_hub(newton[r], r)]
    select_n x0 -> x5, other arithmetic: none -> 31.7 us  [the longest x1 14.3 us: per_device(): first = jnp.where(core == 0, poly_rows, poly_pair)]
  transfers between devices with their start and end apart: 5 -> 18, of which waited for: 5 -> 6; matrix products, arithmetic and copies ran while one was open for 0% -> 15% of each run, Pallas kernels for 0% -> 0%
where the time goes in v1:
time: 1130 us; the launch traced here: 1120 us
  waiting for transfers between devices  322 us (28%)
  matrix products  231 us (20%)
  other arithmetic  222 us (20%)
  blocking collectives  176 us (16%)
  local copies, waits for them, and re-layouts  108 us (10%)
  starting transfers between devices  42.5 us (4%)
  between operations  17.3 us (2%)
    ppermute x3, waiting for transfers between devices, to_hub(): return lax.ppermute(block, 'row', [(r, half), (n_row - 1 - r, half - 1)])  146 us
    concatenate x1, other arithmetic, per_device(): jnp.concatenate([jnp.concatenate([gram_block(i, j) for j in range(n_row)]...  142 us
    psum x1, blocking collectives, per_device(): newton_sq = lax.psum(jnp.where(is_hub, newton_sq, 0.0), ('col', 'row'))  124 us
    dot_general x3, matrix products, per_device(): product = jnp.dot(poly, raw, preferred_element_type=jnp.float32)  103 us
    all_gather x1, waiting for transfers between devices, per_device(): gram_blocks = lax.all_gather(gram_part, 'col', axis=0, tiled=False)  99.2 us
    dot_general x10, matrix products, partial_gram(): lax.dot_general(blocks[i], blocks[j], (((1,), (1,)), ((), ())), preferred...  71.1 us
    reduce_scatter x2, waiting for transfers between devices, scattered(): summed = lax.psum_scatter(stack, 'col', scatter_dimension=0, tiled=False)  58 us
    dot_general x1, matrix products, per_device(): squared = jnp.dot(gram_rows, gram, preferred_element_type=jnp.float32)  57.2 us
  transfers between devices with their start and end apart: 18, of which 6 were waited for; matrix products, arithmetic and copies ran while one was open for 15% of the time, Pallas kernels for 0%

profile of v1, /device:TPU:0, one launch (start us, length us, event | category | flops | bytes accessed | tf_op | source)
XLA Modules:
  0.0 1118.1 jit_solution(16674294655229113573)
XLA Ops:
  6.5 9.8 constant_dynamic-slice_fusion
  39.7 9.3 convolution_convert_fusion.6
  68.2 58.0 %collective-permute-done.2 = bf16[896,2304]{0,1:T(8,128)(2,1)} collective-permute-done((bf16[896,2304]{0,1:T(8,128)(2,1)}, bf16[896,2304]{0,1:T(8,128)(2,1)}, u32[]{:S(2)}, u32[]{:S(2)}) %collective-permute-start.2) | collective-permute-done | bytes 4128800 | tf_op jit(solution)/shard_map/ppermute | solution.py:37
  126.2 8.0 convolution_convert_fusion.7
  145.5 8.3 convolution_convert_fusion.4
  155.2 15.0 %collective-permute-start.1 = (bf16[896,2304]{0,1:T(8,128)(2,1)}, bf16[896,2304]{0,1:T(8,128)(2,1)S(1)}, u32[]{:S(2)}, u32[]{:S(2)}) collective-permute-start(bf16[896,2304]{0,1:T(8,128)(2,1)} %copy.59), channel_id=1, source_target_pairs={{0,2},{3,1},{4,6},{7,5},{8,10},{11,9},{12,14},{15,13},{16,18},{19,... | collective-permute-start | bytes 12386312 | tf_op jit(solution)/shard_map/ppermute | solution.py:37
  170.2 87.6 %collective-permute-done.1 = bf16[896,2304]{0,1:T(8,128)(2,1)S(1)} collective-permute-done((bf16[896,2304]{0,1:T(8,128)(2,1)}, bf16[896,2304]{0,1:T(8,128)(2,1)S(1)}, u32[]{:S(2)}, u32[]{:S(2)}) %collective-permute-start.1) | collective-permute-done | bytes 4128800 | tf_op jit(solution)/shard_map/ppermute | solution.py:37
  257.8 8.2 convolution_convert_fusion
  291.7 57.9 %reduce-scatter.5.cloned.1.call-done = bf16[1,4,224,896]{3,2,1,0:T(8,128)(2,1)} async-done(((bf16[4,4,224,896]{3,2,1,0:T(8,128)(2,1)}), bf16[1,4,224,896]{3,2,1,0:T(8,128)(2,1)}) %reduce-scatter.5.cloned.1.call-update) | async-done | bytes 1605648 | tf_op jit(solution)/shard_map/reduce_scatter | solution.py:68
  351.7 10.5 multiply_reduce_fusion
  362.2 51.8 %psum.14 = f32[]{:T(128)} all-reduce(f32[]{:T(128)} %multiply_reduce_fusion), channel_id=1, replica_groups=mesh['groups'=2,'col'=4,'row'=4] {'col','row'}, use_global_device_ids=true, to_apply=%region_1.2 | all-reduce | flops 1 | bytes 8 | tf_op jit(solution)/shard_map/psum | solution.py:52
  428.5 99.2 %all-gather.2.cloned.1.call-done = bf16[4,10,224,896]{3,2,0,1:T(8,128)(2,1)} async-done(((bf16[1,10,224,896]{3,2,0,1:T(8,128)(2,1)}), bf16[4,10,224,896]{3,2,0,1:T(8,128)(2,1)}) %all-gather.2.cloned.1.call-update) | async-done | bytes 16056336 | tf_op jit(solution)/shard_map/all_gather | solution.py:98
  527.7 10.6 fusion.34
  562.1 141.8 %maximum_maximum_fusion = bf16[3584,3584]{1,0:T(8,128)(2,1)} fusion(bf16[896,896]{1,0:T(8,128)(2,1)} %bitcast.188, bf16[896,896]{1,0:T(8,128)(2,1)S(1)} %bitcast.172, bf16[896,896]{1,0:T(8,128)(2,1)S(1)} %bitcast.174, bf16[896,896]{1,0:T(8,128)(2,1)S(1)} %get-tuple-element.59, bf16[896,896]{1,0:T(8,128)(2,1)} %bitcast.186, bf16[896,896]{1,0:T(8,128)(2,1)} %bitcast.189, ...), kind=kLoop, calls=%fused_computation | loop fusion | flops 411041792 | bytes 51380224 | tf_op jit(solution)/shard_map/concatenate | solution.py:107
  703.9 57.2 %add_convert_fusion = bf16[1792,3584]{1,0:T(8,128)(2,1)} fusion(bf16[3584,3584]{1,0:T(8,128)(2,1)} %maximum_maximum_fusion, s32[]{:T(128)S(6)} %select_n.102), kind=kOutput, calls=%fused_computation.2 | convolution fusion | flops 46068793344 | bytes 64226304 | tf_op jit(solution)/shard_map/dot_general | solution.py:114
  781.0 14.3 %broadcast_select_fusion.1 = (bf16[1792,3584]{1,0:T(8,128)(2,1)}, bf16[1792,3584]{1,0:T(8,128)(2,1)}) fusion(bf16[1792,3584]{1,0:T(8,128)(2,1)S(1)} %bitcast.182, bf16[1792,3584]{1,0:T(8,128)(2,1)} %collective-permute-done.5, pred[]{:T(512)S(6)} %eq.12), kind=kLoop, calls=%fused_computation.7 | loop fusion | flops 12845056 | bytes 51380224 | tf_op jit(solution)/shard_map/jit(_where)/select_n | solution.py:117
  795.3 36.5 %multiply_reduce_fusion.3 = (f32[]{:T(128)}, bf16[3584,768]{0,1:T(8,128)(2,1)}) fusion(bf16[896,768]{0,1:T(8,128)(2,1)S(1)} %get-tuple-element.49, bf16[896,768]{0,1:T(8,128)(2,1)} %get-tuple-element.63, bf16[896,768]{0,1:T(8,128)(2,1)S(1)} %get-tuple-element.43, bf16[896,768]{0,1:T(8,128)(2,1)} %get-tuple-element.40, ...), kind=kOutput, calls=%fused_computation.10 | convolution fusion | flops 19841941504 | bytes 36700168 | tf_op jit(solution)/shard_map/dot_general | solution.py:127
  838.1 33.3 %multiply_reduce_fusion.2 = (f32[]{:T(128)}, bf16[3584,768]{0,1:T(8,128)(2,1)}) fusion(bf16[896,768]{0,1:T(8,128)(2,1)} %get-tuple-element.51, bf16[896,768]{0,1:T(8,128)(2,1)} %get-tuple-element.62, bf16[896,768]{0,1:T(8,128)(2,1)} %get-tuple-element.45, bf16[896,768]{0,1:T(8,128)(2,1)} %get-tuple-element.42, bf16[1792,3584]{1,0:T(8,128)(2,1)} %get-tuple-element.10, ...), kind=kOutput, calls=%fused_computation.9 | convolution fusion | flops 19841941504 | bytes 36700168 | tf_op jit(solution)/shard_map/dot_general | solution.py:127
  880.1 33.0 %multiply_reduce_fusion.1 = (f32[]{:T(128)}, bf16[3584,768]{0,1:T(8,128)(2,1)}) fusion(bf16[896,768]{0,1:T(8,128)(2,1)} %get-tuple-element.50, bf16[896,768]{0,1:T(8,128)(2,1)} %get-tuple-element.61, bf16[896,768]{0,1:T(8,128)(2,1)} %get-tuple-element.44, bf16[896,768]{0,1:T(8,128)(2,1)} %get-tuple-element.41, bf16[1792,3584]{1,0:T(8,128)(2,1)} %get-tuple-element.10, ...), kind=kOutput, calls=%fused_computation.8 | convolution fusion | flops 19841941504 | bytes 36700168 | tf_op jit(solution)/shard_map/dot_general | solution.py:127
  920.3 10.9 collective-permute-done.8
  936.1 124.4 %psum.15 = f32[]{:T(128)} all-reduce(f32[]{:T(128)S(6)} %select_n.111), channel_id=1, replica_groups=mesh['groups'=2,'col'=4,'row'=4] {'col','row'}, use_global_device_ids=true, to_apply=%region_7.8 | all-reduce | flops 1 | bytes 8 | tf_op jit(solution)/shard_map/psum | solution.py:139
  1071.6 12.3 %broadcast_select_fusion.3 = (bf16[896,2304]{0,1:T(8,128)(2,1)}, bf16[896,2304]{0,1:T(8,128)(2,1)}) fusion(pred[]{:T(512)S(6)} %lt.16, bf16[896,768]{0,1:T(8,128)(2,1)S(1)} %fusion.25, bf16[896,768]{0,1:T(8,128)(2,1)S(1)} %fusion.26, bf16[896,768]{0,1:T(8,128)(2,1)S(1)} %fusion.27, bf16[896,768]{0,1:T(8,128)(2,1)S(1)} %add.122, ...), kind=kLoop, calls=%fused_computation.43 | loop fusion | flops 28901376 | bytes 16515073 | tf_op jit(solution)/shard_map/jit(_where)/select_n | solution.py:144
  1083.9 10.2 convert_multiply_fusion
  1094.0 17.2 %copy.58 = f32[896,4608]{1,0:T(8,128)} copy(f32[896,4608]{0,1:T(8,128)} %convert_multiply_fusion) | data formatting | bytes 33030144 | tf_op jit(solution)/shard_map/mul | solution.py:146
  (115 shorter events, 175.4 us)
Async XLA Ops:
  6.5 282.9 %reduce-scatter.3.cloned.1.call-start = ((), (), s32[]{:S(2)}) async-start(), calls=%async_computation.2 | async-start | bytes 12042240 | tf_op jit(solution)/shard_map/reduce_scatter | solution.py:68
  22.7 26.3 %collective-permute-start = (bf16[896,2304]{0,1:T(8,128)(2,1)}, bf16[896,2304]{0,1:T(8,128)(2,1)}, u32[]{:S(2)}, u32[]{:S(2)}) collective-permute-start(bf16[896,2304]{0,1:T(8,128)(2,1)} %copy.59), channel_id=1, source_target_pairs={{1,2},{2,1},{5,6},{6,5},{9,10},{10,9},{13,14},{14,13},{17,18},{18,... | collective-permute-start | bytes 12386312 | tf_op jit(solution)/shard_map/ppermute | solution.py:37
  31.8 17.2 %copy-start = (bf16[896,2304]{0,1:T(8,128)(2,1)S(1)}, bf16[896,2304]{0,1:T(8,128)(2,1)}, u32[]{:S(2)}) copy-start(bf16[896,2304]{0,1:T(8,128)(2,1)} %copy.60) | copy-start | bytes 12386308
  31.8 94.4 %collective-permute-start.2 = (bf16[896,2304]{0,1:T(8,128)(2,1)}, bf16[896,2304]{0,1:T(8,128)(2,1)}, u32[]{:S(2)}, u32[]{:S(2)}) collective-permute-start(bf16[896,2304]{0,1:T(8,128)(2,1)} %copy.60), channel_id=1, source_target_pairs={{3,2},{0,1},{7,6},{4,5},{11,10},{8,9},{15,14},{12,13},{19,18},{16,... | collective-permute-start | bytes 12386312 | tf_op jit(solution)/shard_map/ppermute | solution.py:37
  155.2 194.5 %reduce-scatter.5.cloned.1.call-start = ((), (), s32[]{:S(2)}) async-start(), calls=%async_computation.3 | async-start | bytes 8028160 | tf_op jit(solution)/shard_map/reduce_scatter | solution.py:68
  155.2 102.6 %collective-permute-start.1 = (bf16[896,2304]{0,1:T(8,128)(2,1)}, bf16[896,2304]{0,1:T(8,128)(2,1)S(1)}, u32[]{:S(2)}, u32[]{:S(2)}) collective-permute-start(bf16[896,2304]{0,1:T(8,128)(2,1)} %copy.59), channel_id=1, source_target_pairs={{0,2},{3,1},{4,6},{7,5},{8,10},{11,9},{12,14},{15,13},{16,18},{19,... | collective-permute-start | bytes 12386312 | tf_op jit(solution)/shard_map/ppermute | solution.py:37
  289.4 238.3 %all-gather.2.cloned.1.call-start = ((), (), s32[]{:S(2)}) async-start(), calls=%async_computation.4 | async-start | bytes 20070400 | tf_op jit(solution)/shard_map/all_gather | solution.py:98
  289.5 125.2 %collective-permute-start.3 = (bf16[6,224,896]{2,1,0:T(8,128)(2,1)}, bf16[6,224,896]{2,1,0:T(8,128)(2,1)}, u32[]{:S(2)}, u32[]{:S(2)}) collective-permute-start(bf16[6,224,896]{2,1,0:T(8,128)(2,1)} %bitcast.194), channel_id=1, source_target_pairs={{2,1},{1,2},{6,5},{5,6},{10,9},{9,10},{14,13},{13,14},{18,17},{17,... | collective-permute-start | bytes 7225352 | tf_op jit(solution)/shard_map/ppermute | solution.py:69
  349.7 65.0 %copy-start.9 = (bf16[1,6,224,896]{3,2,1,0:T(8,128)(2,1)S(1)}, bf16[1,6,224,896]{3,2,1,0:T(8,128)(2,1)}, u32[]{:S(2)}) copy-start(bf16[1,6,224,896]{3,2,1,0:T(8,128)(2,1)} %reduce-scatter.3.cloned.1.call-done) | copy-start | bytes 7225348
  349.7 67.3 %collective-permute-start.4 = (bf16[4,224,896]{2,1,0:T(8,128)(2,1)}, bf16[4,224,896]{2,1,0:T(8,128)(2,1)}, u32[]{:S(2)}, u32[]{:S(2)}) collective-permute-start(bf16[4,224,896]{2,1,0:T(8,128)(2,1)} %bitcast.198), channel_id=1, source_target_pairs={{2,1},{1,2},{6,5},{5,6},{10,9},{9,10},{14,13},{13,14},{18,17},{17,... | collective-permute-start | bytes 4816904 | tf_op jit(solution)/shard_map/ppermute | solution.py:69
  761.1 19.9 %collective-permute-start.5 = (bf16[1792,3584]{1,0:T(8,128)(2,1)}, bf16[1792,3584]{1,0:T(8,128)(2,1)}, u32[]{:S(2)}, u32[]{:S(2)}) collective-permute-start(bf16[1792,3584]{1,0:T(8,128)(2,1)} %add_convert_fusion), channel_id=1, source_target_pairs={{0,4},{4,0},{8,12},{12,8},{1,5},{5,1},{9,13},{13,9},{2,6},{6,2},{1... | collective-permute-start | bytes 38535176 | tf_op jit(solution)/shard_map/ppermute | solution.py:116
  765.6 15.4 %slice-start = ((s8[12845056]{0:T(1024)(128)(4,1)}), s8[262144]{0:T(1024)(128)(4,1)S(1)}, s32[]{:S(2)}) async-start(s8[12845056]{0:T(1024)(128)(4,1)} %bitcast.181), calls=%async_computation.5 | async-start | bytes 524288
  765.6 15.4 %slice-start.1 = ((s8[12845056]{0:T(1024)(128)(4,1)}), s8[4194304]{0:T(1024)(128)(4,1)S(1)}, s32[]{:S(2)}) async-start(s8[12845056]{0:T(1024)(128)(4,1)} %bitcast.181), calls=%async_computation.6 | async-start | bytes 8388608
  765.6 15.4 %slice-start.2 = ((s8[12845056]{0:T(1024)(128)(4,1)}), s8[4194304]{0:T(1024)(128)(4,1)S(1)}, s32[]{:S(2)}) async-start(s8[12845056]{0:T(1024)(128)(4,1)} %bitcast.181), calls=%async_computation.7 | async-start | bytes 8388608
  770.8 10.2 slice-start.3
  836.1 77.0 %collective-permute-start.6 = (bf16[896,768]{0,1:T(8,128)(2,1)}, bf16[896,768]{0,1:T(8,128)(2,1)S(1)}, u32[]{:S(2)}, u32[]{:S(2)}) collective-permute-start(bf16[896,768]{0,1:T(8,128)(2,1)} %get-tuple-element.33), channel_id=1, source_target_pairs={{2,0},{1,3},{6,4},{5,7},{10,8},{9,11},{14,12},{13,15},{18,16},{17,... | collective-permute-start | bytes 4128776 | tf_op jit(solution)/shard_map/ppermute | solution.py:40
  837.4 81.6 %collective-permute-start.7 = (bf16[896,768]{0,1:T(8,128)(2,1)}, bf16[896,768]{0,1:T(8,128)(2,1)S(1)}, u32[]{:S(2)}, u32[]{:S(2)}) collective-permute-start(bf16[896,768]{0,1:T(8,128)(2,1)} %get-tuple-element.31), channel_id=1, source_target_pairs={{2,1},{1,2},{6,5},{5,6},{10,9},{9,10},{14,13},{13,14},{18,17},{17,... | collective-permute-start | bytes 4128776 | tf_op jit(solution)/shard_map/ppermute | solution.py:40
  875.8 55.5 %collective-permute-start.8 = (bf16[896,768]{0,1:T(8,128)(2,1)}, bf16[896,768]{0,1:T(8,128)(2,1)}, u32[]{:S(2)}, u32[]{:S(2)}) collective-permute-start(bf16[896,768]{0,1:T(8,128)(2,1)} %get-tuple-element.36), channel_id=1, source_target_pairs={{2,0},{1,3},{6,4},{5,7},{10,8},{9,11},{14,12},{13,15},{18,16},{17,... | collective-permute-start | bytes 4128776 | tf_op jit(solution)/shard_map/ppermute | solution.py:40
  877.0 55.5 %collective-permute-start.9 = (bf16[896,768]{0,1:T(8,128)(2,1)}, bf16[896,768]{0,1:T(8,128)(2,1)}, u32[]{:S(2)}, u32[]{:S(2)}) collective-permute-start(bf16[896,768]{0,1:T(8,128)(2,1)} %get-tuple-element.34), channel_id=1, source_target_pairs={{2,1},{1,2},{6,5},{5,6},{10,9},{9,10},{14,13},{13,14},{18,17},{17,... | collective-permute-start | bytes 4128776 | tf_op jit(solution)/shard_map/ppermute | solution.py:40
  878.8 184.8 %collective-permute-start.12 = (bf16[896,768]{0,1:T(8,128)(2,1)}, bf16[896,768]{0,1:T(8,128)(2,1)}, u32[]{:S(2)}, u32[]{:S(2)}) collective-permute-start(bf16[896,768]{0,1:T(8,128)(2,1)} %get-tuple-element.32), channel_id=1, source_target_pairs={{2,3},{1,0},{6,7},{5,4},{10,11},{9,8},{14,15},{13,12},{18,19},{17,... | collective-permute-start | bytes 4128776 | tf_op jit(solution)/shard_map/ppermute | solution.py:40
  913.2 152.4 %collective-permute-start.13 = (bf16[896,768]{0,1:T(8,128)(2,1)}, bf16[896,768]{0,1:T(8,128)(2,1)}, u32[]{:S(2)}, u32[]{:S(2)}) collective-permute-start(bf16[896,768]{0,1:T(8,128)(2,1)} %get-tuple-element.35), channel_id=1, source_target_pairs={{2,3},{1,0},{6,7},{5,4},{10,11},{9,8},{14,15},{13,12},{18,19},{17,... | collective-permute-start | bytes 4128776 | tf_op jit(solution)/shard_map/ppermute | solution.py:40
  919.0 148.5 %collective-permute-start.14 = (bf16[896,768]{0,1:T(8,128)(2,1)}, bf16[896,768]{0,1:T(8,128)(2,1)}, u32[]{:S(2)}, u32[]{:S(2)}) collective-permute-start(bf16[896,768]{0,1:T(8,128)(2,1)} %get-tuple-element.38), channel_id=1, source_target_pairs={{2,3},{1,0},{6,7},{5,4},{10,11},{9,8},{14,15},{13,12},{18,19},{17,... | collective-permute-start | bytes 4128776 | tf_op jit(solution)/shard_map/ppermute | solution.py:40
  931.2 138.2 %collective-permute-start.10 = (bf16[896,768]{0,1:T(8,128)(2,1)}, bf16[896,768]{0,1:T(8,128)(2,1)}, u32[]{:S(2)}, u32[]{:S(2)}) collective-permute-start(bf16[896,768]{0,1:T(8,128)(2,1)} %get-tuple-element.39), channel_id=1, source_target_pairs={{2,0},{1,3},{6,4},{5,7},{10,8},{9,11},{14,12},{13,15},{18,16},{17,... | collective-permute-start | bytes 4128776 | tf_op jit(solution)/shard_map/ppermute | solution.py:40
  932.5 136.9 %collective-permute-start.11 = (bf16[896,768]{0,1:T(8,128)(2,1)}, bf16[896,768]{0,1:T(8,128)(2,1)}, u32[]{:S(2)}, u32[]{:S(2)}) collective-permute-start(bf16[896,768]{0,1:T(8,128)(2,1)} %get-tuple-element.37), channel_id=1, source_target_pairs={{2,1},{1,2},{6,5},{5,6},{10,9},{9,10},{14,13},{13,14},{18,17},{17,... | collective-permute-start | bytes 4128776 | tf_op jit(solution)/shard_map/ppermute | solution.py:40
  (10 other events, 54.5 us)
Sparse Core Ops, SparseCore 0:
  155.3 90.1 reduce-scatter.2
  289.5 60.1 reduce-scatter.4
  428.6 99.0 all-gather.1

commit v2 on v0

v2 whole, which is shorter than its diff:
```python
import functools
import math

import jax
import jax.numpy as jnp
from jax import lax
from jax.experimental import pallas as pl
from jax.experimental.pallas import tpu as pltpu
from jax.sharding import PartitionSpec as P

M = 3584
N = 18432

coef_linear = 3.4445
coef_cubic = -4.775
coef_quintic = 2.0315

TILE = 256
STRIP = 128
VMEM_BYTES = 56 * 2**20

EARLY = [(1, 2), (1, 1), (2, 2), (3, 3), (3, 2), (3, 1)]
LATE_A = [(0, 0), (0, 1)]
LATE_B = [(0, 2), (0, 3)]
GATHERED = [[(1, 2), (1, 1), (2, 2)], [(0, 0), (3, 3), (0, 1), (3, 2)], [(0, 2), (3, 1), (0, 3)]]


def mirror(pair):
    return pair if sum(pair) == 3 and pair[0] != pair[1] else (3 - pair[0], 3 - pair[1])


def take_kernel(index, x_ref, out_ref, sq_ref):
    @pl.when(pl.program_id(0) == 0)
    def _():
        sq_ref[...] = jnp.zeros_like(sq_ref)

    x = x_ref[...]
    out_ref[...] = x.astype(jnp.bfloat16)
    sq_ref[...] += jnp.sum(x * x, axis=0, keepdims=True)


def take(momentum, index):
    rows, cols = momentum.shape
    width = cols // 2
    step = rows // 4
    return pl.pallas_call(
        take_kernel,
        grid_spec=pltpu.PrefetchScalarGridSpec(
            num_scalar_prefetch=1,
            grid=(4,),
            in_specs=[pl.BlockSpec((step, width), lambda t, index: (t, index[0]))],
            out_specs=[
                pl.BlockSpec((step, width), lambda t, index: (t, 0)),
                pl.BlockSpec((1, width), lambda t, index: (0, 0)),
            ],
        ),
        out_shape=[
            jax.ShapeDtypeStruct((rows, width), jnp.bfloat16),
            jax.ShapeDtypeStruct((1, width), jnp.float32),
        ],
        compiler_params=pltpu.CompilerParams(vmem_limit_bytes=VMEM_BYTES),
        cost_estimate=pl.CostEstimate(
            flops=2 * rows * width, bytes_accessed=6 * rows * width, transcendentals=0
        ),
        name="take_half",
    )(index, momentum)


def transpose_block(ref, rows, source, target):
    @pl.loop(0, rows // STRIP)
    def _(s):
        part = ref[
            pl.ds(pl.multiple_of(source[0] * rows, STRIP), rows),
            pl.ds(pl.multiple_of(source[1] * rows + s * STRIP, STRIP), STRIP),
        ]
        ref[
            pl.ds(pl.multiple_of(target[0] * rows + s * STRIP, STRIP), STRIP),
            pl.ds(pl.multiple_of(target[1] * rows, STRIP), rows),
        ] = part.T


def poly_place(core, b):
    i = jnp.where(core == 0, jnp.where(b < 4, 0, 3), jnp.where(b < 3, 1, 2))
    j = jnp.where(core == 0, jnp.where(b < 4, b, 3), jnp.where(b < 3, b + 1, b - 1))
    return i, j


def poly_kernel(flags, first, second, third, out_ref, gram, sems):
    rows = out_ref.shape[1]
    part = rows // 4
    left = flags[0]
    b = pl.program_id(0)

    @pl.when(b == 0)
    def _():
        copies, turned = [], []
        for group, pairs in zip((first, second, third), GATHERED):
            for k, (i, j) in enumerate(pairs):
                if i != j and i + j == 3:
                    i, j = jnp.where(left == 1, j, i), jnp.where(left == 1, i, j)
                for q in range(4):
                    copies.append(
                        pltpu.make_async_copy(
                            group.at[q, k],
                            gram.at[
                                pl.ds(pl.multiple_of(i * rows + q * part, 16), part),
                                pl.ds(pl.multiple_of(j * rows, STRIP), rows),
                            ],
                            sems.at[len(copies)],
                        )
                    )
                if pairs[k][0] != pairs[k][1]:
                    turned.append((i, j))
        for copy in copies:
            copy.start()
        for copy in copies:
            copy.wait()
        for i, j in turned:
            transpose_block(gram, rows, (i, j), (j, i))

    i, j = poly_place(flags[1], b)
    at_i = pl.multiple_of(i * rows, STRIP)
    width = (rows // STRIP + 1) // 2 * STRIP
    for start in range(0, rows, width):
        size = min(width, rows - start)
        at_j = pl.multiple_of(j * rows + start, STRIP)
        squared = jnp.dot(
            gram[pl.ds(at_i, rows), :], gram[:, pl.ds(at_j, size)], preferred_element_type=jnp.float32
        )
        here = gram[pl.ds(at_i, rows), pl.ds(at_j, size)].astype(jnp.float32)
        out_ref[0, :, start : start + size] = (coef_cubic * here + coef_quintic * squared).astype(jnp.bfloat16)


def poly_blocks(flags, groups):
    rows = groups[0].shape[3]
    order = 4 * rows
    return pl.pallas_call(
        poly_kernel,
        grid_spec=pltpu.PrefetchScalarGridSpec(
            num_scalar_prefetch=1,
            grid=(5,),
            in_specs=[pl.BlockSpec(memory_space=pl.ANY)] * 3,
            out_specs=pl.BlockSpec((1, rows, rows), lambda b, flags: (b, 0, 0)),
            scratch_shapes=[pltpu.VMEM((order, order), jnp.bfloat16), pltpu.SemaphoreType.DMA((40,))],
        ),
        out_shape=jax.ShapeDtypeStruct((5, rows, rows), jnp.bfloat16),
        compiler_params=pltpu.CompilerParams(vmem_limit_bytes=VMEM_BYTES),
        cost_estimate=pl.CostEstimate(
            flops=10 * rows * rows * order, bytes_accessed=30 * rows * rows, transcendentals=0
        ),
        name="poly_blocks",
    )(flags, *groups)


def product_kernel(flags, own, pair, inverse, s0, s1, s2, s3, o0, o1, o2, o3, sq_ref, poly, raw, sems):
    rows = s0.shape[0]

    @pl.when(pl.program_id(0) == 0)
    def _():
        sq_ref[...] = jnp.zeros_like(sq_ref)
        copies = []
        for source, core in ((own, flags[1]), (pair, 1 - flags[1])):
            for b in range(5):
                i, j = poly_place(core, b)
                copies.append(
                    pltpu.make_async_copy(
                        source.at[b],
                        poly.at[
                            pl.ds(pl.multiple_of(i * rows, STRIP), rows),
                            pl.ds(pl.multiple_of(j * rows, STRIP), rows),
                        ],
                        sems.at[len(copies)],
                    )
                )
        for copy in copies:
            copy.start()
        for copy in copies:
            copy.wait()
        for i in range(4):
            for j in range(i + 1, 4):
                transpose_block(poly, rows, (i, j), (j, i))

    for r, s_ref in enumerate((s0, s1, s2, s3)):
        raw[r * rows : (r + 1) * rows, :] = s_ref[...]
    for r, (s_ref, o_ref) in enumerate(zip((s0, s1, s2, s3), (o0, o1, o2, o3))):
        product = jnp.dot(
            poly[r * rows : (r + 1) * rows, :], raw[...], preferred_element_type=jnp.float32
        )
        newton = inverse[0] * (coef_linear * s_ref[...].astype(jnp.float32) + product)
        sq_ref[...] += jnp.sum(newton * newton, axis=0, keepdims=True)
        o_ref[...] = newton.astype(jnp.bfloat16)


def product(flags, own, pair, inverse, blocks, first, tiles):
    rows = own.shape[1]
    order = 4 * rows
    here = pl.BlockSpec((rows, TILE), lambda t, flags: (0, first + t))
    there = pl.BlockSpec((rows, TILE), lambda t, flags: (0, t))
    *newton, squares = pl.pallas_call(
        product_kernel,
        grid_spec=pltpu.PrefetchScalarGridSpec(
            num_scalar_prefetch=1,
            grid=(tiles,),
            in_specs=[
                pl.BlockSpec(memory_space=pl.ANY),
                pl.BlockSpec(memory_space=pl.ANY),
                pl.BlockSpec(memory_space=pltpu.SMEM),
            ]
            + [here] * 4,
            out_specs=[there] * 4 + [pl.BlockSpec((1, TILE), lambda t, flags: (0, 0))],
            scratch_shapes=[
                pltpu.VMEM((order, order), jnp.bfloat16),
                pltpu.VMEM((order, TILE), jnp.bfloat16),
                pltpu.SemaphoreType.DMA((10,)),
            ],
        ),
        out_shape=[jax.ShapeDtypeStruct((rows, tiles * TILE), jnp.bfloat16)] * 4
        + [jax.ShapeDtypeStruct((1, TILE), jnp.float32)],
        compiler_params=pltpu.CompilerParams(vmem_limit_bytes=VMEM_BYTES),
        cost_estimate=pl.CostEstimate(
            flops=2 * order * order * tiles * TILE,
            bytes_accessed=20 * rows * rows + 4 * order * tiles * TILE,
            transcendentals=0,
        ),
        name="product",
    )(flags, own, pair, inverse, *blocks)
    return newton, jnp.sum(squares)


def finish_kernel(flags, factor, own, near, middle, far, *rest):
    out_ref = rest[-1]
    is_hub = flags[2] == 1

    @pl.when((pl.program_id(0) == 0) & is_hub)
    def _():
        out_ref[...] = own[...].astype(jnp.float32) * factor[0]

    @pl.when((pl.program_id(0) == 0) & jnp.logical_not(is_hub))
    def _():
        out_ref[...] = near[...].astype(jnp.float32) * factor[0]

    @pl.when((pl.program_id(0) == 1) & is_hub)
    def _():
        out_ref[...] = middle[...].astype(jnp.float32) * factor[0]

    @pl.when((pl.program_id(0) == 1) & jnp.logical_not(is_hub))
    def _():
        out_ref[...] = far[...].astype(jnp.float32) * factor[0]


def finish(flags, factor, parts, first, shape, before):
    rows, cols = shape
    tiles = parts[0].shape[1] // TILE
    half = cols // 2 // TILE
    near_part = pl.BlockSpec((rows, TILE), lambda p, t, flags: (0, jnp.where(p == 0, t, tiles - 1)))
    far_part = pl.BlockSpec((rows, TILE), lambda p, t, flags: (0, jnp.where(p == 0, 0, t)))
    place = pl.BlockSpec(
        (rows, TILE),
        lambda p, t, flags: (0, jnp.where(p == 0, flags[0], 1 - flags[0]) * half + first + t),
    )
    specs = [pl.BlockSpec(memory_space=pltpu.SMEM), near_part, near_part, far_part, far_part]
    operands = [flags, factor, *parts]
    aliases = {}
    if before is not None:
        specs.append(pl.BlockSpec(memory_space=pl.ANY))
        aliases = {len(operands): 0}
        operands.append(before)
    return pl.pallas_call(
        finish_kernel,
        grid_spec=pltpu.PrefetchScalarGridSpec(
            num_scalar_prefetch=1, grid=(2, tiles), in_specs=specs, out_specs=place
        ),
        out_shape=jax.ShapeDtypeStruct(shape, jnp.float32),
        input_output_aliases=aliases,
        compiler_params=pltpu.CompilerParams(vmem_limit_bytes=VMEM_BYTES),
        cost_estimate=pl.CostEstimate(
            flops=2 * rows * TILE * tiles, bytes_accessed=16 * rows * TILE * tiles, transcendentals=0
        ),
        name="finish",
    )(*operands)


def per_device(momentum):
    rows, cols = momentum.shape
    width = cols // 2
    z = lax.axis_index("row")
    core = lax.axis_index("col") % 2
    left = z < 2
    is_hub = (z == 1) | (z == 2)
    flags = jnp.stack([left.astype(jnp.int32), core.astype(jnp.int32), is_hub.astype(jnp.int32)])
    near_index = left.astype(jnp.int32).reshape(1)

    far, far_sq = take(momentum, 1 - near_index)
    middle = lax.ppermute(far, "row", [(1, 2), (2, 1)])
    near, near_sq = take(momentum, near_index)
    beside = lax.ppermute(near, "row", [(0, 1), (3, 2)])
    norm_sum = lax.psum(jnp.sum(far_sq) + jnp.sum(near_sq), ("col", "row"))
    spectral_edge = 1.0 + math.sqrt(M / N)
    inverse = 1.0 / (jnp.sqrt(norm_sum / M) * spectral_edge + 1e-07)

    far, middle, inverse = lax.optimization_barrier((far, middle, inverse))
    distant = lax.ppermute(far, "row", [(0, 2), (3, 1)])
    blocks = [distant, middle, near, beside]

    def partial_gram(pair):
        i, j = pair
        value = lax.dot_general(
            blocks[i], blocks[j], (((1,), (1,)), ((), ())), preferred_element_type=jnp.float32
        ).astype(jnp.bfloat16)
        if i != j and i + j == 3:
            value = jnp.where(left, value.T, value)
        return value

    mine, other = {}, {}
    for pairs in (EARLY, LATE_A, LATE_B):
        stack = jnp.stack([partial_gram(pair).reshape(4, rows // 4, rows) for pair in pairs], axis=1)
        summed = lax.psum_scatter(stack, "col", scatter_dimension=0, tiled=False)
        received = lax.ppermute(summed, "row", [(1, 2), (2, 1)])
        for k, pair in enumerate(pairs):
            mine[pair], other[mirror(pair)] = summed[k], received[k]

    groups = []
    for pairs in GATHERED:
        gram = jnp.stack([mine[pair].astype(jnp.float32) + other[pair].astype(jnp.float32) for pair in pairs])
        gram = (gram * (inverse * inverse)).astype(jnp.bfloat16)
        groups.append(lax.all_gather(gram, "col", axis=0, tiled=False))

    own = poly_blocks(flags, groups)
    pair = lax.ppermute(own, "col", [(c, c ^ 1) for c in range(4)])

    tiles = width // TILE
    bounds = sorted({0, tiles * 2 // 9, tiles * 5 // 9, tiles})
    newton_sq = jnp.float32(0.0)
    parts = []
    for first, last in zip(bounds[:-1], bounds[1:]):
        newton, squares = product(flags, own, pair, inverse.reshape(1), blocks, first, last - first)
        newton_sq += squares
        parts.append(
            (
                newton[2],
                lax.ppermute(newton[3], "row", [(1, 0), (2, 3)]),
                lax.ppermute(newton[1], "row", [(1, 2), (2, 1)]),
                lax.ppermute(newton[0], "row", [(2, 0), (1, 3)]),
            )
        )
    newton_sq = lax.psum(jnp.where(is_hub, newton_sq, 0.0), ("col", "row"))
    factor = (1.0 / (jnp.sqrt(newton_sq) / math.sqrt(M * N) + 1e-07)).reshape(1)
    out = None
    for first, part in zip(bounds[:-1], parts):
        out = finish(flags, factor, part, first, (rows, cols), out)
    return out


def per_device_general(momentum):
    norm_sum = lax.psum(jnp.sum(momentum * momentum), ("col", "row"))
    spectral_edge = 1.0 + math.sqrt(M / N)
    scaled = (momentum / (jnp.sqrt(norm_sum / M) * spectral_edge + 1e-07)).astype(jnp.bfloat16)
    columns = lax.all_gather(scaled, "row", axis=0, tiled=True)
    gram_tile = lax.psum_scatter(
        lax.dot_general(
            columns, scaled, (((1,), (1,)), ((), ())), preferred_element_type=jnp.float32
        ).astype(jnp.bfloat16),
        "col",
        scatter_dimension=0,
        tiled=True,
    )
    left_rows = lax.all_gather(gram_tile, "row", axis=1, tiled=True)
    squared = jnp.dot(
        left_rows,
        lax.all_gather(gram_tile, "col", axis=0, tiled=True),
        preferred_element_type=jnp.float32,
    )
    poly = (coef_cubic * gram_tile.astype(jnp.float32) + coef_quintic * squared).astype(jnp.bfloat16)
    product = lax.dot_general(
        lax.all_gather(poly, "col", axis=0, tiled=True),
        columns,
        (((0,), (0,)), ((), ())),
        preferred_element_type=jnp.float32,
    )
    newton = coef_linear * scaled.astype(jnp.float32) + product
    newton_sq = lax.psum(jnp.sum(newton * newton), ("col", "row"))
    update_rms = jnp.sqrt(newton_sq) / math.sqrt(M * N)
    return newton / (update_rms + 1e-07)


def solution(mesh):
    def update(momentum):
        n_row, n_col = mesh.shape["row"], mesh.shape["col"]
        rows = momentum.shape[0] // (mesh.shape["groups"] * n_row)
        cols = momentum.shape[1] // n_col
        hubs = n_row == 4 and n_col == 4 and rows % STRIP == 0 and cols % (2 * TILE) == 0
        return jax.shard_map(
            per_device if hubs else per_device_general,
            mesh=mesh,
            in_specs=(P(("groups", "row"), "col"),),
            out_specs=P(("groups", "row"), "col"),
            check_vma=False,
        )(momentum)

    return update
```

time: 1040 us -> 931 us (0.90)
  waiting for transfers between devices: 821 us -> 302 us
  blocking collectives: 69.2 us -> 272 us
  Pallas kernels: 0 us -> 188 us
  starting transfers between devices: 0.34 us -> 29.1 us
  local copies, waits for them, and re-layouts: 0 us -> 20.3 us
  matrix products: 93.4 us -> 73.4 us
  other arithmetic: 36.9 us -> 21.2 us
    all_gather x4 -> x3, waiting for transfers between devices: 763 us -> 141 us  [per_device(): groups.append(lax.all_gather(gram, 'col', axis=0, tiled=False))]
    psum x2, blocking collectives: 69.2 us -> 272 us  [the longest x1 161 us: per_device(): newton_sq = lax.psum(jnp.where(is_hub, newton_sq, 0.0), ('col', 'row'))]
    pallas_call x0 -> x9, Pallas kernels: none -> 188 us  [the longest x3 106 us: product(): pl.pallas_call(product_kernel, grid_spec=pltpu.PrefetchScalarGridSpec(num...]
    ppermute x0 -> x16, waiting for transfers between devices: none -> 98.4 us  [the longest x1 85.8 us: per_device(): distant = lax.ppermute(far, 'row', [(0, 2), (3, 1)])]
    ppermute x0 -> x16, starting transfers between devices: none -> 28.7 us  [the longest x1 7.79 us: per_device(): beside = lax.ppermute(near, 'row', [(0, 1), (3, 2)])]
    dot_general x3 -> x10, matrix products: 93.4 us -> 73.4 us  [partial_gram(): lax.dot_general(blocks[i], blocks[j], (((1,), (1,)), ((), ())), preferred...]
    div x1 -> x0, other arithmetic: 17.6 us -> none  [per_device(): return newton / (update_rms + 1e-07)]
    unnamed x0 -> x39, local copies, waits for them, and re-layouts: none -> 15.4 us
  transfers between devices with their start and end apart: 5 -> 22, of which waited for: 5 -> 7; matrix products, arithmetic and copies ran while one was open for 0% -> 8% of each run, Pallas kernels for 0% -> 10%
where the time goes in v2:
time: 931 us; the launch traced here: 926 us
  waiting for transfers between devices  302 us (32%)
  blocking collectives  272 us (29%)
  Pallas kernels  188 us (20%)
  matrix products  73.4 us (8%)
  starting transfers between devices  29.1 us (3%)
  other arithmetic  21.2 us (2%)
  local copies, waits for them, and re-layouts  20.3 us (2%)
  between operations  19 us (2%)
    psum x1, blocking collectives, per_device(): newton_sq = lax.psum(jnp.where(is_hub, newton_sq, 0.0), ('col', 'row'))  161 us
    all_gather x3, waiting for transfers between devices, per_device(): groups.append(lax.all_gather(gram, 'col', axis=0, tiled=False))  141 us
    psum x1, blocking collectives, per_device(): norm_sum = lax.psum(jnp.sum(far_sq) + jnp.sum(near_sq), ('col', 'row'))  111 us
    pallas_call x3, Pallas kernels, product(): pl.pallas_call(product_kernel, grid_spec=pltpu.PrefetchScalarGridSpec(num...  106 us
    ppermute x1, waiting for transfers between devices, per_device(): distant = lax.ppermute(far, 'row', [(0, 2), (3, 1)])  85.8 us
    dot_general x10, matrix products, partial_gram(): lax.dot_general(blocks[i], blocks[j], (((1,), (1,)), ((), ())), preferred...  73.4 us
    reduce_scatter x3, waiting for transfers between devices, per_device(): summed = lax.psum_scatter(stack, 'col', scatter_dimension=0, tiled=False)  62.8 us
    pallas_call x1, Pallas kernels, poly_blocks(): pl.pallas_call(poly_kernel, grid_spec=pltpu.PrefetchScalarGridSpec(num_sc...  47.4 us
  transfers between devices with their start and end apart: 22, of which 7 were waited for; matrix products, arithmetic and copies ran while one was open for 8% of the time, Pallas kernels for 10%

profile of v2, /device:TPU:0, one launch (start us, length us, event | category | flops | bytes accessed | tf_op | source)
XLA Modules:
  0.0 925.5 jit_solution(10633005089795218483)
XLA Ops:
  21.1 7.8 collective-permute-start.1
  32.2 111.0 %psum.14 = f32[]{:T(128)} all-reduce(f32[]{:T(128)S(6)} %add.70), channel_id=1, replica_groups=mesh['groups'=2,'col'=4,'row'=4] {'col','row'}, use_global_device_ids=true, to_apply=%region_2.3 | all-reduce | flops 1 | bytes 8 | tf_op jit(solution)/shard_map/psum | solution.py:297
  143.9 9.2 convolution_convert_fusion.7
  153.1 6.6 convolution_convert_fusion.9
  163.3 7.9 convolution_convert_fusion.8
  174.4 8.0 convolution_convert_fusion.6
  191.6 7.9 convolution_convert_fusion.4
  202.8 85.8 %collective-permute-done.3.s0 = bf16[896,2304]{1,0:T(8,128)(2,1)S(1)} collective-permute-done((bf16[896,2304]{1,0:T(8,128)(2,1)}, bf16[896,2304]{1,0:T(8,128)(2,1)S(1)}, u32[]{:S(2)}, u32[]{:S(2)}) %collective-permute-start.3) | collective-permute-done | bytes 4128800 | tf_op jit(solution)/shard_map/ppermute | solution.py:302
  288.6 8.1 convolution_convert_fusion
  300.5 6.6 convolution_convert_fusion.1
  309.3 8.0 convolution_convert_fusion.2
  326.0 22.3 %reduce-scatter.8.cloned.1.call-done = bf16[1,2,224,896]{3,2,1,0:T(8,128)(2,1)} async-done(((bf16[4,2,224,896]{3,2,1,0:T(8,128)(2,1)}), bf16[1,2,224,896]{3,2,1,0:T(8,128)(2,1)}) %reduce-scatter.8.cloned.1.call-update) | async-done | bytes 802832 | tf_op jit(solution)/shard_map/reduce_scatter | solution.py:317
  349.0 40.4 %reduce-scatter.6.cloned.1.call-done = bf16[1,2,224,896]{3,2,1,0:T(8,128)(2,1)} async-done(((bf16[4,2,224,896]{3,2,1,0:T(8,128)(2,1)}), bf16[1,2,224,896]{3,2,1,0:T(8,128)(2,1)}) %reduce-scatter.6.cloned.1.call-update) | async-done | bytes 802832 | tf_op jit(solution)/shard_map/reduce_scatter | solution.py:317
  404.5 53.1 %all-gather.4.cloned.1.call-done.first = bf16[4,3,224,896]{3,2,1,0:T(8,128)(2,1)} async-done(((bf16[1,3,224,896]{3,2,1,0:T(8,128)(2,1)}), bf16[4,3,224,896]{3,2,1,0:T(8,128)(2,1)}) %all-gather.4.cloned.1.call-update) | async-done | bytes 4816912 | tf_op jit(solution)/shard_map/all_gather | solution.py:326
  457.6 39.5 %all-gather.8.cloned.1.call-done.third = bf16[4,3,224,896]{3,2,1,0:T(8,128)(2,1)} async-done(((bf16[1,3,224,896]{3,2,1,0:T(8,128)(2,1)}), bf16[4,3,224,896]{3,2,1,0:T(8,128)(2,1)}) %all-gather.8.cloned.1.call-update) | async-done | bytes 4816912 | tf_op jit(solution)/shard_map/all_gather | solution.py:326
  497.1 48.6 %all-gather.6.cloned.1.call-done.second = bf16[4,4,224,896]{3,2,1,0:T(8,128)(2,1)} async-done(((bf16[1,4,224,896]{3,2,1,0:T(8,128)(2,1)}), bf16[4,4,224,896]{3,2,1,0:T(8,128)(2,1)}) %all-gather.6.cloned.1.call-update) | async-done | bytes 6422544 | tf_op jit(solution)/shard_map/all_gather | solution.py:326
  545.7 47.4 %poly_blocks.1.own = bf16[5,896,896]{2,1,0:T(8,128)(2,1)} custom-call(s32[3]{0:T(128)} %pad_add_fusion.flags, bf16[4,3,224,896]{3,2,1,0:T(8,128)(2,1)} %all-gather.4.cloned.1.call-done.first, bf16[4,4,224,896]{3,2,1,0:T(8,128)(2,1)} %all-gather.6.cloned.1.call-done.second, bf16[4,3,224,896]{3,2,1,0:T(8,128)(2,1)} %all-gather.8.cloned.1.call-done.third), custom_call_target="tpu_custom_call" | custom-call | flops 28772925440 | bytes 24084480 | tf_op jit(solution)/shard_map/poly_blocks/pallas_call | solution.py:137
  593.4 12.5 %collective-permute-done.6.pair = bf16[5,896,896]{2,1,0:T(8,128)(2,1)S(1)} collective-permute-done((bf16[5,896,896]{2,1,0:T(8,128)(2,1)}, bf16[5,896,896]{2,1,0:T(8,128)(2,1)S(1)}, u32[]{:S(2)}, u32[]{:S(2)}) %collective-permute-start.6) | collective-permute-done | bytes 8028192 | tf_op jit(solution)/shard_map/ppermute | solution.py:329
  609.2 35.4 %product.4 = (bf16[896,768]{1,0:T(8,128)(2,1)}, bf16[896,768]{1,0:T(8,128)(2,1)}, bf16[896,768]{1,0:T(8,128)(2,1)}, bf16[896,768]{1,0:T(8,128)(2,1)}, f32[1,256]{1,0:T(1,128)}) custom-call(s32[3]{0:T(128)} %pad_add_fusion.flags, bf16[5,896,896]{2,1,0:T(8,128)(2,1)} %poly_blocks.1.own, bf16[5,896,896]{2,1,0:T(8,128)(2,1)} %copy-done.11, f32[1]{0:T(128)} %bitcast.48.inverse, ...), custom_call_target="tpu_custom_call" | custom-call | flops 19730006016 | bytes 27066368 | tf_op jit(solution)/shard_map/product/pallas_call | solution.py:199
  646.1 28.2 %product.3 = (bf16[896,512]{1,0:T(8,128)(2,1)}, bf16[896,512]{1,0:T(8,128)(2,1)}, bf16[896,512]{1,0:T(8,128)(2,1)}, bf16[896,512]{1,0:T(8,128)(2,1)}, f32[1,256]{1,0:T(1,128)}) custom-call(s32[3]{0:T(128)} %pad_add_fusion.flags, bf16[5,896,896]{2,1,0:T(8,128)(2,1)} %poly_blocks.1.own, bf16[5,896,896]{2,1,0:T(8,128)(2,1)} %copy-done.11, f32[1]{0:T(128)} %bitcast.48.inverse, ...), custom_call_target="tpu_custom_call" | custom-call | flops 13153337344 | bytes 23396352 | tf_op jit(solution)/shard_map/product/pallas_call | solution.py:199
  677.6 42.4 %product.5 = (bf16[896,1024]{1,0:T(8,128)(2,1)}, bf16[896,1024]{1,0:T(8,128)(2,1)}, bf16[896,1024]{1,0:T(8,128)(2,1)}, bf16[896,1024]{1,0:T(8,128)(2,1)}, f32[1,256]{1,0:T(1,128)}) custom-call(s32[3]{0:T(128)} %pad_add_fusion.flags, bf16[5,896,896]{2,1,0:T(8,128)(2,1)} %poly_blocks.1.own, bf16[5,896,896]{2,1,0:T(8,128)(2,1)} %copy-done.11, ...), custom_call_target="tpu_custom_call" | custom-call | flops 26306674688 | bytes 30736384 | tf_op jit(solution)/shard_map/product/pallas_call | solution.py:199
  732.3 161.4 %psum.15 = f32[]{:T(128)} all-reduce(f32[]{:T(128)S(6)} %select_n.27), channel_id=1, replica_groups=mesh['groups'=2,'col'=4,'row'=4] {'col','row'}, use_global_device_ids=true, to_apply=%region_9.10 | all-reduce | flops 1 | bytes 8 | tf_op jit(solution)/shard_map/psum | solution.py:346
  900.0 7.4 finish.4.rest_0_
  908.7 9.6 %finish.5 = f32[896,4608]{1,0:T(8,128)} custom-call(s32[3]{0:T(128)} %pad_add_fusion.flags, f32[1]{0:T(128)} %bitcast.49.factor, bf16[896,1024]{1,0:T(8,128)(2,1)} %get-tuple-element.37.own, bf16[896,1024]{1,0:T(8,128)(2,1)} %copy-done, bf16[896,1024]{1,0:T(8,128)(2,1)} %collective-permute-done.8.middle, ...), custom_call_target="tpu_custom_call", output_to_operand_aliasing={{}: (6, {})} | custom-call | flops 1835008 | bytes 14680064 | tf_op jit(solution)/shard_map/finish/pallas_call | solution.py:268
  (104 shorter events, 91.5 us)
Async XLA Ops:
  6.5 317.3 %reduce-scatter.4.cloned.1.call-start = ((), (), s32[]{:S(2)}) async-start(), calls=%async_computation.3 | async-start | bytes 12042240 | tf_op jit(solution)/shard_map/reduce_scatter | solution.py:317
  12.5 140.7 %collective-permute-start = (bf16[896,2304]{1,0:T(8,128)(2,1)}, bf16[896,2304]{1,0:T(8,128)(2,1)}, u32[]{:S(2)}, u32[]{:S(2)}) collective-permute-start(bf16[896,2304]{1,0:T(8,128)(2,1)} %get-tuple-element.33), channel_id=1, source_target_pairs={{1,2},{2,1},{5,6},{6,5},{9,10},{10,9},{13,14},{14,13},{17,18},{18,... | collective-permute-start | bytes 12386312 | tf_op jit(solution)/shard_map/ppermute | solution.py:294
  21.1 153.3 %collective-permute-start.1 = (bf16[896,2304]{1,0:T(8,128)(2,1)}, bf16[896,2304]{1,0:T(8,128)(2,1)}, u32[]{:S(2)}, u32[]{:S(2)}) collective-permute-start(bf16[896,2304]{1,0:T(8,128)(2,1)} %get-tuple-element.31.s2), channel_id=1, source_target_pairs={{0,1},{3,2},{4,5},{7,6},{8,9},{11,10},{12,13},{15,14},{16,17},{19,... | collective-permute-start | bytes 12386312 | tf_op jit(solution)/shard_map/ppermute | solution.py:296
  200.8 147.5 %reduce-scatter.8.cloned.1.call-start = ((), (), s32[]{:S(2)}) async-start(), calls=%async_computation.7 | async-start | bytes 4014080 | tf_op jit(solution)/shard_map/reduce_scatter | solution.py:317
  200.9 87.8 %collective-permute-start.3 = (bf16[896,2304]{1,0:T(8,128)(2,1)}, bf16[896,2304]{1,0:T(8,128)(2,1)S(1)}, u32[]{:S(2)}, u32[]{:S(2)}) collective-permute-start(bf16[896,2304]{1,0:T(8,128)(2,1)} %get-tuple-element.33), channel_id=1, source_target_pairs={{0,2},{3,1},{4,6},{7,5},{8,10},{11,9},{12,14},{15,13},{16,18},{19,... | collective-permute-start | bytes 12386312 | tf_op jit(solution)/shard_map/ppermute | solution.py:302
  309.2 80.2 %reduce-scatter.6.cloned.1.call-start = ((), (), s32[]{:S(2)}) async-start(), calls=%async_computation.5 | async-start | bytes 4014080 | tf_op jit(solution)/shard_map/reduce_scatter | solution.py:317
  323.8 133.8 %all-gather.4.cloned.1.call-start = ((), (), s32[]{:S(2)}) async-start(), calls=%async_computation.4 | async-start | bytes 6021120 | tf_op jit(solution)/shard_map/all_gather | solution.py:326
  323.9 68.1 %collective-permute-start.2 = (bf16[6,224,896]{2,1,0:T(8,128)(2,1)}, bf16[6,224,896]{2,1,0:T(8,128)(2,1)}, u32[]{:S(2)}, u32[]{:S(2)}) collective-permute-start(bf16[6,224,896]{2,1,0:T(8,128)(2,1)} %bitcast.134), channel_id=1, source_target_pairs={{1,2},{2,1},{5,6},{6,5},{9,10},{10,9},{13,14},{14,13},{17,18},{18,... | collective-permute-start | bytes 7225352 | tf_op jit(solution)/shard_map/ppermute | solution.py:318
  348.3 41.8 %collective-permute-start.5 = (bf16[2,224,896]{2,1,0:T(8,128)(2,1)}, bf16[2,224,896]{2,1,0:T(8,128)(2,1)S(1)}, u32[]{:S(2)}, u32[]{:S(2)}) collective-permute-start(bf16[2,224,896]{2,1,0:T(8,128)(2,1)} %bitcast.143), channel_id=1, source_target_pairs={{1,2},{2,1},{5,6},{6,5},{9,10},{10,9},{13,14},{14,13},{17,18},{18,... | collective-permute-start | bytes 2408456 | tf_op jit(solution)/shard_map/ppermute | solution.py:318
  389.4 0.7 collective-permute-start.4
  398.3 98.8 %all-gather.8.cloned.1.call-start = ((), (), s32[]{:S(2)}) async-start(), calls=%async_computation.8 | async-start | bytes 6021120 | tf_op jit(solution)/shard_map/all_gather | solution.py:326
  402.4 143.3 %all-gather.6.cloned.1.call-start = ((), (), s32[]{:S(2)}) async-start(), calls=%async_computation.6 | async-start | bytes 8028160 | tf_op jit(solution)/shard_map/all_gather | solution.py:326
  593.0 12.9 %collective-permute-start.6 = (bf16[5,896,896]{2,1,0:T(8,128)(2,1)}, bf16[5,896,896]{2,1,0:T(8,128)(2,1)S(1)}, u32[]{:S(2)}, u32[]{:S(2)}) collective-permute-start(bf16[5,896,896]{2,1,0:T(8,128)(2,1)} %poly_blocks.1.own), channel_id=1, source_target_pairs={{0,4},{4,0},{8,12},{12,8},{1,5},{5,1},{9,13},{13,9},{2,6},{6,2},{1... | collective-permute-start | bytes 24084488 | tf_op jit(solution)/shard_map/ppermute | solution.py:329
  644.6 81.8 %collective-permute-start.10 = (bf16[896,768]{1,0:T(8,128)(2,1)}, bf16[896,768]{1,0:T(8,128)(2,1)S(1)}, u32[]{:S(2)}, u32[]{:S(2)}) collective-permute-start(bf16[896,768]{1,0:T(8,128)(2,1)} %get-tuple-element.42), channel_id=1, source_target_pairs={{1,0},{2,3},{5,4},{6,7},{9,8},{10,11},{13,12},{14,15},{17,16},{18,... | collective-permute-start | bytes 4128776 | tf_op jit(solution)/shard_map/ppermute | solution.py:341
  674.3 47.1 %collective-permute-start.13 = (bf16[896,512]{1,0:T(8,128)(2,1)}, bf16[896,512]{1,0:T(8,128)(2,1)S(1)}, u32[]{:S(2)}, u32[]{:S(2)}) collective-permute-start(bf16[896,512]{1,0:T(8,128)(2,1)} %get-tuple-element.46), channel_id=1, source_target_pairs={{1,0},{2,3},{5,4},{6,7},{9,8},{10,11},{13,12},{14,15},{17,16},{18,... | collective-permute-start | bytes 2752520 | tf_op jit(solution)/shard_map/ppermute | solution.py:341
  675.6 47.7 %collective-permute-start.14 = (bf16[896,512]{1,0:T(8,128)(2,1)}, bf16[896,512]{1,0:T(8,128)(2,1)S(1)}, u32[]{:S(2)}, u32[]{:S(2)}) collective-permute-start(bf16[896,512]{1,0:T(8,128)(2,1)} %get-tuple-element.47), channel_id=1, source_target_pairs={{1,2},{2,1},{5,6},{6,5},{9,10},{10,9},{13,14},{14,13},{17,18},{18,... | collective-permute-start | bytes 2752520 | tf_op jit(solution)/shard_map/ppermute | solution.py:342
  676.3 52.0 %copy-start.9 = (f32[1,256]{1,0:T(1,128)S(1)}, f32[1,256]{1,0:T(1,128)}, u32[]{:S(2)}) copy-start(f32[1,256]{1,0:T(1,128)} %get-tuple-element.35) | copy-start | bytes 3076
  676.3 48.3 %collective-permute-start.15 = (bf16[896,512]{1,0:T(8,128)(2,1)}, bf16[896,512]{1,0:T(8,128)(2,1)S(1)}, u32[]{:S(2)}, u32[]{:S(2)}) collective-permute-start(bf16[896,512]{1,0:T(8,128)(2,1)} %get-tuple-element.48), channel_id=1, source_target_pairs={{2,0},{1,3},{6,4},{5,7},{10,8},{9,11},{14,12},{13,15},{18,16},{17,... | collective-permute-start | bytes 2752520 | tf_op jit(solution)/shard_map/ppermute | solution.py:343
  720.1 187.4 %collective-permute-start.7 = (bf16[896,1024]{1,0:T(8,128)(2,1)}, bf16[896,1024]{1,0:T(8,128)(2,1)S(1)}, u32[]{:S(2)}, u32[]{:S(2)}) collective-permute-start(bf16[896,1024]{1,0:T(8,128)(2,1)} %get-tuple-element.38), channel_id=1, source_target_pairs={{1,0},{2,3},{5,4},{6,7},{9,8},{10,11},{13,12},{14,15},{17,16},{18,... | collective-permute-start | bytes 5505032 | tf_op jit(solution)/shard_map/ppermute | solution.py:341
  721.4 186.0 %collective-permute-start.8 = (bf16[896,1024]{1,0:T(8,128)(2,1)}, bf16[896,1024]{1,0:T(8,128)(2,1)}, u32[]{:S(2)}, u32[]{:S(2)}) collective-permute-start(bf16[896,1024]{1,0:T(8,128)(2,1)} %get-tuple-element.39), channel_id=1, source_target_pairs={{1,2},{2,1},{5,6},{6,5},{9,10},{10,9},{13,14},{14,13},{17,18},{18,... | collective-permute-start | bytes 5505032 | tf_op jit(solution)/shard_map/ppermute | solution.py:342
  723.3 184.1 %collective-permute-start.9 = (bf16[896,1024]{1,0:T(8,128)(2,1)}, bf16[896,1024]{1,0:T(8,128)(2,1)}, u32[]{:S(2)}, u32[]{:S(2)}) collective-permute-start(bf16[896,1024]{1,0:T(8,128)(2,1)} %get-tuple-element.40), channel_id=1, source_target_pairs={{2,0},{1,3},{6,4},{5,7},{10,8},{9,11},{14,12},{13,15},{18,16},{17,... | collective-permute-start | bytes 5505032 | tf_op jit(solution)/shard_map/ppermute | solution.py:343
  724.6 175.4 %collective-permute-start.11 = (bf16[896,768]{1,0:T(8,128)(2,1)}, bf16[896,768]{1,0:T(8,128)(2,1)}, u32[]{:S(2)}, u32[]{:S(2)}) collective-permute-start(bf16[896,768]{1,0:T(8,128)(2,1)} %get-tuple-element.43), channel_id=1, source_target_pairs={{1,2},{2,1},{5,6},{6,5},{9,10},{10,9},{13,14},{14,13},{17,18},{18,... | collective-permute-start | bytes 4128776 | tf_op jit(solution)/shard_map/ppermute | solution.py:342
  726.4 173.6 %copy-start.2 = (bf16[896,768]{1,0:T(8,128)(2,1)}, bf16[896,768]{1,0:T(8,128)(2,1)S(1)}, u32[]{:S(2)}) copy-start(bf16[896,768]{1,0:T(8,128)(2,1)S(1)} %collective-permute-done.10.near) | copy-start | bytes 4128772
  726.4 173.6 %collective-permute-start.12 = (bf16[896,768]{1,0:T(8,128)(2,1)}, bf16[896,768]{1,0:T(8,128)(2,1)}, u32[]{:S(2)}, u32[]{:S(2)}) collective-permute-start(bf16[896,768]{1,0:T(8,128)(2,1)} %get-tuple-element.44), channel_id=1, source_target_pairs={{2,0},{1,3},{6,4},{5,7},{10,8},{9,11},{14,12},{13,15},{18,16},{17,... | collective-permute-start | bytes 4128776 | tf_op jit(solution)/shard_map/ppermute | solution.py:343
  (15 other events, 124.1 us)
Sparse Core Ops, SparseCore 0:
  200.9 77.8 reduce-scatter.3
  309.3 38.9 reduce-scatter.7
  351.0 38.3 reduce-scatter.5
  398.4 59.1 all-gather.3
  459.0 38.0 all-gather.7
  498.5 47.1 all-gather.5

commit v3 on v2

--- a/solution.py
+++ b/solution.py
@@ -19,9 +19,6 @@
 STRIP = 128
 VMEM_BYTES = 56 * 2**20
 
-EARLY = [(1, 2), (1, 1), (2, 2), (3, 3), (3, 2), (3, 1)]
-LATE_A = [(0, 0), (0, 1)]
-LATE_B = [(0, 2), (0, 3)]
 GATHERED = [[(1, 2), (1, 1), (2, 2)], [(0, 0), (3, 3), (0, 1), (3, 2)], [(0, 2), (3, 1), (0, 3)]]
 
 
@@ -66,6 +63,77 @@
     )(index, momentum)
 
 
+def gram_kernel(pairs, where, pieces, has_total, split, flags, *refs):
+    left, core = flags[0] == 1, flags[1]
+    b, h = pl.program_id(0), pl.program_id(1)
+    count = len(where) * pieces
+    total = refs[count] if has_total else None
+    outs = refs[count + has_total :]
+    share = outs[0].shape[1]
+    at = pl.multiple_of((jnp.where(h == 0, 1 - core, core) if split else h) * share, 16)
+
+    def make(i, j):
+        value = total[0] if has_total else 0.0
+        for p in range(pieces):
+            x, y = refs[where[i] * pieces + p], refs[where[j] * pieces + p]
+            value += lax.dot_general(
+                x[pl.ds(at, share), :], y[...], (((1,), (1,)), ((), ())), preferred_element_type=jnp.float32
+            )
+        if not split:
+            outs[0][0] = value
+            return
+
+        @pl.when(h == 0)
+        def _():
+            outs[1][0] = value.astype(jnp.bfloat16)
+
+        @pl.when(h == 1)
+        def _():
+            outs[0][0] = value.astype(jnp.bfloat16)
+
+    for k, (i, j) in enumerate(pairs):
+        if (i, j) in ((1, 2), (0, 3)):
+            pl.when((b == k) & left)(functools.partial(make, j, i))
+            pl.when((b == k) & jnp.logical_not(left))(functools.partial(make, i, j))
+        else:
+            pl.when(b == k)(functools.partial(make, i, j))
+
+
+def gram_blocks(flags, pairs, operands, total=None, total_at=0, split=True):
+    where = {r: k for k, r in enumerate(operands)}
+    pieces = len(operands[pairs[0][0]])
+    rows = operands[pairs[0][0]][0][0].shape[0]
+    share = rows // 2
+    used = [piece for r in operands for piece in operands[r]]
+    specs = [pl.BlockSpec((rows, width), lambda b, h, flags, at=at: (0, at)) for _, width, at in used]
+    arrays = [array for array, _, _ in used]
+    if total is not None:
+        specs.append(
+            pl.BlockSpec(
+                (1, share, rows),
+                lambda b, h, flags: (total_at + b, jnp.where(h == 0, 1 - flags[1], flags[1]), 0),
+            )
+        )
+        arrays.append(total)
+    count = len(pairs)
+    if split:
+        out_specs = [pl.BlockSpec((1, share, rows), lambda b, h, flags: (b, 0, 0))] * 2
+        out_shape = [jax.ShapeDtypeStruct((count, share, rows), jnp.bfloat16)] * 2
+    else:
+        out_specs = [pl.BlockSpec((1, share, rows), lambda b, h, flags: (b, h, 0))]
+        out_shape = [jax.ShapeDtypeStruct((count, rows, rows), jnp.float32)]
+    return pl.pallas_call(
+        functools.partial(gram_kernel, pairs, where, pieces, int(total is not None), split),
+        grid_spec=pltpu.PrefetchScalarGridSpec(
+            num_scalar_prefetch=1, grid=(count, 2), in_specs=specs, out_specs=out_specs
+        ),
+        out_shape=out_shape,
+        compiler_params=pltpu.CompilerParams(vmem_limit_bytes=VMEM_BYTES),
+        cost_estimate=pl.CostEstimate(flops=0, bytes_accessed=0, transcendentals=0),
+        name="gram_blocks",
+    )(flags, *arrays)
+
+
 def transpose_block(ref, rows, source, target):
     @pl.loop(0, rows // STRIP)
     def _(s):
@@ -85,25 +153,32 @@
     return i, j
 
 
-def poly_kernel(flags, first, second, third, out_ref, gram, sems):
+def poly_kernel(flags, *refs):
+    *parts, out_ref, gram, sems = refs
     rows = out_ref.shape[1]
-    part = rows // 4
-    left = flags[0]
+    quarter = rows // 4
+    left, core, side = flags[0], flags[1], flags[3]
     b = pl.program_id(0)
 
     @pl.when(b == 0)
     def _():
+        places = [
+            2 * core + side,
+            2 * (1 - core) + side,
+            2 * core + 1 - side,
+            2 * (1 - core) + 1 - side,
+        ]
         copies, turned = [], []
-        for group, pairs in zip((first, second, third), GATHERED):
+        for g, pairs in enumerate(GATHERED):
             for k, (i, j) in enumerate(pairs):
-                if i != j and i + j == 3:
+                if (i, j) in ((1, 2), (0, 3)):
                     i, j = jnp.where(left == 1, j, i), jnp.where(left == 1, i, j)
-                for q in range(4):
+                for q, place in enumerate(places):
                     copies.append(
                         pltpu.make_async_copy(
-                            group.at[q, k],
+                            parts[4 * g + q].at[k],
                             gram.at[
-                                pl.ds(pl.multiple_of(i * rows + q * part, 16), part),
+                                pl.ds(pl.multiple_of(i * rows + place * quarter, 16), quarter),
                                 pl.ds(pl.multiple_of(j * rows, STRIP), rows),
                             ],
                             sems.at[len(copies)],
@@ -132,14 +207,14 @@
 
 
 def poly_blocks(flags, groups):
-    rows = groups[0].shape[3]
+    rows = groups[0][0].shape[2]
     order = 4 * rows
     return pl.pallas_call(
         poly_kernel,
         grid_spec=pltpu.PrefetchScalarGridSpec(
             num_scalar_prefetch=1,
             grid=(5,),
-            in_specs=[pl.BlockSpec(memory_space=pl.ANY)] * 3,
+            in_specs=[pl.BlockSpec(memory_space=pl.ANY)] * 12,
             out_specs=pl.BlockSpec((1, rows, rows), lambda b, flags: (b, 0, 0)),
             scratch_shapes=[pltpu.VMEM((order, order), jnp.bfloat16), pltpu.SemaphoreType.DMA((40,))],
         ),
@@ -149,11 +224,13 @@
             flops=10 * rows * rows * order, bytes_accessed=30 * rows * rows, transcendentals=0
         ),
         name="poly_blocks",
-    )(flags, *groups)
-
-
-def product_kernel(flags, own, pair, inverse, s0, s1, s2, s3, o0, o1, o2, o3, sq_ref, poly, raw, sems):
-    rows = s0.shape[0]
+    )(flags, *[x for group in groups for x in group])
+
+
+def product_kernel(first, starts, flags, own, pair, inverse, s1, s2, s3, *refs):
+    distant, (o0, o1, o2, o3, sq_ref, poly, raw, sems) = refs[:-8], refs[-8:]
+    rows = s1.shape[0]
+    tile = first + pl.program_id(0)
 
     @pl.when(pl.program_id(0) == 0)
     def _():
@@ -180,24 +257,37 @@
             for j in range(i + 1, 4):
                 transpose_block(poly, rows, (i, j), (j, i))
 
-    for r, s_ref in enumerate((s0, s1, s2, s3)):
+    for r, s_ref in enumerate((s1, s2, s3), start=1):
         raw[r * rows : (r + 1) * rows, :] = s_ref[...]
-    for r, (s_ref, o_ref) in enumerate(zip((s0, s1, s2, s3), (o0, o1, o2, o3))):
+    for piece, start, end in zip(distant, starts, starts[1:] + [1 << 30]):
+
+        @pl.when((tile >= start) & (tile < end))
+        def _(piece=piece):
+            raw[:rows, :] = piece[...]
+
+    for r, o_ref in enumerate((o0, o1, o2, o3)):
         product = jnp.dot(
             poly[r * rows : (r + 1) * rows, :], raw[...], preferred_element_type=jnp.float32
         )
-        newton = inverse[0] * (coef_linear * s_ref[...].astype(jnp.float32) + product)
+        own_rows = raw[r * rows : (r + 1) * rows, :].astype(jnp.float32)
+        newton = inverse[0] * (coef_linear * own_rows + product)
         sq_ref[...] += jnp.sum(newton * newton, axis=0, keepdims=True)
         o_ref[...] = newton.astype(jnp.bfloat16)
 
 
-def product(flags, own, pair, inverse, blocks, first, tiles):
+def product(flags, own, pair, inverse, blocks, distant, piece, first, tiles):
     rows = own.shape[1]
     order = 4 * rows
     here = pl.BlockSpec((rows, TILE), lambda t, flags: (0, first + t))
+    pieces = [(p * piece, (p + 1) * piece) for p in range(3)]
+    starts = [a // TILE for a, b in pieces]
+    distant_specs = [
+        pl.BlockSpec((rows, TILE), lambda t, flags, a=a // TILE, b=b // TILE: (0, jnp.clip(first + t, a, b - 1) - a))
+        for a, b in pieces
+    ]
     there = pl.BlockSpec((rows, TILE), lambda t, flags: (0, t))
     *newton, squares = pl.pallas_call(
-        product_kernel,
+        functools.partial(product_kernel, first, starts),
         grid_spec=pltpu.PrefetchScalarGridSpec(
             num_scalar_prefetch=1,
             grid=(tiles,),
@@ -206,7 +296,8 @@
                 pl.BlockSpec(memory_space=pl.ANY),
                 pl.BlockSpec(memory_space=pltpu.SMEM),
             ]
-            + [here] * 4,
+            + [here] * 3
+            + distant_specs,
             out_specs=[there] * 4 + [pl.BlockSpec((1, TILE), lambda t, flags: (0, 0))],
             scratch_shapes=[
                 pltpu.VMEM((order, order), jnp.bfloat16),
@@ -223,7 +314,7 @@
             transcendentals=0,
         ),
         name="product",
-    )(flags, own, pair, inverse, *blocks)
+    )(flags, own, pair, inverse, *blocks, *distant)
     return newton, jnp.sum(squares)
 
 
@@ -283,68 +374,162 @@
 def per_device(momentum):
     rows, cols = momentum.shape
     width = cols // 2
+    quarter = rows // 4
+    tiles = width // TILE
     z = lax.axis_index("row")
-    core = lax.axis_index("col") % 2
+    c = lax.axis_index("col")
+    core, side = c % 2, c // 2
     left = z < 2
     is_hub = (z == 1) | (z == 2)
-    flags = jnp.stack([left.astype(jnp.int32), core.astype(jnp.int32), is_hub.astype(jnp.int32)])
+    flags = jnp.stack([v.astype(jnp.int32) for v in (left, core, is_hub, side)])
     near_index = left.astype(jnp.int32).reshape(1)
 
+    def over_core(x):
+        return lax.ppermute(x, "col", [(k, k ^ 1) for k in range(4)])
+
+    def over_side(x):
+        return lax.ppermute(x, "col", [(k, k ^ 2) for k in range(4)])
+
+    def between_hubs(x):
+        return lax.ppermute(x, "row", [(1, 2), (2, 1)])
+
+    def distant_permute(x):
+        return lax.ppermute(x, "row", [(0, 2), (3, 1)])
+
+    def col_total(x):
+        x = jnp.broadcast_to(x, (8, 128))
+        x = x + over_core(x)
+        return x + over_side(x)
+
     far, far_sq = take(momentum, 1 - near_index)
-    middle = lax.ppermute(far, "row", [(1, 2), (2, 1)])
+    middle = between_hubs(far)
     near, near_sq = take(momentum, near_index)
     beside = lax.ppermute(near, "row", [(0, 1), (3, 2)])
-    norm_sum = lax.psum(jnp.sum(far_sq) + jnp.sum(near_sq), ("col", "row"))
+
+    norm_part = col_total(jnp.sum(far_sq) + jnp.sum(near_sq))
+    def added(x, y):
+        return (x.astype(jnp.float32) + y.astype(jnp.float32)).astype(jnp.bfloat16)
+
+    def over_pair(kept_sent):
+        return added(kept_sent[0], over_core(kept_sent[1]))
+
+    def over_sides(half):
+        def rows_of(at):
+            return lax.dynamic_slice(half, (0, at * quarter, 0), (half.shape[0], quarter, rows))
+
+        return added(rows_of(side), over_side(rows_of(1 - side)))
+
+    barrier = lax.optimization_barrier
+    piece = width // 3
+    far_pieces = [far[:, p * piece : (p + 1) * piece] for p in range(3)]
+    far_pieces[0], middle, beside, norm_part = barrier((far_pieces[0], middle, beside, norm_part))
+    whole = {1: [(middle, width, 0)], 2: [(near, width, 0)], 3: [(beside, width, 0)]}
+
+    pairs_1, pairs_2 = [(1, 2), (1, 1), (2, 2)], [(3, 3), (3, 2), (3, 1)]
+    pairs_3, pairs_4 = [(0, 0), (0, 1)], [(0, 2), (0, 3)]
+    arrived_0 = distant_permute(far_pieces[0])
+    norm_sum = (
+        norm_part
+        + lax.ppermute(norm_part, "row", [(0, 1), (3, 2)])
+        + between_hubs(norm_part)
+        + distant_permute(norm_part)
+    )[0, 0]
+    first = gram_blocks(flags, pairs_1, {1: whole[1], 2: whole[2]})
+    arrived_0, far_pieces[1], first = barrier((arrived_0, far_pieces[1], first))
+
+    arrived_1 = distant_permute(far_pieces[1])
+    first = over_pair(first)
+    second = gram_blocks(flags, pairs_2, whole)
+    arrived_1, far_pieces[2], first, second, norm_sum = barrier(
+        (arrived_1, far_pieces[2], first, second, norm_sum)
+    )
+
+    arrived_2 = distant_permute(far_pieces[2])
+    first = over_sides(first)
+    second = over_pair(second)
+    distant = [arrived_0, arrived_1, arrived_2]
+
+    def of_pieces(some):
+        operands = {0: [(distant[p], piece, 0) for p in some]}
+        for r, block in ((1, middle), (2, near), (3, beside)):
+            operands[r] = [(block, piece, p) for p in some]
+        return operands
+
+    (late,) = gram_blocks(flags, pairs_3 + pairs_4, of_pieces([0, 1]), split=False)
+    distant[2], late, first, second = barrier((distant[2], late, first, second))
+
+    other_first = between_hubs(first)
+    second = over_sides(second)
+    last = of_pieces([2])
+    third = over_pair(gram_blocks(flags, pairs_3, {r: last[r] for r in (0, 1)}, total=late))
+    fourth = over_pair(
+        gram_blocks(flags, pairs_4, {r: last[r] for r in (0, 2, 3)}, total=late, total_at=2)
+    )
+    other_first, fourth = barrier((other_first, fourth))
+    other_second = between_hubs(second)
+    third = over_sides(third)
+    fourth = over_sides(fourth)
+    other_second, fourth = barrier((other_second, fourth))
+    other_third = between_hubs(third)
+    other_fourth = between_hubs(fourth)
+
     spectral_edge = 1.0 + math.sqrt(M / N)
     inverse = 1.0 / (jnp.sqrt(norm_sum / M) * spectral_edge + 1e-07)
 
-    far, middle, inverse = lax.optimization_barrier((far, middle, inverse))
-    distant = lax.ppermute(far, "row", [(0, 2), (3, 1)])
-    blocks = [distant, middle, near, beside]
-
-    def partial_gram(pair):
-        i, j = pair
-        value = lax.dot_general(
-            blocks[i], blocks[j], (((1,), (1,)), ((), ())), preferred_element_type=jnp.float32
-        ).astype(jnp.bfloat16)
-        if i != j and i + j == 3:
-            value = jnp.where(left, value.T, value)
-        return value
-
     mine, other = {}, {}
-    for pairs in (EARLY, LATE_A, LATE_B):
-        stack = jnp.stack([partial_gram(pair).reshape(4, rows // 4, rows) for pair in pairs], axis=1)
-        summed = lax.psum_scatter(stack, "col", scatter_dimension=0, tiled=False)
-        received = lax.ppermute(summed, "row", [(1, 2), (2, 1)])
+
+    def known(pairs, summed, received):
         for k, pair in enumerate(pairs):
             mine[pair], other[mirror(pair)] = summed[k], received[k]
 
-    groups = []
-    for pairs in GATHERED:
-        gram = jnp.stack([mine[pair].astype(jnp.float32) + other[pair].astype(jnp.float32) for pair in pairs])
-        gram = (gram * (inverse * inverse)).astype(jnp.bfloat16)
-        groups.append(lax.all_gather(gram, "col", axis=0, tiled=False))
+    def gather(pairs):
+        total = jnp.stack([mine[pair].astype(jnp.float32) + other[pair].astype(jnp.float32) for pair in pairs])
+        here = (total * (inverse * inverse)).astype(jnp.bfloat16)
+        across = over_side(here)
+        return [here, over_core(here), across, over_core(across)]
+
+    known(pairs_1, first, other_first)
+    groups = [gather(GATHERED[0])]
+    known(pairs_2, second, other_second)
+    known(pairs_3, third, other_third)
+    groups.append(gather(GATHERED[1]))
+    groups[0], other_fourth = barrier((groups[0], other_fourth))
+    known(pairs_4, fourth, other_fourth)
+    groups.append(gather(GATHERED[2]))
 
     own = poly_blocks(flags, groups)
-    pair = lax.ppermute(own, "col", [(c, c ^ 1) for c in range(4)])
-
-    tiles = width // TILE
+    pair = over_core(own)
+
     bounds = sorted({0, tiles * 2 // 9, tiles * 5 // 9, tiles})
     newton_sq = jnp.float32(0.0)
+    scale = inverse.reshape(1)
     parts = []
     for first, last in zip(bounds[:-1], bounds[1:]):
-        newton, squares = product(flags, own, pair, inverse.reshape(1), blocks, first, last - first)
+        newton, squares = product(flags, own, pair, scale, (middle, near, beside), distant, piece, first, last - first)
         newton_sq += squares
-        parts.append(
-            (
-                newton[2],
-                lax.ppermute(newton[3], "row", [(1, 0), (2, 3)]),
-                lax.ppermute(newton[1], "row", [(1, 2), (2, 1)]),
-                lax.ppermute(newton[0], "row", [(2, 0), (1, 3)]),
-            )
+        if last == tiles:
+            hub_sq = col_total(newton_sq)
+            total_sq = (
+                jnp.where(is_hub, hub_sq, 0.0)
+                + lax.ppermute(hub_sq, "row", [(1, 0), (2, 3)])
+                + between_hubs(hub_sq)
+                + lax.ppermute(hub_sq, "row", [(2, 0), (1, 3)])
+            )[0, 0]
+            newton, total_sq, parts[-1] = barrier((newton, total_sq, parts[-1]))
+        part = (
+            newton[2],
+            lax.ppermute(newton[3], "row", [(1, 0), (2, 3)]),
+            between_hubs(newton[1]),
+            lax.ppermute(newton[0], "row", [(2, 0), (1, 3)]),
         )
-    newton_sq = lax.psum(jnp.where(is_hub, newton_sq, 0.0), ("col", "row"))
-    factor = (1.0 / (jnp.sqrt(newton_sq) / math.sqrt(M * N) + 1e-07)).reshape(1)
+        if last == tiles:
+            pass
+        elif parts:
+            parts[-1], scale, newton_sq = barrier((parts[-1], scale, newton_sq))
+        else:
+            scale, newton_sq = barrier((scale, newton_sq))
+        parts.append(part)
+    factor = (1.0 / (jnp.sqrt(total_sq) / math.sqrt(M * N) + 1e-07)).reshape(1)
     out = None
     for first, part in zip(bounds[:-1], parts):
         out = finish(flags, factor, part, first, (rows, cols), out)
@@ -388,7 +573,7 @@
         n_row, n_col = mesh.shape["row"], mesh.shape["col"]
         rows = momentum.shape[0] // (mesh.shape["groups"] * n_row)
         cols = momentum.shape[1] // n_col
-        hubs = n_row == 4 and n_col == 4 and rows % STRIP == 0 and cols % (2 * TILE) == 0
+        hubs = n_row == 4 and n_col == 4 and rows % STRIP == 0 and cols % (6 * TILE) == 0
         return jax.shard_map(
             per_device if hubs else per_device_general,
             mesh=mesh,

time: 931 us -> 726 us (0.78)
  blocking collectives: 272 us -> 0 us
  Pallas kernels: 188 us -> 270 us
  matrix products: 73.4 us -> 0 us
  starting transfers between devices: 29.1 us -> 70.6 us
  waiting for transfers between devices: 302 us -> 334 us
  between operations: 19 us -> 5.52 us
    psum x2 -> x0, blocking collectives: 272 us -> none  [the longest x1 161 us: per_device(): newton_sq = lax.psum(jnp.where(is_hub, newton_sq, 0.0), ('col', 'row'))]
    all_gather x3 -> x0, waiting for transfers between devices: 141 us -> none  [per_device(): groups.append(lax.all_gather(gram, 'col', axis=0, tiled=False))]
    pallas_call x3 -> x8, Pallas kernels: 106 us -> 188 us  [the longest x3 109 us: product(): pl.pallas_call(functools.partial(product_kernel, first, starts), grid_spe...]
    ppermute x9 -> x39, waiting for transfers between devices: 98.4 us -> 178 us  [the longest x9 129 us: over_side(): return lax.ppermute(x, 'col', [(k, k ^ 2) for k in range(4)])]
    dot_general x10 -> x0, matrix products: 73.4 us -> none  [partial_gram(): lax.dot_general(blocks[i], blocks[j], (((1,), (1,)), ((), ())), preferred...]
    ppermute x1, waiting for transfers between devices: 0.01 us -> 68.1 us  [per_device(): beside = lax.ppermute(near, 'row', [(0, 1), (3, 2)])]
    ppermute x3, waiting for transfers between devices: 0.01 us -> 64.3 us  [per_device(): lax.ppermute(newton[0], 'row', [(2, 0), (1, 3)])]
    reduce_scatter x3 -> x0, waiting for transfers between devices: 62.8 us -> none  [per_device(): summed = lax.psum_scatter(stack, 'col', scatter_dimension=0, tiled=False)]
  transfers between devices with their start and end apart: 22 -> 46, of which waited for: 7 -> 21; matrix products, arithmetic and copies ran while one was open for 8% -> 4% of each run, Pallas kernels for 10% -> 23%
where the time goes in v3:
time: 726 us; the launch traced here: 718 us
  waiting for transfers between devices  334 us (46%)
  Pallas kernels  270 us (37%)
  starting transfers between devices  70.6 us (10%)
  other arithmetic  22.8 us (3%)
  local copies, waits for them, and re-layouts  15.3 us (2%)
    ppermute x9, waiting for transfers between devices, over_side(): return lax.ppermute(x, 'col', [(k, k ^ 2) for k in range(4)])  129 us
    pallas_call x3, Pallas kernels, product(): pl.pallas_call(functools.partial(product_kernel, first, starts), grid_spe...  109 us
    pallas_call x5, Pallas kernels, gram_blocks(): pl.pallas_call(functools.partial(gram_kernel, pairs, where, pieces, int(t...  79.4 us
    ppermute x1, waiting for transfers between devices, per_device(): beside = lax.ppermute(near, 'row', [(0, 1), (3, 2)])  68.1 us
    ppermute x3, waiting for transfers between devices, per_device(): lax.ppermute(newton[0], 'row', [(2, 0), (1, 3)])  64.3 us
    pallas_call x1, Pallas kernels, poly_blocks(): pl.pallas_call(poly_kernel, grid_spec=pltpu.PrefetchScalarGridSpec(num_sc...  47.5 us
    ppermute x4, starting transfers between devices, distant_permute(): return lax.ppermute(x, 'row', [(0, 2), (3, 1)])  27.2 us
    ppermute x3, waiting for transfers between devices, per_device(): lax.ppermute(newton[3], 'row', [(1, 0), (2, 3)])  23.9 us
  transfers between devices with their start and end apart: 46, of which 21 were waited for; matrix products, arithmetic and copies ran while one was open for 4% of the time, Pallas kernels for 23%

profile of v3, /device:TPU:0, one launch (start us, length us, event | category | flops | bytes accessed | tf_op | source)
XLA Modules:
  0.0 718.1 jit_solution(14195333456467284537)
XLA Ops:
  31.4 68.1 %collective-permute-done.1.refs_2_.refs_6_.refs_7_.s3 = bf16[896,2304]{1,0:T(8,128)(2,1)} collective-permute-done((bf16[896,2304]{1,0:T(8,128)(2,1)}, bf16[896,2304]{1,0:T(8,128)(2,1)}, u32[]{:S(2)}, u32[]{:S(2)}) %collective-permute-start.1) | collective-permute-done | bytes 4128800 | tf_op jit(solution)/shard_map/ppermute | solution.py:407
  99.6 12.7 %collective-permute-start.4 = (bf16[896,768]{1,0:T(8,128)(2,1)S(1)}, bf16[896,768]{1,0:T(8,128)(2,1)S(1)}, u32[]{:S(2)}, u32[]{:S(2)}) collective-permute-start(bf16[896,768]{1,0:T(8,128)(2,1)S(1)} %get-tuple-element.80), channel_id=1, source_target_pairs={{0,2},{3,1},{4,6},{7,5},{8,10},{11,9},{12,14},{15,13},{16,18},{19,... | collective-permute-start | bytes 4128776 | tf_op jit(solution)/shard_map/ppermute | solution.py:397
  112.9 19.9 %gram_blocks.5 = (bf16[3,448,896]{2,1,0:T(8,128)(2,1)}, bf16[3,448,896]{2,1,0:T(8,128)(2,1)}) custom-call(s32[4]{0:T(128)} %pad_add_fusion.flags, bf16[896,2304]{1,0:T(8,128)(2,1)} %collective-permute-done.refs_0_.refs_2_.refs_3_.refs_1_.s1, bf16[896,2304]{1,0:T(8,128)(2,1)} %get-tuple-element.77.refs_1_.refs_4_.refs_5_.s2), custom_call_target="tpu_custom_call" | custom-call | tf_op jit(solution)/shard_map/gram_blocks/pallas_call | solution.py:125
  132.8 7.9 %collective-permute-done.4.refs_0_ = bf16[896,768]{1,0:T(8,128)(2,1)S(1)} collective-permute-done((bf16[896,768]{1,0:T(8,128)(2,1)S(1)}, bf16[896,768]{1,0:T(8,128)(2,1)S(1)}, u32[]{:S(2)}, u32[]{:S(2)}) %collective-permute-start.4) | collective-permute-done | bytes 1376288 | tf_op jit(solution)/shard_map/ppermute | solution.py:397
  151.8 21.1 %gram_blocks.6 = (bf16[3,448,896]{2,1,0:T(8,128)(2,1)}, bf16[3,448,896]{2,1,0:T(8,128)(2,1)}) custom-call(s32[4]{0:T(128)} %pad_add_fusion.flags, bf16[896,2304]{1,0:T(8,128)(2,1)} %collective-permute-done.refs_0_.refs_2_.refs_3_.refs_1_.s1, bf16[896,2304]{1,0:T(8,128)(2,1)} %get-tuple-element.77.refs_1_.refs_4_.refs_5_.s2, ...), custom_call_target="tpu_custom_call" | custom-call | tf_op jit(solution)/shard_map/gram_blocks/pallas_call | solution.py:125
  188.8 19.4 %gram_blocks.7.refs_3_.refs_2_ = f32[4,896,896]{2,1,0:T(8,128)} custom-call(s32[4]{0:T(128)} %pad_add_fusion.flags, bf16[896,768]{1,0:T(8,128)(2,1)} %copy-done.7, bf16[896,768]{1,0:T(8,128)(2,1)} %collective-permute-done.5.refs_1_, bf16[896,2304]{1,0:T(8,128)(2,1)} %collective-permute-done.refs_0_.refs_2_.refs_3_.refs_1_.s1, ...), custom_call_target="tpu_custom_call" | custom-call | tf_op jit(solution)/shard_map/gram_blocks/pallas_call | solution.py:125
  217.6 9.7 %gram_blocks.8 = (bf16[2,448,896]{2,1,0:T(8,128)(2,1)}, bf16[2,448,896]{2,1,0:T(8,128)(2,1)}) custom-call(s32[4]{0:T(128)} %pad_add_fusion.flags, bf16[896,768]{1,0:T(8,128)(2,1)} %collective-permute-done.10.refs_0_.refs_2_, bf16[896,2304]{1,0:T(8,128)(2,1)} %get-tuple-element.77.refs_1_.refs_4_.refs_5_.s2, ...), custom_call_target="tpu_custom_call" | custom-call | tf_op jit(solution)/shard_map/gram_blocks/pallas_call | solution.py:125
  230.8 9.3 %gram_blocks.9 = (bf16[2,448,896]{2,1,0:T(8,128)(2,1)}, bf16[2,448,896]{2,1,0:T(8,128)(2,1)}) custom-call(s32[4]{0:T(128)} %pad_add_fusion.flags, bf16[896,768]{1,0:T(8,128)(2,1)} %collective-permute-done.10.refs_0_.refs_2_, bf16[896,2304]{1,0:T(8,128)(2,1)} %collective-permute-done.refs_0_.refs_2_.refs_3_.refs_1_.s1, f32[4,896,896]{2,1,0:T(8,128)} %gram_blocks.7.refs_3_.refs_2_), custom_call_target="tpu_custom_call" | custom-call | tf_op jit(solution)/shard_map/gram_blocks/pallas_call | solution.py:125
  246.9 12.9 %collective-permute-done.18 = bf16[3,224,896]{2,1,0:T(8,128)(2,1)} collective-permute-done((bf16[3,224,896]{2,1,0:T(8,128)(2,1)}, bf16[3,224,896]{2,1,0:T(8,128)(2,1)}, u32[]{:S(2)}, u32[]{:S(2)}) %collective-permute-start.18) | collective-permute-done | bytes 1204256 | tf_op jit(solution)/shard_map/ppermute | solution.py:391
  266.7 18.8 %collective-permute-done.16.refs_2_ = bf16[3,224,896]{2,1,0:T(8,128)(2,1)S(1)} collective-permute-done((bf16[3,224,896]{2,1,0:T(8,128)(2,1)S(1)}, bf16[3,224,896]{2,1,0:T(8,128)(2,1)S(1)}, u32[]{:S(2)}, u32[]{:S(2)}) %collective-permute-start.16) | collective-permute-done | bytes 1204256 | tf_op jit(solution)/shard_map/ppermute | solution.py:391
  285.5 17.2 %collective-permute-done.20 = bf16[2,224,896]{2,1,0:T(8,128)(2,1)S(1)} collective-permute-done((bf16[2,224,896]{2,1,0:T(8,128)(2,1)S(1)}, bf16[2,224,896]{2,1,0:T(8,128)(2,1)S(1)}, u32[]{:S(2)}, u32[]{:S(2)}) %collective-permute-start.20) | collective-permute-done | bytes 802848 | tf_op jit(solution)/shard_map/ppermute | solution.py:391
  303.7 15.9 %collective-permute-done.23 = bf16[2,224,896]{2,1,0:T(8,128)(2,1)S(1)} collective-permute-done((bf16[2,224,896]{2,1,0:T(8,128)(2,1)S(1)}, bf16[2,224,896]{2,1,0:T(8,128)(2,1)S(1)}, u32[]{:S(2)}, u32[]{:S(2)}) %collective-permute-start.23) | collective-permute-done | bytes 802848 | tf_op jit(solution)/shard_map/ppermute | solution.py:391
  324.9 35.6 %collective-permute-done.26.refs_6_ = bf16[4,224,896]{2,1,0:T(8,128)(2,1)S(1)} collective-permute-done((bf16[4,224,896]{2,1,0:T(8,128)(2,1)S(1)}, bf16[4,224,896]{2,1,0:T(8,128)(2,1)S(1)}, u32[]{:S(2)}, u32[]{:S(2)}) %collective-permute-start.26) | collective-permute-done | bytes 1605664 | tf_op jit(solution)/shard_map/ppermute | solution.py:391
  361.0 24.0 %collective-permute-done.29.refs_10_ = bf16[3,224,896]{2,1,0:T(8,128)(2,1)S(1)} collective-permute-done((bf16[3,224,896]{2,1,0:T(8,128)(2,1)S(1)}, bf16[3,224,896]{2,1,0:T(8,128)(2,1)S(1)}, u32[]{:S(2)}, u32[]{:S(2)}) %collective-permute-start.29) | collective-permute-done | bytes 1204256 | tf_op jit(solution)/shard_map/ppermute | solution.py:391
  390.2 47.5 %poly_blocks.1.own = bf16[5,896,896]{2,1,0:T(8,128)(2,1)} custom-call(s32[4]{0:T(128)} %pad_add_fusion.flags, bf16[3,224,896]{2,1,0:T(8,128)(2,1)} %copy-done.8, bf16[3,224,896]{2,1,0:T(8,128)(2,1)} %copy-done.16, bf16[3,224,896]{2,1,0:T(8,128)(2,1)} %copy-done.15, bf16[3,224,896]{2,1,0:T(8,128)(2,1)} %copy-done.17, bf16[4,224,896]{2,1,0:T(8,128)(2,1)} %copy-done.3, ...), custom_call_target="tpu_custom_call" | custom-call | flops 28772925440 | bytes 24084480 | tf_op jit(solution)/shard_map/poly_blocks/pallas_call | solution.py:212
  437.9 12.7 %collective-permute-done.31.pair = bf16[5,896,896]{2,1,0:T(8,128)(2,1)S(1)} collective-permute-done((bf16[5,896,896]{2,1,0:T(8,128)(2,1)}, bf16[5,896,896]{2,1,0:T(8,128)(2,1)S(1)}, u32[]{:S(2)}, u32[]{:S(2)}) %collective-permute-start.31) | collective-permute-done | bytes 8028192 | tf_op jit(solution)/shard_map/ppermute | solution.py:388
  453.8 28.8 %product.3 = (bf16[896,512]{1,0:T(8,128)(2,1)}, bf16[896,512]{1,0:T(8,128)(2,1)}, bf16[896,512]{1,0:T(8,128)(2,1)}, bf16[896,512]{1,0:T(8,128)(2,1)}, f32[1,256]{1,0:T(1,128)}) custom-call(s32[4]{0:T(128)} %pad_add_fusion.flags, bf16[5,896,896]{2,1,0:T(8,128)(2,1)} %poly_blocks.1.own, bf16[5,896,896]{2,1,0:T(8,128)(2,1)} %copy-done.11, f32[1]{0:T(128)} %bitcast.5.inverse, ...), custom_call_target="tpu_custom_call" | custom-call | flops 13153337344 | bytes 23396352 | tf_op jit(solution)/shard_map/product/pallas_call | solution.py:289
  488.3 36.3 %product.4 = (bf16[896,768]{1,0:T(8,128)(2,1)}, bf16[896,768]{1,0:T(8,128)(2,1)}, bf16[896,768]{1,0:T(8,128)(2,1)}, bf16[896,768]{1,0:T(8,128)(2,1)}, f32[1,256]{1,0:T(1,128)}) custom-call(s32[4]{0:T(128)} %pad_add_fusion.flags, bf16[5,896,896]{2,1,0:T(8,128)(2,1)} %poly_blocks.1.own, bf16[5,896,896]{2,1,0:T(8,128)(2,1)} %copy-done.11, f32[1]{0:T(128)} %bitcast.5.inverse, ...), custom_call_target="tpu_custom_call" | custom-call | flops 19730006016 | bytes 27066368 | tf_op jit(solution)/shard_map/product/pallas_call | solution.py:289
  530.6 21.9 %collective-permute-done.34.far = bf16[896,512]{1,0:T(8,128)(2,1)} collective-permute-done((bf16[896,512]{1,0:T(8,128)(2,1)}, bf16[896,512]{1,0:T(8,128)(2,1)}, u32[]{:S(2)}, u32[]{:S(2)}) %collective-permute-start.34) | collective-permute-done | bytes 917536 | tf_op jit(solution)/shard_map/ppermute | solution.py:523
  552.5 43.4 %product.5 = (bf16[896,1024]{1,0:T(8,128)(2,1)}, bf16[896,1024]{1,0:T(8,128)(2,1)}, bf16[896,1024]{1,0:T(8,128)(2,1)}, bf16[896,1024]{1,0:T(8,128)(2,1)}, f32[1,256]{1,0:T(1,128)}) custom-call(s32[4]{0:T(128)} %pad_add_fusion.flags, bf16[5,896,896]{2,1,0:T(8,128)(2,1)} %poly_blocks.1.own, bf16[5,896,896]{2,1,0:T(8,128)(2,1)} %copy-done.11, ...), custom_call_target="tpu_custom_call" | custom-call | flops 26306674688 | bytes 30736384 | tf_op jit(solution)/shard_map/product/pallas_call | solution.py:289
  604.6 12.1 %collective-permute-done.39 = f32[8,128]{1,0:T(8,128)S(1)} collective-permute-done((f32[8,128]{1,0:T(8,128)S(1)}, f32[8,128]{1,0:T(8,128)S(1)}, u32[]{:S(2)}, u32[]{:S(2)}) %collective-permute-start.39) | collective-permute-done | bytes 4128 | tf_op jit(solution)/shard_map/ppermute | solution.py:516
  642.1 23.9 %collective-permute-done.43.near = bf16[896,1024]{1,0:T(8,128)(2,1)S(1)} collective-permute-done((bf16[896,1024]{1,0:T(8,128)(2,1)}, bf16[896,1024]{1,0:T(8,128)(2,1)S(1)}, u32[]{:S(2)}, u32[]{:S(2)}) %collective-permute-start.43) | collective-permute-done | bytes 1835040 | tf_op jit(solution)/shard_map/ppermute | solution.py:521
  666.0 42.4 %collective-permute-done.45.far = bf16[896,1024]{1,0:T(8,128)(2,1)} collective-permute-done((bf16[896,1024]{1,0:T(8,128)(2,1)}, bf16[896,1024]{1,0:T(8,128)(2,1)}, u32[]{:S(2)}, u32[]{:S(2)}) %collective-permute-start.45) | collective-permute-done | bytes 1835040 | tf_op jit(solution)/shard_map/ppermute | solution.py:523
  708.4 9.6 %finish.5 = f32[896,4608]{1,0:T(8,128)} custom-call(s32[4]{0:T(128)} %pad_add_fusion.flags, f32[1]{0:T(128)} %bitcast.7.factor, bf16[896,1024]{1,0:T(8,128)(2,1)} %get-tuple-element.135.own, bf16[896,1024]{1,0:T(8,128)(2,1)} %copy-done.2, bf16[896,1024]{1,0:T(8,128)(2,1)} %collective-permute-done.44.middle, ...), custom_call_target="tpu_custom_call", output_to_operand_aliasing={{}: (6, {})} | custom-call | flops 1835008 | bytes 14680064 | tf_op jit(solution)/shard_map/finish/pallas_call | solution.py:359
  (160 shorter events, 141.5 us)
Async XLA Ops:
  5.9 93.6 %collective-permute-start.1 = (bf16[896,2304]{1,0:T(8,128)(2,1)}, bf16[896,2304]{1,0:T(8,128)(2,1)}, u32[]{:S(2)}, u32[]{:S(2)}) collective-permute-start(bf16[896,2304]{1,0:T(8,128)(2,1)} %get-tuple-element.77.refs_1_.refs_4_.refs_5_.s2), channel_id=1, source_target_pairs={{0,1},{3,2},{4,5},{7,6},{8,9},{11,10},{12,13},{15,14},{16,17},{19,... | collective-permute-start | bytes 12386312 | tf_op jit(solution)/shard_map/ppermute | solution.py:407
  18.7 80.9 %collective-permute-start = (bf16[896,2304]{1,0:T(8,128)(2,1)}, bf16[896,2304]{1,0:T(8,128)(2,1)}, u32[]{:S(2)}, u32[]{:S(2)}) collective-permute-start(bf16[896,2304]{1,0:T(8,128)(2,1)} %get-tuple-element.76), channel_id=1, source_target_pairs={{1,2},{2,1},{5,6},{6,5},{9,10},{10,9},{13,14},{14,13},{17,18},{18,... | collective-permute-start | bytes 12386312 | tf_op jit(solution)/shard_map/ppermute | solution.py:394
  99.6 41.1 %collective-permute-start.4 = (bf16[896,768]{1,0:T(8,128)(2,1)S(1)}, bf16[896,768]{1,0:T(8,128)(2,1)S(1)}, u32[]{:S(2)}, u32[]{:S(2)}) collective-permute-start(bf16[896,768]{1,0:T(8,128)(2,1)S(1)} %get-tuple-element.80), channel_id=1, source_target_pairs={{0,2},{3,1},{4,6},{7,5},{8,10},{11,9},{12,14},{15,13},{16,18},{19,... | collective-permute-start | bytes 4128776 | tf_op jit(solution)/shard_map/ppermute | solution.py:397
  140.7 36.4 %collective-permute-start.6 = (bf16[3,448,896]{2,1,0:T(8,128)(2,1)}, bf16[3,448,896]{2,1,0:T(8,128)(2,1)}, u32[]{:S(2)}, u32[]{:S(2)}) collective-permute-start(bf16[3,448,896]{2,1,0:T(8,128)(2,1)} %get-tuple-element.86), channel_id=1, source_target_pairs={{0,4},{4,0},{8,12},{12,8},{1,5},{5,1},{9,13},{13,9},{2,6},{6,2},{1... | collective-permute-start | bytes 7225352 | tf_op jit(solution)/shard_map/ppermute | solution.py:388
  140.8 38.7 %collective-permute-start.5 = (bf16[896,768]{1,0:T(8,128)(2,1)}, bf16[896,768]{1,0:T(8,128)(2,1)}, u32[]{:S(2)}, u32[]{:S(2)}) collective-permute-start(bf16[896,768]{1,0:T(8,128)(2,1)} %get-tuple-element.84), channel_id=1, source_target_pairs={{0,2},{3,1},{4,6},{7,5},{8,10},{11,9},{12,14},{15,13},{16,18},{19,... | collective-permute-start | bytes 4128776 | tf_op jit(solution)/shard_map/ppermute | solution.py:397
  182.2 35.4 %collective-permute-start.10 = (bf16[896,768]{1,0:T(8,128)(2,1)}, bf16[896,768]{1,0:T(8,128)(2,1)}, u32[]{:S(2)}, u32[]{:S(2)}) collective-permute-start(bf16[896,768]{1,0:T(8,128)(2,1)} %get-tuple-element.91), channel_id=1, source_target_pairs={{0,2},{3,1},{4,6},{7,5},{8,10},{11,9},{12,14},{15,13},{16,18},{19,... | collective-permute-start | bytes 4128776 | tf_op jit(solution)/shard_map/ppermute | solution.py:397
  245.4 40.1 %collective-permute-start.16 = (bf16[3,224,896]{2,1,0:T(8,128)(2,1)S(1)}, bf16[3,224,896]{2,1,0:T(8,128)(2,1)S(1)}, u32[]{:S(2)}, u32[]{:S(2)}) collective-permute-start(bf16[3,224,896]{2,1,0:T(8,128)(2,1)S(1)} %fusion.1.refs_0_), channel_id=1, source_target_pairs={{0,8},{4,12},{8,0},{12,4},{1,9},{5,13},{9,1},{13,5},{2,10},{6,14},... | collective-permute-start | bytes 3612680 | tf_op jit(solution)/shard_map/ppermute | solution.py:391
  261.4 41.5 %collective-permute-start.19 = (bf16[3,224,896]{2,1,0:T(8,128)(2,1)S(1)}, bf16[3,224,896]{2,1,0:T(8,128)(2,1)S(1)}, u32[]{:S(2)}, u32[]{:S(2)}) collective-permute-start(bf16[3,224,896]{2,1,0:T(8,128)(2,1)S(1)} %add_convert_fusion.4), channel_id=1, source_target_pairs={{1,2},{2,1},{5,6},{6,5},{9,10},{10,9},{13,14},{14,13},{17,18},{18,... | collective-permute-start | bytes 3612680 | tf_op jit(solution)/shard_map/ppermute | solution.py:394
  262.6 40.1 %collective-permute-start.20 = (bf16[2,224,896]{2,1,0:T(8,128)(2,1)S(1)}, bf16[2,224,896]{2,1,0:T(8,128)(2,1)S(1)}, u32[]{:S(2)}, u32[]{:S(2)}) collective-permute-start(bf16[2,224,896]{2,1,0:T(8,128)(2,1)S(1)} %constant_dynamic-slice_fusion.1), channel_id=1, source_target_pairs={{0,8},{4,12},{8,0},{12,4},{1,9},{5,13},{9,1},{13,5},{2,10},{6,14},... | collective-permute-start | bytes 2408456 | tf_op jit(solution)/shard_map/ppermute | solution.py:391
  265.1 54.4 %collective-permute-start.23 = (bf16[2,224,896]{2,1,0:T(8,128)(2,1)S(1)}, bf16[2,224,896]{2,1,0:T(8,128)(2,1)S(1)}, u32[]{:S(2)}, u32[]{:S(2)}) collective-permute-start(bf16[2,224,896]{2,1,0:T(8,128)(2,1)S(1)} %constant_dynamic-slice_fusion), channel_id=1, source_target_pairs={{0,8},{4,12},{8,0},{12,4},{1,9},{5,13},{9,1},{13,5},{2,10},{6,14},... | collective-permute-start | bytes 2408456 | tf_op jit(solution)/shard_map/ppermute | solution.py:391
  266.7 54.0 %collective-permute-start.15 = (bf16[3,224,896]{2,1,0:T(8,128)(2,1)S(1)}, bf16[3,224,896]{2,1,0:T(8,128)(2,1)S(1)}, u32[]{:S(2)}, u32[]{:S(2)}) collective-permute-start(bf16[3,224,896]{2,1,0:T(8,128)(2,1)S(1)} %fusion.1.refs_0_), channel_id=1, source_target_pairs={{0,4},{4,0},{8,12},{12,8},{1,5},{5,1},{9,13},{13,9},{2,6},{6,2},{1... | collective-permute-start | bytes 3612680 | tf_op jit(solution)/shard_map/ppermute | solution.py:388
  285.5 35.2 %collective-permute-start.17 = (bf16[3,224,896]{2,1,0:T(8,128)(2,1)S(1)}, bf16[3,224,896]{2,1,0:T(8,128)(2,1)S(1)}, u32[]{:S(2)}, u32[]{:S(2)}) collective-permute-start(bf16[3,224,896]{2,1,0:T(8,128)(2,1)S(1)} %collective-permute-done.16.refs_2_), channel_id=1, source_target_pairs={{0,4},{4,0},{8,12},{12,8},{1,5},{5,1},{9,13},{13,9},{2,6},{6,2},{1... | collective-permute-start | bytes 3612680 | tf_op jit(solution)/shard_map/ppermute | solution.py:388
  322.4 38.1 %collective-permute-start.26 = (bf16[4,224,896]{2,1,0:T(8,128)(2,1)S(1)}, bf16[4,224,896]{2,1,0:T(8,128)(2,1)S(1)}, u32[]{:S(2)}, u32[]{:S(2)}) collective-permute-start(bf16[4,224,896]{2,1,0:T(8,128)(2,1)S(1)} %fusion.refs_4_), channel_id=1, source_target_pairs={{0,8},{4,12},{8,0},{12,4},{1,9},{5,13},{9,1},{13,5},{2,10},{6,14},... | collective-permute-start | bytes 4816904 | tf_op jit(solution)/shard_map/ppermute | solution.py:391
  323.3 61.7 %collective-permute-start.29 = (bf16[3,224,896]{2,1,0:T(8,128)(2,1)S(1)}, bf16[3,224,896]{2,1,0:T(8,128)(2,1)S(1)}, u32[]{:S(2)}, u32[]{:S(2)}) collective-permute-start(bf16[3,224,896]{2,1,0:T(8,128)(2,1)S(1)} %fusion.2.refs_8_), channel_id=1, source_target_pairs={{0,8},{4,12},{8,0},{12,4},{1,9},{5,13},{9,1},{13,5},{2,10},{6,14},... | collective-permute-start | bytes 3612680 | tf_op jit(solution)/shard_map/ppermute | solution.py:391
  324.9 60.2 %collective-permute-start.25 = (bf16[4,224,896]{2,1,0:T(8,128)(2,1)S(1)}, bf16[4,224,896]{2,1,0:T(8,128)(2,1)S(1)}, u32[]{:S(2)}, u32[]{:S(2)}) collective-permute-start(bf16[4,224,896]{2,1,0:T(8,128)(2,1)S(1)} %fusion.refs_4_), channel_id=1, source_target_pairs={{0,4},{4,0},{8,12},{12,8},{1,5},{5,1},{9,13},{13,9},{2,6},{6,2},{1... | collective-permute-start | bytes 4816904 | tf_op jit(solution)/shard_map/ppermute | solution.py:388
  483.9 45.3 %collective-permute-start.32 = (bf16[896,512]{1,0:T(8,128)(2,1)}, bf16[896,512]{1,0:T(8,128)(2,1)}, u32[]{:S(2)}, u32[]{:S(2)}) collective-permute-start(bf16[896,512]{1,0:T(8,128)(2,1)} %get-tuple-element.116), channel_id=1, source_target_pairs={{1,0},{2,3},{5,4},{6,7},{9,8},{10,11},{13,12},{14,15},{17,16},{18,... | collective-permute-start | bytes 2752520 | tf_op jit(solution)/shard_map/ppermute | solution.py:521
  485.2 45.3 %collective-permute-start.33 = (bf16[896,512]{1,0:T(8,128)(2,1)}, bf16[896,512]{1,0:T(8,128)(2,1)}, u32[]{:S(2)}, u32[]{:S(2)}) collective-permute-start(bf16[896,512]{1,0:T(8,128)(2,1)} %get-tuple-element.117), channel_id=1, source_target_pairs={{1,2},{2,1},{5,6},{6,5},{9,10},{10,9},{13,14},{14,13},{17,18},{18,... | collective-permute-start | bytes 2752520 | tf_op jit(solution)/shard_map/ppermute | solution.py:394
  486.9 65.6 %collective-permute-start.34 = (bf16[896,512]{1,0:T(8,128)(2,1)}, bf16[896,512]{1,0:T(8,128)(2,1)}, u32[]{:S(2)}, u32[]{:S(2)}) collective-permute-start(bf16[896,512]{1,0:T(8,128)(2,1)} %get-tuple-element.118), channel_id=1, source_target_pairs={{2,0},{1,3},{6,4},{5,7},{10,8},{9,11},{14,12},{13,15},{18,16},{17,... | collective-permute-start | bytes 2752520 | tf_op jit(solution)/shard_map/ppermute | solution.py:523
  526.0 96.8 %collective-permute-start.40 = (bf16[896,768]{1,0:T(8,128)(2,1)}, bf16[896,768]{1,0:T(8,128)(2,1)S(1)}, u32[]{:S(2)}, u32[]{:S(2)}) collective-permute-start(bf16[896,768]{1,0:T(8,128)(2,1)} %get-tuple-element.131), channel_id=1, source_target_pairs={{1,0},{2,3},{5,4},{6,7},{9,8},{10,11},{13,12},{14,15},{17,16},{18,... | collective-permute-start | bytes 4128776 | tf_op jit(solution)/shard_map/ppermute | solution.py:521
  527.2 95.5 %collective-permute-start.41 = (bf16[896,768]{1,0:T(8,128)(2,1)}, bf16[896,768]{1,0:T(8,128)(2,1)S(1)}, u32[]{:S(2)}, u32[]{:S(2)}) collective-permute-start(bf16[896,768]{1,0:T(8,128)(2,1)} %get-tuple-element.132), channel_id=1, source_target_pairs={{1,2},{2,1},{5,6},{6,5},{9,10},{10,9},{13,14},{14,13},{17,18},{18,... | collective-permute-start | bytes 4128776 | tf_op jit(solution)/shard_map/ppermute | solution.py:394
  529.3 93.5 %collective-permute-start.42 = (bf16[896,768]{1,0:T(8,128)(2,1)}, bf16[896,768]{1,0:T(8,128)(2,1)}, u32[]{:S(2)}, u32[]{:S(2)}) collective-permute-start(bf16[896,768]{1,0:T(8,128)(2,1)} %get-tuple-element.133), channel_id=1, source_target_pairs={{2,0},{1,3},{6,4},{5,7},{10,8},{9,11},{14,12},{13,15},{18,16},{17,... | collective-permute-start | bytes 4128776 | tf_op jit(solution)/shard_map/ppermute | solution.py:523
  623.9 42.1 %collective-permute-start.43 = (bf16[896,1024]{1,0:T(8,128)(2,1)}, bf16[896,1024]{1,0:T(8,128)(2,1)S(1)}, u32[]{:S(2)}, u32[]{:S(2)}) collective-permute-start(bf16[896,1024]{1,0:T(8,128)(2,1)} %get-tuple-element.136), channel_id=1, source_target_pairs={{1,0},{2,3},{5,4},{6,7},{9,8},{10,11},{13,12},{14,15},{17,16},{18,... | collective-permute-start | bytes 5505032 | tf_op jit(solution)/shard_map/ppermute | solution.py:521
  625.1 40.8 %collective-permute-start.44 = (bf16[896,1024]{1,0:T(8,128)(2,1)}, bf16[896,1024]{1,0:T(8,128)(2,1)}, u32[]{:S(2)}, u32[]{:S(2)}) collective-permute-start(bf16[896,1024]{1,0:T(8,128)(2,1)} %get-tuple-element.137), channel_id=1, source_target_pairs={{1,2},{2,1},{5,6},{6,5},{9,10},{10,9},{13,14},{14,13},{17,18},{18,... | collective-permute-start | bytes 5505032 | tf_op jit(solution)/shard_map/ppermute | solution.py:394
  627.1 81.3 %collective-permute-start.45 = (bf16[896,1024]{1,0:T(8,128)(2,1)}, bf16[896,1024]{1,0:T(8,128)(2,1)}, u32[]{:S(2)}, u32[]{:S(2)}) collective-permute-start(bf16[896,1024]{1,0:T(8,128)(2,1)} %get-tuple-element.138), channel_id=1, source_target_pairs={{2,0},{1,3},{6,4},{5,7},{10,8},{9,11},{14,12},{13,15},{18,16},{17,... | collective-permute-start | bytes 5505032 | tf_op jit(solution)/shard_map/ppermute | solution.py:523
  (43 other events, 687.8 us)

commit v4 on v3

--- a/solution.py
+++ b/solution.py
@@ -227,7 +227,7 @@
     )(flags, *[x for group in groups for x in group])
 
 
-def product_kernel(first, starts, flags, own, pair, inverse, s1, s2, s3, *refs):
+def product_kernel(first, strips, flags, own, pair, inverse, s1, s2, s3, *refs):
     distant, (o0, o1, o2, o3, sq_ref, poly, raw, sems) = refs[:-8], refs[-8:]
     rows = s1.shape[0]
     tile = first + pl.program_id(0)
@@ -259,11 +259,12 @@
 
     for r, s_ref in enumerate((s1, s2, s3), start=1):
         raw[r * rows : (r + 1) * rows, :] = s_ref[...]
-    for piece, start, end in zip(distant, starts, starts[1:] + [1 << 30]):
-
-        @pl.when((tile >= start) & (tile < end))
-        def _(piece=piece):
-            raw[:rows, :] = piece[...]
+    for k, strip in enumerate(distant):
+        side, p = divmod(k, 2)
+
+        @pl.when((2 * tile + side >= strips) == (p == 1))
+        def _(side=side, strip=strip):
+            raw[:rows, side * STRIP : (side + 1) * STRIP] = strip[...]
 
     for r, o_ref in enumerate((o0, o1, o2, o3)):
         product = jnp.dot(
@@ -279,15 +280,21 @@
     rows = own.shape[1]
     order = 4 * rows
     here = pl.BlockSpec((rows, TILE), lambda t, flags: (0, first + t))
-    pieces = [(p * piece, (p + 1) * piece) for p in range(3)]
-    starts = [a // TILE for a, b in pieces]
+    strips = piece // STRIP
     distant_specs = [
-        pl.BlockSpec((rows, TILE), lambda t, flags, a=a // TILE, b=b // TILE: (0, jnp.clip(first + t, a, b - 1) - a))
-        for a, b in pieces
+        pl.BlockSpec(
+            (rows, STRIP),
+            lambda t, flags, start=p * strips, side=side: (
+                0,
+                jnp.clip(2 * (first + t) + side - start, 0, strips - 1),
+            ),
+        )
+        for side in range(2)
+        for p in range(2)
     ]
     there = pl.BlockSpec((rows, TILE), lambda t, flags: (0, t))
     *newton, squares = pl.pallas_call(
-        functools.partial(product_kernel, first, starts),
+        functools.partial(product_kernel, first, strips),
         grid_spec=pltpu.PrefetchScalarGridSpec(
             num_scalar_prefetch=1,
             grid=(tiles,),
@@ -314,7 +321,7 @@
             transcendentals=0,
         ),
         name="product",
-    )(flags, own, pair, inverse, *blocks, *distant)
+    )(flags, own, pair, inverse, *blocks, *distant, *distant)
     return newton, jnp.sum(squares)
 
 
@@ -401,12 +408,12 @@
         x = x + over_core(x)
         return x + over_side(x)
 
+    near, near_sq = take(momentum, near_index)
+    beside = lax.ppermute(near, "row", [(0, 1), (3, 2)])
     far, far_sq = take(momentum, 1 - near_index)
     middle = between_hubs(far)
-    near, near_sq = take(momentum, near_index)
-    beside = lax.ppermute(near, "row", [(0, 1), (3, 2)])
-
     norm_part = col_total(jnp.sum(far_sq) + jnp.sum(near_sq))
+
     def added(x, y):
         return (x.astype(jnp.float32) + y.astype(jnp.float32)).astype(jnp.bfloat16)
 
@@ -420,57 +427,44 @@
         return added(rows_of(side), over_side(rows_of(1 - side)))
 
     barrier = lax.optimization_barrier
-    piece = width // 3
-    far_pieces = [far[:, p * piece : (p + 1) * piece] for p in range(3)]
-    far_pieces[0], middle, beside, norm_part = barrier((far_pieces[0], middle, beside, norm_part))
+    piece = width // 2
+    far_first, beside, norm_part = barrier((far[:, :piece], beside, norm_part))
+    arrived = distant_permute(far_first)
     whole = {1: [(middle, width, 0)], 2: [(near, width, 0)], 3: [(beside, width, 0)]}
-
-    pairs_1, pairs_2 = [(1, 2), (1, 1), (2, 2)], [(3, 3), (3, 2), (3, 1)]
+    pairs_1, pairs_2 = [(2, 2), (3, 3), (3, 2)], [(1, 2), (1, 1), (3, 1)]
     pairs_3, pairs_4 = [(0, 0), (0, 1)], [(0, 2), (0, 3)]
-    arrived_0 = distant_permute(far_pieces[0])
+    first = gram_blocks(flags, pairs_1, {r: whole[r] for r in (2, 3)})
+    second = gram_blocks(flags, pairs_2, whole)
+    arrived, far_second, first, second = barrier((arrived, far[:, piece:], first, second))
+
+    def halves(h):
+        blocks = {1: middle, 2: near, 3: beside}
+        return {0: [(distant[h], piece, 0)]} | {r: [(blocks[r], piece, h)] for r in blocks}
+
+    distant = [arrived, distant_permute(far_second)]
+    first = over_pair(first)
+    second = over_pair(second)
+    (late,) = gram_blocks(flags, pairs_3 + pairs_4, halves(0), split=False)
+    first = over_sides(first)
+    distant[1], late, first, second, norm_part = barrier((distant[1], late, first, second, norm_part))
+
     norm_sum = (
         norm_part
         + lax.ppermute(norm_part, "row", [(0, 1), (3, 2)])
         + between_hubs(norm_part)
         + distant_permute(norm_part)
     )[0, 0]
-    first = gram_blocks(flags, pairs_1, {1: whole[1], 2: whole[2]})
-    arrived_0, far_pieces[1], first = barrier((arrived_0, far_pieces[1], first))
-
-    arrived_1 = distant_permute(far_pieces[1])
-    first = over_pair(first)
-    second = gram_blocks(flags, pairs_2, whole)
-    arrived_1, far_pieces[2], first, second, norm_sum = barrier(
-        (arrived_1, far_pieces[2], first, second, norm_sum)
-    )
-
-    arrived_2 = distant_permute(far_pieces[2])
-    first = over_sides(first)
-    second = over_pair(second)
-    distant = [arrived_0, arrived_1, arrived_2]
-
-    def of_pieces(some):
-        operands = {0: [(distant[p], piece, 0) for p in some]}
-        for r, block in ((1, middle), (2, near), (3, beside)):
-            operands[r] = [(block, piece, p) for p in some]
-        return operands
-
-    (late,) = gram_blocks(flags, pairs_3 + pairs_4, of_pieces([0, 1]), split=False)
-    distant[2], late, first, second = barrier((distant[2], late, first, second))
-
     other_first = between_hubs(first)
     second = over_sides(second)
-    last = of_pieces([2])
-    third = over_pair(gram_blocks(flags, pairs_3, {r: last[r] for r in (0, 1)}, total=late))
-    fourth = over_pair(
-        gram_blocks(flags, pairs_4, {r: last[r] for r in (0, 2, 3)}, total=late, total_at=2)
-    )
-    other_first, fourth = barrier((other_first, fourth))
+    third = gram_blocks(flags, pairs_3, {r: halves(1)[r] for r in (0, 1)}, total=late)
+    fourth = gram_blocks(flags, pairs_4, {r: halves(1)[r] for r in (0, 2, 3)}, total=late, total_at=2)
+    other_first, second, fourth = barrier((other_first, second, fourth))
     other_second = between_hubs(second)
-    third = over_sides(third)
-    fourth = over_sides(fourth)
+    third = over_sides(over_pair(third))
+    norm_sum, third = barrier((norm_sum, third))
+    other_third = between_hubs(third)
+    fourth = over_sides(over_pair(fourth))
     other_second, fourth = barrier((other_second, fourth))
-    other_third = between_hubs(third)
     other_fourth = between_hubs(fourth)
 
     spectral_edge = 1.0 + math.sqrt(M / N)
@@ -489,18 +483,19 @@
         return [here, over_core(here), across, over_core(across)]
 
     known(pairs_1, first, other_first)
+    known(pairs_2, second, other_second)
     groups = [gather(GATHERED[0])]
-    known(pairs_2, second, other_second)
+    groups[0][1], groups[0][2], other_third = barrier((groups[0][1], groups[0][2], other_third))
     known(pairs_3, third, other_third)
     groups.append(gather(GATHERED[1]))
-    groups[0], other_fourth = barrier((groups[0], other_fourth))
+    groups[1][1], other_fourth = barrier((groups[1][1], other_fourth))
     known(pairs_4, fourth, other_fourth)
     groups.append(gather(GATHERED[2]))
 
     own = poly_blocks(flags, groups)
     pair = over_core(own)
 
-    bounds = sorted({0, tiles * 2 // 9, tiles * 5 // 9, tiles})
+    bounds = sorted({0, tiles * 2 // 9, tiles * 5 // 9, tiles * 7 // 9, tiles})
     newton_sq = jnp.float32(0.0)
     scale = inverse.reshape(1)
     parts = []
@@ -573,7 +568,7 @@
         n_row, n_col = mesh.shape["row"], mesh.shape["col"]
         rows = momentum.shape[0] // (mesh.shape["groups"] * n_row)
         cols = momentum.shape[1] // n_col
-        hubs = n_row == 4 and n_col == 4 and rows % STRIP == 0 and cols % (6 * TILE) == 0
+        hubs = n_row == 4 and n_col == 4 and rows % STRIP == 0 and cols % (2 * TILE) == 0
         return jax.shard_map(
             per_device if hubs else per_device_general,
             mesh=mesh,

time: 726 us -> 713 us (0.982)
  waiting for transfers between devices: 334 us -> 276 us
  starting transfers between devices: 70.6 us -> 95.4 us
  Pallas kernels: 270 us -> 286 us
    ppermute x3 -> x4, waiting for transfers between devices: 23.9 us -> 0.01 us  [per_device(): lax.ppermute(newton[3], 'row', [(1, 0), (2, 3)])]
    ppermute x9, waiting for transfers between devices: 129 us -> 113 us  [over_side(): return lax.ppermute(x, 'col', [(k, k ^ 2) for k in range(4)])]
    ppermute x4 -> x3, starting transfers between devices: 27.2 us -> 42.8 us  [distant_permute(): return lax.ppermute(x, 'row', [(0, 2), (3, 1)])]
    pallas_call x3 -> x4, Pallas kernels: 109 us -> 123 us  [product(): pl.pallas_call(functools.partial(product_kernel, first, strips), grid_spe...]
    ppermute x3 -> x4, waiting for transfers between devices: 64.3 us -> 56.4 us  [per_device(): lax.ppermute(newton[0], 'row', [(2, 0), (1, 3)])]
    ppermute x1, waiting for transfers between devices: 12.1 us -> 4.43 us  [per_device(): lax.ppermute(hub_sq, 'row', [(2, 0), (1, 3)])]
    pallas_call x3 -> x4, Pallas kernels: 22.5 us -> 24.2 us  [finish(): pl.pallas_call(finish_kernel, grid_spec=pltpu.PrefetchScalarGridSpec(num_...]
  transfers between devices with their start and end apart: 46 -> 48, of which waited for: 21 -> 23; matrix products, arithmetic and copies ran while one was open for 4% -> 4% of each run, Pallas kernels for 23% -> 28%
where the time goes in v4:
time: 713 us; the launch traced here: 703 us
  Pallas kernels  286 us (40%)
  waiting for transfers between devices  276 us (39%)
  starting transfers between devices  95.4 us (13%)
  other arithmetic  23.9 us (3%)
  local copies, waits for them, and re-layouts  15.3 us (2%)
    pallas_call x4, Pallas kernels, product(): pl.pallas_call(functools.partial(product_kernel, first, strips), grid_spe...  123 us
    ppermute x9, waiting for transfers between devices, over_side(): return lax.ppermute(x, 'col', [(k, k ^ 2) for k in range(4)])  113 us
    pallas_call x5, Pallas kernels, gram_blocks(): pl.pallas_call(functools.partial(gram_kernel, pairs, where, pieces, int(t...  79.8 us
    ppermute x1, waiting for transfers between devices, per_device(): beside = lax.ppermute(near, 'row', [(0, 1), (3, 2)])  67.8 us
    ppermute x4, waiting for transfers between devices, per_device(): lax.ppermute(newton[0], 'row', [(2, 0), (1, 3)])  56.4 us
    pallas_call x1, Pallas kernels, poly_blocks(): pl.pallas_call(poly_kernel, grid_spec=pltpu.PrefetchScalarGridSpec(num_sc...  47.4 us
    ppermute x3, starting transfers between devices, distant_permute(): return lax.ppermute(x, 'row', [(0, 2), (3, 1)])  42.8 us
    pallas_call x4, Pallas kernels, finish(): pl.pallas_call(finish_kernel, grid_spec=pltpu.PrefetchScalarGridSpec(num_...  24.2 us
  transfers between devices with their start and end apart: 48, of which 23 were waited for; matrix products, arithmetic and copies ran while one was open for 4% of the time, Pallas kernels for 28%

profile of v4, /device:TPU:0, one launch (start us, length us, event | category | flops | bytes accessed | tf_op | source)
XLA Modules:
  0.0 702.7 jit_solution(5666148632049939203)
XLA Ops:
  5.9 6.9 collective-permute-start
  31.8 67.8 %collective-permute-done.refs_1_.refs_2_.refs_3_.s3 = bf16[896,2304]{1,0:T(8,128)(2,1)} collective-permute-done((bf16[896,2304]{1,0:T(8,128)(2,1)}, bf16[896,2304]{1,0:T(8,128)(2,1)}, u32[]{:S(2)}, u32[]{:S(2)}) %collective-permute-start) | collective-permute-done | bytes 4128800 | tf_op jit(solution)/shard_map/ppermute | solution.py:412
  105.8 19.9 %gram_blocks.5 = (bf16[3,448,896]{2,1,0:T(8,128)(2,1)}, bf16[3,448,896]{2,1,0:T(8,128)(2,1)}) custom-call(s32[4]{0:T(128)} %pad_add_fusion.flags, bf16[896,2304]{1,0:T(8,128)(2,1)} %get-tuple-element.88.refs_0_.refs_1_.refs_2_.s2, bf16[896,2304]{1,0:T(8,128)(2,1)} %collective-permute-done.refs_1_.refs_2_.refs_3_.s3), custom_call_target="tpu_custom_call" | custom-call | tf_op jit(solution)/shard_map/gram_blocks/pallas_call | solution.py:125
  125.7 21.1 %gram_blocks.6 = (bf16[3,448,896]{2,1,0:T(8,128)(2,1)}, bf16[3,448,896]{2,1,0:T(8,128)(2,1)}) custom-call(s32[4]{0:T(128)} %pad_add_fusion.flags, bf16[896,2304]{1,0:T(8,128)(2,1)} %collective-permute-done.4.refs_0_.refs_1_.s1, bf16[896,2304]{1,0:T(8,128)(2,1)} %get-tuple-element.88.refs_0_.refs_1_.refs_2_.s2, ...), custom_call_target="tpu_custom_call" | custom-call | tf_op jit(solution)/shard_map/gram_blocks/pallas_call | solution.py:125
  149.1 30.4 %collective-permute-start.5 = (bf16[896,1152]{1,0:T(8,128)(2,1)}, bf16[896,1152]{1,0:T(8,128)(2,1)}, u32[]{:S(2)}, u32[]{:S(2)}) collective-permute-start(bf16[896,1152]{1,0:T(8,128)(2,1)} %get-tuple-element.97), channel_id=1, source_target_pairs={{0,2},{3,1},{4,6},{7,5},{8,10},{11,9},{12,14},{15,13},{16,18},{19,... | collective-permute-start | bytes 6193160 | tf_op jit(solution)/shard_map/ppermute | solution.py:404
  185.2 16.4 %gram_blocks.7.refs_3_.refs_2_ = f32[4,896,896]{2,1,0:T(8,128)} custom-call(s32[4]{0:T(128)} %pad_add_fusion.flags, bf16[896,1152]{1,0:T(8,128)(2,1)} %copy-done.3, bf16[896,2304]{1,0:T(8,128)(2,1)} %collective-permute-done.4.refs_0_.refs_1_.s1, bf16[896,2304]{1,0:T(8,128)(2,1)} %get-tuple-element.88.refs_0_.refs_1_.refs_2_.s2, ...), custom_call_target="tpu_custom_call" | custom-call | tf_op jit(solution)/shard_map/gram_blocks/pallas_call | solution.py:125
  204.5 7.7 %collective-permute-done.7 = bf16[3,224,896]{2,1,0:T(8,128)(2,1)} collective-permute-done((bf16[3,224,896]{2,1,0:T(8,128)(2,1)}, bf16[3,224,896]{2,1,0:T(8,128)(2,1)}, u32[]{:S(2)}, u32[]{:S(2)}) %collective-permute-start.7) | collective-permute-done | bytes 1204256 | tf_op jit(solution)/shard_map/ppermute | solution.py:398
  213.8 9.0 %collective-permute-done.5.refs_0_.refs_1_.refs_3_ = bf16[896,1152]{1,0:T(8,128)(2,1)} collective-permute-done((bf16[896,1152]{1,0:T(8,128)(2,1)}, bf16[896,1152]{1,0:T(8,128)(2,1)}, u32[]{:S(2)}, u32[]{:S(2)}) %collective-permute-start.5) | collective-permute-done | bytes 2064416 | tf_op jit(solution)/shard_map/ppermute | solution.py:404
  226.5 10.9 %gram_blocks.9 = (bf16[2,448,896]{2,1,0:T(8,128)(2,1)}, bf16[2,448,896]{2,1,0:T(8,128)(2,1)}) custom-call(s32[4]{0:T(128)} %pad_add_fusion.flags, bf16[896,1152]{1,0:T(8,128)(2,1)} %collective-permute-done.5.refs_0_.refs_1_.refs_3_, bf16[896,2304]{1,0:T(8,128)(2,1)} %collective-permute-done.4.refs_0_.refs_1_.s1, f32[4,896,896]{2,1,0:T(8,128)} %gram_blocks.7.refs_3_.refs_2_), custom_call_target="tpu_custom_call" | custom-call | tf_op jit(solution)/shard_map/gram_blocks/pallas_call | solution.py:125
  237.5 11.5 %gram_blocks.8 = (bf16[2,448,896]{2,1,0:T(8,128)(2,1)}, bf16[2,448,896]{2,1,0:T(8,128)(2,1)}) custom-call(s32[4]{0:T(128)} %pad_add_fusion.flags, bf16[896,1152]{1,0:T(8,128)(2,1)} %collective-permute-done.5.refs_0_.refs_1_.refs_3_, bf16[896,2304]{1,0:T(8,128)(2,1)} %get-tuple-element.88.refs_0_.refs_1_.refs_2_.s2, ...), custom_call_target="tpu_custom_call" | custom-call | tf_op jit(solution)/shard_map/gram_blocks/pallas_call | solution.py:125
  259.5 6.8 collective-permute-start.16
  278.0 15.0 %collective-permute-done.13 = bf16[2,224,896]{2,1,0:T(8,128)(2,1)} collective-permute-done((bf16[2,224,896]{2,1,0:T(8,128)(2,1)}, bf16[2,224,896]{2,1,0:T(8,128)(2,1)}, u32[]{:S(2)}, u32[]{:S(2)}) %collective-permute-start.13) | collective-permute-done | bytes 802848 | tf_op jit(solution)/shard_map/ppermute | solution.py:398
  298.8 25.9 %collective-permute-done.20.refs_2_ = bf16[3,224,896]{2,1,0:T(8,128)(2,1)S(1)} collective-permute-done((bf16[3,224,896]{2,1,0:T(8,128)(2,1)S(1)}, bf16[3,224,896]{2,1,0:T(8,128)(2,1)S(1)}, u32[]{:S(2)}, u32[]{:S(2)}) %collective-permute-start.20) | collective-permute-done | bytes 1204256 | tf_op jit(solution)/shard_map/ppermute | solution.py:398
  332.6 32.1 %collective-permute-done.25.refs_6_ = bf16[4,224,896]{2,1,0:T(8,128)(2,1)S(1)} collective-permute-done((bf16[4,224,896]{2,1,0:T(8,128)(2,1)S(1)}, bf16[4,224,896]{2,1,0:T(8,128)(2,1)S(1)}, u32[]{:S(2)}, u32[]{:S(2)}) %collective-permute-start.25) | collective-permute-done | bytes 1605664 | tf_op jit(solution)/shard_map/ppermute | solution.py:398
  365.3 24.8 %collective-permute-done.28.refs_10_ = bf16[3,224,896]{2,1,0:T(8,128)(2,1)S(1)} collective-permute-done((bf16[3,224,896]{2,1,0:T(8,128)(2,1)S(1)}, bf16[3,224,896]{2,1,0:T(8,128)(2,1)S(1)}, u32[]{:S(2)}, u32[]{:S(2)}) %collective-permute-start.28) | collective-permute-done | bytes 1204256 | tf_op jit(solution)/shard_map/ppermute | solution.py:398
  393.2 47.4 %poly_blocks.1.own = bf16[5,896,896]{2,1,0:T(8,128)(2,1)} custom-call(s32[4]{0:T(128)} %pad_add_fusion.flags, bf16[3,224,896]{2,1,0:T(8,128)(2,1)} %copy-done.11, bf16[3,224,896]{2,1,0:T(8,128)(2,1)} %copy-done.23, bf16[3,224,896]{2,1,0:T(8,128)(2,1)} %copy-done.22, bf16[3,224,896]{2,1,0:T(8,128)(2,1)} %copy-done.25, bf16[4,224,896]{2,1,0:T(8,128)(2,1)} %copy-done.4, ...), custom_call_target="tpu_custom_call" | custom-call | flops 28772925440 | bytes 24084480 | tf_op jit(solution)/shard_map/poly_blocks/pallas_call | solution.py:212
  440.8 12.7 %collective-permute-done.30.pair = bf16[5,896,896]{2,1,0:T(8,128)(2,1)S(1)} collective-permute-done((bf16[5,896,896]{2,1,0:T(8,128)(2,1)}, bf16[5,896,896]{2,1,0:T(8,128)(2,1)S(1)}, u32[]{:S(2)}, u32[]{:S(2)}) %collective-permute-start.30) | collective-permute-done | bytes 8028192 | tf_op jit(solution)/shard_map/ppermute | solution.py:395
  456.7 28.9 %product.4 = (bf16[896,512]{1,0:T(8,128)(2,1)}, bf16[896,512]{1,0:T(8,128)(2,1)}, bf16[896,512]{1,0:T(8,128)(2,1)}, bf16[896,512]{1,0:T(8,128)(2,1)}, f32[1,256]{1,0:T(1,128)}) custom-call(s32[4]{0:T(128)} %pad_add_fusion.flags, bf16[5,896,896]{2,1,0:T(8,128)(2,1)} %poly_blocks.1.own, bf16[5,896,896]{2,1,0:T(8,128)(2,1)} %copy-done.17, f32[1]{0:T(128)} %bitcast.5.inverse, ...), custom_call_target="tpu_custom_call" | custom-call | flops 13153337344 | bytes 23396352 | tf_op jit(solution)/shard_map/product/pallas_call | solution.py:296
  491.3 36.2 %product.5 = (bf16[896,768]{1,0:T(8,128)(2,1)}, bf16[896,768]{1,0:T(8,128)(2,1)}, bf16[896,768]{1,0:T(8,128)(2,1)}, bf16[896,768]{1,0:T(8,128)(2,1)}, f32[1,256]{1,0:T(1,128)}) custom-call(s32[4]{0:T(128)} %pad_add_fusion.flags, bf16[5,896,896]{2,1,0:T(8,128)(2,1)} %poly_blocks.1.own, bf16[5,896,896]{2,1,0:T(8,128)(2,1)} %copy-done.17, f32[1]{0:T(128)} %bitcast.5.inverse, ...), custom_call_target="tpu_custom_call" | custom-call | flops 19730006016 | bytes 27066368 | tf_op jit(solution)/shard_map/product/pallas_call | solution.py:296
  539.3 28.9 %product.6 = (bf16[896,512]{1,0:T(8,128)(2,1)}, bf16[896,512]{1,0:T(8,128)(2,1)}, bf16[896,512]{1,0:T(8,128)(2,1)}, bf16[896,512]{1,0:T(8,128)(2,1)}, f32[1,256]{1,0:T(1,128)}) custom-call(s32[4]{0:T(128)} %pad_add_fusion.flags, bf16[5,896,896]{2,1,0:T(8,128)(2,1)} %poly_blocks.1.own, bf16[5,896,896]{2,1,0:T(8,128)(2,1)} %copy-done.17, f32[1]{0:T(128)} %bitcast.5.inverse, ...), custom_call_target="tpu_custom_call" | custom-call | flops 13153337344 | bytes 23396352 | tf_op jit(solution)/shard_map/product/pallas_call | solution.py:296
  574.5 28.9 %collective-permute-done.33.far = bf16[896,768]{1,0:T(8,128)(2,1)} collective-permute-done((bf16[896,768]{1,0:T(8,128)(2,1)}, bf16[896,768]{1,0:T(8,128)(2,1)}, u32[]{:S(2)}, u32[]{:S(2)}) %collective-permute-start.33) | collective-permute-done | bytes 1376288 | tf_op jit(solution)/shard_map/ppermute | solution.py:518
  603.4 28.8 %product.7 = (bf16[896,512]{1,0:T(8,128)(2,1)}, bf16[896,512]{1,0:T(8,128)(2,1)}, bf16[896,512]{1,0:T(8,128)(2,1)}, bf16[896,512]{1,0:T(8,128)(2,1)}, f32[1,256]{1,0:T(1,128)}) custom-call(s32[4]{0:T(128)} %pad_add_fusion.flags, bf16[5,896,896]{2,1,0:T(8,128)(2,1)} %poly_blocks.1.own, bf16[5,896,896]{2,1,0:T(8,128)(2,1)} %copy-done.17, f32[1]{0:T(128)} %bitcast.5.inverse, ...), custom_call_target="tpu_custom_call" | custom-call | flops 13153337344 | bytes 23396352 | tf_op jit(solution)/shard_map/product/pallas_call | solution.py:296
  661.1 7.4 %finish.5.rest_0_ = f32[896,4608]{1,0:T(8,128)} custom-call(s32[4]{0:T(128)} %pad_add_fusion.flags, f32[1]{0:T(128)} %bitcast.7.factor, bf16[896,768]{1,0:T(8,128)(2,1)} %get-tuple-element.161.own, bf16[896,768]{1,0:T(8,128)(2,1)} %copy-done.7, bf16[896,768]{1,0:T(8,128)(2,1)} %copy-done.8, ...), custom_call_target="tpu_custom_call", output_to_operand_aliasing={{}: (6, {})} | custom-call | flops 1376256 | bytes 11010048 | tf_op jit(solution)/shard_map/finish/pallas_call | solution.py:366
  674.1 21.6 %collective-permute-done.47.far = bf16[896,512]{1,0:T(8,128)(2,1)S(1)} collective-permute-done((bf16[896,512]{1,0:T(8,128)(2,1)}, bf16[896,512]{1,0:T(8,128)(2,1)S(1)}, u32[]{:S(2)}, u32[]{:S(2)}) %collective-permute-start.47) | collective-permute-done | bytes 917536 | tf_op jit(solution)/shard_map/ppermute | solution.py:518
  (178 shorter events, 149.4 us)
Async XLA Ops:
  5.9 93.6 %collective-permute-start = (bf16[896,2304]{1,0:T(8,128)(2,1)}, bf16[896,2304]{1,0:T(8,128)(2,1)}, u32[]{:S(2)}, u32[]{:S(2)}) collective-permute-start(bf16[896,2304]{1,0:T(8,128)(2,1)} %get-tuple-element.88.refs_0_.refs_1_.refs_2_.s2), channel_id=1, source_target_pairs={{0,1},{3,2},{4,5},{7,6},{8,9},{11,10},{12,13},{15,14},{16,17},{19,... | collective-permute-start | bytes 12386312 | tf_op jit(solution)/shard_map/ppermute | solution.py:412
  18.7 107.0 %collective-permute-start.4 = (bf16[896,2304]{1,0:T(8,128)(2,1)}, bf16[896,2304]{1,0:T(8,128)(2,1)}, u32[]{:S(2)}, u32[]{:S(2)}) collective-permute-start(bf16[896,2304]{1,0:T(8,128)(2,1)} %get-tuple-element.87), channel_id=1, source_target_pairs={{1,2},{2,1},{5,6},{6,5},{9,10},{10,9},{13,14},{14,13},{17,18},{18,... | collective-permute-start | bytes 12386312 | tf_op jit(solution)/shard_map/ppermute | solution.py:401
  99.6 49.1 %collective-permute-start.3 = (bf16[896,1152]{1,0:T(8,128)(2,1)}, bf16[896,1152]{1,0:T(8,128)(2,1)S(1)}, u32[]{:S(2)}, u32[]{:S(2)}) collective-permute-start(bf16[896,1152]{1,0:T(8,128)(2,1)} %get-tuple-element.91), channel_id=1, source_target_pairs={{0,2},{3,1},{4,6},{7,5},{8,10},{11,9},{12,14},{15,13},{16,18},{19,... | collective-permute-start | bytes 6193160 | tf_op jit(solution)/shard_map/ppermute | solution.py:404
  148.6 30.9 %collective-permute-start.6 = (bf16[3,448,896]{2,1,0:T(8,128)(2,1)}, bf16[3,448,896]{2,1,0:T(8,128)(2,1)}, u32[]{:S(2)}, u32[]{:S(2)}) collective-permute-start(bf16[3,448,896]{2,1,0:T(8,128)(2,1)} %get-tuple-element.100), channel_id=1, source_target_pairs={{0,4},{4,0},{8,12},{12,8},{1,5},{5,1},{9,13},{13,9},{2,6},{6,2},{1... | collective-permute-start | bytes 7225352 | tf_op jit(solution)/shard_map/ppermute | solution.py:395
  148.6 52.9 %collective-permute-start.8 = (bf16[3,448,896]{2,1,0:T(8,128)(2,1)}, bf16[3,448,896]{2,1,0:T(8,128)(2,1)}, u32[]{:S(2)}, u32[]{:S(2)}) collective-permute-start(bf16[3,448,896]{2,1,0:T(8,128)(2,1)} %get-tuple-element.102), channel_id=1, source_target_pairs={{0,4},{4,0},{8,12},{12,8},{1,5},{5,1},{9,13},{13,9},{2,6},{6,2},{1... | collective-permute-start | bytes 7225352 | tf_op jit(solution)/shard_map/ppermute | solution.py:395
  149.1 73.7 %collective-permute-start.5 = (bf16[896,1152]{1,0:T(8,128)(2,1)}, bf16[896,1152]{1,0:T(8,128)(2,1)}, u32[]{:S(2)}, u32[]{:S(2)}) collective-permute-start(bf16[896,1152]{1,0:T(8,128)(2,1)} %get-tuple-element.97), channel_id=1, source_target_pairs={{0,2},{3,1},{4,6},{7,5},{8,10},{11,9},{12,14},{15,13},{16,18},{19,... | collective-permute-start | bytes 6193160 | tf_op jit(solution)/shard_map/ppermute | solution.py:404
  183.7 28.5 %collective-permute-start.7 = (bf16[3,224,896]{2,1,0:T(8,128)(2,1)}, bf16[3,224,896]{2,1,0:T(8,128)(2,1)}, u32[]{:S(2)}, u32[]{:S(2)}) collective-permute-start(bf16[3,224,896]{2,1,0:T(8,128)(2,1)} %constant_dynamic-slice_fusion.3), channel_id=1, source_target_pairs={{0,8},{4,12},{8,0},{12,4},{1,9},{5,13},{9,1},{13,5},{2,10},{6,14},... | collective-permute-start | bytes 3612680 | tf_op jit(solution)/shard_map/ppermute | solution.py:398
  223.9 27.8 %collective-permute-start.10 = (bf16[3,224,896]{2,1,0:T(8,128)(2,1)}, bf16[3,224,896]{2,1,0:T(8,128)(2,1)S(1)}, u32[]{:S(2)}, u32[]{:S(2)}) collective-permute-start(bf16[3,224,896]{2,1,0:T(8,128)(2,1)} %constant_dynamic-slice_fusion.2), channel_id=1, source_target_pairs={{0,8},{4,12},{8,0},{12,4},{1,9},{5,13},{9,1},{13,5},{2,10},{6,14},... | collective-permute-start | bytes 3612680 | tf_op jit(solution)/shard_map/ppermute | solution.py:398
  225.4 27.7 %collective-permute-start.9 = (bf16[3,224,896]{2,1,0:T(8,128)(2,1)S(1)}, bf16[3,224,896]{2,1,0:T(8,128)(2,1)S(1)}, u32[]{:S(2)}, u32[]{:S(2)}) collective-permute-start(bf16[3,224,896]{2,1,0:T(8,128)(2,1)S(1)} %add_convert_fusion.5), channel_id=1, source_target_pairs={{1,2},{2,1},{5,6},{6,5},{9,10},{10,9},{13,14},{14,13},{17,18},{18,... | collective-permute-start | bytes 3612680 | tf_op jit(solution)/shard_map/ppermute | solution.py:401
  253.1 41.2 %collective-permute-start.11 = (bf16[3,224,896]{2,1,0:T(8,128)(2,1)}, bf16[3,224,896]{2,1,0:T(8,128)(2,1)}, u32[]{:S(2)}, u32[]{:S(2)}) collective-permute-start(bf16[3,224,896]{2,1,0:T(8,128)(2,1)} %add_convert_fusion.4), channel_id=1, source_target_pairs={{1,2},{2,1},{5,6},{6,5},{9,10},{10,9},{13,14},{14,13},{17,18},{18,... | collective-permute-start | bytes 3612680 | tf_op jit(solution)/shard_map/ppermute | solution.py:401
  258.3 34.7 %collective-permute-start.13 = (bf16[2,224,896]{2,1,0:T(8,128)(2,1)}, bf16[2,224,896]{2,1,0:T(8,128)(2,1)}, u32[]{:S(2)}, u32[]{:S(2)}) collective-permute-start(bf16[2,224,896]{2,1,0:T(8,128)(2,1)} %constant_dynamic-slice_fusion.1), channel_id=1, source_target_pairs={{0,8},{4,12},{8,0},{12,4},{1,9},{5,13},{9,1},{13,5},{2,10},{6,14},... | collective-permute-start | bytes 2408456 | tf_op jit(solution)/shard_map/ppermute | solution.py:398
  296.5 28.2 %collective-permute-start.20 = (bf16[3,224,896]{2,1,0:T(8,128)(2,1)S(1)}, bf16[3,224,896]{2,1,0:T(8,128)(2,1)S(1)}, u32[]{:S(2)}, u32[]{:S(2)}) collective-permute-start(bf16[3,224,896]{2,1,0:T(8,128)(2,1)S(1)} %fusion.1.refs_0_), channel_id=1, source_target_pairs={{0,8},{4,12},{8,0},{12,4},{1,9},{5,13},{9,1},{13,5},{2,10},{6,14},... | collective-permute-start | bytes 3612680 | tf_op jit(solution)/shard_map/ppermute | solution.py:398
  326.7 38.0 %collective-permute-start.25 = (bf16[4,224,896]{2,1,0:T(8,128)(2,1)S(1)}, bf16[4,224,896]{2,1,0:T(8,128)(2,1)S(1)}, u32[]{:S(2)}, u32[]{:S(2)}) collective-permute-start(bf16[4,224,896]{2,1,0:T(8,128)(2,1)S(1)} %fusion.refs_4_), channel_id=1, source_target_pairs={{0,8},{4,12},{8,0},{12,4},{1,9},{5,13},{9,1},{13,5},{2,10},{6,14},... | collective-permute-start | bytes 4816904 | tf_op jit(solution)/shard_map/ppermute | solution.py:398
  331.0 59.1 %collective-permute-start.28 = (bf16[3,224,896]{2,1,0:T(8,128)(2,1)S(1)}, bf16[3,224,896]{2,1,0:T(8,128)(2,1)S(1)}, u32[]{:S(2)}, u32[]{:S(2)}) collective-permute-start(bf16[3,224,896]{2,1,0:T(8,128)(2,1)S(1)} %fusion.2.refs_8_), channel_id=1, source_target_pairs={{0,8},{4,12},{8,0},{12,4},{1,9},{5,13},{9,1},{13,5},{2,10},{6,14},... | collective-permute-start | bytes 3612680 | tf_op jit(solution)/shard_map/ppermute | solution.py:398
  486.9 42.7 %collective-permute-start.34 = (bf16[896,512]{1,0:T(8,128)(2,1)}, bf16[896,512]{1,0:T(8,128)(2,1)}, u32[]{:S(2)}, u32[]{:S(2)}) collective-permute-start(bf16[896,512]{1,0:T(8,128)(2,1)} %get-tuple-element.133), channel_id=1, source_target_pairs={{1,0},{2,3},{5,4},{6,7},{9,8},{10,11},{13,12},{14,15},{17,16},{18,... | collective-permute-start | bytes 2752520 | tf_op jit(solution)/shard_map/ppermute | solution.py:516
  488.2 45.3 %collective-permute-start.35 = (bf16[896,512]{1,0:T(8,128)(2,1)}, bf16[896,512]{1,0:T(8,128)(2,1)}, u32[]{:S(2)}, u32[]{:S(2)}) collective-permute-start(bf16[896,512]{1,0:T(8,128)(2,1)} %get-tuple-element.134), channel_id=1, source_target_pairs={{1,2},{2,1},{5,6},{6,5},{9,10},{10,9},{13,14},{14,13},{17,18},{18,... | collective-permute-start | bytes 2752520 | tf_op jit(solution)/shard_map/ppermute | solution.py:401
  489.8 49.6 %collective-permute-start.36 = (bf16[896,512]{1,0:T(8,128)(2,1)}, bf16[896,512]{1,0:T(8,128)(2,1)}, u32[]{:S(2)}, u32[]{:S(2)}) collective-permute-start(bf16[896,512]{1,0:T(8,128)(2,1)} %get-tuple-element.135), channel_id=1, source_target_pairs={{2,0},{1,3},{6,4},{5,7},{10,8},{9,11},{14,12},{13,15},{18,16},{17,... | collective-permute-start | bytes 2752520 | tf_op jit(solution)/shard_map/ppermute | solution.py:518
  527.5 45.4 %collective-permute-start.31 = (bf16[896,768]{1,0:T(8,128)(2,1)}, bf16[896,768]{1,0:T(8,128)(2,1)S(1)}, u32[]{:S(2)}, u32[]{:S(2)}) collective-permute-start(bf16[896,768]{1,0:T(8,128)(2,1)} %get-tuple-element.129), channel_id=1, source_target_pairs={{1,0},{2,3},{5,4},{6,7},{9,8},{10,11},{13,12},{14,15},{17,16},{18,... | collective-permute-start | bytes 4128776 | tf_op jit(solution)/shard_map/ppermute | solution.py:516
  528.8 45.7 %collective-permute-start.32 = (bf16[896,768]{1,0:T(8,128)(2,1)}, bf16[896,768]{1,0:T(8,128)(2,1)S(1)}, u32[]{:S(2)}, u32[]{:S(2)}) collective-permute-start(bf16[896,768]{1,0:T(8,128)(2,1)} %get-tuple-element.130), channel_id=1, source_target_pairs={{1,2},{2,1},{5,6},{6,5},{9,10},{10,9},{13,14},{14,13},{17,18},{18,... | collective-permute-start | bytes 4128776 | tf_op jit(solution)/shard_map/ppermute | solution.py:401
  529.5 73.8 %collective-permute-start.33 = (bf16[896,768]{1,0:T(8,128)(2,1)}, bf16[896,768]{1,0:T(8,128)(2,1)}, u32[]{:S(2)}, u32[]{:S(2)}) collective-permute-start(bf16[896,768]{1,0:T(8,128)(2,1)} %get-tuple-element.131), channel_id=1, source_target_pairs={{2,0},{1,3},{6,4},{5,7},{10,8},{9,11},{14,12},{13,15},{18,16},{17,... | collective-permute-start | bytes 4128776 | tf_op jit(solution)/shard_map/ppermute | solution.py:518
  569.4 82.0 %collective-permute-start.42 = (bf16[896,512]{1,0:T(8,128)(2,1)}, bf16[896,512]{1,0:T(8,128)(2,1)}, u32[]{:S(2)}, u32[]{:S(2)}) collective-permute-start(bf16[896,512]{1,0:T(8,128)(2,1)} %get-tuple-element.149), channel_id=1, source_target_pairs={{1,0},{2,3},{5,4},{6,7},{9,8},{10,11},{13,12},{14,15},{17,16},{18,... | collective-permute-start | bytes 2752520 | tf_op jit(solution)/shard_map/ppermute | solution.py:516
  570.7 80.7 %collective-permute-start.43 = (bf16[896,512]{1,0:T(8,128)(2,1)}, bf16[896,512]{1,0:T(8,128)(2,1)}, u32[]{:S(2)}, u32[]{:S(2)}) collective-permute-start(bf16[896,512]{1,0:T(8,128)(2,1)} %get-tuple-element.150), channel_id=1, source_target_pairs={{1,2},{2,1},{5,6},{6,5},{9,10},{10,9},{13,14},{14,13},{17,18},{18,... | collective-permute-start | bytes 2752520 | tf_op jit(solution)/shard_map/ppermute | solution.py:401
  572.9 78.5 %collective-permute-start.44 = (bf16[896,512]{1,0:T(8,128)(2,1)}, bf16[896,512]{1,0:T(8,128)(2,1)}, u32[]{:S(2)}, u32[]{:S(2)}) collective-permute-start(bf16[896,512]{1,0:T(8,128)(2,1)} %get-tuple-element.151), channel_id=1, source_target_pairs={{2,0},{1,3},{6,4},{5,7},{10,8},{9,11},{14,12},{13,15},{18,16},{17,... | collective-permute-start | bytes 2752520 | tf_op jit(solution)/shard_map/ppermute | solution.py:518
  653.4 42.3 %collective-permute-start.47 = (bf16[896,512]{1,0:T(8,128)(2,1)}, bf16[896,512]{1,0:T(8,128)(2,1)S(1)}, u32[]{:S(2)}, u32[]{:S(2)}) collective-permute-start(bf16[896,512]{1,0:T(8,128)(2,1)} %get-tuple-element.156), channel_id=1, source_target_pairs={{2,0},{1,3},{6,4},{5,7},{10,8},{9,11},{14,12},{13,15},{18,16},{17,... | collective-permute-start | bytes 2752520 | tf_op jit(solution)/shard_map/ppermute | solution.py:518
  (51 other events, 731.2 us)

commit v5 on v4

--- a/solution.py
+++ b/solution.py
@@ -26,70 +26,68 @@
     return pair if sum(pair) == 3 and pair[0] != pair[1] else (3 - pair[0], 3 - pair[1])
 
 
-def take_kernel(index, x_ref, out_ref, sq_ref):
+def take_kernel(index, near_ref, far_ref, near_out, far_out, sq_ref):
     @pl.when(pl.program_id(0) == 0)
     def _():
         sq_ref[...] = jnp.zeros_like(sq_ref)
 
-    x = x_ref[...]
-    out_ref[...] = x.astype(jnp.bfloat16)
-    sq_ref[...] += jnp.sum(x * x, axis=0, keepdims=True)
+    near, far = near_ref[...], far_ref[...]
+    near_out[...] = near.astype(jnp.bfloat16)
+    far_out[...] = far.astype(jnp.bfloat16)
+    sq_ref[...] += jnp.sum(near * near + far * far, axis=0, keepdims=True)
 
 
 def take(momentum, index):
     rows, cols = momentum.shape
     width = cols // 2
-    step = rows // 4
+    step = rows // 8
+    half = jax.ShapeDtypeStruct((rows, width), jnp.bfloat16)
     return pl.pallas_call(
         take_kernel,
         grid_spec=pltpu.PrefetchScalarGridSpec(
             num_scalar_prefetch=1,
-            grid=(4,),
-            in_specs=[pl.BlockSpec((step, width), lambda t, index: (t, index[0]))],
+            grid=(8,),
+            in_specs=[
+                pl.BlockSpec((step, width), lambda t, index: (t, index[0])),
+                pl.BlockSpec((step, width), lambda t, index: (t, 1 - index[0])),
+            ],
             out_specs=[
+                pl.BlockSpec((step, width), lambda t, index: (t, 0)),
                 pl.BlockSpec((step, width), lambda t, index: (t, 0)),
                 pl.BlockSpec((1, width), lambda t, index: (0, 0)),
             ],
         ),
-        out_shape=[
-            jax.ShapeDtypeStruct((rows, width), jnp.bfloat16),
-            jax.ShapeDtypeStruct((1, width), jnp.float32),
-        ],
+        out_shape=[half, half, jax.ShapeDtypeStruct((1, width), jnp.float32)],
         compiler_params=pltpu.CompilerParams(vmem_limit_bytes=VMEM_BYTES),
         cost_estimate=pl.CostEstimate(
-            flops=2 * rows * width, bytes_accessed=6 * rows * width, transcendentals=0
-        ),
-        name="take_half",
-    )(index, momentum)
+            flops=4 * rows * width, bytes_accessed=12 * rows * width, transcendentals=0
+        ),
+        name="take_halves",
+    )(index, momentum, momentum)
 
 
 def gram_kernel(pairs, where, pieces, has_total, split, flags, *refs):
     left, core = flags[0] == 1, flags[1]
-    b, h = pl.program_id(0), pl.program_id(1)
+    b = pl.program_id(0)
     count = len(where) * pieces
     total = refs[count] if has_total else None
     outs = refs[count + has_total :]
-    share = outs[0].shape[1]
-    at = pl.multiple_of((jnp.where(h == 0, 1 - core, core) if split else h) * share, 16)
 
     def make(i, j):
         value = total[0] if has_total else 0.0
         for p in range(pieces):
             x, y = refs[where[i] * pieces + p], refs[where[j] * pieces + p]
             value += lax.dot_general(
-                x[pl.ds(at, share), :], y[...], (((1,), (1,)), ((), ())), preferred_element_type=jnp.float32
+                x[...], y[...], (((1,), (1,)), ((), ())), preferred_element_type=jnp.float32
             )
         if not split:
             outs[0][0] = value
             return
-
-        @pl.when(h == 0)
-        def _():
-            outs[1][0] = value.astype(jnp.bfloat16)
-
-        @pl.when(h == 1)
-        def _():
-            outs[0][0] = value.astype(jnp.bfloat16)
+        keep, send, whole = outs
+        share = keep.shape[1]
+        whole[...] = value.astype(jnp.bfloat16)
+        keep[0] = whole[pl.ds(pl.multiple_of(core * share, 16), share), :]
+        send[0] = whole[pl.ds(pl.multiple_of((1 - core) * share, 16), share), :]
 
     for k, (i, j) in enumerate(pairs):
         if (i, j) in ((1, 2), (0, 3)):
@@ -105,27 +103,28 @@
     rows = operands[pairs[0][0]][0][0].shape[0]
     share = rows // 2
     used = [piece for r in operands for piece in operands[r]]
-    specs = [pl.BlockSpec((rows, width), lambda b, h, flags, at=at: (0, at)) for _, width, at in used]
+    specs = [pl.BlockSpec((rows, width), lambda b, flags, at=at: (0, at)) for _, width, at in used]
     arrays = [array for array, _, _ in used]
     if total is not None:
         specs.append(
             pl.BlockSpec(
-                (1, share, rows),
-                lambda b, h, flags: (total_at + b, jnp.where(h == 0, 1 - flags[1], flags[1]), 0),
+                (1, rows, rows), lambda b, flags: (total_at + b, 0, 0)
             )
         )
         arrays.append(total)
     count = len(pairs)
     if split:
-        out_specs = [pl.BlockSpec((1, share, rows), lambda b, h, flags: (b, 0, 0))] * 2
+        out_specs = [pl.BlockSpec((1, share, rows), lambda b, flags: (b, 0, 0))] * 2
+        scratch = [pltpu.VMEM((rows, rows), jnp.bfloat16)]
         out_shape = [jax.ShapeDtypeStruct((count, share, rows), jnp.bfloat16)] * 2
     else:
-        out_specs = [pl.BlockSpec((1, share, rows), lambda b, h, flags: (b, h, 0))]
+        out_specs = [pl.BlockSpec((1, rows, rows), lambda b, flags: (b, 0, 0))]
+        scratch = []
         out_shape = [jax.ShapeDtypeStruct((count, rows, rows), jnp.float32)]
     return pl.pallas_call(
         functools.partial(gram_kernel, pairs, where, pieces, int(total is not None), split),
         grid_spec=pltpu.PrefetchScalarGridSpec(
-            num_scalar_prefetch=1, grid=(count, 2), in_specs=specs, out_specs=out_specs
+            num_scalar_prefetch=1, grid=(count,), in_specs=specs, out_specs=out_specs, scratch_shapes=scratch
         ),
         out_shape=out_shape,
         compiler_params=pltpu.CompilerParams(vmem_limit_bytes=VMEM_BYTES),
@@ -408,11 +407,10 @@
         x = x + over_core(x)
         return x + over_side(x)
 
-    near, near_sq = take(momentum, near_index)
+    near, far, squares = take(momentum, near_index)
     beside = lax.ppermute(near, "row", [(0, 1), (3, 2)])
-    far, far_sq = take(momentum, 1 - near_index)
     middle = between_hubs(far)
-    norm_part = col_total(jnp.sum(far_sq) + jnp.sum(near_sq))
+    norm_part = col_total(jnp.sum(squares))
 
     def added(x, y):
         return (x.astype(jnp.float32) + y.astype(jnp.float32)).astype(jnp.bfloat16)
@@ -435,25 +433,27 @@
     pairs_3, pairs_4 = [(0, 0), (0, 1)], [(0, 2), (0, 3)]
     first = gram_blocks(flags, pairs_1, {r: whole[r] for r in (2, 3)})
     second = gram_blocks(flags, pairs_2, whole)
-    arrived, far_second, first, second = barrier((arrived, far[:, piece:], first, second))
-
-    def halves(h):
-        blocks = {1: middle, 2: near, 3: beside}
-        return {0: [(distant[h], piece, 0)]} | {r: [(blocks[r], piece, h)] for r in blocks}
-
-    distant = [arrived, distant_permute(far_second)]
-    first = over_pair(first)
-    second = over_pair(second)
-    (late,) = gram_blocks(flags, pairs_3 + pairs_4, halves(0), split=False)
-    first = over_sides(first)
-    distant[1], late, first, second, norm_part = barrier((distant[1], late, first, second, norm_part))
-
     norm_sum = (
         norm_part
         + lax.ppermute(norm_part, "row", [(0, 1), (3, 2)])
         + between_hubs(norm_part)
         + distant_permute(norm_part)
     )[0, 0]
+    arrived, far_second, first, second, norm_sum = barrier(
+        (arrived, far[:, piece:], first, second, norm_sum)
+    )
+
+    def halves(h):
+        blocks = {1: middle, 2: near, 3: beside}
+        return {0: [(distant[h], piece, 0)]} | {r: [(blocks[r], piece, h)] for r in blocks}
+
+    distant = [arrived, distant_permute(far_second)]
+    first = over_pair(first)
+    second = over_pair(second)
+    (late,) = gram_blocks(flags, pairs_3 + pairs_4, halves(0), split=False)
+    first = over_sides(first)
+    distant[1], late, first, second = barrier((distant[1], late, first, second))
+
     other_first = between_hubs(first)
     second = over_sides(second)
     third = gram_blocks(flags, pairs_3, {r: halves(1)[r] for r in (0, 1)}, total=late)
@@ -461,7 +461,6 @@
     other_first, second, fourth = barrier((other_first, second, fourth))
     other_second = between_hubs(second)
     third = over_sides(over_pair(third))
-    norm_sum, third = barrier((norm_sum, third))
     other_third = between_hubs(third)
     fourth = over_sides(over_pair(fourth))
     other_second, fourth = barrier((other_second, fourth))

time: 713 us -> 693 us (0.972)
  starting transfers between devices: 95.4 us -> 61.1 us
  waiting for transfers between devices: 276 us -> 295 us
    ppermute x3, starting transfers between devices: 42.8 us -> 11.6 us  [distant_permute(): return lax.ppermute(x, 'row', [(0, 2), (3, 1)])]
    ppermute x9, waiting for transfers between devices: 113 us -> 130 us  [over_side(): return lax.ppermute(x, 'col', [(k, k ^ 2) for k in range(4)])]
  transfers between devices with their start and end apart: 48 -> 48, of which waited for: 23 -> 20; matrix products, arithmetic and copies ran while one was open for 4% -> 4% of each run, Pallas kernels for 28% -> 28%
where the time goes in v5:
time: 693 us; the launch traced here: 686 us
  waiting for transfers between devices  295 us (43%)
  Pallas kernels  282 us (41%)
  starting transfers between devices  61.1 us (9%)
  other arithmetic  24.7 us (4%)
  local copies, waits for them, and re-layouts  17 us (2%)
    ppermute x9, waiting for transfers between devices, over_side(): return lax.ppermute(x, 'col', [(k, k ^ 2) for k in range(4)])  130 us
    pallas_call x4, Pallas kernels, product(): pl.pallas_call(functools.partial(product_kernel, first, strips), grid_spe...  123 us
    pallas_call x5, Pallas kernels, gram_blocks(): pl.pallas_call(functools.partial(gram_kernel, pairs, where, pieces, int(t...  77.4 us
    ppermute x1, waiting for transfers between devices, per_device(): beside = lax.ppermute(near, 'row', [(0, 1), (3, 2)])  73.7 us
    ppermute x4, waiting for transfers between devices, per_device(): lax.ppermute(newton[0], 'row', [(2, 0), (1, 3)])  56.5 us
    pallas_call x1, Pallas kernels, poly_blocks(): pl.pallas_call(poly_kernel, grid_spec=pltpu.PrefetchScalarGridSpec(num_sc...  47.4 us
    pallas_call x4, Pallas kernels, finish(): pl.pallas_call(finish_kernel, grid_spec=pltpu.PrefetchScalarGridSpec(num_...  24.2 us
    ppermute x13, waiting for transfers between devices, over_core(): return lax.ppermute(x, 'col', [(k, k ^ 1) for k in range(4)])  17.8 us
  transfers between devices with their start and end apart: 48, of which 20 were waited for; matrix products, arithmetic and copies ran while one was open for 4% of the time, Pallas kernels for 28%

profile of v5, /device:TPU:0, one launch (start us, length us, event | category | flops | bytes accessed | tf_op | source)
XLA Modules:
  0.0 685.6 jit_solution(1848147468011480717)
XLA Ops:
  0.0 10.6 %take_halves.1 = (bf16[896,2304]{1,0:T(8,128)(2,1)}, bf16[896,2304]{1,0:T(8,128)(2,1)}, f32[1,2304]{1,0:T(1,128)}) custom-call(s32[1]{0:T(128)} %bitcast.index, f32[896,4608]{1,0:T(8,128)} %far_ref.1, f32[896,4608]{1,0:T(8,128)} %far_ref.1), custom_call_target="tpu_custom_call" | custom-call | flops 8257536 | bytes 24772608 | tf_op jit(solution)/shard_map/take_halves/pallas_call | solution.py:45
  10.6 7.0 %collective-permute-start = (bf16[896,2304]{1,0:T(8,128)(2,1)}, bf16[896,2304]{1,0:T(8,128)(2,1)}, u32[]{:S(2)}, u32[]{:S(2)}) collective-permute-start(bf16[896,2304]{1,0:T(8,128)(2,1)} %get-tuple-element.85.refs_0_.refs_1_.refs_2_.s2), channel_id=1, source_target_pairs={{0,1},{3,2},{4,5},{7,6},{8,9},{11,10},{12,13},{15,14},{16,17},{19,... | collective-permute-start | bytes 12386312 | tf_op jit(solution)/shard_map/ppermute | solution.py:411
  30.5 73.7 %collective-permute-done.refs_1_.refs_2_.refs_3_.s3 = bf16[896,2304]{1,0:T(8,128)(2,1)} collective-permute-done((bf16[896,2304]{1,0:T(8,128)(2,1)}, bf16[896,2304]{1,0:T(8,128)(2,1)}, u32[]{:S(2)}, u32[]{:S(2)}) %collective-permute-start) | collective-permute-done | bytes 4128800 | tf_op jit(solution)/shard_map/ppermute | solution.py:411
  115.4 19.1 %gram_blocks.5 = (bf16[3,448,896]{2,1,0:T(8,128)(2,1)}, bf16[3,448,896]{2,1,0:T(8,128)(2,1)}) custom-call(s32[4]{0:T(128)} %pad_add_fusion.flags, bf16[896,2304]{1,0:T(8,128)(2,1)} %get-tuple-element.85.refs_0_.refs_1_.refs_2_.s2, bf16[896,2304]{1,0:T(8,128)(2,1)} %collective-permute-done.refs_1_.refs_2_.refs_3_.s3), custom_call_target="tpu_custom_call" | custom-call | tf_op jit(solution)/shard_map/gram_blocks/pallas_call | solution.py:124
  134.5 20.5 %gram_blocks.6 = (bf16[3,448,896]{2,1,0:T(8,128)(2,1)}, bf16[3,448,896]{2,1,0:T(8,128)(2,1)}) custom-call(s32[4]{0:T(128)} %pad_add_fusion.flags, bf16[896,2304]{1,0:T(8,128)(2,1)} %collective-permute-done.4.refs_0_.refs_1_.s1, bf16[896,2304]{1,0:T(8,128)(2,1)} %get-tuple-element.85.refs_0_.refs_1_.refs_2_.s2, ...), custom_call_target="tpu_custom_call" | custom-call | tf_op jit(solution)/shard_map/gram_blocks/pallas_call | solution.py:124
  166.6 16.4 %gram_blocks.7.refs_3_.refs_2_ = f32[4,896,896]{2,1,0:T(8,128)} custom-call(s32[4]{0:T(128)} %pad_add_fusion.flags, bf16[896,1152]{1,0:T(8,128)(2,1)} %copy-done.2, bf16[896,2304]{1,0:T(8,128)(2,1)} %collective-permute-done.4.refs_0_.refs_1_.s1, bf16[896,2304]{1,0:T(8,128)(2,1)} %get-tuple-element.85.refs_0_.refs_1_.refs_2_.s2, ...), custom_call_target="tpu_custom_call" | custom-call | tf_op jit(solution)/shard_map/gram_blocks/pallas_call | solution.py:124
  186.0 7.6 %collective-permute-done.10 = bf16[3,224,896]{2,1,0:T(8,128)(2,1)} collective-permute-done((bf16[3,224,896]{2,1,0:T(8,128)(2,1)}, bf16[3,224,896]{2,1,0:T(8,128)(2,1)}, u32[]{:S(2)}, u32[]{:S(2)}) %collective-permute-start.10) | collective-permute-done | bytes 1204256 | tf_op jit(solution)/shard_map/ppermute | solution.py:397
  195.2 9.2 %collective-permute-done.8.refs_0_.refs_1_.refs_3_ = bf16[896,1152]{1,0:T(8,128)(2,1)} collective-permute-done((bf16[896,1152]{1,0:T(8,128)(2,1)}, bf16[896,1152]{1,0:T(8,128)(2,1)}, u32[]{:S(2)}, u32[]{:S(2)}) %collective-permute-start.8) | collective-permute-done | bytes 2064416 | tf_op jit(solution)/shard_map/ppermute | solution.py:403
  207.8 10.5 %gram_blocks.9 = (bf16[2,448,896]{2,1,0:T(8,128)(2,1)}, bf16[2,448,896]{2,1,0:T(8,128)(2,1)}) custom-call(s32[4]{0:T(128)} %pad_add_fusion.flags, bf16[896,1152]{1,0:T(8,128)(2,1)} %collective-permute-done.8.refs_0_.refs_1_.refs_3_, bf16[896,2304]{1,0:T(8,128)(2,1)} %collective-permute-done.4.refs_0_.refs_1_.s1, f32[4,896,896]{2,1,0:T(8,128)} %gram_blocks.7.refs_3_.refs_2_), custom_call_target="tpu_custom_call" | custom-call | tf_op jit(solution)/shard_map/gram_blocks/pallas_call | solution.py:124
  218.3 10.9 %gram_blocks.8 = (bf16[2,448,896]{2,1,0:T(8,128)(2,1)}, bf16[2,448,896]{2,1,0:T(8,128)(2,1)}) custom-call(s32[4]{0:T(128)} %pad_add_fusion.flags, bf16[896,1152]{1,0:T(8,128)(2,1)} %collective-permute-done.8.refs_0_.refs_1_.refs_3_, bf16[896,2304]{1,0:T(8,128)(2,1)} %get-tuple-element.85.refs_0_.refs_1_.refs_2_.s2, ...), custom_call_target="tpu_custom_call" | custom-call | tf_op jit(solution)/shard_map/gram_blocks/pallas_call | solution.py:124
  242.2 16.7 %collective-permute-done.20 = bf16[2,224,896]{2,1,0:T(8,128)(2,1)} collective-permute-done((bf16[2,224,896]{2,1,0:T(8,128)(2,1)}, bf16[2,224,896]{2,1,0:T(8,128)(2,1)}, u32[]{:S(2)}, u32[]{:S(2)}) %collective-permute-start.20) | collective-permute-done | bytes 802848 | tf_op jit(solution)/shard_map/ppermute | solution.py:397
  260.3 15.5 %collective-permute-done.16 = bf16[2,224,896]{2,1,0:T(8,128)(2,1)} collective-permute-done((bf16[2,224,896]{2,1,0:T(8,128)(2,1)}, bf16[2,224,896]{2,1,0:T(8,128)(2,1)}, u32[]{:S(2)}, u32[]{:S(2)}) %collective-permute-start.16) | collective-permute-done | bytes 802848 | tf_op jit(solution)/shard_map/ppermute | solution.py:397
  281.7 25.7 %collective-permute-done.18.refs_2_ = bf16[3,224,896]{2,1,0:T(8,128)(2,1)S(1)} collective-permute-done((bf16[3,224,896]{2,1,0:T(8,128)(2,1)S(1)}, bf16[3,224,896]{2,1,0:T(8,128)(2,1)S(1)}, u32[]{:S(2)}, u32[]{:S(2)}) %collective-permute-start.18) | collective-permute-done | bytes 1204256 | tf_op jit(solution)/shard_map/ppermute | solution.py:397
  315.7 31.9 %collective-permute-done.25.refs_6_ = bf16[4,224,896]{2,1,0:T(8,128)(2,1)S(1)} collective-permute-done((bf16[4,224,896]{2,1,0:T(8,128)(2,1)S(1)}, bf16[4,224,896]{2,1,0:T(8,128)(2,1)S(1)}, u32[]{:S(2)}, u32[]{:S(2)}) %collective-permute-start.25) | collective-permute-done | bytes 1605664 | tf_op jit(solution)/shard_map/ppermute | solution.py:397
  348.2 24.8 %collective-permute-done.28.refs_10_ = bf16[3,224,896]{2,1,0:T(8,128)(2,1)S(1)} collective-permute-done((bf16[3,224,896]{2,1,0:T(8,128)(2,1)S(1)}, bf16[3,224,896]{2,1,0:T(8,128)(2,1)S(1)}, u32[]{:S(2)}, u32[]{:S(2)}) %collective-permute-start.28) | collective-permute-done | bytes 1204256 | tf_op jit(solution)/shard_map/ppermute | solution.py:397
  376.1 47.4 %poly_blocks.1.own = bf16[5,896,896]{2,1,0:T(8,128)(2,1)} custom-call(s32[4]{0:T(128)} %pad_add_fusion.flags, bf16[3,224,896]{2,1,0:T(8,128)(2,1)} %copy-done.8, bf16[3,224,896]{2,1,0:T(8,128)(2,1)} %copy-done.21, bf16[3,224,896]{2,1,0:T(8,128)(2,1)} %copy-done.20, bf16[3,224,896]{2,1,0:T(8,128)(2,1)} %copy-done.23, bf16[4,224,896]{2,1,0:T(8,128)(2,1)} %copy-done.3, ...), custom_call_target="tpu_custom_call" | custom-call | flops 28772925440 | bytes 24084480 | tf_op jit(solution)/shard_map/poly_blocks/pallas_call | solution.py:211
  423.7 12.7 %collective-permute-done.30.pair = bf16[5,896,896]{2,1,0:T(8,128)(2,1)S(1)} collective-permute-done((bf16[5,896,896]{2,1,0:T(8,128)(2,1)}, bf16[5,896,896]{2,1,0:T(8,128)(2,1)S(1)}, u32[]{:S(2)}, u32[]{:S(2)}) %collective-permute-start.30) | collective-permute-done | bytes 8028192 | tf_op jit(solution)/shard_map/ppermute | solution.py:394
  439.6 28.9 %product.4 = (bf16[896,512]{1,0:T(8,128)(2,1)}, bf16[896,512]{1,0:T(8,128)(2,1)}, bf16[896,512]{1,0:T(8,128)(2,1)}, bf16[896,512]{1,0:T(8,128)(2,1)}, f32[1,256]{1,0:T(1,128)}) custom-call(s32[4]{0:T(128)} %pad_add_fusion.flags, bf16[5,896,896]{2,1,0:T(8,128)(2,1)} %poly_blocks.1.own, bf16[5,896,896]{2,1,0:T(8,128)(2,1)} %copy-done.15, f32[1]{0:T(128)} %bitcast.5.inverse, ...), custom_call_target="tpu_custom_call" | custom-call | flops 13153337344 | bytes 23396352 | tf_op jit(solution)/shard_map/product/pallas_call | solution.py:295
  474.3 36.2 %product.5 = (bf16[896,768]{1,0:T(8,128)(2,1)}, bf16[896,768]{1,0:T(8,128)(2,1)}, bf16[896,768]{1,0:T(8,128)(2,1)}, bf16[896,768]{1,0:T(8,128)(2,1)}, f32[1,256]{1,0:T(1,128)}) custom-call(s32[4]{0:T(128)} %pad_add_fusion.flags, bf16[5,896,896]{2,1,0:T(8,128)(2,1)} %poly_blocks.1.own, bf16[5,896,896]{2,1,0:T(8,128)(2,1)} %copy-done.15, f32[1]{0:T(128)} %bitcast.5.inverse, ...), custom_call_target="tpu_custom_call" | custom-call | flops 19730006016 | bytes 27066368 | tf_op jit(solution)/shard_map/product/pallas_call | solution.py:295
  522.4 28.9 %product.6 = (bf16[896,512]{1,0:T(8,128)(2,1)}, bf16[896,512]{1,0:T(8,128)(2,1)}, bf16[896,512]{1,0:T(8,128)(2,1)}, bf16[896,512]{1,0:T(8,128)(2,1)}, f32[1,256]{1,0:T(1,128)}) custom-call(s32[4]{0:T(128)} %pad_add_fusion.flags, bf16[5,896,896]{2,1,0:T(8,128)(2,1)} %poly_blocks.1.own, bf16[5,896,896]{2,1,0:T(8,128)(2,1)} %copy-done.15, f32[1]{0:T(128)} %bitcast.5.inverse, ...), custom_call_target="tpu_custom_call" | custom-call | flops 13153337344 | bytes 23396352 | tf_op jit(solution)/shard_map/product/pallas_call | solution.py:295
  557.4 29.0 %collective-permute-done.33.far = bf16[896,768]{1,0:T(8,128)(2,1)} collective-permute-done((bf16[896,768]{1,0:T(8,128)(2,1)}, bf16[896,768]{1,0:T(8,128)(2,1)}, u32[]{:S(2)}, u32[]{:S(2)}) %collective-permute-start.33) | collective-permute-done | bytes 1376288 | tf_op jit(solution)/shard_map/ppermute | solution.py:517
  586.5 28.8 %product.7 = (bf16[896,512]{1,0:T(8,128)(2,1)}, bf16[896,512]{1,0:T(8,128)(2,1)}, bf16[896,512]{1,0:T(8,128)(2,1)}, bf16[896,512]{1,0:T(8,128)(2,1)}, f32[1,256]{1,0:T(1,128)}) custom-call(s32[4]{0:T(128)} %pad_add_fusion.flags, bf16[5,896,896]{2,1,0:T(8,128)(2,1)} %poly_blocks.1.own, bf16[5,896,896]{2,1,0:T(8,128)(2,1)} %copy-done.15, f32[1]{0:T(128)} %bitcast.5.inverse, ...), custom_call_target="tpu_custom_call" | custom-call | flops 13153337344 | bytes 23396352 | tf_op jit(solution)/shard_map/product/pallas_call | solution.py:295
  644.2 7.4 %finish.5.rest_0_ = f32[896,4608]{1,0:T(8,128)} custom-call(s32[4]{0:T(128)} %pad_add_fusion.flags, f32[1]{0:T(128)} %bitcast.7.factor, bf16[896,768]{1,0:T(8,128)(2,1)} %get-tuple-element.155.own, bf16[896,768]{1,0:T(8,128)(2,1)} %copy-done.6, bf16[896,768]{1,0:T(8,128)(2,1)} %copy-done.7, ...), custom_call_target="tpu_custom_call", output_to_operand_aliasing={{}: (6, {})} | custom-call | flops 1376256 | bytes 11010048 | tf_op jit(solution)/shard_map/finish/pallas_call | solution.py:365
  657.2 21.6 %collective-permute-done.47.far = bf16[896,512]{1,0:T(8,128)(2,1)S(1)} collective-permute-done((bf16[896,512]{1,0:T(8,128)(2,1)}, bf16[896,512]{1,0:T(8,128)(2,1)S(1)}, u32[]{:S(2)}, u32[]{:S(2)}) %collective-permute-start.47) | collective-permute-done | bytes 917536 | tf_op jit(solution)/shard_map/ppermute | solution.py:517
  (172 shorter events, 139.6 us)
Async XLA Ops:
  10.6 93.7 %collective-permute-start = (bf16[896,2304]{1,0:T(8,128)(2,1)}, bf16[896,2304]{1,0:T(8,128)(2,1)}, u32[]{:S(2)}, u32[]{:S(2)}) collective-permute-start(bf16[896,2304]{1,0:T(8,128)(2,1)} %get-tuple-element.85.refs_0_.refs_1_.refs_2_.s2), channel_id=1, source_target_pairs={{0,1},{3,2},{4,5},{7,6},{8,9},{11,10},{12,13},{15,14},{16,17},{19,... | collective-permute-start | bytes 12386312 | tf_op jit(solution)/shard_map/ppermute | solution.py:411
  17.6 117.0 %collective-permute-start.4 = (bf16[896,2304]{1,0:T(8,128)(2,1)}, bf16[896,2304]{1,0:T(8,128)(2,1)}, u32[]{:S(2)}, u32[]{:S(2)}) collective-permute-start(bf16[896,2304]{1,0:T(8,128)(2,1)} %get-tuple-element.84), channel_id=1, source_target_pairs={{1,2},{2,1},{5,6},{6,5},{9,10},{10,9},{13,14},{14,13},{17,18},{18,... | collective-permute-start | bytes 12386312 | tf_op jit(solution)/shard_map/ppermute | solution.py:400
  104.2 51.5 %collective-permute-start.3 = (bf16[896,1152]{1,0:T(8,128)(2,1)}, bf16[896,1152]{1,0:T(8,128)(2,1)S(1)}, u32[]{:S(2)}, u32[]{:S(2)}) collective-permute-start(bf16[896,1152]{1,0:T(8,128)(2,1)} %get-tuple-element.87), channel_id=1, source_target_pairs={{0,2},{3,1},{4,6},{7,5},{8,10},{11,9},{12,14},{15,13},{16,18},{19,... | collective-permute-start | bytes 6193160 | tf_op jit(solution)/shard_map/ppermute | solution.py:403
  109.8 45.3 %collective-permute-start.7 = (f32[8,128]{1,0:T(8,128)S(1)}, f32[8,128]{1,0:T(8,128)S(1)}, u32[]{:S(2)}, u32[]{:S(2)}) collective-permute-start(f32[8,128]{1,0:T(8,128)S(1)} %fusion.5), channel_id=1, source_target_pairs={{0,2},{3,1},{4,6},{7,5},{8,10},{11,9},{12,14},{15,13},{16,18},{19,... | collective-permute-start | bytes 12296 | tf_op jit(solution)/shard_map/ppermute | solution.py:403
  111.1 44.0 %collective-permute-start.6 = (f32[8,128]{1,0:T(8,128)S(1)}, f32[8,128]{1,0:T(8,128)S(1)}, u32[]{:S(2)}, u32[]{:S(2)}) collective-permute-start(f32[8,128]{1,0:T(8,128)S(1)} %fusion.5), channel_id=1, source_target_pairs={{1,2},{2,1},{5,6},{6,5},{9,10},{10,9},{13,14},{14,13},{17,18},{18,... | collective-permute-start | bytes 12296 | tf_op jit(solution)/shard_map/ppermute | solution.py:400
  111.8 43.3 %collective-permute-start.5 = (f32[8,128]{1,0:T(8,128)S(1)}, f32[8,128]{1,0:T(8,128)S(1)}, u32[]{:S(2)}, u32[]{:S(2)}) collective-permute-start(f32[8,128]{1,0:T(8,128)S(1)} %fusion.5), channel_id=1, source_target_pairs={{0,1},{3,2},{4,5},{7,6},{8,9},{11,10},{12,13},{15,14},{16,17},{19,... | collective-permute-start | bytes 12296 | tf_op jit(solution)/shard_map/ppermute | solution.py:438
  156.2 48.2 %collective-permute-start.8 = (bf16[896,1152]{1,0:T(8,128)(2,1)}, bf16[896,1152]{1,0:T(8,128)(2,1)}, u32[]{:S(2)}, u32[]{:S(2)}) collective-permute-start(bf16[896,1152]{1,0:T(8,128)(2,1)} %get-tuple-element.94), channel_id=1, source_target_pairs={{0,2},{3,1},{4,6},{7,5},{8,10},{11,9},{12,14},{15,13},{16,18},{19,... | collective-permute-start | bytes 6193160 | tf_op jit(solution)/shard_map/ppermute | solution.py:403
  165.1 28.5 %collective-permute-start.10 = (bf16[3,224,896]{2,1,0:T(8,128)(2,1)}, bf16[3,224,896]{2,1,0:T(8,128)(2,1)}, u32[]{:S(2)}, u32[]{:S(2)}) collective-permute-start(bf16[3,224,896]{2,1,0:T(8,128)(2,1)} %constant_dynamic-slice_fusion.3), channel_id=1, source_target_pairs={{0,8},{4,12},{8,0},{12,4},{1,9},{5,13},{9,1},{13,5},{2,10},{6,14},... | collective-permute-start | bytes 3612680 | tf_op jit(solution)/shard_map/ppermute | solution.py:397
  205.6 27.8 %collective-permute-start.13 = (bf16[3,224,896]{2,1,0:T(8,128)(2,1)}, bf16[3,224,896]{2,1,0:T(8,128)(2,1)S(1)}, u32[]{:S(2)}, u32[]{:S(2)}) collective-permute-start(bf16[3,224,896]{2,1,0:T(8,128)(2,1)} %constant_dynamic-slice_fusion.2), channel_id=1, source_target_pairs={{0,8},{4,12},{8,0},{12,4},{1,9},{5,13},{9,1},{13,5},{2,10},{6,14},... | collective-permute-start | bytes 3612680 | tf_op jit(solution)/shard_map/ppermute | solution.py:397
  234.8 42.3 %collective-permute-start.14 = (bf16[3,224,896]{2,1,0:T(8,128)(2,1)}, bf16[3,224,896]{2,1,0:T(8,128)(2,1)}, u32[]{:S(2)}, u32[]{:S(2)}) collective-permute-start(bf16[3,224,896]{2,1,0:T(8,128)(2,1)} %add_convert_fusion.4), channel_id=1, source_target_pairs={{1,2},{2,1},{5,6},{6,5},{9,10},{10,9},{13,14},{14,13},{17,18},{18,... | collective-permute-start | bytes 3612680 | tf_op jit(solution)/shard_map/ppermute | solution.py:400
  240.8 34.9 %collective-permute-start.16 = (bf16[2,224,896]{2,1,0:T(8,128)(2,1)}, bf16[2,224,896]{2,1,0:T(8,128)(2,1)}, u32[]{:S(2)}, u32[]{:S(2)}) collective-permute-start(bf16[2,224,896]{2,1,0:T(8,128)(2,1)} %constant_dynamic-slice_fusion.1), channel_id=1, source_target_pairs={{0,8},{4,12},{8,0},{12,4},{1,9},{5,13},{9,1},{13,5},{2,10},{6,14},... | collective-permute-start | bytes 2408456 | tf_op jit(solution)/shard_map/ppermute | solution.py:397
  279.2 28.2 %collective-permute-start.18 = (bf16[3,224,896]{2,1,0:T(8,128)(2,1)S(1)}, bf16[3,224,896]{2,1,0:T(8,128)(2,1)S(1)}, u32[]{:S(2)}, u32[]{:S(2)}) collective-permute-start(bf16[3,224,896]{2,1,0:T(8,128)(2,1)S(1)} %fusion.1.refs_0_), channel_id=1, source_target_pairs={{0,8},{4,12},{8,0},{12,4},{1,9},{5,13},{9,1},{13,5},{2,10},{6,14},... | collective-permute-start | bytes 3612680 | tf_op jit(solution)/shard_map/ppermute | solution.py:397
  309.7 38.0 %collective-permute-start.25 = (bf16[4,224,896]{2,1,0:T(8,128)(2,1)S(1)}, bf16[4,224,896]{2,1,0:T(8,128)(2,1)S(1)}, u32[]{:S(2)}, u32[]{:S(2)}) collective-permute-start(bf16[4,224,896]{2,1,0:T(8,128)(2,1)S(1)} %fusion.refs_4_), channel_id=1, source_target_pairs={{0,8},{4,12},{8,0},{12,4},{1,9},{5,13},{9,1},{13,5},{2,10},{6,14},... | collective-permute-start | bytes 4816904 | tf_op jit(solution)/shard_map/ppermute | solution.py:397
  314.1 58.9 %collective-permute-start.28 = (bf16[3,224,896]{2,1,0:T(8,128)(2,1)S(1)}, bf16[3,224,896]{2,1,0:T(8,128)(2,1)S(1)}, u32[]{:S(2)}, u32[]{:S(2)}) collective-permute-start(bf16[3,224,896]{2,1,0:T(8,128)(2,1)S(1)} %fusion.2.refs_8_), channel_id=1, source_target_pairs={{0,8},{4,12},{8,0},{12,4},{1,9},{5,13},{9,1},{13,5},{2,10},{6,14},... | collective-permute-start | bytes 3612680 | tf_op jit(solution)/shard_map/ppermute | solution.py:397
  469.8 42.8 %collective-permute-start.34 = (bf16[896,512]{1,0:T(8,128)(2,1)}, bf16[896,512]{1,0:T(8,128)(2,1)}, u32[]{:S(2)}, u32[]{:S(2)}) collective-permute-start(bf16[896,512]{1,0:T(8,128)(2,1)} %get-tuple-element.127), channel_id=1, source_target_pairs={{1,0},{2,3},{5,4},{6,7},{9,8},{10,11},{13,12},{14,15},{17,16},{18,... | collective-permute-start | bytes 2752520 | tf_op jit(solution)/shard_map/ppermute | solution.py:515
  471.1 45.5 %collective-permute-start.35 = (bf16[896,512]{1,0:T(8,128)(2,1)}, bf16[896,512]{1,0:T(8,128)(2,1)}, u32[]{:S(2)}, u32[]{:S(2)}) collective-permute-start(bf16[896,512]{1,0:T(8,128)(2,1)} %get-tuple-element.128), channel_id=1, source_target_pairs={{1,2},{2,1},{5,6},{6,5},{9,10},{10,9},{13,14},{14,13},{17,18},{18,... | collective-permute-start | bytes 2752520 | tf_op jit(solution)/shard_map/ppermute | solution.py:400
  472.7 49.7 %collective-permute-start.36 = (bf16[896,512]{1,0:T(8,128)(2,1)}, bf16[896,512]{1,0:T(8,128)(2,1)}, u32[]{:S(2)}, u32[]{:S(2)}) collective-permute-start(bf16[896,512]{1,0:T(8,128)(2,1)} %get-tuple-element.129), channel_id=1, source_target_pairs={{2,0},{1,3},{6,4},{5,7},{10,8},{9,11},{14,12},{13,15},{18,16},{17,... | collective-permute-start | bytes 2752520 | tf_op jit(solution)/shard_map/ppermute | solution.py:517
  510.6 45.4 %collective-permute-start.31 = (bf16[896,768]{1,0:T(8,128)(2,1)}, bf16[896,768]{1,0:T(8,128)(2,1)S(1)}, u32[]{:S(2)}, u32[]{:S(2)}) collective-permute-start(bf16[896,768]{1,0:T(8,128)(2,1)} %get-tuple-element.123), channel_id=1, source_target_pairs={{1,0},{2,3},{5,4},{6,7},{9,8},{10,11},{13,12},{14,15},{17,16},{18,... | collective-permute-start | bytes 4128776 | tf_op jit(solution)/shard_map/ppermute | solution.py:515
  511.9 45.5 %collective-permute-start.32 = (bf16[896,768]{1,0:T(8,128)(2,1)}, bf16[896,768]{1,0:T(8,128)(2,1)S(1)}, u32[]{:S(2)}, u32[]{:S(2)}) collective-permute-start(bf16[896,768]{1,0:T(8,128)(2,1)} %get-tuple-element.124), channel_id=1, source_target_pairs={{1,2},{2,1},{5,6},{6,5},{9,10},{10,9},{13,14},{14,13},{17,18},{18,... | collective-permute-start | bytes 4128776 | tf_op jit(solution)/shard_map/ppermute | solution.py:400
  512.6 73.8 %collective-permute-start.33 = (bf16[896,768]{1,0:T(8,128)(2,1)}, bf16[896,768]{1,0:T(8,128)(2,1)}, u32[]{:S(2)}, u32[]{:S(2)}) collective-permute-start(bf16[896,768]{1,0:T(8,128)(2,1)} %get-tuple-element.125), channel_id=1, source_target_pairs={{2,0},{1,3},{6,4},{5,7},{10,8},{9,11},{14,12},{13,15},{18,16},{17,... | collective-permute-start | bytes 4128776 | tf_op jit(solution)/shard_map/ppermute | solution.py:517
  552.4 82.1 %collective-permute-start.42 = (bf16[896,512]{1,0:T(8,128)(2,1)}, bf16[896,512]{1,0:T(8,128)(2,1)}, u32[]{:S(2)}, u32[]{:S(2)}) collective-permute-start(bf16[896,512]{1,0:T(8,128)(2,1)} %get-tuple-element.143), channel_id=1, source_target_pairs={{1,0},{2,3},{5,4},{6,7},{9,8},{10,11},{13,12},{14,15},{17,16},{18,... | collective-permute-start | bytes 2752520 | tf_op jit(solution)/shard_map/ppermute | solution.py:515
  553.7 80.8 %collective-permute-start.43 = (bf16[896,512]{1,0:T(8,128)(2,1)}, bf16[896,512]{1,0:T(8,128)(2,1)}, u32[]{:S(2)}, u32[]{:S(2)}) collective-permute-start(bf16[896,512]{1,0:T(8,128)(2,1)} %get-tuple-element.144), channel_id=1, source_target_pairs={{1,2},{2,1},{5,6},{6,5},{9,10},{10,9},{13,14},{14,13},{17,18},{18,... | collective-permute-start | bytes 2752520 | tf_op jit(solution)/shard_map/ppermute | solution.py:400
  555.9 78.6 %collective-permute-start.44 = (bf16[896,512]{1,0:T(8,128)(2,1)}, bf16[896,512]{1,0:T(8,128)(2,1)}, u32[]{:S(2)}, u32[]{:S(2)}) collective-permute-start(bf16[896,512]{1,0:T(8,128)(2,1)} %get-tuple-element.145), channel_id=1, source_target_pairs={{2,0},{1,3},{6,4},{5,7},{10,8},{9,11},{14,12},{13,15},{18,16},{17,... | collective-permute-start | bytes 2752520 | tf_op jit(solution)/shard_map/ppermute | solution.py:517
  636.5 42.3 %collective-permute-start.47 = (bf16[896,512]{1,0:T(8,128)(2,1)}, bf16[896,512]{1,0:T(8,128)(2,1)S(1)}, u32[]{:S(2)}, u32[]{:S(2)}) collective-permute-start(bf16[896,512]{1,0:T(8,128)(2,1)} %get-tuple-element.150), channel_id=1, source_target_pairs={{2,0},{1,3},{6,4},{5,7},{10,8},{9,11},{14,12},{13,15},{18,16},{17,... | collective-permute-start | bytes 2752520 | tf_op jit(solution)/shard_map/ppermute | solution.py:517
  (49 other events, 759.4 us)

commit v6 on v5

--- a/solution.py
+++ b/solution.py
@@ -146,15 +146,9 @@
         ] = part.T
 
 
-def poly_place(core, b):
-    i = jnp.where(core == 0, jnp.where(b < 4, 0, 3), jnp.where(b < 3, 1, 2))
-    j = jnp.where(core == 0, jnp.where(b < 4, b, 3), jnp.where(b < 3, b + 1, b - 1))
-    return i, j
-
-
 def poly_kernel(flags, *refs):
     *parts, out_ref, gram, sems = refs
-    rows = out_ref.shape[1]
+    rows = out_ref.shape[0]
     quarter = rows // 4
     left, core, side = flags[0], flags[1], flags[3]
     b = pl.program_id(0)
@@ -192,170 +186,150 @@
         for i, j in turned:
             transpose_block(gram, rows, (i, j), (j, i))
 
-    i, j = poly_place(flags[1], b)
-    at_i = pl.multiple_of(i * rows, STRIP)
-    width = (rows // STRIP + 1) // 2 * STRIP
-    for start in range(0, rows, width):
-        size = min(width, rows - start)
-        at_j = pl.multiple_of(j * rows + start, STRIP)
-        squared = jnp.dot(
-            gram[pl.ds(at_i, rows), :], gram[:, pl.ds(at_j, size)], preferred_element_type=jnp.float32
-        )
-        here = gram[pl.ds(at_i, rows), pl.ds(at_j, size)].astype(jnp.float32)
-        out_ref[0, :, start : start + size] = (coef_cubic * here + coef_quintic * squared).astype(jnp.bfloat16)
-
-
-def poly_blocks(flags, groups):
+    at_i = pl.multiple_of((2 + core) * rows, STRIP)
+    width = out_ref.shape[1]
+    at_j = pl.multiple_of(b * width, STRIP)
+    squared = jnp.dot(
+        gram[pl.ds(at_i, rows), :], gram[:, pl.ds(at_j, width)], preferred_element_type=jnp.float32
+    )
+    here = gram[pl.ds(at_i, rows), pl.ds(at_j, width)].astype(jnp.float32)
+    out_ref[...] = (coef_cubic * here + coef_quintic * squared).astype(jnp.bfloat16)
+
+
+def poly_rows(flags, groups):
     rows = groups[0][0].shape[2]
     order = 4 * rows
+    width = 2 * TILE
     return pl.pallas_call(
         poly_kernel,
         grid_spec=pltpu.PrefetchScalarGridSpec(
             num_scalar_prefetch=1,
-            grid=(5,),
+            grid=(order // width,),
             in_specs=[pl.BlockSpec(memory_space=pl.ANY)] * 12,
-            out_specs=pl.BlockSpec((1, rows, rows), lambda b, flags: (b, 0, 0)),
+            out_specs=pl.BlockSpec((rows, width), lambda b, flags: (0, b)),
             scratch_shapes=[pltpu.VMEM((order, order), jnp.bfloat16), pltpu.SemaphoreType.DMA((40,))],
         ),
-        out_shape=jax.ShapeDtypeStruct((5, rows, rows), jnp.bfloat16),
+        out_shape=jax.ShapeDtypeStruct((rows, order), jnp.bfloat16),
         compiler_params=pltpu.CompilerParams(vmem_limit_bytes=VMEM_BYTES),
-        cost_estimate=pl.CostEstimate(
-            flops=10 * rows * rows * order, bytes_accessed=30 * rows * rows, transcendentals=0
-        ),
-        name="poly_blocks",
+        cost_estimate=pl.CostEstimate(flops=0, bytes_accessed=0, transcendentals=0),
+        name="poly_rows",
     )(flags, *[x for group in groups for x in group])
 
 
-def product_kernel(first, strips, flags, own, pair, inverse, s1, s2, s3, *refs):
-    distant, (o0, o1, o2, o3, sq_ref, poly, raw, sems) = refs[:-8], refs[-8:]
-    rows = s1.shape[0]
-    tile = first + pl.program_id(0)
+def product_kernel(is_far, flags, own, pair, *refs):
+    end_row, refs = (None, refs) if is_far else (refs[0], refs[1:])
+    inverse, blocks, outs = refs[0], refs[1:5], refs[5:-4]
+    sq_ref, poly, raw, sems = refs[-4:]
+    rows = own.shape[0]
 
     @pl.when(pl.program_id(0) == 0)
     def _():
         sq_ref[...] = jnp.zeros_like(sq_ref)
-        copies = []
-        for source, core in ((own, flags[1]), (pair, 1 - flags[1])):
-            for b in range(5):
-                i, j = poly_place(core, b)
-                copies.append(
-                    pltpu.make_async_copy(
-                        source.at[b],
-                        poly.at[
-                            pl.ds(pl.multiple_of(i * rows, STRIP), rows),
-                            pl.ds(pl.multiple_of(j * rows, STRIP), rows),
-                        ],
-                        sems.at[len(copies)],
-                    )
+
+        def load(pairs):
+            copies = [
+                pltpu.make_async_copy(source, target, sems.at[k]) for k, (source, target) in enumerate(pairs)
+            ]
+            for copy in copies:
+                copy.start()
+            for copy in copies:
+                copy.wait()
+
+        if is_far:
+            at = pl.multiple_of(flags[1] * rows, 16)
+            load([(own, poly.at[pl.ds(at, rows), :]), (pair, poly.at[pl.ds(rows - at, rows), :])])
+        else:
+            @pl.when((flags[2] == 1) & (flags[1] == 0))
+            def _():
+                load([(own, poly)])
+
+            @pl.when((flags[2] == 1) & (flags[1] == 1))
+            def _():
+                load([(pair, poly)])
+
+            @pl.when(flags[2] == 0)
+            def _():
+                load(
+                    [
+                        (end_row.at[:, m * rows : (m + 1) * rows], poly.at[:, (m ^ 1) * rows : ((m ^ 1) + 1) * rows])
+                        for m in range(4)
+                    ]
                 )
-        for copy in copies:
-            copy.start()
-        for copy in copies:
-            copy.wait()
-        for i in range(4):
-            for j in range(i + 1, 4):
-                transpose_block(poly, rows, (i, j), (j, i))
-
-    for r, s_ref in enumerate((s1, s2, s3), start=1):
-        raw[r * rows : (r + 1) * rows, :] = s_ref[...]
-    for k, strip in enumerate(distant):
-        side, p = divmod(k, 2)
-
-        @pl.when((2 * tile + side >= strips) == (p == 1))
-        def _(side=side, strip=strip):
-            raw[:rows, side * STRIP : (side + 1) * STRIP] = strip[...]
-
-    for r, o_ref in enumerate((o0, o1, o2, o3)):
-        product = jnp.dot(
-            poly[r * rows : (r + 1) * rows, :], raw[...], preferred_element_type=jnp.float32
-        )
-        own_rows = raw[r * rows : (r + 1) * rows, :].astype(jnp.float32)
+
+    for r, block in enumerate(blocks):
+        raw[r * rows : (r + 1) * rows, :] = block[...]
+    for k, out in enumerate(outs):
+        product = jnp.dot(poly[k * rows : (k + 1) * rows, :], raw[...], preferred_element_type=jnp.float32)
+        own_rows = raw[(2 + k) * rows : (3 + k) * rows, :].astype(jnp.float32)
         newton = inverse[0] * (coef_linear * own_rows + product)
         sq_ref[...] += jnp.sum(newton * newton, axis=0, keepdims=True)
-        o_ref[...] = newton.astype(jnp.bfloat16)
-
-
-def product(flags, own, pair, inverse, blocks, distant, piece, first, tiles):
-    rows = own.shape[1]
-    order = 4 * rows
-    here = pl.BlockSpec((rows, TILE), lambda t, flags: (0, first + t))
-    strips = piece // STRIP
-    distant_specs = [
-        pl.BlockSpec(
-            (rows, STRIP),
-            lambda t, flags, start=p * strips, side=side: (
-                0,
-                jnp.clip(2 * (first + t) + side - start, 0, strips - 1),
-            ),
-        )
-        for side in range(2)
-        for p in range(2)
+        out[...] = newton.astype(jnp.bfloat16)
+
+
+def product(flags, polys, inverse, blocks, tiles, is_far):
+    rows, order = polys[0].shape
+    count = 2 if is_far else 1
+    block_specs = [
+        pl.BlockSpec((rows, TILE), lambda t, flags, at=at: (0, at + t))
+        if lead is None
+        else pl.BlockSpec((None, rows, TILE), lambda t, flags, at=at, lead=lead: (lead, 0, at + t))
+        for _, lead, at in blocks
     ]
     there = pl.BlockSpec((rows, TILE), lambda t, flags: (0, t))
     *newton, squares = pl.pallas_call(
-        functools.partial(product_kernel, first, strips),
+        functools.partial(product_kernel, is_far),
         grid_spec=pltpu.PrefetchScalarGridSpec(
             num_scalar_prefetch=1,
             grid=(tiles,),
-            in_specs=[
-                pl.BlockSpec(memory_space=pl.ANY),
-                pl.BlockSpec(memory_space=pl.ANY),
-                pl.BlockSpec(memory_space=pltpu.SMEM),
-            ]
-            + [here] * 3
-            + distant_specs,
-            out_specs=[there] * 4 + [pl.BlockSpec((1, TILE), lambda t, flags: (0, 0))],
+            in_specs=[pl.BlockSpec(memory_space=pl.ANY)] * len(polys)
+            + [pl.BlockSpec(memory_space=pltpu.SMEM)]
+            + block_specs,
+            out_specs=[there] * count + [pl.BlockSpec((1, TILE), lambda t, flags: (0, 0))],
             scratch_shapes=[
-                pltpu.VMEM((order, order), jnp.bfloat16),
+                pltpu.VMEM((count * rows, order), jnp.bfloat16),
                 pltpu.VMEM((order, TILE), jnp.bfloat16),
-                pltpu.SemaphoreType.DMA((10,)),
+                pltpu.SemaphoreType.DMA((4,)),
             ],
         ),
-        out_shape=[jax.ShapeDtypeStruct((rows, tiles * TILE), jnp.bfloat16)] * 4
+        out_shape=[jax.ShapeDtypeStruct((rows, tiles * TILE), jnp.bfloat16)] * count
         + [jax.ShapeDtypeStruct((1, TILE), jnp.float32)],
         compiler_params=pltpu.CompilerParams(vmem_limit_bytes=VMEM_BYTES),
-        cost_estimate=pl.CostEstimate(
-            flops=2 * order * order * tiles * TILE,
-            bytes_accessed=20 * rows * rows + 4 * order * tiles * TILE,
-            transcendentals=0,
-        ),
-        name="product",
-    )(flags, own, pair, inverse, *blocks, *distant, *distant)
+        cost_estimate=pl.CostEstimate(flops=0, bytes_accessed=0, transcendentals=0),
+        name="product_far" if is_far else "product_near",
+    )(flags, *polys, inverse, *[array for array, _, _ in blocks])
     return newton, jnp.sum(squares)
 
 
-def finish_kernel(flags, factor, own, near, middle, far, *rest):
-    out_ref = rest[-1]
-    is_hub = flags[2] == 1
-
-    @pl.when((pl.program_id(0) == 0) & is_hub)
-    def _():
-        out_ref[...] = own[...].astype(jnp.float32) * factor[0]
-
-    @pl.when((pl.program_id(0) == 0) & jnp.logical_not(is_hub))
-    def _():
-        out_ref[...] = near[...].astype(jnp.float32) * factor[0]
-
-    @pl.when((pl.program_id(0) == 1) & is_hub)
-    def _():
-        out_ref[...] = middle[...].astype(jnp.float32) * factor[0]
-
-    @pl.when((pl.program_id(0) == 1) & jnp.logical_not(is_hub))
-    def _():
-        out_ref[...] = far[...].astype(jnp.float32) * factor[0]
-
-
-def finish(flags, factor, parts, first, shape, before):
+def finish_kernel(starts, flags, factor, *refs):
+    out_ref = refs[-1]
+    t = pl.program_id(0)
+    chunks = len(starts) - 1
+    for k, ref in enumerate(refs[: chunks if chunks == 1 else 2 * chunks]):
+        here = (t >= starts[k % chunks]) & (t < starts[k % chunks + 1])
+        if chunks > 1:
+            here &= (flags[2] == 1) == (k < chunks)
+
+        @pl.when(here)
+        def _(ref=ref):
+            out_ref[...] = ref[...].astype(jnp.float32) * factor[0]
+
+
+def finish(flags, factor, parts, starts, shape, before):
     rows, cols = shape
-    tiles = parts[0].shape[1] // TILE
+    chunks = len(starts) - 1
     half = cols // 2 // TILE
-    near_part = pl.BlockSpec((rows, TILE), lambda p, t, flags: (0, jnp.where(p == 0, t, tiles - 1)))
-    far_part = pl.BlockSpec((rows, TILE), lambda p, t, flags: (0, jnp.where(p == 0, 0, t)))
     place = pl.BlockSpec(
-        (rows, TILE),
-        lambda p, t, flags: (0, jnp.where(p == 0, flags[0], 1 - flags[0]) * half + first + t),
-    )
-    specs = [pl.BlockSpec(memory_space=pltpu.SMEM), near_part, near_part, far_part, far_part]
+        (rows, TILE), lambda t, flags: (0, (flags[0] if chunks == 1 else 1 - flags[0]) * half + t)
+    )
+    specs = [pl.BlockSpec(memory_space=pltpu.SMEM)]
+    for k in range(len(parts)):
+        first, last = starts[k % chunks : k % chunks + 2]
+        specs.append(
+            pl.BlockSpec(
+                (rows, TILE),
+                lambda t, flags, first=first, last=last: (0, jnp.clip(t, first, last - 1) - first),
+            )
+        )
     operands = [flags, factor, *parts]
     aliases = {}
     if before is not None:
@@ -363,16 +337,14 @@
         aliases = {len(operands): 0}
         operands.append(before)
     return pl.pallas_call(
-        finish_kernel,
+        functools.partial(finish_kernel, starts),
         grid_spec=pltpu.PrefetchScalarGridSpec(
-            num_scalar_prefetch=1, grid=(2, tiles), in_specs=specs, out_specs=place
+            num_scalar_prefetch=1, grid=(starts[-1],), in_specs=specs, out_specs=place
         ),
         out_shape=jax.ShapeDtypeStruct(shape, jnp.float32),
         input_output_aliases=aliases,
         compiler_params=pltpu.CompilerParams(vmem_limit_bytes=VMEM_BYTES),
-        cost_estimate=pl.CostEstimate(
-            flops=2 * rows * TILE * tiles, bytes_accessed=16 * rows * TILE * tiles, transcendentals=0
-        ),
+        cost_estimate=pl.CostEstimate(flops=0, bytes_accessed=0, transcendentals=0),
         name="finish",
     )(*operands)
 
@@ -399,8 +371,17 @@
     def between_hubs(x):
         return lax.ppermute(x, "row", [(1, 2), (2, 1)])
 
-    def distant_permute(x):
-        return lax.ppermute(x, "row", [(0, 2), (3, 1)])
+    def skip_one(x):
+        return lax.ppermute(x, "row", [(0, 2), (2, 0), (1, 3), (3, 1)])
+
+    def with_end(x):
+        return lax.ppermute(x, "row", [(0, 1), (1, 0), (2, 3), (3, 2)])
+
+    def to_end(x):
+        return lax.ppermute(x, "row", [(1, 0), (2, 3)])
+
+    def past_hub(x):
+        return lax.ppermute(x, "row", [(0, 2), (3, 1), (1, 0), (2, 3)])
 
     def col_total(x):
         x = jnp.broadcast_to(x, (8, 128))
@@ -408,9 +389,10 @@
         return x + over_side(x)
 
     near, far, squares = take(momentum, near_index)
-    beside = lax.ppermute(near, "row", [(0, 1), (3, 2)])
+    beside = with_end(near)
     middle = between_hubs(far)
     norm_part = col_total(jnp.sum(squares))
+    norm_part += with_end(norm_part)
 
     def added(x, y):
         return (x.astype(jnp.float32) + y.astype(jnp.float32)).astype(jnp.bfloat16)
@@ -426,28 +408,24 @@
 
     barrier = lax.optimization_barrier
     piece = width // 2
-    far_first, beside, norm_part = barrier((far[:, :piece], beside, norm_part))
-    arrived = distant_permute(far_first)
+    outward = [jnp.where(is_hub, middle[:, at : at + piece], far[:, at : at + piece]) for at in (0, piece)]
+    outward[0], beside, norm_part = barrier((outward[0], beside, norm_part))
+    arrived = past_hub(outward[0])
     whole = {1: [(middle, width, 0)], 2: [(near, width, 0)], 3: [(beside, width, 0)]}
     pairs_1, pairs_2 = [(2, 2), (3, 3), (3, 2)], [(1, 2), (1, 1), (3, 1)]
     pairs_3, pairs_4 = [(0, 0), (0, 1)], [(0, 2), (0, 3)]
     first = gram_blocks(flags, pairs_1, {r: whole[r] for r in (2, 3)})
     second = gram_blocks(flags, pairs_2, whole)
-    norm_sum = (
-        norm_part
-        + lax.ppermute(norm_part, "row", [(0, 1), (3, 2)])
-        + between_hubs(norm_part)
-        + distant_permute(norm_part)
-    )[0, 0]
-    arrived, far_second, first, second, norm_sum = barrier(
-        (arrived, far[:, piece:], first, second, norm_sum)
+    norm_sum = (norm_part + skip_one(norm_part))[0, 0]
+    arrived, outward_second, first, second, norm_sum = barrier(
+        (arrived, outward[1], first, second, norm_sum)
     )
 
     def halves(h):
         blocks = {1: middle, 2: near, 3: beside}
         return {0: [(distant[h], piece, 0)]} | {r: [(blocks[r], piece, h)] for r in blocks}
 
-    distant = [arrived, distant_permute(far_second)]
+    distant = [arrived, past_hub(outward_second)]
     first = over_pair(first)
     second = over_pair(second)
     (late,) = gram_blocks(flags, pairs_3 + pairs_4, halves(0), split=False)
@@ -487,47 +465,60 @@
     groups[0][1], groups[0][2], other_third = barrier((groups[0][1], groups[0][2], other_third))
     known(pairs_3, third, other_third)
     groups.append(gather(GATHERED[1]))
-    groups[1][1], other_fourth = barrier((groups[1][1], other_fourth))
+    passed = jnp.concatenate(distant, axis=1)
+    inward = jnp.where(is_hub, passed, far)
+    tile_bounds = [0, max(1, tiles * 4 // 9), max(2, tiles * 7 // 9), tiles]
+    cuts = [t * TILE for t in tile_bounds]
+    inward_first = with_end(inward[:, : cuts[1]])
+    groups[1][1], inward_first, other_fourth = barrier((groups[1][1], inward_first, other_fourth))
     known(pairs_4, fourth, other_fourth)
     groups.append(gather(GATHERED[2]))
 
-    own = poly_blocks(flags, groups)
+    inward_second = with_end(inward[:, cuts[1] :])
+    swaps = [jnp.stack([block[:, a:b] for block in (beside, near)]) for a, b in zip(cuts[:-1], cuts[1:])]
+    swaps[0], other_fourth = barrier((swaps[0], other_fourth))
+    swaps[0] = between_hubs(swaps[0])
+    groups[2], inward_second = barrier((groups[2], inward_second))
+    own, swaps[0] = barrier((poly_rows(flags, groups), swaps[0]))
     pair = over_core(own)
-
-    bounds = sorted({0, tiles * 2 // 9, tiles * 5 // 9, tiles * 7 // 9, tiles})
-    newton_sq = jnp.float32(0.0)
+    swaps[1] = between_hubs(swaps[1])
+    row_share = to_end(
+        jnp.where(
+            core == 0,
+            lax.dynamic_slice(pair, (c * quarter, 0), (quarter, 4 * rows)),
+            lax.dynamic_slice(own, (c * quarter, 0), (quarter, 4 * rows)),
+        )
+    )
     scale = inverse.reshape(1)
-    parts = []
-    for first, last in zip(bounds[:-1], bounds[1:]):
-        newton, squares = product(flags, own, pair, scale, (middle, near, beside), distant, piece, first, last - first)
-        newton_sq += squares
-        if last == tiles:
-            hub_sq = col_total(newton_sq)
-            total_sq = (
-                jnp.where(is_hub, hub_sq, 0.0)
-                + lax.ppermute(hub_sq, "row", [(1, 0), (2, 3)])
-                + between_hubs(hub_sq)
-                + lax.ppermute(hub_sq, "row", [(2, 0), (1, 3)])
-            )[0, 0]
-            newton, total_sq, parts[-1] = barrier((newton, total_sq, parts[-1]))
-        part = (
-            newton[2],
-            lax.ppermute(newton[3], "row", [(1, 0), (2, 3)]),
-            between_hubs(newton[1]),
-            lax.ppermute(newton[0], "row", [(2, 0), (1, 3)]),
-        )
-        if last == tiles:
-            pass
-        elif parts:
-            parts[-1], scale, newton_sq = barrier((parts[-1], scale, newton_sq))
-        else:
-            scale, newton_sq = barrier((scale, newton_sq))
-        parts.append(part)
-    factor = (1.0 / (jnp.sqrt(total_sq) / math.sqrt(M * N) + 1e-07)).reshape(1)
-    out = None
-    for first, part in zip(bounds[:-1], parts):
-        out = finish(flags, factor, part, first, (rows, cols), out)
-    return out
+    inwards = [(inward_first, 0), (inward_second, 0), (inward_second, tile_bounds[2] - tile_bounds[1])]
+    at_hub, at_end = [], []
+
+    def far_product(k, scale):
+        block, at = inwards[k]
+        first, last = tile_bounds[k : k + 2]
+        blocks = [(swaps[k], 0, 0), (swaps[k], 1, 0), (far, None, first), (block, None, at)]
+        (here, there), squares = product(flags, (own, pair), scale, blocks, last - first, True)
+        at_hub.append(here)
+        at_end.append(to_end(there))
+        return squares
+
+    hub_sq = far_product(0, scale)
+    scale, hub_sq, row_share, swaps[1] = barrier((scale, hub_sq, row_share, swaps[1]))
+    swaps[2] = between_hubs(swaps[2])
+    end_row = lax.all_gather(row_share, "col", axis=0, tiled=True)
+    hub_sq += far_product(1, scale)
+    scale, hub_sq, swaps[2], inward_first = barrier((scale, hub_sq, swaps[2], inward_first))
+    hub_sq += far_product(2, scale)
+    scale, hub_sq, at_end[0], at_end[1] = barrier((scale, hub_sq, at_end[0], at_end[1]))
+    inward = jnp.concatenate([inward_first, inward_second], axis=1)
+    blocks = [(passed, None, 0), (jnp.where(is_hub, middle, inward), None, 0), (near, None, 0), (beside, None, 0)]
+    (near_part,), near_sq = product(flags, (own, pair, end_row), scale, blocks, tiles, False)
+    total_sq = col_total(near_sq + jnp.where(is_hub, hub_sq, 0.0))
+    total_sq += with_end(total_sq)
+    total_sq += skip_one(total_sq)
+    factor = (1.0 / (jnp.sqrt(total_sq[0, 0]) / math.sqrt(M * N) + 1e-07)).reshape(1)
+    out = finish(flags, factor, [near_part], [0, tiles], (rows, cols), None)
+    return finish(flags, factor, at_hub + at_end, tile_bounds, (rows, cols), out)
 
 
 def per_device_general(momentum):
@@ -567,7 +558,7 @@
         n_row, n_col = mesh.shape["row"], mesh.shape["col"]
         rows = momentum.shape[0] // (mesh.shape["groups"] * n_row)
         cols = momentum.shape[1] // n_col
-        hubs = n_row == 4 and n_col == 4 and rows % STRIP == 0 and cols % (2 * TILE) == 0
+        hubs = n_row == 4 and n_col == 4 and rows % STRIP == 0 and cols % (6 * TILE) == 0
         return jax.shard_map(
             per_device if hubs else per_device_general,
             mesh=mesh,

time: 693 us -> 680 us (0.981)
  Pallas kernels: 282 us -> 224 us
  other arithmetic: 24.7 us -> 44 us
  between operations: 4.89 us -> 18.6 us
  waiting for transfers between devices: 295 us -> 308 us
    pallas_call x9 -> x7, Pallas kernels: 194 us -> 136 us  [the longest x4 79.5 us: product(): pl.pallas_call(functools.partial(product_kernel, is_far), grid_spec=pltpu...]
    ppermute x15 -> x13, waiting for transfers between devices: 148 us -> 169 us  [the longest x5 96.9 us: with_end(): return lax.ppermute(x, 'row', [(0, 1), (1, 0), (2, 3), (3, 2)])]
    select_n x0 -> x4, other arithmetic: none -> 12.3 us  [the longest x1 5.79 us: per_device(): jnp.where(is_hub, middle[:, at:at + piece], far[:, at:at + piece])]
    ppermute x15 -> x13, starting transfers between devices: 35 us -> 29.2 us  [the longest x5 16.4 us: with_end(): return lax.ppermute(x, 'row', [(0, 1), (1, 0), (2, 3), (3, 2)])]
  transfers between devices with their start and end apart: 48 -> 44, of which waited for: 20 -> 24; matrix products, arithmetic and copies ran while one was open for 4% -> 8% of each run, Pallas kernels for 28% -> 30%
where the time goes in v6:
time: 680 us; the launch traced here: 672 us
  waiting for transfers between devices  308 us (45%)
  Pallas kernels  224 us (33%)
  starting transfers between devices  54.6 us (8%)
  other arithmetic  44 us (6%)
  local copies, waits for them, and re-layouts  22.7 us (3%)
  between operations  18.6 us (3%)
    ppermute x9, waiting for transfers between devices, over_side(): return lax.ppermute(x, 'col', [(k, k ^ 2) for k in range(4)])  126 us
    ppermute x5, waiting for transfers between devices, with_end(): return lax.ppermute(x, 'row', [(0, 1), (1, 0), (2, 3), (3, 2)])  96.9 us
    pallas_call x4, Pallas kernels, product(): pl.pallas_call(functools.partial(product_kernel, is_far), grid_spec=pltpu...  79.5 us
    pallas_call x5, Pallas kernels, gram_blocks(): pl.pallas_call(functools.partial(gram_kernel, pairs, where, pieces, int(t...  77.3 us
    ppermute x4, waiting for transfers between devices, to_end(): return lax.ppermute(x, 'row', [(1, 0), (2, 3)])  57.6 us
    pallas_call x1, Pallas kernels, poly_rows(): pl.pallas_call(poly_kernel, grid_spec=pltpu.PrefetchScalarGridSpec(num_sc...  37.5 us
    pallas_call x2, Pallas kernels, finish(): pl.pallas_call(functools.partial(finish_kernel, starts), grid_spec=pltpu....  19 us
    ppermute x5, starting transfers between devices, with_end(): return lax.ppermute(x, 'row', [(0, 1), (1, 0), (2, 3), (3, 2)])  16.4 us
  transfers between devices with their start and end apart: 44, of which 24 were waited for; matrix products, arithmetic and copies ran while one was open for 8% of the time, Pallas kernels for 30%

profile of v6, /device:TPU:0, one launch (start us, length us, event | category | flops | bytes accessed | tf_op | source)
XLA Modules:
  0.0 672.1 jit_solution(1478005908782862874)
XLA Ops:
  6.5 10.6 %take_halves.1 = (bf16[896,2304]{1,0:T(8,128)(2,1)}, bf16[896,2304]{1,0:T(8,128)(2,1)}, f32[1,2304]{1,0:T(1,128)}) custom-call(s32[1]{0:T(128)} %bitcast.index, f32[896,4608]{1,0:T(8,128)} %far_ref.1, f32[896,4608]{1,0:T(8,128)} %far_ref.1), custom_call_target="tpu_custom_call" | custom-call | flops 8257536 | bytes 24772608 | tf_op jit(solution)/shard_map/take_halves/pallas_call | solution.py:45
  32.0 81.0 %collective-permute-done.4 = f32[8,128]{1,0:T(8,128)S(1)} collective-permute-done((f32[8,128]{1,0:T(8,128)S(1)}, f32[8,128]{1,0:T(8,128)S(1)}, u32[]{:S(2)}, u32[]{:S(2)}) %collective-permute-start.4) | collective-permute-done | bytes 4128 | tf_op jit(solution)/shard_map/ppermute | solution.py:378
  123.1 19.1 %gram_blocks.5 = (bf16[3,448,896]{2,1,0:T(8,128)(2,1)}, bf16[3,448,896]{2,1,0:T(8,128)(2,1)}) custom-call(s32[4]{0:T(128)} %pad_add_fusion.flags, bf16[896,2304]{1,0:T(8,128)(2,1)} %get-tuple-element.74.refs_0_.refs_1_.refs_2_.refs_4_, bf16[896,2304]{1,0:T(8,128)(2,1)} %collective-permute-done.1.refs_1_.refs_2_.refs_3_.refs_5_), custom_call_target="tpu_custom_call" | custom-call | tf_op jit(solution)/shard_map/gram_blocks/pallas_call | solution.py:124
  142.2 20.5 %gram_blocks.6 = (bf16[3,448,896]{2,1,0:T(8,128)(2,1)}, bf16[3,448,896]{2,1,0:T(8,128)(2,1)}) custom-call(s32[4]{0:T(128)} %pad_add_fusion.flags, bf16[896,2304]{1,0:T(8,128)(2,1)} %collective-permute-done.refs_0_.refs_1_, bf16[896,2304]{1,0:T(8,128)(2,1)} %get-tuple-element.74.refs_0_.refs_1_.refs_2_.refs_4_, ...), custom_call_target="tpu_custom_call" | custom-call | tf_op jit(solution)/shard_map/gram_blocks/pallas_call | solution.py:124
  177.3 16.4 %gram_blocks.7.refs_3_.refs_2_ = f32[4,896,896]{2,1,0:T(8,128)} custom-call(s32[4]{0:T(128)} %pad_add_fusion.flags, bf16[896,1152]{1,0:T(8,128)(2,1)} %copy-done.10, bf16[896,2304]{1,0:T(8,128)(2,1)} %collective-permute-done.refs_0_.refs_1_, bf16[896,2304]{1,0:T(8,128)(2,1)} %get-tuple-element.74.refs_0_.refs_1_.refs_2_.refs_4_, ...), custom_call_target="tpu_custom_call" | custom-call | tf_op jit(solution)/shard_map/gram_blocks/pallas_call | solution.py:124
  206.3 8.8 %collective-permute-done.7.refs_0_ = bf16[896,1152]{1,0:T(8,128)(2,1)S(1)} collective-permute-done((bf16[896,1152]{1,0:T(8,128)(2,1)}, bf16[896,1152]{1,0:T(8,128)(2,1)S(1)}, u32[]{:S(2)}, u32[]{:S(2)}) %collective-permute-start.7) | collective-permute-done | bytes 2064416 | tf_op jit(solution)/shard_map/ppermute | solution.py:384
  219.5 10.4 %gram_blocks.9 = (bf16[2,448,896]{2,1,0:T(8,128)(2,1)}, bf16[2,448,896]{2,1,0:T(8,128)(2,1)}) custom-call(s32[4]{0:T(128)} %pad_add_fusion.flags, bf16[896,1152]{1,0:T(8,128)(2,1)} %copy-done.5, bf16[896,2304]{1,0:T(8,128)(2,1)} %collective-permute-done.refs_0_.refs_1_, f32[4,896,896]{2,1,0:T(8,128)} %gram_blocks.7.refs_3_.refs_2_), custom_call_target="tpu_custom_call" | custom-call | tf_op jit(solution)/shard_map/gram_blocks/pallas_call | solution.py:124
  230.0 10.9 %gram_blocks.8 = (bf16[2,448,896]{2,1,0:T(8,128)(2,1)}, bf16[2,448,896]{2,1,0:T(8,128)(2,1)}) custom-call(s32[4]{0:T(128)} %pad_add_fusion.flags, bf16[896,1152]{1,0:T(8,128)(2,1)} %copy-done.5, bf16[896,2304]{1,0:T(8,128)(2,1)} %get-tuple-element.74.refs_0_.refs_1_.refs_2_.refs_4_, bf16[896,2304]{1,0:T(8,128)(2,1)} %collective-permute-done.1.refs_1_.refs_2_.refs_3_.refs_5_, ...), custom_call_target="tpu_custom_call" | custom-call | tf_op jit(solution)/shard_map/gram_blocks/pallas_call | solution.py:124
  255.8 16.2 %collective-permute-done.19 = bf16[2,224,896]{2,1,0:T(8,128)(2,1)} collective-permute-done((bf16[2,224,896]{2,1,0:T(8,128)(2,1)}, bf16[2,224,896]{2,1,0:T(8,128)(2,1)}, u32[]{:S(2)}, u32[]{:S(2)}) %collective-permute-start.19) | collective-permute-done | bytes 802848 | tf_op jit(solution)/shard_map/ppermute | solution.py:369
  273.3 15.4 %collective-permute-done.15 = bf16[2,224,896]{2,1,0:T(8,128)(2,1)} collective-permute-done((bf16[2,224,896]{2,1,0:T(8,128)(2,1)}, bf16[2,224,896]{2,1,0:T(8,128)(2,1)}, u32[]{:S(2)}, u32[]{:S(2)}) %collective-permute-start.15) | collective-permute-done | bytes 802848 | tf_op jit(solution)/shard_map/ppermute | solution.py:369
  303.4 19.4 %collective-permute-done.17.refs_2_ = bf16[3,224,896]{2,1,0:T(8,128)(2,1)S(1)} collective-permute-done((bf16[3,224,896]{2,1,0:T(8,128)(2,1)S(1)}, bf16[3,224,896]{2,1,0:T(8,128)(2,1)S(1)}, u32[]{:S(2)}, u32[]{:S(2)}) %collective-permute-start.17) | collective-permute-done | bytes 1204256 | tf_op jit(solution)/shard_map/ppermute | solution.py:369
  330.7 12.3 %collective-permute-done.23.refs_4_ = bf16[896,1024]{1,0:T(8,128)(2,1)S(1)} collective-permute-done((bf16[896,1024]{1,0:T(8,128)(2,1)S(1)}, bf16[896,1024]{1,0:T(8,128)(2,1)S(1)}, u32[]{:S(2)}, u32[]{:S(2)}) %collective-permute-start.23) | collective-permute-done | bytes 1835040 | tf_op jit(solution)/shard_map/ppermute | solution.py:378
  356.9 34.5 %collective-permute-done.25.refs_6_ = bf16[4,224,896]{2,1,0:T(8,128)(2,1)S(1)} collective-permute-done((bf16[4,224,896]{2,1,0:T(8,128)(2,1)S(1)}, bf16[4,224,896]{2,1,0:T(8,128)(2,1)S(1)}, u32[]{:S(2)}, u32[]{:S(2)}) %collective-permute-start.25) | collective-permute-done | bytes 1605664 | tf_op jit(solution)/shard_map/ppermute | solution.py:369
  391.9 23.2 %collective-permute-done.28.refs_10_ = bf16[3,224,896]{2,1,0:T(8,128)(2,1)S(1)} collective-permute-done((bf16[3,224,896]{2,1,0:T(8,128)(2,1)S(1)}, bf16[3,224,896]{2,1,0:T(8,128)(2,1)S(1)}, u32[]{:S(2)}, u32[]{:S(2)}) %collective-permute-start.28) | collective-permute-done | bytes 1204256 | tf_op jit(solution)/shard_map/ppermute | solution.py:369
  420.8 37.5 %poly_rows.1.own = bf16[896,3584]{1,0:T(8,128)(2,1)} custom-call(s32[4]{0:T(128)} %pad_add_fusion.flags, bf16[3,224,896]{2,1,0:T(8,128)(2,1)} %copy-done.20, bf16[3,224,896]{2,1,0:T(8,128)(2,1)} %copy-done.33, bf16[3,224,896]{2,1,0:T(8,128)(2,1)} %copy-done.34, bf16[3,224,896]{2,1,0:T(8,128)(2,1)} %copy-done.39, bf16[4,224,896]{2,1,0:T(8,128)(2,1)} %copy-done.15, ...), custom_call_target="tpu_custom_call" | custom-call | tf_op jit(solution)/shard_map/poly_rows/pallas_call | solution.py:203
  474.1 22.5 %product_far.3 = (bf16[896,1024]{1,0:T(8,128)(2,1)}, bf16[896,1024]{1,0:T(8,128)(2,1)}, f32[1,256]{1,0:T(1,128)}) custom-call(s32[4]{0:T(128)} %pad_add_fusion.flags, bf16[896,3584]{1,0:T(8,128)(2,1)} %poly_rows.1.own, bf16[896,3584]{1,0:T(8,128)(2,1)} %collective-permute-done.32.pair, f32[1]{0:T(128)} %bitcast.7.refs_0_.refs_1_, ...), custom_call_target="tpu_custom_call" | custom-call | tf_op jit(solution)/shard_map/product_far/pallas_call | solution.py:279
  497.9 14.0 %collective-permute-done.33 = bf16[224,3584]{1,0:T(8,128)(2,1)} collective-permute-done((bf16[224,3584]{1,0:T(8,128)(2,1)}, bf16[224,3584]{1,0:T(8,128)(2,1)}, u32[]{:S(2)}, u32[]{:S(2)}) %collective-permute-start.33) | collective-permute-done | bytes 1605664 | tf_op jit(solution)/shard_map/ppermute | solution.py:381
  517.8 18.9 %product_far.4 = (bf16[896,768]{1,0:T(8,128)(2,1)}, bf16[896,768]{1,0:T(8,128)(2,1)}, f32[1,256]{1,0:T(1,128)}) custom-call(s32[4]{0:T(128)} %pad_add_fusion.flags, bf16[896,3584]{1,0:T(8,128)(2,1)} %poly_rows.1.own, bf16[896,3584]{1,0:T(8,128)(2,1)} %collective-permute-done.32.pair, f32[1]{0:T(128)} %bitcast.7.refs_0_.refs_1_, ...), custom_call_target="tpu_custom_call" | custom-call | tf_op jit(solution)/shard_map/product_far/pallas_call | solution.py:279
  541.8 15.4 %product_far.5 = (bf16[896,512]{1,0:T(8,128)(2,1)}, bf16[896,512]{1,0:T(8,128)(2,1)}, f32[1,256]{1,0:T(1,128)}) custom-call(s32[4]{0:T(128)} %pad_add_fusion.flags, bf16[896,3584]{1,0:T(8,128)(2,1)} %poly_rows.1.own, bf16[896,3584]{1,0:T(8,128)(2,1)} %collective-permute-done.32.pair, f32[1]{0:T(128)} %bitcast.7.refs_0_.refs_1_, ...), custom_call_target="tpu_custom_call" | custom-call | tf_op jit(solution)/shard_map/product_far/pallas_call | solution.py:279
  562.4 14.2 %collective-permute-done.36.refs_3_ = bf16[896,1024]{1,0:T(8,128)(2,1)} collective-permute-done((bf16[896,1024]{1,0:T(8,128)(2,1)}, bf16[896,1024]{1,0:T(8,128)(2,1)}, u32[]{:S(2)}, u32[]{:S(2)}) %collective-permute-start.36) | collective-permute-done | bytes 1835040 | tf_op jit(solution)/shard_map/ppermute | solution.py:381
  576.6 29.4 %collective-permute-done.37.refs_4_ = bf16[896,768]{1,0:T(8,128)(2,1)S(1)} collective-permute-done((bf16[896,768]{1,0:T(8,128)(2,1)}, bf16[896,768]{1,0:T(8,128)(2,1)S(1)}, u32[]{:S(2)}, u32[]{:S(2)}) %collective-permute-start.37) | collective-permute-done | bytes 1376288 | tf_op jit(solution)/shard_map/ppermute | solution.py:381
  606.0 22.8 %product_near.1 = (bf16[896,2304]{1,0:T(8,128)(2,1)}, f32[1,256]{1,0:T(1,128)}) custom-call(s32[4]{0:T(128)} %pad_add_fusion.flags, bf16[896,3584]{1,0:T(8,128)(2,1)} %poly_rows.1.own, bf16[896,3584]{1,0:T(8,128)(2,1)} %collective-permute-done.32.pair, bf16[896,3584]{1,0:T(8,128)(2,1)} %all-gather.2.cloned.1.call-done.refs_0_, f32[1]{0:T(128)} %bitcast.7.refs_0_.refs_1_, ...), custom_call_target="tpu_custom_call" | custom-call | tf_op jit(solution)/shard_map/product_near/pallas_call | solution.py:279
  644.9 8.6 %finish.2.refs_6_ = f32[896,4608]{1,0:T(8,128)} custom-call(s32[4]{0:T(128)} %pad_add_fusion.flags, f32[1]{0:T(128)} %bitcast.12.factor, bf16[896,2304]{1,0:T(8,128)(2,1)} %get-tuple-element.140.refs_0_), custom_call_target="tpu_custom_call" | custom-call | tf_op jit(solution)/shard_map/finish/pallas_call | solution.py:339
  654.5 10.4 %finish.3 = f32[896,4608]{1,0:T(8,128)} custom-call(s32[4]{0:T(128)} %pad_add_fusion.flags, f32[1]{0:T(128)} %bitcast.12.factor, bf16[896,1024]{1,0:T(8,128)(2,1)} %get-tuple-element.134.refs_0_, bf16[896,768]{1,0:T(8,128)(2,1)} %get-tuple-element.135.refs_1_, bf16[896,512]{1,0:T(8,128)(2,1)} %get-tuple-element.136.refs_2_, ...), custom_call_target="tpu_custom_call", output_to_operand_aliasing={{}: (8, {})} | custom-call | tf_op jit(solution)/shard_map/finish/pallas_call | solution.py:339
  (217 shorter events, 161.2 us)
Async XLA Ops:
  6.5 599.5 %all-gather.2.cloned.1.call-start = ((), (), s32[]{:S(2)}) async-start(), calls=%async_computation | async-start | bytes 8028160 | tf_op jit(solution)/shard_map/all_gather | solution.py:508
  17.2 95.8 %collective-permute-start = (bf16[896,2304]{1,0:T(8,128)(2,1)}, bf16[896,2304]{1,0:T(8,128)(2,1)}, u32[]{:S(2)}, u32[]{:S(2)}) collective-permute-start(bf16[896,2304]{1,0:T(8,128)(2,1)} %get-tuple-element.73.refs_3_), channel_id=1, source_target_pairs={{1,2},{2,1},{5,6},{6,5},{9,10},{10,9},{13,14},{14,13},{17,18},{18,... | collective-permute-start | bytes 12386312 | tf_op jit(solution)/shard_map/ppermute | solution.py:372
  19.8 98.9 %collective-permute-start.1 = (bf16[896,2304]{1,0:T(8,128)(2,1)}, bf16[896,2304]{1,0:T(8,128)(2,1)}, u32[]{:S(2)}, u32[]{:S(2)}) collective-permute-start(bf16[896,2304]{1,0:T(8,128)(2,1)} %get-tuple-element.74.refs_0_.refs_1_.refs_2_.refs_4_), channel_id=1, source_target_pairs={{0,1},{1,0},{2,3},{3,2},{4,5},{5,4},{6,7},{7,6},{8,9},{9,8},{10,11... | collective-permute-start | bytes 12386312 | tf_op jit(solution)/shard_map/ppermute | solution.py:378
  31.9 81.1 %collective-permute-start.4 = (f32[8,128]{1,0:T(8,128)S(1)}, f32[8,128]{1,0:T(8,128)S(1)}, u32[]{:S(2)}, u32[]{:S(2)}) collective-permute-start(f32[8,128]{1,0:T(8,128)S(1)} %fusion.4), channel_id=1, source_target_pairs={{0,1},{1,0},{2,3},{3,2},{4,5},{5,4},{6,7},{7,6},{8,9},{9,8},{10,11... | collective-permute-start | bytes 12296 | tf_op jit(solution)/shard_map/ppermute | solution.py:378
  118.8 46.4 %collective-permute-start.5 = (bf16[896,1152]{1,0:T(8,128)(2,1)}, bf16[896,1152]{1,0:T(8,128)(2,1)S(1)}, u32[]{:S(2)}, u32[]{:S(2)}) collective-permute-start(bf16[896,1152]{1,0:T(8,128)(2,1)} %get-tuple-element.76), channel_id=1, source_target_pairs={{0,2},{3,1},{1,0},{2,3},{4,6},{7,5},{5,4},{6,7},{8,10},{11,9},{9,8... | collective-permute-start | bytes 6193160 | tf_op jit(solution)/shard_map/ppermute | solution.py:384
  120.8 43.8 %collective-permute-start.6 = (f32[8,128]{1,0:T(8,128)S(1)}, f32[8,128]{1,0:T(8,128)S(1)}, u32[]{:S(2)}, u32[]{:S(2)}) collective-permute-start(f32[8,128]{1,0:T(8,128)S(1)} %add.128), channel_id=1, source_target_pairs={{0,2},{2,0},{1,3},{3,1},{4,6},{6,4},{5,7},{7,5},{8,10},{10,8},{9,1... | collective-permute-start | bytes 12296 | tf_op jit(solution)/shard_map/ppermute | solution.py:375
  166.5 48.5 %collective-permute-start.7 = (bf16[896,1152]{1,0:T(8,128)(2,1)}, bf16[896,1152]{1,0:T(8,128)(2,1)S(1)}, u32[]{:S(2)}, u32[]{:S(2)}) collective-permute-start(bf16[896,1152]{1,0:T(8,128)(2,1)} %get-tuple-element.83), channel_id=1, source_target_pairs={{0,2},{3,1},{1,0},{2,3},{4,6},{7,5},{5,4},{6,7},{8,10},{11,9},{9,8... | collective-permute-start | bytes 6193160 | tf_op jit(solution)/shard_map/ppermute | solution.py:384
  175.8 28.9 %collective-permute-start.9 = (bf16[3,224,896]{2,1,0:T(8,128)(2,1)}, bf16[3,224,896]{2,1,0:T(8,128)(2,1)}, u32[]{:S(2)}, u32[]{:S(2)}) collective-permute-start(bf16[3,224,896]{2,1,0:T(8,128)(2,1)} %constant_dynamic-slice_fusion.3), channel_id=1, source_target_pairs={{0,8},{4,12},{8,0},{12,4},{1,9},{5,13},{9,1},{13,5},{2,10},{6,14},... | collective-permute-start | bytes 3612680 | tf_op jit(solution)/shard_map/ppermute | solution.py:369
  216.3 28.6 %collective-permute-start.12 = (bf16[3,224,896]{2,1,0:T(8,128)(2,1)}, bf16[3,224,896]{2,1,0:T(8,128)(2,1)}, u32[]{:S(2)}, u32[]{:S(2)}) collective-permute-start(bf16[3,224,896]{2,1,0:T(8,128)(2,1)} %constant_dynamic-slice_fusion.2), channel_id=1, source_target_pairs={{0,8},{4,12},{8,0},{12,4},{1,9},{5,13},{9,1},{13,5},{2,10},{6,14},... | collective-permute-start | bytes 3612680 | tf_op jit(solution)/shard_map/ppermute | solution.py:369
  217.8 29.7 %collective-permute-start.11 = (bf16[3,224,896]{2,1,0:T(8,128)(2,1)S(1)}, bf16[3,224,896]{2,1,0:T(8,128)(2,1)}, u32[]{:S(2)}, u32[]{:S(2)}) collective-permute-start(bf16[3,224,896]{2,1,0:T(8,128)(2,1)S(1)} %add_convert_fusion.5), channel_id=1, source_target_pairs={{1,2},{2,1},{5,6},{6,5},{9,10},{10,9},{13,14},{14,13},{17,18},{18,... | collective-permute-start | bytes 3612680 | tf_op jit(solution)/shard_map/ppermute | solution.py:372
  247.5 42.6 %collective-permute-start.13 = (bf16[3,224,896]{2,1,0:T(8,128)(2,1)}, bf16[3,224,896]{2,1,0:T(8,128)(2,1)}, u32[]{:S(2)}, u32[]{:S(2)}) collective-permute-start(bf16[3,224,896]{2,1,0:T(8,128)(2,1)} %add_convert_fusion.4), channel_id=1, source_target_pairs={{1,2},{2,1},{5,6},{6,5},{9,10},{10,9},{13,14},{14,13},{17,18},{18,... | collective-permute-start | bytes 3612680 | tf_op jit(solution)/shard_map/ppermute | solution.py:372
  254.3 34.5 %collective-permute-start.15 = (bf16[2,224,896]{2,1,0:T(8,128)(2,1)}, bf16[2,224,896]{2,1,0:T(8,128)(2,1)}, u32[]{:S(2)}, u32[]{:S(2)}) collective-permute-start(bf16[2,224,896]{2,1,0:T(8,128)(2,1)} %constant_dynamic-slice_fusion.1), channel_id=1, source_target_pairs={{0,8},{4,12},{8,0},{12,4},{1,9},{5,13},{9,1},{13,5},{2,10},{6,14},... | collective-permute-start | bytes 2408456 | tf_op jit(solution)/shard_map/ppermute | solution.py:369
  293.9 28.9 %collective-permute-start.17 = (bf16[3,224,896]{2,1,0:T(8,128)(2,1)S(1)}, bf16[3,224,896]{2,1,0:T(8,128)(2,1)S(1)}, u32[]{:S(2)}, u32[]{:S(2)}) collective-permute-start(bf16[3,224,896]{2,1,0:T(8,128)(2,1)S(1)} %fusion.1.refs_0_), channel_id=1, source_target_pairs={{0,8},{4,12},{8,0},{12,4},{1,9},{5,13},{9,1},{13,5},{2,10},{6,14},... | collective-permute-start | bytes 3612680 | tf_op jit(solution)/shard_map/ppermute | solution.py:369
  298.1 44.9 %collective-permute-start.23 = (bf16[896,1024]{1,0:T(8,128)(2,1)S(1)}, bf16[896,1024]{1,0:T(8,128)(2,1)S(1)}, u32[]{:S(2)}, u32[]{:S(2)}) collective-permute-start(bf16[896,1024]{1,0:T(8,128)(2,1)S(1)} %slice.140), channel_id=1, source_target_pairs={{0,1},{1,0},{2,3},{3,2},{4,5},{5,4},{6,7},{7,6},{8,9},{9,8},{10,11... | collective-permute-start | bytes 5505032 | tf_op jit(solution)/shard_map/ppermute | solution.py:378
  343.1 115.3 %collective-permute-start.31 = (bf16[2,896,1024]{2,1,0:T(8,128)(2,1)}, bf16[2,896,1024]{2,1,0:T(8,128)(2,1)}, u32[]{:S(2)}, u32[]{:S(2)}) collective-permute-start(bf16[2,896,1024]{2,1,0:T(8,128)(2,1)} %pad_maximum_fusion), channel_id=1, source_target_pairs={{1,2},{2,1},{5,6},{6,5},{9,10},{10,9},{13,14},{14,13},{17,18},{18,... | collective-permute-start | bytes 11010056 | tf_op jit(solution)/shard_map/ppermute | solution.py:372
  346.2 69.0 %collective-permute-start.30 = (bf16[896,1280]{1,0:T(8,128)(2,1)S(1)}, bf16[896,1280]{1,0:T(8,128)(2,1)S(1)}, u32[]{:S(2)}, u32[]{:S(2)}) collective-permute-start(bf16[896,1280]{1,0:T(8,128)(2,1)S(1)} %slice.141), channel_id=1, source_target_pairs={{0,1},{1,0},{2,3},{3,2},{4,5},{5,4},{6,7},{7,6},{8,9},{9,8},{10,11... | collective-permute-start | bytes 6881288 | tf_op jit(solution)/shard_map/ppermute | solution.py:378
  353.3 38.0 %collective-permute-start.25 = (bf16[4,224,896]{2,1,0:T(8,128)(2,1)S(1)}, bf16[4,224,896]{2,1,0:T(8,128)(2,1)S(1)}, u32[]{:S(2)}, u32[]{:S(2)}) collective-permute-start(bf16[4,224,896]{2,1,0:T(8,128)(2,1)S(1)} %fusion.refs_4_), channel_id=1, source_target_pairs={{0,8},{4,12},{8,0},{12,4},{1,9},{5,13},{9,1},{13,5},{2,10},{6,14},... | collective-permute-start | bytes 4816904 | tf_op jit(solution)/shard_map/ppermute | solution.py:369
  356.0 59.2 %collective-permute-start.28 = (bf16[3,224,896]{2,1,0:T(8,128)(2,1)S(1)}, bf16[3,224,896]{2,1,0:T(8,128)(2,1)S(1)}, u32[]{:S(2)}, u32[]{:S(2)}) collective-permute-start(bf16[3,224,896]{2,1,0:T(8,128)(2,1)S(1)} %fusion.2.refs_8_), channel_id=1, source_target_pairs={{0,8},{4,12},{8,0},{12,4},{1,9},{5,13},{9,1},{13,5},{2,10},{6,14},... | collective-permute-start | bytes 3612680 | tf_op jit(solution)/shard_map/ppermute | solution.py:369
  391.4 29.4 %collective-permute-start.26 = (bf16[4,224,896]{2,1,0:T(8,128)(2,1)S(1)}, bf16[4,224,896]{2,1,0:T(8,128)(2,1)}, u32[]{:S(2)}, u32[]{:S(2)}) collective-permute-start(bf16[4,224,896]{2,1,0:T(8,128)(2,1)S(1)} %collective-permute-done.25.refs_6_), channel_id=1, source_target_pairs={{0,4},{4,0},{8,12},{12,8},{1,5},{5,1},{9,13},{13,9},{2,6},{6,2},{1... | collective-permute-start | bytes 4816904 | tf_op jit(solution)/shard_map/ppermute | solution.py:366
  461.9 35.9 %collective-permute-start.34 = (bf16[2,896,768]{2,1,0:T(8,128)(2,1)}, bf16[2,896,768]{2,1,0:T(8,128)(2,1)S(1)}, u32[]{:S(2)}, u32[]{:S(2)}) collective-permute-start(bf16[2,896,768]{2,1,0:T(8,128)(2,1)} %pad_maximum_fusion.1), channel_id=1, source_target_pairs={{1,2},{2,1},{5,6},{6,5},{9,10},{10,9},{13,14},{14,13},{17,18},{18,... | collective-permute-start | bytes 8257544 | tf_op jit(solution)/shard_map/ppermute | solution.py:372
  472.5 39.3 %collective-permute-start.33 = (bf16[224,3584]{1,0:T(8,128)(2,1)}, bf16[224,3584]{1,0:T(8,128)(2,1)}, u32[]{:S(2)}, u32[]{:S(2)}) collective-permute-start(bf16[224,3584]{1,0:T(8,128)(2,1)} %dynamic-slice_select_fusion), channel_id=1, source_target_pairs={{1,0},{2,3},{5,4},{6,7},{9,8},{10,11},{13,12},{14,15},{17,16},{18,... | collective-permute-start | bytes 4816904 | tf_op jit(solution)/shard_map/ppermute | solution.py:381
  516.5 60.1 %collective-permute-start.36 = (bf16[896,1024]{1,0:T(8,128)(2,1)}, bf16[896,1024]{1,0:T(8,128)(2,1)}, u32[]{:S(2)}, u32[]{:S(2)}) collective-permute-start(bf16[896,1024]{1,0:T(8,128)(2,1)} %get-tuple-element.128), channel_id=1, source_target_pairs={{1,0},{2,3},{5,4},{6,7},{9,8},{10,11},{13,12},{14,15},{17,16},{18,... | collective-permute-start | bytes 5505032 | tf_op jit(solution)/shard_map/ppermute | solution.py:381
  536.7 69.3 %collective-permute-start.37 = (bf16[896,768]{1,0:T(8,128)(2,1)}, bf16[896,768]{1,0:T(8,128)(2,1)S(1)}, u32[]{:S(2)}, u32[]{:S(2)}) collective-permute-start(bf16[896,768]{1,0:T(8,128)(2,1)} %get-tuple-element.129), channel_id=1, source_target_pairs={{1,0},{2,3},{5,4},{6,7},{9,8},{10,11},{13,12},{14,15},{17,16},{18,... | collective-permute-start | bytes 4128776 | tf_op jit(solution)/shard_map/ppermute | solution.py:381
  557.2 96.3 %collective-permute-start.42 = (bf16[896,512]{1,0:T(8,128)(2,1)}, bf16[896,512]{1,0:T(8,128)(2,1)S(1)}, u32[]{:S(2)}, u32[]{:S(2)}) collective-permute-start(bf16[896,512]{1,0:T(8,128)(2,1)} %get-tuple-element.139), channel_id=1, source_target_pairs={{1,0},{2,3},{5,4},{6,7},{9,8},{10,11},{13,12},{14,15},{17,16},{18,... | collective-permute-start | bytes 2752520 | tf_op jit(solution)/shard_map/ppermute | solution.py:381
  (63 other events, 878.3 us)
Sparse Core Ops, SparseCore 0:
  512.0 59.6 all-gather.1

commit v7 on v6

--- a/solution.py
+++ b/solution.py
@@ -217,7 +217,7 @@
 
 
 def product_kernel(is_far, flags, own, pair, *refs):
-    end_row, refs = (None, refs) if is_far else (refs[0], refs[1:])
+    end_rows, refs = ((), refs) if is_far else (refs[:4], refs[4:])
     inverse, blocks, outs = refs[0], refs[1:5], refs[5:-4]
     sq_ref, poly, raw, sems = refs[-4:]
     rows = own.shape[0]
@@ -249,9 +249,19 @@
 
             @pl.when(flags[2] == 0)
             def _():
+                core, side = flags[1], flags[3]
+                quarter = rows // 4
+                places = [2 * side + core, 2 * side + 1 - core, 2 * (1 - side) + core, 2 * (1 - side) + 1 - core]
                 load(
                     [
-                        (end_row.at[:, m * rows : (m + 1) * rows], poly.at[:, (m ^ 1) * rows : ((m ^ 1) + 1) * rows])
+                        (
+                            part.at[:, m * rows : (m + 1) * rows],
+                            poly.at[
+                                pl.ds(pl.multiple_of(place * quarter, 16), quarter),
+                                (m ^ 1) * rows : ((m ^ 1) + 1) * rows,
+                            ],
+                        )
+                        for part, place in zip(end_rows, places)
                         for m in range(4)
                     ]
                 )
@@ -288,7 +298,7 @@
             scratch_shapes=[
                 pltpu.VMEM((count * rows, order), jnp.bfloat16),
                 pltpu.VMEM((order, TILE), jnp.bfloat16),
-                pltpu.SemaphoreType.DMA((4,)),
+                pltpu.SemaphoreType.DMA((16,)),
             ],
         ),
         out_shape=[jax.ShapeDtypeStruct((rows, tiles * TILE), jnp.bfloat16)] * count
@@ -300,36 +310,24 @@
     return newton, jnp.sum(squares)
 
 
-def finish_kernel(starts, flags, factor, *refs):
+def finish_kernel(cuts, flags, factor, *refs):
     out_ref = refs[-1]
-    t = pl.program_id(0)
-    chunks = len(starts) - 1
+    chunks = len(cuts) - 1
     for k, ref in enumerate(refs[: chunks if chunks == 1 else 2 * chunks]):
-        here = (t >= starts[k % chunks]) & (t < starts[k % chunks + 1])
-        if chunks > 1:
-            here &= (flags[2] == 1) == (k < chunks)
-
-        @pl.when(here)
-        def _(ref=ref):
-            out_ref[...] = ref[...].astype(jnp.float32) * factor[0]
-
-
-def finish(flags, factor, parts, starts, shape, before):
+
+        @pl.when((chunks == 1) | ((flags[2] == 1) == (k < chunks)))
+        def _(k=k, ref=ref):
+            out_ref[:, cuts[k % chunks] : cuts[k % chunks + 1]] = ref[...].astype(jnp.float32) * factor[0]
+
+
+def finish(flags, factor, parts, cuts, shape, before):
     rows, cols = shape
-    chunks = len(starts) - 1
-    half = cols // 2 // TILE
+    step = rows // 8
     place = pl.BlockSpec(
-        (rows, TILE), lambda t, flags: (0, (flags[0] if chunks == 1 else 1 - flags[0]) * half + t)
+        (step, cols // 2), lambda t, flags: (t, flags[0] if len(parts) == 1 else 1 - flags[0])
     )
     specs = [pl.BlockSpec(memory_space=pltpu.SMEM)]
-    for k in range(len(parts)):
-        first, last = starts[k % chunks : k % chunks + 2]
-        specs.append(
-            pl.BlockSpec(
-                (rows, TILE),
-                lambda t, flags, first=first, last=last: (0, jnp.clip(t, first, last - 1) - first),
-            )
-        )
+    specs += [pl.BlockSpec((step, part.shape[1]), lambda t, flags: (t, 0)) for part in parts]
     operands = [flags, factor, *parts]
     aliases = {}
     if before is not None:
@@ -337,9 +335,9 @@
         aliases = {len(operands): 0}
         operands.append(before)
     return pl.pallas_call(
-        functools.partial(finish_kernel, starts),
+        functools.partial(finish_kernel, cuts),
         grid_spec=pltpu.PrefetchScalarGridSpec(
-            num_scalar_prefetch=1, grid=(starts[-1],), in_specs=specs, out_specs=place
+            num_scalar_prefetch=1, grid=(8,), in_specs=specs, out_specs=place
         ),
         out_shape=jax.ShapeDtypeStruct(shape, jnp.float32),
         input_output_aliases=aliases,
@@ -408,24 +406,24 @@
 
     barrier = lax.optimization_barrier
     piece = width // 2
-    outward = [jnp.where(is_hub, middle[:, at : at + piece], far[:, at : at + piece]) for at in (0, piece)]
-    outward[0], beside, norm_part = barrier((outward[0], beside, norm_part))
-    arrived = past_hub(outward[0])
+    outward = jnp.where(is_hub, middle[:, :piece], far[:, :piece])
+    outward, beside, norm_part = barrier((outward, beside, norm_part))
+    arrived = past_hub(outward)
     whole = {1: [(middle, width, 0)], 2: [(near, width, 0)], 3: [(beside, width, 0)]}
     pairs_1, pairs_2 = [(2, 2), (3, 3), (3, 2)], [(1, 2), (1, 1), (3, 1)]
     pairs_3, pairs_4 = [(0, 0), (0, 1)], [(0, 2), (0, 3)]
     first = gram_blocks(flags, pairs_1, {r: whole[r] for r in (2, 3)})
     second = gram_blocks(flags, pairs_2, whole)
     norm_sum = (norm_part + skip_one(norm_part))[0, 0]
-    arrived, outward_second, first, second, norm_sum = barrier(
-        (arrived, outward[1], first, second, norm_sum)
-    )
+    middle_later, far_later, first = barrier((middle, far, first))
+    outward = jnp.where(is_hub, middle_later[:, piece:], far_later[:, piece:])
+    arrived, outward, first, second, norm_sum = barrier((arrived, outward, first, second, norm_sum))
 
     def halves(h):
         blocks = {1: middle, 2: near, 3: beside}
         return {0: [(distant[h], piece, 0)]} | {r: [(blocks[r], piece, h)] for r in blocks}
 
-    distant = [arrived, past_hub(outward_second)]
+    distant = [arrived, past_hub(outward)]
     first = over_pair(first)
     second = over_pair(second)
     (late,) = gram_blocks(flags, pairs_3 + pairs_4, halves(0), split=False)
@@ -470,16 +468,17 @@
     tile_bounds = [0, max(1, tiles * 4 // 9), max(2, tiles * 7 // 9), tiles]
     cuts = [t * TILE for t in tile_bounds]
     inward_first = with_end(inward[:, : cuts[1]])
-    groups[1][1], inward_first, other_fourth = barrier((groups[1][1], inward_first, other_fourth))
-    known(pairs_4, fourth, other_fourth)
-    groups.append(gather(GATHERED[2]))
-
-    inward_second = with_end(inward[:, cuts[1] :])
     swaps = [jnp.stack([block[:, a:b] for block in (beside, near)]) for a, b in zip(cuts[:-1], cuts[1:])]
     swaps[0], other_fourth = barrier((swaps[0], other_fourth))
     swaps[0] = between_hubs(swaps[0])
-    groups[2], inward_second = barrier((groups[2], inward_second))
-    own, swaps[0] = barrier((poly_rows(flags, groups), swaps[0]))
+    groups[1][1], groups[1][2], inward_first, other_fourth = barrier(
+        (groups[1][1], groups[1][2], inward_first, other_fourth)
+    )
+    known(pairs_4, fourth, other_fourth)
+    groups.append(gather(GATHERED[2]))
+
+    inward_second = with_end(inward[:, cuts[1] :])
+    own, inward_second, *swaps = barrier((poly_rows(flags, groups), inward_second, *swaps))
     pair = over_core(own)
     swaps[1] = between_hubs(swaps[1])
     row_share = to_end(
@@ -503,22 +502,24 @@
         return squares
 
     hub_sq = far_product(0, scale)
-    scale, hub_sq, row_share, swaps[1] = barrier((scale, hub_sq, row_share, swaps[1]))
+    scale, hub_sq, row_share = barrier((scale, hub_sq, row_share))
+    row_across = over_side(row_share)
+    end_rows = [row_share, over_core(row_share), row_across, over_core(row_across)]
     swaps[2] = between_hubs(swaps[2])
-    end_row = lax.all_gather(row_share, "col", axis=0, tiled=True)
     hub_sq += far_product(1, scale)
-    scale, hub_sq, swaps[2], inward_first = barrier((scale, hub_sq, swaps[2], inward_first))
-    hub_sq += far_product(2, scale)
-    scale, hub_sq, at_end[0], at_end[1] = barrier((scale, hub_sq, at_end[0], at_end[1]))
+    at_end[0], scale, hub_sq, inward_first = barrier((at_end[0], scale, hub_sq, inward_first))
     inward = jnp.concatenate([inward_first, inward_second], axis=1)
     blocks = [(passed, None, 0), (jnp.where(is_hub, middle, inward), None, 0), (near, None, 0), (beside, None, 0)]
-    (near_part,), near_sq = product(flags, (own, pair, end_row), scale, blocks, tiles, False)
+    (near_part,), near_sq = product(flags, (own, pair, *end_rows), scale, blocks, tiles, False)
+    scale, near_sq = barrier((scale, near_sq))
+    hub_sq += far_product(2, scale)
+    at_end[1], hub_sq = barrier((at_end[1], hub_sq))
     total_sq = col_total(near_sq + jnp.where(is_hub, hub_sq, 0.0))
     total_sq += with_end(total_sq)
     total_sq += skip_one(total_sq)
     factor = (1.0 / (jnp.sqrt(total_sq[0, 0]) / math.sqrt(M * N) + 1e-07)).reshape(1)
-    out = finish(flags, factor, [near_part], [0, tiles], (rows, cols), None)
-    return finish(flags, factor, at_hub + at_end, tile_bounds, (rows, cols), out)
+    out = finish(flags, factor, [near_part], [0, width], (rows, cols), None)
+    return finish(flags, factor, at_hub + at_end, cuts, (rows, cols), out)
 
 
 def per_device_general(momentum):

time: 680 us -> 645 us (0.949)
  waiting for transfers between devices: 308 us -> 287 us
  between operations: 18.6 us -> 4.92 us
    ppermute x4, waiting for transfers between devices: 57.6 us -> 12.7 us  [to_end(): return lax.ppermute(x, 'row', [(1, 0), (2, 3)])]
    ppermute x9 -> x10, waiting for transfers between devices: 126 us -> 143 us  [over_side(): return lax.ppermute(x, 'col', [(k, k ^ 2) for k in range(4)])]
    ppermute x5, waiting for transfers between devices: 96.9 us -> 104 us  [with_end(): return lax.ppermute(x, 'row', [(0, 1), (1, 0), (2, 3), (3, 2)])]
    ppermute x9 -> x10, starting transfers between devices: 11.4 us -> 13.7 us  [over_side(): return lax.ppermute(x, 'col', [(k, k ^ 2) for k in range(4)])]
    ppermute x13 -> x15, waiting for transfers between devices: 12.9 us -> 14.5 us  [over_core(): return lax.ppermute(x, 'col', [(k, k ^ 1) for k in range(4)])]
  transfers between devices with their start and end apart: 44 -> 46, of which waited for: 24 -> 20; matrix products, arithmetic and copies ran while one was open for 8% -> 8% of each run, Pallas kernels for 30% -> 32%
where the time goes in v7:
time: 645 us; the launch traced here: 637 us
  waiting for transfers between devices  287 us (44%)
  Pallas kernels  223 us (35%)
  starting transfers between devices  56.6 us (9%)
  other arithmetic  45.9 us (7%)
  local copies, waits for them, and re-layouts  19.5 us (3%)
    ppermute x10, waiting for transfers between devices, over_side(): return lax.ppermute(x, 'col', [(k, k ^ 2) for k in range(4)])  143 us
    ppermute x5, waiting for transfers between devices, with_end(): return lax.ppermute(x, 'row', [(0, 1), (1, 0), (2, 3), (3, 2)])  104 us
    pallas_call x4, Pallas kernels, product(): pl.pallas_call(functools.partial(product_kernel, is_far), grid_spec=pltpu...  79.7 us
    pallas_call x5, Pallas kernels, gram_blocks(): pl.pallas_call(functools.partial(gram_kernel, pairs, where, pieces, int(t...  77.8 us
    pallas_call x1, Pallas kernels, poly_rows(): pl.pallas_call(poly_kernel, grid_spec=pltpu.PrefetchScalarGridSpec(num_sc...  37.7 us
    pallas_call x2, Pallas kernels, finish(): pl.pallas_call(functools.partial(finish_kernel, cuts), grid_spec=pltpu.Pr...  17.5 us
    ppermute x5, starting transfers between devices, with_end(): return lax.ppermute(x, 'row', [(0, 1), (1, 0), (2, 3), (3, 2)])  16.2 us
    ppermute x8, starting transfers between devices, between_hubs(): return lax.ppermute(x, 'row', [(1, 2), (2, 1)])  14.5 us
  transfers between devices with their start and end apart: 46, of which 20 were waited for; matrix products, arithmetic and copies ran while one was open for 8% of the time, Pallas kernels for 32%

profile of v7, /device:TPU:0, one launch (start us, length us, event | category | flops | bytes accessed | tf_op | source)
XLA Modules:
  0.0 637.2 jit_solution(15171034725314682016)
XLA Ops:
  0.0 10.7 %take_halves.1 = (bf16[896,2304]{1,0:T(8,128)(2,1)}, bf16[896,2304]{1,0:T(8,128)(2,1)}, f32[1,2304]{1,0:T(1,128)}) custom-call(s32[1]{0:T(128)} %bitcast.index, f32[896,4608]{1,0:T(8,128)} %far_ref.1, f32[896,4608]{1,0:T(8,128)} %far_ref.1), custom_call_target="tpu_custom_call" | custom-call | flops 8257536 | bytes 24772608 | tf_op jit(solution)/shard_map/take_halves/pallas_call | solution.py:45
  25.3 81.2 %collective-permute-done.4 = f32[8,128]{1,0:T(8,128)S(1)} collective-permute-done((f32[8,128]{1,0:T(8,128)S(1)}, f32[8,128]{1,0:T(8,128)S(1)}, u32[]{:S(2)}, u32[]{:S(2)}) %collective-permute-start.4) | collective-permute-done | bytes 4128 | tf_op jit(solution)/shard_map/ppermute | solution.py:376
  112.8 19.6 %gram_blocks.5 = (bf16[3,448,896]{2,1,0:T(8,128)(2,1)}, bf16[3,448,896]{2,1,0:T(8,128)(2,1)}) custom-call(s32[4]{0:T(128)} %pad_add_fusion.flags, bf16[896,2304]{1,0:T(8,128)(2,1)} %get-tuple-element.77.refs_0_.refs_1_.refs_2_.refs_7_, bf16[896,2304]{1,0:T(8,128)(2,1)} %collective-permute-done.1.refs_1_.refs_2_.refs_3_.refs_8_), custom_call_target="tpu_custom_call" | custom-call | tf_op jit(solution)/shard_map/gram_blocks/pallas_call | solution.py:124
  137.2 20.5 %gram_blocks.6 = (bf16[3,448,896]{2,1,0:T(8,128)(2,1)}, bf16[3,448,896]{2,1,0:T(8,128)(2,1)}) custom-call(s32[4]{0:T(128)} %pad_add_fusion.flags, bf16[896,2304]{1,0:T(8,128)(2,1)} %collective-permute-done.refs_0_.refs_1_, bf16[896,2304]{1,0:T(8,128)(2,1)} %get-tuple-element.77.refs_0_.refs_1_.refs_2_.refs_7_, ...), custom_call_target="tpu_custom_call" | custom-call | tf_op jit(solution)/shard_map/gram_blocks/pallas_call | solution.py:124
  170.3 16.4 %gram_blocks.7.refs_3_.refs_2_ = f32[4,896,896]{2,1,0:T(8,128)} custom-call(s32[4]{0:T(128)} %pad_add_fusion.flags, bf16[896,1152]{1,0:T(8,128)(2,1)} %copy-done.10, bf16[896,2304]{1,0:T(8,128)(2,1)} %collective-permute-done.refs_0_.refs_1_, bf16[896,2304]{1,0:T(8,128)(2,1)} %get-tuple-element.77.refs_0_.refs_1_.refs_2_.refs_7_, ...), custom_call_target="tpu_custom_call" | custom-call | tf_op jit(solution)/shard_map/gram_blocks/pallas_call | solution.py:124
  189.1 8.6 %collective-permute-done.9 = bf16[3,224,896]{2,1,0:T(8,128)(2,1)} collective-permute-done((bf16[3,224,896]{2,1,0:T(8,128)(2,1)}, bf16[3,224,896]{2,1,0:T(8,128)(2,1)}, u32[]{:S(2)}, u32[]{:S(2)}) %collective-permute-start.9) | collective-permute-done | bytes 1204256 | tf_op jit(solution)/shard_map/ppermute | solution.py:367
  211.6 10.5 %gram_blocks.9 = (bf16[2,448,896]{2,1,0:T(8,128)(2,1)}, bf16[2,448,896]{2,1,0:T(8,128)(2,1)}) custom-call(s32[4]{0:T(128)} %pad_add_fusion.flags, bf16[896,1152]{1,0:T(8,128)(2,1)} %copy-done.6, bf16[896,2304]{1,0:T(8,128)(2,1)} %collective-permute-done.refs_0_.refs_1_, f32[4,896,896]{2,1,0:T(8,128)} %gram_blocks.7.refs_3_.refs_2_), custom_call_target="tpu_custom_call" | custom-call | tf_op jit(solution)/shard_map/gram_blocks/pallas_call | solution.py:124
  222.1 10.9 %gram_blocks.8 = (bf16[2,448,896]{2,1,0:T(8,128)(2,1)}, bf16[2,448,896]{2,1,0:T(8,128)(2,1)}) custom-call(s32[4]{0:T(128)} %pad_add_fusion.flags, bf16[896,1152]{1,0:T(8,128)(2,1)} %copy-done.6, bf16[896,2304]{1,0:T(8,128)(2,1)} %get-tuple-element.77.refs_0_.refs_1_.refs_2_.refs_7_, bf16[896,2304]{1,0:T(8,128)(2,1)} %collective-permute-done.1.refs_1_.refs_2_.refs_3_.refs_8_, ...), custom_call_target="tpu_custom_call" | custom-call | tf_op jit(solution)/shard_map/gram_blocks/pallas_call | solution.py:124
  247.7 16.3 %collective-permute-done.19 = bf16[2,224,896]{2,1,0:T(8,128)(2,1)} collective-permute-done((bf16[2,224,896]{2,1,0:T(8,128)(2,1)}, bf16[2,224,896]{2,1,0:T(8,128)(2,1)}, u32[]{:S(2)}, u32[]{:S(2)}) %collective-permute-start.19) | collective-permute-done | bytes 802848 | tf_op jit(solution)/shard_map/ppermute | solution.py:367
  265.3 15.4 %collective-permute-done.15 = bf16[2,224,896]{2,1,0:T(8,128)(2,1)} collective-permute-done((bf16[2,224,896]{2,1,0:T(8,128)(2,1)}, bf16[2,224,896]{2,1,0:T(8,128)(2,1)}, u32[]{:S(2)}, u32[]{:S(2)}) %collective-permute-start.15) | collective-permute-done | bytes 802848 | tf_op jit(solution)/shard_map/ppermute | solution.py:367
  293.7 19.9 %collective-permute-done.17.refs_2_ = bf16[3,224,896]{2,1,0:T(8,128)(2,1)S(1)} collective-permute-done((bf16[3,224,896]{2,1,0:T(8,128)(2,1)S(1)}, bf16[3,224,896]{2,1,0:T(8,128)(2,1)S(1)}, u32[]{:S(2)}, u32[]{:S(2)}) %collective-permute-start.17) | collective-permute-done | bytes 1204256 | tf_op jit(solution)/shard_map/ppermute | solution.py:367
  324.1 9.3 %collective-permute-done.24.refs_4_ = bf16[896,1024]{1,0:T(8,128)(2,1)S(1)} collective-permute-done((bf16[896,1024]{1,0:T(8,128)(2,1)S(1)}, bf16[896,1024]{1,0:T(8,128)(2,1)S(1)}, u32[]{:S(2)}, u32[]{:S(2)}) %collective-permute-start.24) | collective-permute-done | bytes 1835040 | tf_op jit(solution)/shard_map/ppermute | solution.py:376
  333.4 19.3 %collective-permute-done.23.refs_6_ = bf16[4,224,896]{2,1,0:T(8,128)(2,1)S(1)} collective-permute-done((bf16[4,224,896]{2,1,0:T(8,128)(2,1)S(1)}, bf16[4,224,896]{2,1,0:T(8,128)(2,1)S(1)}, u32[]{:S(2)}, u32[]{:S(2)}) %collective-permute-start.23) | collective-permute-done | bytes 1605664 | tf_op jit(solution)/shard_map/ppermute | solution.py:367
  359.6 22.9 %collective-permute-done.28.refs_10_ = bf16[3,224,896]{2,1,0:T(8,128)(2,1)S(1)} collective-permute-done((bf16[3,224,896]{2,1,0:T(8,128)(2,1)S(1)}, bf16[3,224,896]{2,1,0:T(8,128)(2,1)S(1)}, u32[]{:S(2)}, u32[]{:S(2)}) %collective-permute-start.28) | collective-permute-done | bytes 1204256 | tf_op jit(solution)/shard_map/ppermute | solution.py:367
  390.4 37.7 %poly_rows.1.own = bf16[896,3584]{1,0:T(8,128)(2,1)} custom-call(s32[4]{0:T(128)} %pad_add_fusion.flags, bf16[3,224,896]{2,1,0:T(8,128)(2,1)} %copy-done.18, bf16[3,224,896]{2,1,0:T(8,128)(2,1)} %copy-done.26, bf16[3,224,896]{2,1,0:T(8,128)(2,1)} %copy-done.27, bf16[3,224,896]{2,1,0:T(8,128)(2,1)} %copy-done.29, bf16[4,224,896]{2,1,0:T(8,128)(2,1)} %copy-done.13, ...), custom_call_target="tpu_custom_call" | custom-call | tf_op jit(solution)/shard_map/poly_rows/pallas_call | solution.py:203
  428.4 10.4 %collective-permute-done.32.pair = bf16[896,3584]{1,0:T(8,128)(2,1)} collective-permute-done((bf16[896,3584]{1,0:T(8,128)(2,1)}, bf16[896,3584]{1,0:T(8,128)(2,1)}, u32[]{:S(2)}, u32[]{:S(2)}) %collective-permute-start.32) | collective-permute-done | bytes 6422560 | tf_op jit(solution)/shard_map/ppermute | solution.py:364
  446.0 22.6 %product_far.3 = (bf16[896,1024]{1,0:T(8,128)(2,1)}, bf16[896,1024]{1,0:T(8,128)(2,1)}, f32[1,256]{1,0:T(1,128)}) custom-call(s32[4]{0:T(128)} %pad_add_fusion.flags, bf16[896,3584]{1,0:T(8,128)(2,1)} %poly_rows.1.own, bf16[896,3584]{1,0:T(8,128)(2,1)} %collective-permute-done.32.pair, f32[1]{0:T(128)} %bitcast.11.refs_0_.refs_4_, ...), custom_call_target="tpu_custom_call" | custom-call | tf_op jit(solution)/shard_map/product_far/pallas_call | solution.py:289
  469.9 12.7 %collective-permute-done.34.refs_0_ = bf16[224,3584]{1,0:T(8,128)(2,1)} collective-permute-done((bf16[224,3584]{1,0:T(8,128)(2,1)}, bf16[224,3584]{1,0:T(8,128)(2,1)}, u32[]{:S(2)}, u32[]{:S(2)}) %collective-permute-start.34) | collective-permute-done | bytes 1605664 | tf_op jit(solution)/shard_map/ppermute | solution.py:379
  487.2 32.4 %collective-permute-done.37.refs_2_ = bf16[224,3584]{1,0:T(8,128)(2,1)} collective-permute-done((bf16[224,3584]{1,0:T(8,128)(2,1)}, bf16[224,3584]{1,0:T(8,128)(2,1)}, u32[]{:S(2)}, u32[]{:S(2)}) %collective-permute-start.37) | collective-permute-done | bytes 1605664 | tf_op jit(solution)/shard_map/ppermute | solution.py:367
  519.7 18.9 %product_far.4 = (bf16[896,768]{1,0:T(8,128)(2,1)}, bf16[896,768]{1,0:T(8,128)(2,1)}, f32[1,256]{1,0:T(1,128)}) custom-call(s32[4]{0:T(128)} %pad_add_fusion.flags, bf16[896,3584]{1,0:T(8,128)(2,1)} %poly_rows.1.own, bf16[896,3584]{1,0:T(8,128)(2,1)} %collective-permute-done.32.pair, f32[1]{0:T(128)} %bitcast.11.refs_0_.refs_4_, ...), custom_call_target="tpu_custom_call" | custom-call | tf_op jit(solution)/shard_map/product_far/pallas_call | solution.py:289
  546.2 22.9 %product_near.1 = (bf16[896,2304]{1,0:T(8,128)(2,1)}, f32[1,256]{1,0:T(1,128)}) custom-call(s32[4]{0:T(128)} %pad_add_fusion.flags, bf16[896,3584]{1,0:T(8,128)(2,1)} %poly_rows.1.own, bf16[896,3584]{1,0:T(8,128)(2,1)} %collective-permute-done.32.pair, bf16[224,3584]{1,0:T(8,128)(2,1)} %collective-permute-done.34.refs_0_, ...), custom_call_target="tpu_custom_call" | custom-call | tf_op jit(solution)/shard_map/product_near/pallas_call | solution.py:289
  570.4 15.3 %product_far.5 = (bf16[896,512]{1,0:T(8,128)(2,1)}, bf16[896,512]{1,0:T(8,128)(2,1)}, f32[1,256]{1,0:T(1,128)}) custom-call(s32[4]{0:T(128)} %pad_add_fusion.flags, bf16[896,3584]{1,0:T(8,128)(2,1)} %poly_rows.1.own, bf16[896,3584]{1,0:T(8,128)(2,1)} %collective-permute-done.32.pair, f32[1]{0:T(128)} %bitcast.11.refs_0_.refs_4_, ...), custom_call_target="tpu_custom_call" | custom-call | tf_op jit(solution)/shard_map/product_far/pallas_call | solution.py:289
  599.0 13.6 %collective-permute-done.43 = f32[8,128]{1,0:T(8,128)S(1)} collective-permute-done((f32[8,128]{1,0:T(8,128)S(1)}, f32[8,128]{1,0:T(8,128)S(1)}, u32[]{:S(2)}, u32[]{:S(2)}) %collective-permute-start.43) | collective-permute-done | bytes 4128 | tf_op jit(solution)/shard_map/ppermute | solution.py:376
  627.2 9.6 %finish.3 = f32[896,4608]{1,0:T(8,128)} custom-call(s32[4]{0:T(128)} %pad_add_fusion.flags, f32[1]{0:T(128)} %bitcast.12.factor, bf16[896,1024]{1,0:T(8,128)(2,1)} %get-tuple-element.140.refs_0_, bf16[896,768]{1,0:T(8,128)(2,1)} %get-tuple-element.141.refs_1_, bf16[896,512]{1,0:T(8,128)(2,1)} %get-tuple-element.142.refs_2_, ...), custom_call_target="tpu_custom_call", output_to_operand_aliasing={{}: (8, {})} | custom-call | tf_op jit(solution)/shard_map/finish/pallas_call | solution.py:337
  (203 shorter events, 154.8 us)
Async XLA Ops:
  10.7 95.8 %collective-permute-start = (bf16[896,2304]{1,0:T(8,128)(2,1)}, bf16[896,2304]{1,0:T(8,128)(2,1)}, u32[]{:S(2)}, u32[]{:S(2)}) collective-permute-start(bf16[896,2304]{1,0:T(8,128)(2,1)} %get-tuple-element.84.refs_3_), channel_id=1, source_target_pairs={{1,2},{2,1},{5,6},{6,5},{9,10},{10,9},{13,14},{14,13},{17,18},{18,... | collective-permute-start | bytes 12386312 | tf_op jit(solution)/shard_map/ppermute | solution.py:370
  13.2 97.0 %collective-permute-start.1 = (bf16[896,2304]{1,0:T(8,128)(2,1)}, bf16[896,2304]{1,0:T(8,128)(2,1)}, u32[]{:S(2)}, u32[]{:S(2)}) collective-permute-start(bf16[896,2304]{1,0:T(8,128)(2,1)} %get-tuple-element.77.refs_0_.refs_1_.refs_2_.refs_7_), channel_id=1, source_target_pairs={{0,1},{1,0},{2,3},{3,2},{4,5},{5,4},{6,7},{7,6},{8,9},{9,8},{10,11... | collective-permute-start | bytes 12386312 | tf_op jit(solution)/shard_map/ppermute | solution.py:376
  25.2 81.3 %collective-permute-start.4 = (f32[8,128]{1,0:T(8,128)S(1)}, f32[8,128]{1,0:T(8,128)S(1)}, u32[]{:S(2)}, u32[]{:S(2)}) collective-permute-start(f32[8,128]{1,0:T(8,128)S(1)} %fusion.4), channel_id=1, source_target_pairs={{0,1},{1,0},{2,3},{3,2},{4,5},{5,4},{6,7},{7,6},{8,9},{9,8},{10,11... | collective-permute-start | bytes 12296 | tf_op jit(solution)/shard_map/ppermute | solution.py:376
  110.3 48.0 %collective-permute-start.5 = (bf16[896,1152]{1,0:T(8,128)(2,1)}, bf16[896,1152]{1,0:T(8,128)(2,1)S(1)}, u32[]{:S(2)}, u32[]{:S(2)}) collective-permute-start(bf16[896,1152]{1,0:T(8,128)(2,1)} %slice_select_fusion), channel_id=1, source_target_pairs={{0,2},{3,1},{1,0},{2,3},{4,6},{7,5},{5,4},{6,7},{8,10},{11,9},{9,8... | collective-permute-start | bytes 6193160 | tf_op jit(solution)/shard_map/ppermute | solution.py:382
  159.6 47.6 %collective-permute-start.7 = (bf16[896,1152]{1,0:T(8,128)(2,1)}, bf16[896,1152]{1,0:T(8,128)(2,1)S(1)}, u32[]{:S(2)}, u32[]{:S(2)}) collective-permute-start(bf16[896,1152]{1,0:T(8,128)(2,1)} %slice_select_fusion.1), channel_id=1, source_target_pairs={{0,2},{3,1},{1,0},{2,3},{4,6},{7,5},{5,4},{6,7},{8,10},{11,9},{9,8... | collective-permute-start | bytes 6193160 | tf_op jit(solution)/shard_map/ppermute | solution.py:382
  209.9 29.6 %collective-permute-start.11 = (bf16[3,224,896]{2,1,0:T(8,128)(2,1)S(1)}, bf16[3,224,896]{2,1,0:T(8,128)(2,1)}, u32[]{:S(2)}, u32[]{:S(2)}) collective-permute-start(bf16[3,224,896]{2,1,0:T(8,128)(2,1)S(1)} %add_convert_fusion.5), channel_id=1, source_target_pairs={{1,2},{2,1},{5,6},{6,5},{9,10},{10,9},{13,14},{14,13},{17,18},{18,... | collective-permute-start | bytes 3612680 | tf_op jit(solution)/shard_map/ppermute | solution.py:370
  239.5 42.7 %collective-permute-start.13 = (bf16[3,224,896]{2,1,0:T(8,128)(2,1)}, bf16[3,224,896]{2,1,0:T(8,128)(2,1)}, u32[]{:S(2)}, u32[]{:S(2)}) collective-permute-start(bf16[3,224,896]{2,1,0:T(8,128)(2,1)} %add_convert_fusion.4), channel_id=1, source_target_pairs={{1,2},{2,1},{5,6},{6,5},{9,10},{10,9},{13,14},{14,13},{17,18},{18,... | collective-permute-start | bytes 3612680 | tf_op jit(solution)/shard_map/ppermute | solution.py:370
  246.3 34.5 %collective-permute-start.15 = (bf16[2,224,896]{2,1,0:T(8,128)(2,1)}, bf16[2,224,896]{2,1,0:T(8,128)(2,1)}, u32[]{:S(2)}, u32[]{:S(2)}) collective-permute-start(bf16[2,224,896]{2,1,0:T(8,128)(2,1)} %constant_dynamic-slice_fusion.1), channel_id=1, source_target_pairs={{0,8},{4,12},{8,0},{12,4},{1,9},{5,13},{9,1},{13,5},{2,10},{6,14},... | collective-permute-start | bytes 2408456 | tf_op jit(solution)/shard_map/ppermute | solution.py:367
  284.8 28.9 %collective-permute-start.17 = (bf16[3,224,896]{2,1,0:T(8,128)(2,1)S(1)}, bf16[3,224,896]{2,1,0:T(8,128)(2,1)S(1)}, u32[]{:S(2)}, u32[]{:S(2)}) collective-permute-start(bf16[3,224,896]{2,1,0:T(8,128)(2,1)S(1)} %fusion.1.refs_0_), channel_id=1, source_target_pairs={{0,8},{4,12},{8,0},{12,4},{1,9},{5,13},{9,1},{13,5},{2,10},{6,14},... | collective-permute-start | bytes 3612680 | tf_op jit(solution)/shard_map/ppermute | solution.py:367
  289.0 44.4 %collective-permute-start.24 = (bf16[896,1024]{1,0:T(8,128)(2,1)S(1)}, bf16[896,1024]{1,0:T(8,128)(2,1)S(1)}, u32[]{:S(2)}, u32[]{:S(2)}) collective-permute-start(bf16[896,1024]{1,0:T(8,128)(2,1)S(1)} %slice.139), channel_id=1, source_target_pairs={{0,1},{1,0},{2,3},{3,2},{4,5},{5,4},{6,7},{7,6},{8,9},{9,8},{10,11... | collective-permute-start | bytes 5505032 | tf_op jit(solution)/shard_map/ppermute | solution.py:376
  315.1 37.5 %collective-permute-start.23 = (bf16[4,224,896]{2,1,0:T(8,128)(2,1)S(1)}, bf16[4,224,896]{2,1,0:T(8,128)(2,1)S(1)}, u32[]{:S(2)}, u32[]{:S(2)}) collective-permute-start(bf16[4,224,896]{2,1,0:T(8,128)(2,1)S(1)} %fusion.refs_4_), channel_id=1, source_target_pairs={{0,8},{4,12},{8,0},{12,4},{1,9},{5,13},{9,1},{13,5},{2,10},{6,14},... | collective-permute-start | bytes 4816904 | tf_op jit(solution)/shard_map/ppermute | solution.py:367
  321.6 106.6 %collective-permute-start.31 = (bf16[2,896,1024]{2,1,0:T(8,128)(2,1)}, bf16[2,896,1024]{2,1,0:T(8,128)(2,1)}, u32[]{:S(2)}, u32[]{:S(2)}) collective-permute-start(bf16[2,896,1024]{2,1,0:T(8,128)(2,1)} %pad_maximum_fusion), channel_id=1, source_target_pairs={{1,2},{2,1},{5,6},{6,5},{9,10},{10,9},{13,14},{14,13},{17,18},{18,... | collective-permute-start | bytes 11010056 | tf_op jit(solution)/shard_map/ppermute | solution.py:370
  324.0 35.0 %collective-permute-start.21 = (bf16[3,224,896]{2,1,0:T(8,128)(2,1)S(1)}, bf16[3,224,896]{2,1,0:T(8,128)(2,1)S(1)}, u32[]{:S(2)}, u32[]{:S(2)}) collective-permute-start(bf16[3,224,896]{2,1,0:T(8,128)(2,1)S(1)} %copy-done.28), channel_id=1, source_target_pairs={{0,4},{4,0},{8,12},{12,8},{1,5},{5,1},{9,13},{13,9},{2,6},{6,2},{1... | collective-permute-start | bytes 3612680 | tf_op jit(solution)/shard_map/ppermute | solution.py:364
  356.1 72.0 %collective-permute-start.30 = (bf16[896,1280]{1,0:T(8,128)(2,1)S(1)}, bf16[896,1280]{1,0:T(8,128)(2,1)S(1)}, u32[]{:S(2)}, u32[]{:S(2)}) collective-permute-start(bf16[896,1280]{1,0:T(8,128)(2,1)S(1)} %slice.140), channel_id=1, source_target_pairs={{0,1},{1,0},{2,3},{3,2},{4,5},{5,4},{6,7},{7,6},{8,9},{9,8},{10,11... | collective-permute-start | bytes 6881288 | tf_op jit(solution)/shard_map/ppermute | solution.py:376
  359.0 29.9 %collective-permute-start.26 = (bf16[4,224,896]{2,1,0:T(8,128)(2,1)S(1)}, bf16[4,224,896]{2,1,0:T(8,128)(2,1)S(1)}, u32[]{:S(2)}, u32[]{:S(2)}) collective-permute-start(bf16[4,224,896]{2,1,0:T(8,128)(2,1)S(1)} %collective-permute-done.23.refs_6_), channel_id=1, source_target_pairs={{0,4},{4,0},{8,12},{12,8},{1,5},{5,1},{9,13},{13,9},{2,6},{6,2},{1... | collective-permute-start | bytes 4816904 | tf_op jit(solution)/shard_map/ppermute | solution.py:364
  359.1 29.8 %collective-permute-start.27 = (bf16[3,224,896]{2,1,0:T(8,128)(2,1)S(1)}, bf16[3,224,896]{2,1,0:T(8,128)(2,1)S(1)}, u32[]{:S(2)}, u32[]{:S(2)}) collective-permute-start(bf16[3,224,896]{2,1,0:T(8,128)(2,1)S(1)} %fusion.2.refs_8_), channel_id=1, source_target_pairs={{0,4},{4,0},{8,12},{12,8},{1,5},{5,1},{9,13},{13,9},{2,6},{6,2},{1... | collective-permute-start | bytes 3612680 | tf_op jit(solution)/shard_map/ppermute | solution.py:364
  442.3 40.3 %collective-permute-start.34 = (bf16[224,3584]{1,0:T(8,128)(2,1)}, bf16[224,3584]{1,0:T(8,128)(2,1)}, u32[]{:S(2)}, u32[]{:S(2)}) collective-permute-start(bf16[224,3584]{1,0:T(8,128)(2,1)} %dynamic-slice_select_fusion), channel_id=1, source_target_pairs={{1,0},{2,3},{5,4},{6,7},{9,8},{10,11},{13,12},{14,15},{17,16},{18,... | collective-permute-start | bytes 4816904 | tf_op jit(solution)/shard_map/ppermute | solution.py:379
  443.6 76.1 %collective-permute-start.35 = (bf16[2,896,768]{2,1,0:T(8,128)(2,1)}, bf16[2,896,768]{2,1,0:T(8,128)(2,1)}, u32[]{:S(2)}, u32[]{:S(2)}) collective-permute-start(bf16[2,896,768]{2,1,0:T(8,128)(2,1)} %pad_maximum_fusion.1), channel_id=1, source_target_pairs={{1,2},{2,1},{5,6},{6,5},{9,10},{10,9},{13,14},{14,13},{17,18},{18,... | collective-permute-start | bytes 8257544 | tf_op jit(solution)/shard_map/ppermute | solution.py:370
  482.6 37.1 %collective-permute-start.37 = (bf16[224,3584]{1,0:T(8,128)(2,1)}, bf16[224,3584]{1,0:T(8,128)(2,1)}, u32[]{:S(2)}, u32[]{:S(2)}) collective-permute-start(bf16[224,3584]{1,0:T(8,128)(2,1)} %collective-permute-done.34.refs_0_), channel_id=1, source_target_pairs={{0,8},{4,12},{8,0},{12,4},{1,9},{5,13},{9,1},{13,5},{2,10},{6,14},... | collective-permute-start | bytes 4816904 | tf_op jit(solution)/shard_map/ppermute | solution.py:367
  483.9 58.6 %collective-permute-start.33 = (bf16[896,1024]{1,0:T(8,128)(2,1)}, bf16[896,1024]{1,0:T(8,128)(2,1)}, u32[]{:S(2)}, u32[]{:S(2)}) collective-permute-start(bf16[896,1024]{1,0:T(8,128)(2,1)} %get-tuple-element.122), channel_id=1, source_target_pairs={{1,0},{2,3},{5,4},{6,7},{9,8},{10,11},{13,12},{14,15},{17,16},{18,... | collective-permute-start | bytes 5505032 | tf_op jit(solution)/shard_map/ppermute | solution.py:379
  485.3 85.1 %collective-permute-start.40 = (bf16[2,896,512]{2,1,0:T(8,128)(2,1)}, bf16[2,896,512]{2,1,0:T(8,128)(2,1)}, u32[]{:S(2)}, u32[]{:S(2)}) collective-permute-start(bf16[2,896,512]{2,1,0:T(8,128)(2,1)} %pad_maximum_fusion.2), channel_id=1, source_target_pairs={{1,2},{2,1},{5,6},{6,5},{9,10},{10,9},{13,14},{14,13},{17,18},{18,... | collective-permute-start | bytes 5505032 | tf_op jit(solution)/shard_map/ppermute | solution.py:370
  487.2 59.0 %collective-permute-start.36 = (bf16[224,3584]{1,0:T(8,128)(2,1)}, bf16[224,3584]{1,0:T(8,128)(2,1)}, u32[]{:S(2)}, u32[]{:S(2)}) collective-permute-start(bf16[224,3584]{1,0:T(8,128)(2,1)} %collective-permute-done.34.refs_0_), channel_id=1, source_target_pairs={{0,4},{4,0},{8,12},{12,8},{1,5},{5,1},{9,13},{13,9},{2,6},{6,2},{1... | collective-permute-start | bytes 4816904 | tf_op jit(solution)/shard_map/ppermute | solution.py:364
  540.0 48.9 %collective-permute-start.39 = (bf16[896,768]{1,0:T(8,128)(2,1)}, bf16[896,768]{1,0:T(8,128)(2,1)}, u32[]{:S(2)}, u32[]{:S(2)}) collective-permute-start(bf16[896,768]{1,0:T(8,128)(2,1)} %get-tuple-element.134), channel_id=1, source_target_pairs={{1,0},{2,3},{5,4},{6,7},{9,8},{10,11},{13,12},{14,15},{17,16},{18,... | collective-permute-start | bytes 4128776 | tf_op jit(solution)/shard_map/ppermute | solution.py:379
  585.7 40.6 %collective-permute-start.45 = (bf16[896,512]{1,0:T(8,128)(2,1)}, bf16[896,512]{1,0:T(8,128)(2,1)S(1)}, u32[]{:S(2)}, u32[]{:S(2)}) collective-permute-start(bf16[896,512]{1,0:T(8,128)(2,1)} %get-tuple-element.145), channel_id=1, source_target_pairs={{1,0},{2,3},{5,4},{6,7},{9,8},{10,11},{13,12},{14,15},{17,16},{18,... | collective-permute-start | bytes 2752520 | tf_op jit(solution)/shard_map/ppermute | solution.py:379
  (56 other events, 637.0 us)

commit v8 on v7

--- a/solution.py
+++ b/solution.py
@@ -216,9 +216,9 @@
     )(flags, *[x for group in groups for x in group])
 
 
-def product_kernel(is_far, flags, own, pair, *refs):
+def product_kernel(is_far, cut, flags, own, pair, *refs):
     end_rows, refs = ((), refs) if is_far else (refs[:4], refs[4:])
-    inverse, blocks, outs = refs[0], refs[1:5], refs[5:-4]
+    inverse, blocks, inward, outs = refs[0], refs[1:5], () if is_far else refs[5:7], refs[5 if is_far else 7 : -4]
     sq_ref, poly, raw, sems = refs[-4:]
     rows = own.shape[0]
 
@@ -268,6 +268,12 @@
 
     for r, block in enumerate(blocks):
         raw[r * rows : (r + 1) * rows, :] = block[...]
+    for k, block in enumerate(inward):
+
+        @pl.when((flags[2] == 0) & ((pl.program_id(0) >= cut) == (k == 1)))
+        def _(block=block):
+            raw[rows : 2 * rows, :] = block[...]
+
     for k, out in enumerate(outs):
         product = jnp.dot(poly[k * rows : (k + 1) * rows, :], raw[...], preferred_element_type=jnp.float32)
         own_rows = raw[(2 + k) * rows : (3 + k) * rows, :].astype(jnp.float32)
@@ -276,7 +282,7 @@
         out[...] = newton.astype(jnp.bfloat16)
 
 
-def product(flags, polys, inverse, blocks, tiles, is_far):
+def product(flags, polys, inverse, blocks, tiles, is_far, inward=()):
     rows, order = polys[0].shape
     count = 2 if is_far else 1
     block_specs = [
@@ -284,10 +290,13 @@
         if lead is None
         else pl.BlockSpec((None, rows, TILE), lambda t, flags, at=at, lead=lead: (lead, 0, at + t))
         for _, lead, at in blocks
+    ] + [
+        pl.BlockSpec((rows, TILE), lambda t, flags, a=a, b=b: (0, jnp.clip(t, a, b - 1) - a))
+        for _, a, b in inward
     ]
     there = pl.BlockSpec((rows, TILE), lambda t, flags: (0, t))
     *newton, squares = pl.pallas_call(
-        functools.partial(product_kernel, is_far),
+        functools.partial(product_kernel, is_far, inward[0][2] if inward else 0),
         grid_spec=pltpu.PrefetchScalarGridSpec(
             num_scalar_prefetch=1,
             grid=(tiles,),
@@ -306,45 +315,44 @@
         compiler_params=pltpu.CompilerParams(vmem_limit_bytes=VMEM_BYTES),
         cost_estimate=pl.CostEstimate(flops=0, bytes_accessed=0, transcendentals=0),
         name="product_far" if is_far else "product_near",
-    )(flags, *polys, inverse, *[array for array, _, _ in blocks])
+    )(flags, *polys, inverse, *[array for array, _, _ in (*blocks, *inward)])
     return newton, jnp.sum(squares)
 
 
-def finish_kernel(cuts, flags, factor, *refs):
+def finish_kernel(cuts, flags, factor, near, *refs):
     out_ref = refs[-1]
     chunks = len(cuts) - 1
-    for k, ref in enumerate(refs[: chunks if chunks == 1 else 2 * chunks]):
-
-        @pl.when((chunks == 1) | ((flags[2] == 1) == (k < chunks)))
-        def _(k=k, ref=ref):
-            out_ref[:, cuts[k % chunks] : cuts[k % chunks + 1]] = ref[...].astype(jnp.float32) * factor[0]
-
-
-def finish(flags, factor, parts, cuts, shape, before):
+    width = near.shape[1]
+    near_at = pl.multiple_of(flags[0] * width, STRIP)
+    far_at = width - near_at
+    out_ref[:, pl.ds(near_at, width)] = near[...].astype(jnp.float32) * factor[0]
+    for k, ref in enumerate(refs[:-1]):
+        first, last = cuts[k % chunks : k % chunks + 2]
+
+        @pl.when((flags[2] == 1) == (k < chunks))
+        def _(ref=ref, first=first, last=last):
+            place = pl.ds(pl.multiple_of(far_at + first, STRIP), last - first)
+            out_ref[:, place] = ref[...].astype(jnp.float32) * factor[0]
+
+
+def finish(flags, factor, near, parts, cuts, shape):
     rows, cols = shape
     step = rows // 8
-    place = pl.BlockSpec(
-        (step, cols // 2), lambda t, flags: (t, flags[0] if len(parts) == 1 else 1 - flags[0])
-    )
     specs = [pl.BlockSpec(memory_space=pltpu.SMEM)]
-    specs += [pl.BlockSpec((step, part.shape[1]), lambda t, flags: (t, 0)) for part in parts]
-    operands = [flags, factor, *parts]
-    aliases = {}
-    if before is not None:
-        specs.append(pl.BlockSpec(memory_space=pl.ANY))
-        aliases = {len(operands): 0}
-        operands.append(before)
+    specs += [pl.BlockSpec((step, part.shape[1]), lambda t, flags: (t, 0)) for part in (near, *parts)]
     return pl.pallas_call(
         functools.partial(finish_kernel, cuts),
         grid_spec=pltpu.PrefetchScalarGridSpec(
-            num_scalar_prefetch=1, grid=(8,), in_specs=specs, out_specs=place
+            num_scalar_prefetch=1,
+            grid=(8,),
+            in_specs=specs,
+            out_specs=pl.BlockSpec((step, cols), lambda t, flags: (t, 0)),
         ),
         out_shape=jax.ShapeDtypeStruct(shape, jnp.float32),
-        input_output_aliases=aliases,
         compiler_params=pltpu.CompilerParams(vmem_limit_bytes=VMEM_BYTES),
         cost_estimate=pl.CostEstimate(flops=0, bytes_accessed=0, transcendentals=0),
         name="finish",
-    )(*operands)
+    )(flags, factor, near, *parts)
 
 
 def per_device(momentum):
@@ -469,7 +477,7 @@
     cuts = [t * TILE for t in tile_bounds]
     inward_first = with_end(inward[:, : cuts[1]])
     swaps = [jnp.stack([block[:, a:b] for block in (beside, near)]) for a, b in zip(cuts[:-1], cuts[1:])]
-    swaps[0], other_fourth = barrier((swaps[0], other_fourth))
+    *swaps, other_fourth = barrier((*swaps, other_fourth))
     swaps[0] = between_hubs(swaps[0])
     groups[1][1], groups[1][2], inward_first, other_fourth = barrier(
         (groups[1][1], groups[1][2], inward_first, other_fourth)
@@ -502,15 +510,16 @@
         return squares
 
     hub_sq = far_product(0, scale)
-    scale, hub_sq, row_share = barrier((scale, hub_sq, row_share))
+    hub_sq, row_share = barrier((hub_sq, row_share))
     row_across = over_side(row_share)
-    end_rows = [row_share, over_core(row_share), row_across, over_core(row_across)]
+    scale, hub_sq, swaps[1] = barrier((scale, hub_sq, swaps[1]))
     swaps[2] = between_hubs(swaps[2])
     hub_sq += far_product(1, scale)
-    at_end[0], scale, hub_sq, inward_first = barrier((at_end[0], scale, hub_sq, inward_first))
-    inward = jnp.concatenate([inward_first, inward_second], axis=1)
-    blocks = [(passed, None, 0), (jnp.where(is_hub, middle, inward), None, 0), (near, None, 0), (beside, None, 0)]
-    (near_part,), near_sq = product(flags, (own, pair, *end_rows), scale, blocks, tiles, False)
+    at_end[0], scale, hub_sq, row_across = barrier((at_end[0], scale, hub_sq, row_across))
+    end_rows = [row_share, over_core(row_share), row_across, over_core(row_across)]
+    blocks = [(passed, None, 0), (middle, None, 0), (near, None, 0), (beside, None, 0)]
+    inward = [(inward_first, 0, tile_bounds[1]), (inward_second, tile_bounds[1], tiles)]
+    (near_part,), near_sq = product(flags, (own, pair, *end_rows), scale, blocks, tiles, False, inward)
     scale, near_sq = barrier((scale, near_sq))
     hub_sq += far_product(2, scale)
     at_end[1], hub_sq = barrier((at_end[1], hub_sq))
@@ -518,8 +527,7 @@
     total_sq += with_end(total_sq)
     total_sq += skip_one(total_sq)
     factor = (1.0 / (jnp.sqrt(total_sq[0, 0]) / math.sqrt(M * N) + 1e-07)).reshape(1)
-    out = finish(flags, factor, [near_part], [0, width], (rows, cols), None)
-    return finish(flags, factor, at_hub + at_end, cuts, (rows, cols), out)
+    return finish(flags, factor, near_part, at_hub + at_end, cuts, (rows, cols))
 
 
 def per_device_general(momentum):

time: 645 us -> 629 us (0.975)
  waiting for transfers between devices: 287 us -> 259 us
  starting transfers between devices: 56.6 us -> 65.6 us
  local copies, waits for them, and re-layouts: 19.5 us -> 26.3 us
    ppermute x10, waiting for transfers between devices: 143 us -> 101 us  [over_side(): return lax.ppermute(x, 'col', [(k, k ^ 2) for k in range(4)])]
    ppermute x4, waiting for transfers between devices: 12.7 us -> 24.7 us  [to_end(): return lax.ppermute(x, 'row', [(1, 0), (2, 3)])]
    ppermute x5, starting transfers between devices: 16.2 us -> 25.9 us  [with_end(): return lax.ppermute(x, 'row', [(0, 1), (1, 0), (2, 3), (3, 2)])]
    pallas_call x2 -> x1, Pallas kernels: 17.5 us -> 12.7 us  [finish(): pl.pallas_call(functools.partial(finish_kernel, cuts), grid_spec=pltpu.Pr...]
  transfers between devices with their start and end apart: 46 -> 46, of which waited for: 20 -> 22; matrix products, arithmetic and copies ran while one was open for 8% -> 8% of each run, Pallas kernels for 32% -> 32%
where the time goes in v8:
time: 629 us; the launch traced here: 622 us
  waiting for transfers between devices  259 us (41%)
  Pallas kernels  220 us (35%)
  starting transfers between devices  65.6 us (10%)
  other arithmetic  44.9 us (7%)
  local copies, waits for them, and re-layouts  26.3 us (4%)
    ppermute x5, waiting for transfers between devices, with_end(): return lax.ppermute(x, 'row', [(0, 1), (1, 0), (2, 3), (3, 2)])  101 us
    ppermute x10, waiting for transfers between devices, over_side(): return lax.ppermute(x, 'col', [(k, k ^ 2) for k in range(4)])  101 us
    pallas_call x4, Pallas kernels, product(): pl.pallas_call(functools.partial(product_kernel, is_far, inward[0][2] if...  81.7 us
    pallas_call x5, Pallas kernels, gram_blocks(): pl.pallas_call(functools.partial(gram_kernel, pairs, where, pieces, int(t...  77.9 us
    pallas_call x1, Pallas kernels, poly_rows(): pl.pallas_call(poly_kernel, grid_spec=pltpu.PrefetchScalarGridSpec(num_sc...  37.5 us
    ppermute x5, starting transfers between devices, with_end(): return lax.ppermute(x, 'row', [(0, 1), (1, 0), (2, 3), (3, 2)])  25.9 us
    ppermute x4, waiting for transfers between devices, to_end(): return lax.ppermute(x, 'row', [(1, 0), (2, 3)])  24.7 us
    ppermute x15, waiting for transfers between devices, over_core(): return lax.ppermute(x, 'col', [(k, k ^ 1) for k in range(4)])  18.5 us
  transfers between devices with their start and end apart: 46, of which 22 were waited for; matrix products, arithmetic and copies ran while one was open for 8% of the time, Pallas kernels for 32%

profile of v8, /device:TPU:0, one launch (start us, length us, event | category | flops | bytes accessed | tf_op | source)
XLA Modules:
  0.0 621.9 jit_solution(8034491407285711236)
XLA Ops:
  0.0 10.6 %take_halves.1 = (bf16[896,2304]{1,0:T(8,128)(2,1)}, bf16[896,2304]{1,0:T(8,128)(2,1)}, f32[1,2304]{1,0:T(1,128)}) custom-call(s32[1]{0:T(128)} %bitcast.index, f32[896,4608]{1,0:T(8,128)} %far_ref.1, f32[896,4608]{1,0:T(8,128)} %far_ref.1), custom_call_target="tpu_custom_call" | custom-call | flops 8257536 | bytes 24772608 | tf_op jit(solution)/shard_map/take_halves/pallas_call | solution.py:45
  25.6 80.8 %collective-permute-done.4 = f32[8,128]{1,0:T(8,128)S(1)} collective-permute-done((f32[8,128]{1,0:T(8,128)S(1)}, f32[8,128]{1,0:T(8,128)S(1)}, u32[]{:S(2)}, u32[]{:S(2)}) %collective-permute-start.4) | collective-permute-done | bytes 4128 | tf_op jit(solution)/shard_map/ppermute | solution.py:384
  114.5 19.0 %gram_blocks.5 = (bf16[3,448,896]{2,1,0:T(8,128)(2,1)}, bf16[3,448,896]{2,1,0:T(8,128)(2,1)}) custom-call(s32[4]{0:T(128)} %pad_add_fusion.flags, bf16[896,2304]{1,0:T(8,128)(2,1)} %get-tuple-element.81.refs_0_.refs_1_.refs_2_.refs_7_, bf16[896,2304]{1,0:T(8,128)(2,1)} %collective-permute-done.1.refs_1_.refs_2_.refs_3_.refs_8_), custom_call_target="tpu_custom_call" | custom-call | tf_op jit(solution)/shard_map/gram_blocks/pallas_call | solution.py:124
  136.7 20.5 %gram_blocks.6 = (bf16[3,448,896]{2,1,0:T(8,128)(2,1)}, bf16[3,448,896]{2,1,0:T(8,128)(2,1)}) custom-call(s32[4]{0:T(128)} %pad_add_fusion.flags, bf16[896,2304]{1,0:T(8,128)(2,1)} %collective-permute-done.refs_0_.refs_1_.refs_6_, bf16[896,2304]{1,0:T(8,128)(2,1)} %get-tuple-element.81.refs_0_.refs_1_.refs_2_.refs_7_, ...), custom_call_target="tpu_custom_call" | custom-call | tf_op jit(solution)/shard_map/gram_blocks/pallas_call | solution.py:124
  168.9 16.4 %gram_blocks.7.refs_3_.refs_2_ = f32[4,896,896]{2,1,0:T(8,128)} custom-call(s32[4]{0:T(128)} %pad_add_fusion.flags, bf16[896,1152]{1,0:T(8,128)(2,1)} %copy-done.12, bf16[896,2304]{1,0:T(8,128)(2,1)} %collective-permute-done.refs_0_.refs_1_.refs_6_, bf16[896,2304]{1,0:T(8,128)(2,1)} %get-tuple-element.81.refs_0_.refs_1_.refs_2_.refs_7_, ...), custom_call_target="tpu_custom_call" | custom-call | tf_op jit(solution)/shard_map/gram_blocks/pallas_call | solution.py:124
  197.6 9.0 %collective-permute-done.7.refs_0_ = bf16[896,1152]{1,0:T(8,128)(2,1)S(1)} collective-permute-done((bf16[896,1152]{1,0:T(8,128)(2,1)}, bf16[896,1152]{1,0:T(8,128)(2,1)S(1)}, u32[]{:S(2)}, u32[]{:S(2)}) %collective-permute-start.7) | collective-permute-done | bytes 2064416 | tf_op jit(solution)/shard_map/ppermute | solution.py:390
  211.0 10.5 %gram_blocks.9 = (bf16[2,448,896]{2,1,0:T(8,128)(2,1)}, bf16[2,448,896]{2,1,0:T(8,128)(2,1)}) custom-call(s32[4]{0:T(128)} %pad_add_fusion.flags, bf16[896,1152]{1,0:T(8,128)(2,1)} %copy-done.5, bf16[896,2304]{1,0:T(8,128)(2,1)} %collective-permute-done.refs_0_.refs_1_.refs_6_, f32[4,896,896]{2,1,0:T(8,128)} %gram_blocks.7.refs_3_.refs_2_), custom_call_target="tpu_custom_call" | custom-call | tf_op jit(solution)/shard_map/gram_blocks/pallas_call | solution.py:124
  221.6 11.5 %gram_blocks.8 = (bf16[2,448,896]{2,1,0:T(8,128)(2,1)}, bf16[2,448,896]{2,1,0:T(8,128)(2,1)}) custom-call(s32[4]{0:T(128)} %pad_add_fusion.flags, bf16[896,1152]{1,0:T(8,128)(2,1)} %copy-done.5, bf16[896,2304]{1,0:T(8,128)(2,1)} %get-tuple-element.81.refs_0_.refs_1_.refs_2_.refs_7_, bf16[896,2304]{1,0:T(8,128)(2,1)} %collective-permute-done.1.refs_1_.refs_2_.refs_3_.refs_8_, ...), custom_call_target="tpu_custom_call" | custom-call | tf_op jit(solution)/shard_map/gram_blocks/pallas_call | solution.py:124
  256.2 14.0 %collective-permute-done.19 = bf16[2,224,896]{2,1,0:T(8,128)(2,1)} collective-permute-done((bf16[2,224,896]{2,1,0:T(8,128)(2,1)}, bf16[2,224,896]{2,1,0:T(8,128)(2,1)}, u32[]{:S(2)}, u32[]{:S(2)}) %collective-permute-start.19) | collective-permute-done | bytes 802848 | tf_op jit(solution)/shard_map/ppermute | solution.py:375
  271.5 15.5 %collective-permute-done.15 = bf16[2,224,896]{2,1,0:T(8,128)(2,1)} collective-permute-done((bf16[2,224,896]{2,1,0:T(8,128)(2,1)}, bf16[2,224,896]{2,1,0:T(8,128)(2,1)}, u32[]{:S(2)}, u32[]{:S(2)}) %collective-permute-start.15) | collective-permute-done | bytes 802848 | tf_op jit(solution)/shard_map/ppermute | solution.py:375
  302.0 18.0 %collective-permute-done.17.refs_2_ = bf16[3,224,896]{2,1,0:T(8,128)(2,1)S(1)} collective-permute-done((bf16[3,224,896]{2,1,0:T(8,128)(2,1)S(1)}, bf16[3,224,896]{2,1,0:T(8,128)(2,1)S(1)}, u32[]{:S(2)}, u32[]{:S(2)}) %collective-permute-start.17) | collective-permute-done | bytes 1204256 | tf_op jit(solution)/shard_map/ppermute | solution.py:375
  341.1 16.5 %collective-permute-done.23.refs_6_ = bf16[4,224,896]{2,1,0:T(8,128)(2,1)S(1)} collective-permute-done((bf16[4,224,896]{2,1,0:T(8,128)(2,1)S(1)}, bf16[4,224,896]{2,1,0:T(8,128)(2,1)S(1)}, u32[]{:S(2)}, u32[]{:S(2)}) %collective-permute-start.23) | collective-permute-done | bytes 1605664 | tf_op jit(solution)/shard_map/ppermute | solution.py:375
  364.4 21.3 %collective-permute-done.28.refs_10_ = bf16[3,224,896]{2,1,0:T(8,128)(2,1)S(1)} collective-permute-done((bf16[3,224,896]{2,1,0:T(8,128)(2,1)S(1)}, bf16[3,224,896]{2,1,0:T(8,128)(2,1)S(1)}, u32[]{:S(2)}, u32[]{:S(2)}) %collective-permute-start.28) | collective-permute-done | bytes 1204256 | tf_op jit(solution)/shard_map/ppermute | solution.py:375
  388.7 37.5 %poly_rows.1.own = bf16[896,3584]{1,0:T(8,128)(2,1)} custom-call(s32[4]{0:T(128)} %pad_add_fusion.flags, bf16[3,224,896]{2,1,0:T(8,128)(2,1)} %copy-done.22, bf16[3,224,896]{2,1,0:T(8,128)(2,1)} %copy-done.38, bf16[3,224,896]{2,1,0:T(8,128)(2,1)} %copy-done.36, bf16[3,224,896]{2,1,0:T(8,128)(2,1)} %copy-done.39, bf16[4,224,896]{2,1,0:T(8,128)(2,1)} %copy-done.16, ...), custom_call_target="tpu_custom_call" | custom-call | tf_op jit(solution)/shard_map/poly_rows/pallas_call | solution.py:203
  426.4 10.6 %collective-permute-done.32.pair = bf16[896,3584]{1,0:T(8,128)(2,1)} collective-permute-done((bf16[896,3584]{1,0:T(8,128)(2,1)}, bf16[896,3584]{1,0:T(8,128)(2,1)}, u32[]{:S(2)}, u32[]{:S(2)}) %collective-permute-start.32) | collective-permute-done | bytes 6422560 | tf_op jit(solution)/shard_map/ppermute | solution.py:372
  442.5 22.6 %product_far.3 = (bf16[896,1024]{1,0:T(8,128)(2,1)}, bf16[896,1024]{1,0:T(8,128)(2,1)}, f32[1,256]{1,0:T(1,128)}) custom-call(s32[4]{0:T(128)} %pad_add_fusion.flags, bf16[896,3584]{1,0:T(8,128)(2,1)} %poly_rows.1.own, bf16[896,3584]{1,0:T(8,128)(2,1)} %collective-permute-done.32.pair, f32[1]{0:T(128)} %bitcast.11.refs_0_.refs_4_, ...), custom_call_target="tpu_custom_call" | custom-call | tf_op jit(solution)/shard_map/product_far/pallas_call | solution.py:298
  468.0 12.6 %collective-permute-done.34.refs_0_ = bf16[224,3584]{1,0:T(8,128)(2,1)} collective-permute-done((bf16[224,3584]{1,0:T(8,128)(2,1)}, bf16[224,3584]{1,0:T(8,128)(2,1)}, u32[]{:S(2)}, u32[]{:S(2)}) %collective-permute-start.34) | collective-permute-done | bytes 1605664 | tf_op jit(solution)/shard_map/ppermute | solution.py:387
  485.6 19.0 %product_far.4 = (bf16[896,768]{1,0:T(8,128)(2,1)}, bf16[896,768]{1,0:T(8,128)(2,1)}, f32[1,256]{1,0:T(1,128)}) custom-call(s32[4]{0:T(128)} %pad_add_fusion.flags, bf16[896,3584]{1,0:T(8,128)(2,1)} %poly_rows.1.own, bf16[896,3584]{1,0:T(8,128)(2,1)} %collective-permute-done.32.pair, f32[1]{0:T(128)} %bitcast.11.refs_0_.refs_4_, ...), custom_call_target="tpu_custom_call" | custom-call | tf_op jit(solution)/shard_map/product_far/pallas_call | solution.py:298
  507.4 12.1 %collective-permute-done.33.refs_3_ = bf16[896,1024]{1,0:T(8,128)(2,1)} collective-permute-done((bf16[896,1024]{1,0:T(8,128)(2,1)}, bf16[896,1024]{1,0:T(8,128)(2,1)}, u32[]{:S(2)}, u32[]{:S(2)}) %collective-permute-start.33) | collective-permute-done | bytes 1835040 | tf_op jit(solution)/shard_map/ppermute | solution.py:387
  524.3 24.8 %product_near.1 = (bf16[896,2304]{1,0:T(8,128)(2,1)}, f32[1,256]{1,0:T(1,128)}) custom-call(s32[4]{0:T(128)} %pad_add_fusion.flags, bf16[896,3584]{1,0:T(8,128)(2,1)} %poly_rows.1.own, bf16[896,3584]{1,0:T(8,128)(2,1)} %collective-permute-done.32.pair, bf16[224,3584]{1,0:T(8,128)(2,1)} %collective-permute-done.34.refs_0_, ...), custom_call_target="tpu_custom_call" | custom-call | tf_op jit(solution)/shard_map/product_near/pallas_call | solution.py:298
  550.5 15.3 %product_far.5 = (bf16[896,512]{1,0:T(8,128)(2,1)}, bf16[896,512]{1,0:T(8,128)(2,1)}, f32[1,256]{1,0:T(1,128)}) custom-call(s32[4]{0:T(128)} %pad_add_fusion.flags, bf16[896,3584]{1,0:T(8,128)(2,1)} %poly_rows.1.own, bf16[896,3584]{1,0:T(8,128)(2,1)} %collective-permute-done.32.pair, f32[1]{0:T(128)} %bitcast.11.refs_0_.refs_4_, ...), custom_call_target="tpu_custom_call" | custom-call | tf_op jit(solution)/shard_map/product_far/pallas_call | solution.py:298
  574.6 14.0 %collective-permute-start.43 = (f32[8,128]{1,0:T(8,128)S(1)}, f32[8,128]{1,0:T(8,128)S(1)}, u32[]{:S(2)}, u32[]{:S(2)}) collective-permute-start(f32[8,128]{1,0:T(8,128)S(1)} %fusion.3), channel_id=1, source_target_pairs={{0,1},{1,0},{2,3},{3,2},{4,5},{5,4},{6,7},{7,6},{8,9},{9,8},{10,11... | collective-permute-start | bytes 12296 | tf_op jit(solution)/shard_map/ppermute | solution.py:384
  588.7 13.4 %collective-permute-done.43 = f32[8,128]{1,0:T(8,128)S(1)} collective-permute-done((f32[8,128]{1,0:T(8,128)S(1)}, f32[8,128]{1,0:T(8,128)S(1)}, u32[]{:S(2)}, u32[]{:S(2)}) %collective-permute-start.43) | collective-permute-done | bytes 4128 | tf_op jit(solution)/shard_map/ppermute | solution.py:384
  608.8 12.7 %finish.1 = f32[896,4608]{1,0:T(8,128)} custom-call(s32[4]{0:T(128)} %pad_add_fusion.flags, f32[1]{0:T(128)} %bitcast.12.factor, bf16[896,2304]{1,0:T(8,128)(2,1)} %get-tuple-element.148.near, bf16[896,1024]{1,0:T(8,128)(2,1)} %get-tuple-element.149.refs_0_, bf16[896,768]{1,0:T(8,128)(2,1)} %get-tuple-element.150.refs_1_, ...), custom_call_target="tpu_custom_call" | custom-call | tf_op jit(solution)/shard_map/finish/pallas_call | solution.py:343
  (221 shorter events, 158.5 us)
Async XLA Ops:
  10.6 95.8 %collective-permute-start = (bf16[896,2304]{1,0:T(8,128)(2,1)}, bf16[896,2304]{1,0:T(8,128)(2,1)}, u32[]{:S(2)}, u32[]{:S(2)}) collective-permute-start(bf16[896,2304]{1,0:T(8,128)(2,1)} %get-tuple-element.88.refs_3_), channel_id=1, source_target_pairs={{1,2},{2,1},{5,6},{6,5},{9,10},{10,9},{13,14},{14,13},{17,18},{18,... | collective-permute-start | bytes 12386312 | tf_op jit(solution)/shard_map/ppermute | solution.py:378
  13.2 97.0 %collective-permute-start.1 = (bf16[896,2304]{1,0:T(8,128)(2,1)}, bf16[896,2304]{1,0:T(8,128)(2,1)}, u32[]{:S(2)}, u32[]{:S(2)}) collective-permute-start(bf16[896,2304]{1,0:T(8,128)(2,1)} %get-tuple-element.81.refs_0_.refs_1_.refs_2_.refs_7_), channel_id=1, source_target_pairs={{0,1},{1,0},{2,3},{3,2},{4,5},{5,4},{6,7},{7,6},{8,9},{9,8},{10,11... | collective-permute-start | bytes 12386312 | tf_op jit(solution)/shard_map/ppermute | solution.py:384
  25.5 80.9 %collective-permute-start.4 = (f32[8,128]{1,0:T(8,128)S(1)}, f32[8,128]{1,0:T(8,128)S(1)}, u32[]{:S(2)}, u32[]{:S(2)}) collective-permute-start(f32[8,128]{1,0:T(8,128)S(1)} %fusion.4), channel_id=1, source_target_pairs={{0,1},{1,0},{2,3},{3,2},{4,5},{5,4},{6,7},{7,6},{8,9},{9,8},{10,11... | collective-permute-start | bytes 12296 | tf_op jit(solution)/shard_map/ppermute | solution.py:384
  110.2 47.6 %collective-permute-start.5 = (bf16[896,1152]{1,0:T(8,128)(2,1)}, bf16[896,1152]{1,0:T(8,128)(2,1)S(1)}, u32[]{:S(2)}, u32[]{:S(2)}) collective-permute-start(bf16[896,1152]{1,0:T(8,128)(2,1)} %slice_select_fusion), channel_id=1, source_target_pairs={{0,2},{3,1},{1,0},{2,3},{4,6},{7,5},{5,4},{6,7},{8,10},{11,9},{9,8... | collective-permute-start | bytes 6193160 | tf_op jit(solution)/shard_map/ppermute | solution.py:390
  112.8 44.4 %collective-permute-start.6 = (f32[8,128]{1,0:T(8,128)S(1)}, f32[8,128]{1,0:T(8,128)S(1)}, u32[]{:S(2)}, u32[]{:S(2)}) collective-permute-start(f32[8,128]{1,0:T(8,128)S(1)} %add.128), channel_id=1, source_target_pairs={{0,2},{2,0},{1,3},{3,1},{4,6},{6,4},{5,7},{7,5},{8,10},{10,8},{9,1... | collective-permute-start | bytes 12296 | tf_op jit(solution)/shard_map/ppermute | solution.py:381
  159.1 47.6 %collective-permute-start.7 = (bf16[896,1152]{1,0:T(8,128)(2,1)}, bf16[896,1152]{1,0:T(8,128)(2,1)S(1)}, u32[]{:S(2)}, u32[]{:S(2)}) collective-permute-start(bf16[896,1152]{1,0:T(8,128)(2,1)} %slice_select_fusion.1), channel_id=1, source_target_pairs={{0,2},{3,1},{1,0},{2,3},{4,6},{7,5},{5,4},{6,7},{8,10},{11,9},{9,8... | collective-permute-start | bytes 6193160 | tf_op jit(solution)/shard_map/ppermute | solution.py:390
  209.3 29.5 %collective-permute-start.11 = (bf16[3,224,896]{2,1,0:T(8,128)(2,1)S(1)}, bf16[3,224,896]{2,1,0:T(8,128)(2,1)}, u32[]{:S(2)}, u32[]{:S(2)}) collective-permute-start(bf16[3,224,896]{2,1,0:T(8,128)(2,1)S(1)} %add_convert_fusion.5), channel_id=1, source_target_pairs={{1,2},{2,1},{5,6},{6,5},{9,10},{10,9},{13,14},{14,13},{17,18},{18,... | collective-permute-start | bytes 3612680 | tf_op jit(solution)/shard_map/ppermute | solution.py:378
  244.2 44.2 %collective-permute-start.13 = (bf16[3,224,896]{2,1,0:T(8,128)(2,1)}, bf16[3,224,896]{2,1,0:T(8,128)(2,1)}, u32[]{:S(2)}, u32[]{:S(2)}) collective-permute-start(bf16[3,224,896]{2,1,0:T(8,128)(2,1)} %add_convert_fusion.4), channel_id=1, source_target_pairs={{1,2},{2,1},{5,6},{6,5},{9,10},{10,9},{13,14},{14,13},{17,18},{18,... | collective-permute-start | bytes 3612680 | tf_op jit(solution)/shard_map/ppermute | solution.py:378
  252.6 34.4 %collective-permute-start.15 = (bf16[2,224,896]{2,1,0:T(8,128)(2,1)}, bf16[2,224,896]{2,1,0:T(8,128)(2,1)}, u32[]{:S(2)}, u32[]{:S(2)}) collective-permute-start(bf16[2,224,896]{2,1,0:T(8,128)(2,1)} %constant_dynamic-slice_fusion.1), channel_id=1, source_target_pairs={{0,8},{4,12},{8,0},{12,4},{1,9},{5,13},{9,1},{13,5},{2,10},{6,14},... | collective-permute-start | bytes 2408456 | tf_op jit(solution)/shard_map/ppermute | solution.py:375
  296.2 44.9 %collective-permute-start.24 = (bf16[896,1024]{1,0:T(8,128)(2,1)S(1)}, bf16[896,1024]{1,0:T(8,128)(2,1)S(1)}, u32[]{:S(2)}, u32[]{:S(2)}) collective-permute-start(bf16[896,1024]{1,0:T(8,128)(2,1)S(1)} %slice.139), channel_id=1, source_target_pairs={{0,1},{1,0},{2,3},{3,2},{4,5},{5,4},{6,7},{7,6},{8,9},{9,8},{10,11... | collective-permute-start | bytes 5505032 | tf_op jit(solution)/shard_map/ppermute | solution.py:384
  301.2 29.5 %collective-permute-start.25 = (bf16[2,224,896]{2,1,0:T(8,128)(2,1)S(1)}, bf16[2,224,896]{2,1,0:T(8,128)(2,1)S(1)}, u32[]{:S(2)}, u32[]{:S(2)}) collective-permute-start(bf16[2,224,896]{2,1,0:T(8,128)(2,1)S(1)} %add_convert_fusion.7), channel_id=1, source_target_pairs={{1,2},{2,1},{5,6},{6,5},{9,10},{10,9},{13,14},{14,13},{17,18},{18,... | collective-permute-start | bytes 2408456 | tf_op jit(solution)/shard_map/ppermute | solution.py:378
  321.7 35.9 %collective-permute-start.23 = (bf16[4,224,896]{2,1,0:T(8,128)(2,1)S(1)}, bf16[4,224,896]{2,1,0:T(8,128)(2,1)S(1)}, u32[]{:S(2)}, u32[]{:S(2)}) collective-permute-start(bf16[4,224,896]{2,1,0:T(8,128)(2,1)S(1)} %fusion.refs_4_), channel_id=1, source_target_pairs={{0,8},{4,12},{8,0},{12,4},{1,9},{5,13},{9,1},{13,5},{2,10},{6,14},... | collective-permute-start | bytes 4816904 | tf_op jit(solution)/shard_map/ppermute | solution.py:375
  323.3 34.3 %collective-permute-start.22 = (bf16[4,224,896]{2,1,0:T(8,128)(2,1)S(1)}, bf16[4,224,896]{2,1,0:T(8,128)(2,1)}, u32[]{:S(2)}, u32[]{:S(2)}) collective-permute-start(bf16[4,224,896]{2,1,0:T(8,128)(2,1)S(1)} %fusion.refs_4_), channel_id=1, source_target_pairs={{0,4},{4,0},{8,12},{12,8},{1,5},{5,1},{9,13},{13,9},{2,6},{6,2},{1... | collective-permute-start | bytes 4816904 | tf_op jit(solution)/shard_map/ppermute | solution.py:372
  330.8 95.5 %collective-permute-start.31 = (bf16[2,896,1024]{2,1,0:T(8,128)(2,1)}, bf16[2,896,1024]{2,1,0:T(8,128)(2,1)}, u32[]{:S(2)}, u32[]{:S(2)}) collective-permute-start(bf16[2,896,1024]{2,1,0:T(8,128)(2,1)} %pad_maximum_fusion), channel_id=1, source_target_pairs={{1,2},{2,1},{5,6},{6,5},{9,10},{10,9},{13,14},{14,13},{17,18},{18,... | collective-permute-start | bytes 11010056 | tf_op jit(solution)/shard_map/ppermute | solution.py:378
  333.5 30.3 %collective-permute-start.21 = (bf16[3,224,896]{2,1,0:T(8,128)(2,1)S(1)}, bf16[3,224,896]{2,1,0:T(8,128)(2,1)S(1)}, u32[]{:S(2)}, u32[]{:S(2)}) collective-permute-start(bf16[3,224,896]{2,1,0:T(8,128)(2,1)S(1)} %copy-done.37), channel_id=1, source_target_pairs={{0,4},{4,0},{8,12},{12,8},{1,5},{5,1},{9,13},{13,9},{2,6},{6,2},{1... | collective-permute-start | bytes 3612680 | tf_op jit(solution)/shard_map/ppermute | solution.py:372
  361.0 65.2 %collective-permute-start.30 = (bf16[896,1280]{1,0:T(8,128)(2,1)S(1)}, bf16[896,1280]{1,0:T(8,128)(2,1)S(1)}, u32[]{:S(2)}, u32[]{:S(2)}) collective-permute-start(bf16[896,1280]{1,0:T(8,128)(2,1)S(1)} %slice.140), channel_id=1, source_target_pairs={{0,1},{1,0},{2,3},{3,2},{4,5},{5,4},{6,7},{7,6},{8,9},{9,8},{10,11... | collective-permute-start | bytes 6881288 | tf_op jit(solution)/shard_map/ppermute | solution.py:384
  440.4 40.2 %collective-permute-start.34 = (bf16[224,3584]{1,0:T(8,128)(2,1)}, bf16[224,3584]{1,0:T(8,128)(2,1)}, u32[]{:S(2)}, u32[]{:S(2)}) collective-permute-start(bf16[224,3584]{1,0:T(8,128)(2,1)} %dynamic-slice_select_fusion), channel_id=1, source_target_pairs={{1,0},{2,3},{5,4},{6,7},{9,8},{10,11},{13,12},{14,15},{17,16},{18,... | collective-permute-start | bytes 4816904 | tf_op jit(solution)/shard_map/ppermute | solution.py:387
  441.7 42.3 %collective-permute-start.35 = (bf16[2,896,768]{2,1,0:T(8,128)(2,1)}, bf16[2,896,768]{2,1,0:T(8,128)(2,1)S(1)}, u32[]{:S(2)}, u32[]{:S(2)}) collective-permute-start(bf16[2,896,768]{2,1,0:T(8,128)(2,1)} %pad_maximum_fusion.1), channel_id=1, source_target_pairs={{1,2},{2,1},{5,6},{6,5},{9,10},{10,9},{13,14},{14,13},{17,18},{18,... | collective-permute-start | bytes 8257544 | tf_op jit(solution)/shard_map/ppermute | solution.py:378
  465.1 54.4 %collective-permute-start.33 = (bf16[896,1024]{1,0:T(8,128)(2,1)}, bf16[896,1024]{1,0:T(8,128)(2,1)}, u32[]{:S(2)}, u32[]{:S(2)}) collective-permute-start(bf16[896,1024]{1,0:T(8,128)(2,1)} %get-tuple-element.128), channel_id=1, source_target_pairs={{1,0},{2,3},{5,4},{6,7},{9,8},{10,11},{13,12},{14,15},{17,16},{18,... | collective-permute-start | bytes 5505032 | tf_op jit(solution)/shard_map/ppermute | solution.py:387
  480.6 38.8 %collective-permute-start.36 = (bf16[224,3584]{1,0:T(8,128)(2,1)}, bf16[224,3584]{1,0:T(8,128)(2,1)}, u32[]{:S(2)}, u32[]{:S(2)}) collective-permute-start(bf16[224,3584]{1,0:T(8,128)(2,1)} %collective-permute-done.34.refs_0_), channel_id=1, source_target_pairs={{0,8},{4,12},{8,0},{12,4},{1,9},{5,13},{9,1},{13,5},{2,10},{6,14},... | collective-permute-start | bytes 4816904 | tf_op jit(solution)/shard_map/ppermute | solution.py:375
  482.1 68.4 %collective-permute-start.40 = (bf16[2,896,512]{2,1,0:T(8,128)(2,1)}, bf16[2,896,512]{2,1,0:T(8,128)(2,1)}, u32[]{:S(2)}, u32[]{:S(2)}) collective-permute-start(bf16[2,896,512]{2,1,0:T(8,128)(2,1)} %pad_maximum_fusion.2), channel_id=1, source_target_pairs={{1,2},{2,1},{5,6},{6,5},{9,10},{10,9},{13,14},{14,13},{17,18},{18,... | collective-permute-start | bytes 5505032 | tf_op jit(solution)/shard_map/ppermute | solution.py:378
  484.0 36.8 %collective-permute-start.37 = (bf16[224,3584]{1,0:T(8,128)(2,1)}, bf16[224,3584]{1,0:T(8,128)(2,1)}, u32[]{:S(2)}, u32[]{:S(2)}) collective-permute-start(bf16[224,3584]{1,0:T(8,128)(2,1)} %collective-permute-done.34.refs_0_), channel_id=1, source_target_pairs={{0,4},{4,0},{8,12},{12,8},{1,5},{5,1},{9,13},{13,9},{2,6},{6,2},{1... | collective-permute-start | bytes 4816904 | tf_op jit(solution)/shard_map/ppermute | solution.py:372
  519.5 49.6 %collective-permute-start.39 = (bf16[896,768]{1,0:T(8,128)(2,1)}, bf16[896,768]{1,0:T(8,128)(2,1)S(1)}, u32[]{:S(2)}, u32[]{:S(2)}) collective-permute-start(bf16[896,768]{1,0:T(8,128)(2,1)} %get-tuple-element.142), channel_id=1, source_target_pairs={{1,0},{2,3},{5,4},{6,7},{9,8},{10,11},{13,12},{14,15},{17,16},{18,... | collective-permute-start | bytes 4128776 | tf_op jit(solution)/shard_map/ppermute | solution.py:387
  565.8 42.0 %collective-permute-start.45 = (bf16[896,512]{1,0:T(8,128)(2,1)}, bf16[896,512]{1,0:T(8,128)(2,1)S(1)}, u32[]{:S(2)}, u32[]{:S(2)}) collective-permute-start(bf16[896,512]{1,0:T(8,128)(2,1)} %get-tuple-element.154), channel_id=1, source_target_pairs={{1,0},{2,3},{5,4},{6,7},{9,8},{10,11},{13,12},{14,15},{17,16},{18,... | collective-permute-start | bytes 2752520 | tf_op jit(solution)/shard_map/ppermute | solution.py:387
  (66 other events, 744.1 us)

commit v9 on v8

--- a/solution.py
+++ b/solution.py
@@ -468,6 +468,7 @@
     known(pairs_1, first, other_first)
     known(pairs_2, second, other_second)
     groups = [gather(GATHERED[0])]
+    near_later, beside_later, other_third = barrier((near, beside, other_third))
     groups[0][1], groups[0][2], other_third = barrier((groups[0][1], groups[0][2], other_third))
     known(pairs_3, third, other_third)
     groups.append(gather(GATHERED[1]))
@@ -476,7 +477,9 @@
     tile_bounds = [0, max(1, tiles * 4 // 9), max(2, tiles * 7 // 9), tiles]
     cuts = [t * TILE for t in tile_bounds]
     inward_first = with_end(inward[:, : cuts[1]])
-    swaps = [jnp.stack([block[:, a:b] for block in (beside, near)]) for a, b in zip(cuts[:-1], cuts[1:])]
+    swaps = [
+        jnp.stack([block[:, a:b] for block in (beside_later, near_later)]) for a, b in zip(cuts[:-1], cuts[1:])
+    ]
     *swaps, other_fourth = barrier((*swaps, other_fourth))
     swaps[0] = between_hubs(swaps[0])
     groups[1][1], groups[1][2], inward_first, other_fourth = barrier(
@@ -510,19 +513,18 @@
         return squares
 
     hub_sq = far_product(0, scale)
-    hub_sq, row_share = barrier((hub_sq, row_share))
+    scale, hub_sq, row_share, swaps[1] = barrier((scale, hub_sq, row_share, swaps[1]))
     row_across = over_side(row_share)
-    scale, hub_sq, swaps[1] = barrier((scale, hub_sq, swaps[1]))
     swaps[2] = between_hubs(swaps[2])
     hub_sq += far_product(1, scale)
-    at_end[0], scale, hub_sq, row_across = barrier((at_end[0], scale, hub_sq, row_across))
+    at_end[0], scale, hub_sq, swaps[2], row_across = barrier((at_end[0], scale, hub_sq, swaps[2], row_across))
+    hub_sq += far_product(2, scale)
+    scale, hub_sq = barrier((scale, hub_sq))
     end_rows = [row_share, over_core(row_share), row_across, over_core(row_across)]
     blocks = [(passed, None, 0), (middle, None, 0), (near, None, 0), (beside, None, 0)]
     inward = [(inward_first, 0, tile_bounds[1]), (inward_second, tile_bounds[1], tiles)]
     (near_part,), near_sq = product(flags, (own, pair, *end_rows), scale, blocks, tiles, False, inward)
-    scale, near_sq = barrier((scale, near_sq))
-    hub_sq += far_product(2, scale)
-    at_end[1], hub_sq = barrier((at_end[1], hub_sq))
+    at_end[1], near_sq = barrier((at_end[1], near_sq))
     total_sq = col_total(near_sq + jnp.where(is_hub, hub_sq, 0.0))
     total_sq += with_end(total_sq)
     total_sq += skip_one(total_sq)

time: 629 us -> 607 us (0.965)
  waiting for transfers between devices: 259 us -> 246 us
  local copies, waits for them, and re-layouts: 26.3 us -> 17.3 us
    ppermute x5, waiting for transfers between devices: 101 us -> 87.9 us  [with_end(): return lax.ppermute(x, 'row', [(0, 1), (1, 0), (2, 3), (3, 2)])]
    ppermute x4, waiting for transfers between devices: 24.7 us -> 31.5 us  [to_end(): return lax.ppermute(x, 'row', [(1, 0), (2, 3)])]
  transfers between devices with their start and end apart: 46 -> 46, of which waited for: 22 -> 21; matrix products, arithmetic and copies ran while one was open for 8% -> 8% of each run, Pallas kernels for 32% -> 33%
where the time goes in v9:
time: 607 us; the launch traced here: 599 us
  waiting for transfers between devices  246 us (41%)
  Pallas kernels  220 us (36%)
  starting transfers between devices  68.2 us (11%)
  other arithmetic  43 us (7%)
  local copies, waits for them, and re-layouts  17.3 us (3%)
    ppermute x10, waiting for transfers between devices, over_side(): return lax.ppermute(x, 'col', [(k, k ^ 2) for k in range(4)])  103 us
    ppermute x5, waiting for transfers between devices, with_end(): return lax.ppermute(x, 'row', [(0, 1), (1, 0), (2, 3), (3, 2)])  87.9 us
    pallas_call x4, Pallas kernels, product(): pl.pallas_call(functools.partial(product_kernel, is_far, inward[0][2] if...  81.6 us
    pallas_call x5, Pallas kernels, gram_blocks(): pl.pallas_call(functools.partial(gram_kernel, pairs, where, pieces, int(t...  77.1 us
    pallas_call x1, Pallas kernels, poly_rows(): pl.pallas_call(poly_kernel, grid_spec=pltpu.PrefetchScalarGridSpec(num_sc...  37.5 us
    ppermute x4, waiting for transfers between devices, to_end(): return lax.ppermute(x, 'row', [(1, 0), (2, 3)])  31.5 us
    ppermute x5, starting transfers between devices, with_end(): return lax.ppermute(x, 'row', [(0, 1), (1, 0), (2, 3), (3, 2)])  28.1 us
    convert_element_type x8, other arithmetic, added(): return (x.astype(jnp.float32) + y.astype(jnp.float32)).astype(jnp.bfloat16)  13.9 us
  transfers between devices with their start and end apart: 46, of which 21 were waited for; matrix products, arithmetic and copies ran while one was open for 8% of the time, Pallas kernels for 33%

profile of v9, /device:TPU:0, one launch (start us, length us, event | category | flops | bytes accessed | tf_op | source)
XLA Modules:
  0.0 599.4 jit_solution(11623675365470830117)
XLA Ops:
  0.0 10.6 %take_halves.1 = (bf16[896,2304]{1,0:T(8,128)(2,1)}, bf16[896,2304]{1,0:T(8,128)(2,1)}, f32[1,2304]{1,0:T(1,128)}) custom-call(s32[1]{0:T(128)} %bitcast.index, f32[896,4608]{1,0:T(8,128)} %far_ref.1, f32[896,4608]{1,0:T(8,128)} %far_ref.1), custom_call_target="tpu_custom_call" | custom-call | flops 8257536 | bytes 24772608 | tf_op jit(solution)/shard_map/take_halves/pallas_call | solution.py:45
  25.7 80.8 %collective-permute-done.4 = f32[8,128]{1,0:T(8,128)S(1)} collective-permute-done((f32[8,128]{1,0:T(8,128)S(1)}, f32[8,128]{1,0:T(8,128)S(1)}, u32[]{:S(2)}, u32[]{:S(2)}) %collective-permute-start.4) | collective-permute-done | bytes 4128 | tf_op jit(solution)/shard_map/ppermute | solution.py:384
  114.6 19.0 %gram_blocks.5 = (bf16[3,448,896]{2,1,0:T(8,128)(2,1)}, bf16[3,448,896]{2,1,0:T(8,128)(2,1)}) custom-call(s32[4]{0:T(128)} %pad_add_fusion.flags, bf16[896,2304]{1,0:T(8,128)(2,1)} %get-tuple-element.122.refs_0_.refs_1_.refs_2_.refs_7_, bf16[896,2304]{1,0:T(8,128)(2,1)} %collective-permute-done.1.refs_1_.refs_2_.refs_3_.refs_8_), custom_call_target="tpu_custom_call" | custom-call | tf_op jit(solution)/shard_map/gram_blocks/pallas_call | solution.py:124
  136.8 20.5 %gram_blocks.6 = (bf16[3,448,896]{2,1,0:T(8,128)(2,1)}, bf16[3,448,896]{2,1,0:T(8,128)(2,1)}) custom-call(s32[4]{0:T(128)} %pad_add_fusion.flags, bf16[896,2304]{1,0:T(8,128)(2,1)} %collective-permute-done.refs_0_.refs_1_.refs_6_, bf16[896,2304]{1,0:T(8,128)(2,1)} %get-tuple-element.122.refs_0_.refs_1_.refs_2_.refs_7_, ...), custom_call_target="tpu_custom_call" | custom-call | tf_op jit(solution)/shard_map/gram_blocks/pallas_call | solution.py:124
  168.8 16.3 %gram_blocks.7.refs_3_.refs_2_ = f32[4,896,896]{2,1,0:T(8,128)} custom-call(s32[4]{0:T(128)} %pad_add_fusion.flags, bf16[896,1152]{1,0:T(8,128)(2,1)} %copy-done.9, bf16[896,2304]{1,0:T(8,128)(2,1)} %collective-permute-done.refs_0_.refs_1_.refs_6_, bf16[896,2304]{1,0:T(8,128)(2,1)} %get-tuple-element.122.refs_0_.refs_1_.refs_2_.refs_7_, ...), custom_call_target="tpu_custom_call" | custom-call | tf_op jit(solution)/shard_map/gram_blocks/pallas_call | solution.py:124
  188.2 7.8 %collective-permute-done.9 = bf16[3,224,896]{2,1,0:T(8,128)(2,1)} collective-permute-done((bf16[3,224,896]{2,1,0:T(8,128)(2,1)S(1)}, bf16[3,224,896]{2,1,0:T(8,128)(2,1)}, u32[]{:S(2)}, u32[]{:S(2)}) %collective-permute-start.9) | collective-permute-done | bytes 1204256 | tf_op jit(solution)/shard_map/ppermute | solution.py:375
  197.5 9.2 %collective-permute-done.7.refs_0_ = bf16[896,1152]{1,0:T(8,128)(2,1)S(1)} collective-permute-done((bf16[896,1152]{1,0:T(8,128)(2,1)}, bf16[896,1152]{1,0:T(8,128)(2,1)S(1)}, u32[]{:S(2)}, u32[]{:S(2)}) %collective-permute-start.7) | collective-permute-done | bytes 2064416 | tf_op jit(solution)/shard_map/ppermute | solution.py:390
  210.1 10.4 %gram_blocks.9 = (bf16[2,448,896]{2,1,0:T(8,128)(2,1)}, bf16[2,448,896]{2,1,0:T(8,128)(2,1)}) custom-call(s32[4]{0:T(128)} %pad_add_fusion.flags, bf16[896,1152]{1,0:T(8,128)(2,1)} %copy-done.5, bf16[896,2304]{1,0:T(8,128)(2,1)} %collective-permute-done.refs_0_.refs_1_.refs_6_, f32[4,896,896]{2,1,0:T(8,128)} %gram_blocks.7.refs_3_.refs_2_), custom_call_target="tpu_custom_call" | custom-call | tf_op jit(solution)/shard_map/gram_blocks/pallas_call | solution.py:124
  220.6 10.9 %gram_blocks.8 = (bf16[2,448,896]{2,1,0:T(8,128)(2,1)}, bf16[2,448,896]{2,1,0:T(8,128)(2,1)}) custom-call(s32[4]{0:T(128)} %pad_add_fusion.flags, bf16[896,1152]{1,0:T(8,128)(2,1)} %copy-done.5, bf16[896,2304]{1,0:T(8,128)(2,1)} %get-tuple-element.122.refs_0_.refs_1_.refs_2_.refs_7_, ...), custom_call_target="tpu_custom_call" | custom-call | tf_op jit(solution)/shard_map/gram_blocks/pallas_call | solution.py:124
  248.3 15.4 %collective-permute-done.19 = bf16[2,224,896]{2,1,0:T(8,128)(2,1)S(1)} collective-permute-done((bf16[2,224,896]{2,1,0:T(8,128)(2,1)S(1)}, bf16[2,224,896]{2,1,0:T(8,128)(2,1)S(1)}, u32[]{:S(2)}, u32[]{:S(2)}) %collective-permute-start.19) | collective-permute-done | bytes 802848 | tf_op jit(solution)/shard_map/ppermute | solution.py:375
  265.7 14.8 %collective-permute-done.15 = bf16[2,224,896]{2,1,0:T(8,128)(2,1)S(1)} collective-permute-done((bf16[2,224,896]{2,1,0:T(8,128)(2,1)S(1)}, bf16[2,224,896]{2,1,0:T(8,128)(2,1)S(1)}, u32[]{:S(2)}, u32[]{:S(2)}) %collective-permute-start.15) | collective-permute-done | bytes 802848 | tf_op jit(solution)/shard_map/ppermute | solution.py:375
  294.3 16.5 %collective-permute-done.17.refs_2_ = bf16[3,224,896]{2,1,0:T(8,128)(2,1)S(1)} collective-permute-done((bf16[3,224,896]{2,1,0:T(8,128)(2,1)S(1)}, bf16[3,224,896]{2,1,0:T(8,128)(2,1)S(1)}, u32[]{:S(2)}, u32[]{:S(2)}) %collective-permute-start.17) | collective-permute-done | bytes 1204256 | tf_op jit(solution)/shard_map/ppermute | solution.py:375
  330.3 18.4 %collective-permute-done.23.refs_6_ = bf16[4,224,896]{2,1,0:T(8,128)(2,1)S(1)} collective-permute-done((bf16[4,224,896]{2,1,0:T(8,128)(2,1)S(1)}, bf16[4,224,896]{2,1,0:T(8,128)(2,1)S(1)}, u32[]{:S(2)}, u32[]{:S(2)}) %collective-permute-start.23) | collective-permute-done | bytes 1605664 | tf_op jit(solution)/shard_map/ppermute | solution.py:375
  356.4 19.8 %collective-permute-done.28.refs_10_ = bf16[3,224,896]{2,1,0:T(8,128)(2,1)S(1)} collective-permute-done((bf16[3,224,896]{2,1,0:T(8,128)(2,1)S(1)}, bf16[3,224,896]{2,1,0:T(8,128)(2,1)S(1)}, u32[]{:S(2)}, u32[]{:S(2)}) %collective-permute-start.28) | collective-permute-done | bytes 1204256 | tf_op jit(solution)/shard_map/ppermute | solution.py:375
  379.3 37.5 %poly_rows.1.own = bf16[896,3584]{1,0:T(8,128)(2,1)} custom-call(s32[4]{0:T(128)} %pad_add_fusion.flags, bf16[3,224,896]{2,1,0:T(8,128)(2,1)} %copy-done.14, bf16[3,224,896]{2,1,0:T(8,128)(2,1)} %collective-permute-done.16.refs_1_, bf16[3,224,896]{2,1,0:T(8,128)(2,1)} %copy-done.24, bf16[3,224,896]{2,1,0:T(8,128)(2,1)} %copy-done.26, ...), custom_call_target="tpu_custom_call" | custom-call | tf_op jit(solution)/shard_map/poly_rows/pallas_call | solution.py:203
  419.2 8.4 %collective-permute-done.32.pair = bf16[896,3584]{1,0:T(8,128)(2,1)} collective-permute-done((bf16[896,3584]{1,0:T(8,128)(2,1)}, bf16[896,3584]{1,0:T(8,128)(2,1)}, u32[]{:S(2)}, u32[]{:S(2)}) %collective-permute-start.32) | collective-permute-done | bytes 6422560 | tf_op jit(solution)/shard_map/ppermute | solution.py:372
  433.1 22.6 %product_far.3 = (bf16[896,1024]{1,0:T(8,128)(2,1)}, bf16[896,1024]{1,0:T(8,128)(2,1)}, f32[1,256]{1,0:T(1,128)}) custom-call(s32[4]{0:T(128)} %pad_add_fusion.flags, bf16[896,3584]{1,0:T(8,128)(2,1)} %poly_rows.1.own, bf16[896,3584]{1,0:T(8,128)(2,1)} %collective-permute-done.32.pair, f32[1]{0:T(128)} %bitcast.11.refs_0_.refs_4_, ...), custom_call_target="tpu_custom_call" | custom-call | tf_op jit(solution)/shard_map/product_far/pallas_call | solution.py:298
  458.6 14.9 %collective-permute-done.33.refs_0_ = bf16[224,3584]{1,0:T(8,128)(2,1)} collective-permute-done((bf16[224,3584]{1,0:T(8,128)(2,1)}, bf16[224,3584]{1,0:T(8,128)(2,1)}, u32[]{:S(2)}, u32[]{:S(2)}) %collective-permute-start.33) | collective-permute-done | bytes 1605664 | tf_op jit(solution)/shard_map/ppermute | solution.py:387
  474.1 18.9 %product_far.4 = (bf16[896,768]{1,0:T(8,128)(2,1)}, bf16[896,768]{1,0:T(8,128)(2,1)}, f32[1,256]{1,0:T(1,128)}) custom-call(s32[4]{0:T(128)} %pad_add_fusion.flags, bf16[896,3584]{1,0:T(8,128)(2,1)} %poly_rows.1.own, bf16[896,3584]{1,0:T(8,128)(2,1)} %collective-permute-done.32.pair, f32[1]{0:T(128)} %bitcast.11.refs_0_.refs_4_, ...), custom_call_target="tpu_custom_call" | custom-call | tf_op jit(solution)/shard_map/product_far/pallas_call | solution.py:298
  495.8 16.6 %collective-permute-done.37.refs_3_ = bf16[896,1024]{1,0:T(8,128)(2,1)} collective-permute-done((bf16[896,1024]{1,0:T(8,128)(2,1)}, bf16[896,1024]{1,0:T(8,128)(2,1)}, u32[]{:S(2)}, u32[]{:S(2)}) %collective-permute-start.37) | collective-permute-done | bytes 1835040 | tf_op jit(solution)/shard_map/ppermute | solution.py:387
  513.7 15.3 %product_far.5 = (bf16[896,512]{1,0:T(8,128)(2,1)}, bf16[896,512]{1,0:T(8,128)(2,1)}, f32[1,256]{1,0:T(1,128)}) custom-call(s32[4]{0:T(128)} %pad_add_fusion.flags, bf16[896,3584]{1,0:T(8,128)(2,1)} %poly_rows.1.own, bf16[896,3584]{1,0:T(8,128)(2,1)} %collective-permute-done.32.pair, f32[1]{0:T(128)} %bitcast.11.refs_0_.refs_4_, ...), custom_call_target="tpu_custom_call" | custom-call | tf_op jit(solution)/shard_map/product_far/pallas_call | solution.py:298
  532.1 24.8 %product_near.1 = (bf16[896,2304]{1,0:T(8,128)(2,1)}, f32[1,256]{1,0:T(1,128)}) custom-call(s32[4]{0:T(128)} %pad_add_fusion.flags, bf16[896,3584]{1,0:T(8,128)(2,1)} %poly_rows.1.own, bf16[896,3584]{1,0:T(8,128)(2,1)} %collective-permute-done.32.pair, bf16[224,3584]{1,0:T(8,128)(2,1)} %collective-permute-done.33.refs_0_, ...), custom_call_target="tpu_custom_call" | custom-call | tf_op jit(solution)/shard_map/product_near/pallas_call | solution.py:298
  563.9 14.1 %collective-permute-start.43 = (f32[8,128]{1,0:T(8,128)S(1)}, f32[8,128]{1,0:T(8,128)S(1)}, u32[]{:S(2)}, u32[]{:S(2)}) collective-permute-start(f32[8,128]{1,0:T(8,128)S(1)} %fusion.3), channel_id=1, source_target_pairs={{0,1},{1,0},{2,3},{3,2},{4,5},{5,4},{6,7},{7,6},{8,9},{9,8},{10,11... | collective-permute-start | bytes 12296 | tf_op jit(solution)/shard_map/ppermute | solution.py:384
  586.3 12.7 %finish.1 = f32[896,4608]{1,0:T(8,128)} custom-call(s32[4]{0:T(128)} %pad_add_fusion.flags, f32[1]{0:T(128)} %bitcast.12.factor, bf16[896,2304]{1,0:T(8,128)(2,1)} %get-tuple-element.154.near, bf16[896,1024]{1,0:T(8,128)(2,1)} %get-tuple-element.155.refs_0_, bf16[896,768]{1,0:T(8,128)(2,1)} %get-tuple-element.156.refs_1_, ...), custom_call_target="tpu_custom_call" | custom-call | tf_op jit(solution)/shard_map/finish/pallas_call | solution.py:343
  (194 shorter events, 138.2 us)
Async XLA Ops:
  10.6 95.8 %collective-permute-start = (bf16[896,2304]{1,0:T(8,128)(2,1)}, bf16[896,2304]{1,0:T(8,128)(2,1)}, u32[]{:S(2)}, u32[]{:S(2)}) collective-permute-start(bf16[896,2304]{1,0:T(8,128)(2,1)} %get-tuple-element.91.refs_3_), channel_id=1, source_target_pairs={{1,2},{2,1},{5,6},{6,5},{9,10},{10,9},{13,14},{14,13},{17,18},{18,... | collective-permute-start | bytes 12386312 | tf_op jit(solution)/shard_map/ppermute | solution.py:378
  13.3 97.0 %collective-permute-start.1 = (bf16[896,2304]{1,0:T(8,128)(2,1)}, bf16[896,2304]{1,0:T(8,128)(2,1)}, u32[]{:S(2)}, u32[]{:S(2)}) collective-permute-start(bf16[896,2304]{1,0:T(8,128)(2,1)} %get-tuple-element.122.refs_0_.refs_1_.refs_2_.refs_7_), channel_id=1, source_target_pairs={{0,1},{1,0},{2,3},{3,2},{4,5},{5,4},{6,7},{7,6},{8,9},{9,8},{10,11... | collective-permute-start | bytes 12386312 | tf_op jit(solution)/shard_map/ppermute | solution.py:384
  25.6 80.8 %collective-permute-start.4 = (f32[8,128]{1,0:T(8,128)S(1)}, f32[8,128]{1,0:T(8,128)S(1)}, u32[]{:S(2)}, u32[]{:S(2)}) collective-permute-start(f32[8,128]{1,0:T(8,128)S(1)} %fusion.4), channel_id=1, source_target_pairs={{0,1},{1,0},{2,3},{3,2},{4,5},{5,4},{6,7},{7,6},{8,9},{9,8},{10,11... | collective-permute-start | bytes 12296 | tf_op jit(solution)/shard_map/ppermute | solution.py:384
  110.2 47.6 %collective-permute-start.5 = (bf16[896,1152]{1,0:T(8,128)(2,1)}, bf16[896,1152]{1,0:T(8,128)(2,1)S(1)}, u32[]{:S(2)}, u32[]{:S(2)}) collective-permute-start(bf16[896,1152]{1,0:T(8,128)(2,1)} %slice_select_fusion), channel_id=1, source_target_pairs={{0,2},{3,1},{1,0},{2,3},{4,6},{7,5},{5,4},{6,7},{8,10},{11,9},{9,8... | collective-permute-start | bytes 6193160 | tf_op jit(solution)/shard_map/ppermute | solution.py:390
  112.9 44.4 %collective-permute-start.6 = (f32[8,128]{1,0:T(8,128)S(1)}, f32[8,128]{1,0:T(8,128)S(1)}, u32[]{:S(2)}, u32[]{:S(2)}) collective-permute-start(f32[8,128]{1,0:T(8,128)S(1)} %add.128), channel_id=1, source_target_pairs={{0,2},{2,0},{1,3},{3,1},{4,6},{6,4},{5,7},{7,5},{8,10},{10,8},{9,1... | collective-permute-start | bytes 12296 | tf_op jit(solution)/shard_map/ppermute | solution.py:381
  159.2 47.6 %collective-permute-start.7 = (bf16[896,1152]{1,0:T(8,128)(2,1)}, bf16[896,1152]{1,0:T(8,128)(2,1)S(1)}, u32[]{:S(2)}, u32[]{:S(2)}) collective-permute-start(bf16[896,1152]{1,0:T(8,128)(2,1)} %slice_select_fusion.1), channel_id=1, source_target_pairs={{0,2},{3,1},{1,0},{2,3},{4,6},{7,5},{5,4},{6,7},{8,10},{11,9},{9,8... | collective-permute-start | bytes 6193160 | tf_op jit(solution)/shard_map/ppermute | solution.py:390
  167.2 28.7 %collective-permute-start.9 = (bf16[3,224,896]{2,1,0:T(8,128)(2,1)S(1)}, bf16[3,224,896]{2,1,0:T(8,128)(2,1)}, u32[]{:S(2)}, u32[]{:S(2)}) collective-permute-start(bf16[3,224,896]{2,1,0:T(8,128)(2,1)S(1)} %constant_dynamic-slice_fusion.3), channel_id=1, source_target_pairs={{0,8},{4,12},{8,0},{12,4},{1,9},{5,13},{9,1},{13,5},{2,10},{6,14},... | collective-permute-start | bytes 3612680 | tf_op jit(solution)/shard_map/ppermute | solution.py:375
  209.4 28.5 %collective-permute-start.11 = (bf16[3,224,896]{2,1,0:T(8,128)(2,1)S(1)}, bf16[3,224,896]{2,1,0:T(8,128)(2,1)S(1)}, u32[]{:S(2)}, u32[]{:S(2)}) collective-permute-start(bf16[3,224,896]{2,1,0:T(8,128)(2,1)S(1)} %add_convert_fusion.5), channel_id=1, source_target_pairs={{1,2},{2,1},{5,6},{6,5},{9,10},{10,9},{13,14},{14,13},{17,18},{18,... | collective-permute-start | bytes 3612680 | tf_op jit(solution)/shard_map/ppermute | solution.py:378
  239.6 41.1 %collective-permute-start.13 = (bf16[3,224,896]{2,1,0:T(8,128)(2,1)S(1)}, bf16[3,224,896]{2,1,0:T(8,128)(2,1)S(1)}, u32[]{:S(2)}, u32[]{:S(2)}) collective-permute-start(bf16[3,224,896]{2,1,0:T(8,128)(2,1)S(1)} %add_convert_fusion.4), channel_id=1, source_target_pairs={{1,2},{2,1},{5,6},{6,5},{9,10},{10,9},{13,14},{14,13},{17,18},{18,... | collective-permute-start | bytes 3612680 | tf_op jit(solution)/shard_map/ppermute | solution.py:378
  246.4 34.1 %collective-permute-start.15 = (bf16[2,224,896]{2,1,0:T(8,128)(2,1)S(1)}, bf16[2,224,896]{2,1,0:T(8,128)(2,1)S(1)}, u32[]{:S(2)}, u32[]{:S(2)}) collective-permute-start(bf16[2,224,896]{2,1,0:T(8,128)(2,1)S(1)} %constant_dynamic-slice_fusion.1), channel_id=1, source_target_pairs={{0,8},{4,12},{8,0},{12,4},{1,9},{5,13},{9,1},{13,5},{2,10},{6,14},... | collective-permute-start | bytes 2408456 | tf_op jit(solution)/shard_map/ppermute | solution.py:375
  284.9 45.4 %collective-permute-start.24 = (bf16[896,1024]{1,0:T(8,128)(2,1)S(1)}, bf16[896,1024]{1,0:T(8,128)(2,1)S(1)}, u32[]{:S(2)}, u32[]{:S(2)}) collective-permute-start(bf16[896,1024]{1,0:T(8,128)(2,1)S(1)} %slice.139), channel_id=1, source_target_pairs={{0,1},{1,0},{2,3},{3,2},{4,5},{5,4},{6,7},{7,6},{8,9},{9,8},{10,11... | collective-permute-start | bytes 5505032 | tf_op jit(solution)/shard_map/ppermute | solution.py:384
  312.8 35.9 %collective-permute-start.23 = (bf16[4,224,896]{2,1,0:T(8,128)(2,1)S(1)}, bf16[4,224,896]{2,1,0:T(8,128)(2,1)S(1)}, u32[]{:S(2)}, u32[]{:S(2)}) collective-permute-start(bf16[4,224,896]{2,1,0:T(8,128)(2,1)S(1)} %fusion.refs_4_), channel_id=1, source_target_pairs={{0,8},{4,12},{8,0},{12,4},{1,9},{5,13},{9,1},{13,5},{2,10},{6,14},... | collective-permute-start | bytes 4816904 | tf_op jit(solution)/shard_map/ppermute | solution.py:375
  314.4 34.4 %collective-permute-start.22 = (bf16[4,224,896]{2,1,0:T(8,128)(2,1)S(1)}, bf16[4,224,896]{2,1,0:T(8,128)(2,1)S(1)}, u32[]{:S(2)}, u32[]{:S(2)}) collective-permute-start(bf16[4,224,896]{2,1,0:T(8,128)(2,1)S(1)} %fusion.refs_4_), channel_id=1, source_target_pairs={{0,4},{4,0},{8,12},{12,8},{1,5},{5,1},{9,13},{13,9},{2,6},{6,2},{1... | collective-permute-start | bytes 4816904 | tf_op jit(solution)/shard_map/ppermute | solution.py:372
  321.7 95.1 %collective-permute-start.31 = (bf16[2,896,1024]{2,1,0:T(8,128)(2,1)}, bf16[2,896,1024]{2,1,0:T(8,128)(2,1)}, u32[]{:S(2)}, u32[]{:S(2)}) collective-permute-start(bf16[2,896,1024]{2,1,0:T(8,128)(2,1)} %pad_maximum_fusion), channel_id=1, source_target_pairs={{1,2},{2,1},{5,6},{6,5},{9,10},{10,9},{13,14},{14,13},{17,18},{18,... | collective-permute-start | bytes 11010056 | tf_op jit(solution)/shard_map/ppermute | solution.py:378
  324.3 31.6 %collective-permute-start.21 = (bf16[3,224,896]{2,1,0:T(8,128)(2,1)S(1)}, bf16[3,224,896]{2,1,0:T(8,128)(2,1)S(1)}, u32[]{:S(2)}, u32[]{:S(2)}) collective-permute-start(bf16[3,224,896]{2,1,0:T(8,128)(2,1)S(1)} %copy-done.25), channel_id=1, source_target_pairs={{0,4},{4,0},{8,12},{12,8},{1,5},{5,1},{9,13},{13,9},{2,6},{6,2},{1... | collective-permute-start | bytes 3612680 | tf_op jit(solution)/shard_map/ppermute | solution.py:372
  351.6 65.2 %collective-permute-start.30 = (bf16[896,1280]{1,0:T(8,128)(2,1)S(1)}, bf16[896,1280]{1,0:T(8,128)(2,1)S(1)}, u32[]{:S(2)}, u32[]{:S(2)}) collective-permute-start(bf16[896,1280]{1,0:T(8,128)(2,1)S(1)} %slice.140), channel_id=1, source_target_pairs={{0,1},{1,0},{2,3},{3,2},{4,5},{5,4},{6,7},{7,6},{8,9},{9,8},{10,11... | collective-permute-start | bytes 6881288 | tf_op jit(solution)/shard_map/ppermute | solution.py:384
  417.0 41.6 %collective-permute-start.34 = (bf16[2,896,768]{2,1,0:T(8,128)(2,1)}, bf16[2,896,768]{2,1,0:T(8,128)(2,1)}, u32[]{:S(2)}, u32[]{:S(2)}) collective-permute-start(bf16[2,896,768]{2,1,0:T(8,128)(2,1)} %pad_maximum_fusion.1), channel_id=1, source_target_pairs={{1,2},{2,1},{5,6},{6,5},{9,10},{10,9},{13,14},{14,13},{17,18},{18,... | collective-permute-start | bytes 8257544 | tf_op jit(solution)/shard_map/ppermute | solution.py:378
  431.0 42.5 %collective-permute-start.33 = (bf16[224,3584]{1,0:T(8,128)(2,1)}, bf16[224,3584]{1,0:T(8,128)(2,1)}, u32[]{:S(2)}, u32[]{:S(2)}) collective-permute-start(bf16[224,3584]{1,0:T(8,128)(2,1)} %dynamic-slice_select_fusion), channel_id=1, source_target_pairs={{1,0},{2,3},{5,4},{6,7},{9,8},{10,11},{13,12},{14,15},{17,16},{18,... | collective-permute-start | bytes 4816904 | tf_op jit(solution)/shard_map/ppermute | solution.py:387
  432.3 63.4 %collective-permute-start.38 = (bf16[2,896,512]{2,1,0:T(8,128)(2,1)}, bf16[2,896,512]{2,1,0:T(8,128)(2,1)S(1)}, u32[]{:S(2)}, u32[]{:S(2)}) collective-permute-start(bf16[2,896,512]{2,1,0:T(8,128)(2,1)} %pad_maximum_fusion.2), channel_id=1, source_target_pairs={{1,2},{2,1},{5,6},{6,5},{9,10},{10,9},{13,14},{14,13},{17,18},{18,... | collective-permute-start | bytes 5505032 | tf_op jit(solution)/shard_map/ppermute | solution.py:378
  455.7 56.7 %collective-permute-start.37 = (bf16[896,1024]{1,0:T(8,128)(2,1)}, bf16[896,1024]{1,0:T(8,128)(2,1)}, u32[]{:S(2)}, u32[]{:S(2)}) collective-permute-start(bf16[896,1024]{1,0:T(8,128)(2,1)} %get-tuple-element.141), channel_id=1, source_target_pairs={{1,0},{2,3},{5,4},{6,7},{9,8},{10,11},{13,12},{14,15},{17,16},{18,... | collective-permute-start | bytes 5505032 | tf_op jit(solution)/shard_map/ppermute | solution.py:387
  473.5 38.8 %collective-permute-start.39 = (bf16[224,3584]{1,0:T(8,128)(2,1)}, bf16[224,3584]{1,0:T(8,128)(2,1)S(1)}, u32[]{:S(2)}, u32[]{:S(2)}) collective-permute-start(bf16[224,3584]{1,0:T(8,128)(2,1)} %collective-permute-done.33.refs_0_), channel_id=1, source_target_pairs={{0,8},{4,12},{8,0},{12,4},{1,9},{5,13},{9,1},{13,5},{2,10},{6,14},... | collective-permute-start | bytes 4816904 | tf_op jit(solution)/shard_map/ppermute | solution.py:375
  474.0 58.1 %collective-permute-start.36 = (bf16[224,3584]{1,0:T(8,128)(2,1)}, bf16[224,3584]{1,0:T(8,128)(2,1)}, u32[]{:S(2)}, u32[]{:S(2)}) collective-permute-start(bf16[224,3584]{1,0:T(8,128)(2,1)} %collective-permute-done.33.refs_0_), channel_id=1, source_target_pairs={{0,4},{4,0},{8,12},{12,8},{1,5},{5,1},{9,13},{13,9},{2,6},{6,2},{1... | collective-permute-start | bytes 4816904 | tf_op jit(solution)/shard_map/ppermute | solution.py:372
  512.4 45.8 %collective-permute-start.35 = (bf16[896,768]{1,0:T(8,128)(2,1)}, bf16[896,768]{1,0:T(8,128)(2,1)}, u32[]{:S(2)}, u32[]{:S(2)}) collective-permute-start(bf16[896,768]{1,0:T(8,128)(2,1)} %get-tuple-element.139), channel_id=1, source_target_pairs={{1,0},{2,3},{5,4},{6,7},{9,8},{10,11},{13,12},{14,15},{17,16},{18,... | collective-permute-start | bytes 4128776 | tf_op jit(solution)/shard_map/ppermute | solution.py:387
  529.0 56.4 %collective-permute-start.45 = (bf16[896,512]{1,0:T(8,128)(2,1)}, bf16[896,512]{1,0:T(8,128)(2,1)S(1)}, u32[]{:S(2)}, u32[]{:S(2)}) collective-permute-start(bf16[896,512]{1,0:T(8,128)(2,1)} %get-tuple-element.160), channel_id=1, source_target_pairs={{1,0},{2,3},{5,4},{6,7},{9,8},{10,11},{13,12},{14,15},{17,16},{18,... | collective-permute-start | bytes 2752520 | tf_op jit(solution)/shard_map/ppermute | solution.py:387
  (54 other events, 658.5 us)

commit v10 on v9

--- a/solution.py
+++ b/solution.py
@@ -26,44 +26,41 @@
     return pair if sum(pair) == 3 and pair[0] != pair[1] else (3 - pair[0], 3 - pair[1])
 
 
-def take_kernel(index, near_ref, far_ref, near_out, far_out, sq_ref):
+def take_kernel(index, x_ref, out_ref, sq_ref):
     @pl.when(pl.program_id(0) == 0)
     def _():
         sq_ref[...] = jnp.zeros_like(sq_ref)
 
-    near, far = near_ref[...], far_ref[...]
-    near_out[...] = near.astype(jnp.bfloat16)
-    far_out[...] = far.astype(jnp.bfloat16)
-    sq_ref[...] += jnp.sum(near * near + far * far, axis=0, keepdims=True)
+    x = x_ref[...]
+    out_ref[...] = x.astype(jnp.bfloat16)
+    sq_ref[...] += jnp.sum(x * x, axis=0, keepdims=True)
 
 
 def take(momentum, index):
     rows, cols = momentum.shape
     width = cols // 2
     step = rows // 8
-    half = jax.ShapeDtypeStruct((rows, width), jnp.bfloat16)
     return pl.pallas_call(
         take_kernel,
         grid_spec=pltpu.PrefetchScalarGridSpec(
             num_scalar_prefetch=1,
             grid=(8,),
-            in_specs=[
-                pl.BlockSpec((step, width), lambda t, index: (t, index[0])),
-                pl.BlockSpec((step, width), lambda t, index: (t, 1 - index[0])),
-            ],
+            in_specs=[pl.BlockSpec((step, width), lambda t, index: (t, index[0]))],
             out_specs=[
-                pl.BlockSpec((step, width), lambda t, index: (t, 0)),
                 pl.BlockSpec((step, width), lambda t, index: (t, 0)),
                 pl.BlockSpec((1, width), lambda t, index: (0, 0)),
             ],
         ),
-        out_shape=[half, half, jax.ShapeDtypeStruct((1, width), jnp.float32)],
+        out_shape=[
+            jax.ShapeDtypeStruct((rows, width), jnp.bfloat16),
+            jax.ShapeDtypeStruct((1, width), jnp.float32),
+        ],
         compiler_params=pltpu.CompilerParams(vmem_limit_bytes=VMEM_BYTES),
         cost_estimate=pl.CostEstimate(
-            flops=4 * rows * width, bytes_accessed=12 * rows * width, transcendentals=0
+            flops=2 * rows * width, bytes_accessed=6 * rows * width, transcendentals=0
         ),
-        name="take_halves",
-    )(index, momentum, momentum)
+        name="take_half",
+    )(index, momentum)
 
 
 def gram_kernel(pairs, where, pieces, has_total, split, flags, *refs):
@@ -394,10 +391,11 @@
         x = x + over_core(x)
         return x + over_side(x)
 
-    near, far, squares = take(momentum, near_index)
+    near, near_sq = take(momentum, near_index)
     beside = with_end(near)
+    far, far_sq = take(momentum, 1 - near_index)
     middle = between_hubs(far)
-    norm_part = col_total(jnp.sum(squares))
+    norm_part = col_total(jnp.sum(near_sq) + jnp.sum(far_sq))
     norm_part += with_end(norm_part)
 
     def added(x, y):

time: 607 us -> 612 us (level)
    pallas_call x1 -> x2, Pallas kernels: 10.6 us -> 15.6 us  [take(): pl.pallas_call(take_kernel, grid_spec=pltpu.PrefetchScalarGridSpec(num_sc...]
  transfers between devices with their start and end apart: 46 -> 46, of which waited for: 21 -> 21; matrix products, arithmetic and copies ran while one was open for 8% -> 8% of each run, Pallas kernels for 33% -> 34%
where the time goes in v10:
time: 612 us; the launch traced here: 605 us
  waiting for transfers between devices  247 us (40%)
  Pallas kernels  225 us (37%)
  starting transfers between devices  68.6 us (11%)
  other arithmetic  42 us (7%)
  local copies, waits for them, and re-layouts  16.6 us (3%)
  between operations  6.12 us (1%)
    ppermute x10, waiting for transfers between devices, over_side(): return lax.ppermute(x, 'col', [(k, k ^ 2) for k in range(4)])  102 us
    ppermute x5, waiting for transfers between devices, with_end(): return lax.ppermute(x, 'row', [(0, 1), (1, 0), (2, 3), (3, 2)])  88.4 us
    pallas_call x4, Pallas kernels, product(): pl.pallas_call(functools.partial(product_kernel, is_far, inward[0][2] if...  81.6 us
    pallas_call x5, Pallas kernels, gram_blocks(): pl.pallas_call(functools.partial(gram_kernel, pairs, where, pieces, int(t...  77.1 us
    pallas_call x1, Pallas kernels, poly_rows(): pl.pallas_call(poly_kernel, grid_spec=pltpu.PrefetchScalarGridSpec(num_sc...  37.5 us
    ppermute x4, waiting for transfers between devices, to_end(): return lax.ppermute(x, 'row', [(1, 0), (2, 3)])  32 us
    ppermute x5, starting transfers between devices, with_end(): return lax.ppermute(x, 'row', [(0, 1), (1, 0), (2, 3), (3, 2)])  28.1 us
    pallas_call x2, Pallas kernels, take(): pl.pallas_call(take_kernel, grid_spec=pltpu.PrefetchScalarGridSpec(num_sc...  15.6 us
  transfers between devices with their start and end apart: 46, of which 21 were waited for; matrix products, arithmetic and copies ran while one was open for 8% of the time, Pallas kernels for 34%

profile of v10, /device:TPU:0, one launch (start us, length us, event | category | flops | bytes accessed | tf_op | source)
XLA Modules:
  0.0 604.7 jit_solution(17565101037404911135)
XLA Ops:
  0.0 7.9 %take_half.2 = (bf16[896,2304]{1,0:T(8,128)(2,1)}, f32[1,2304]{1,0:T(1,128)}) custom-call(s32[1]{0:T(128)S(6)} %sub.14.index, f32[896,4608]{1,0:T(8,128)} %x_ref.3), custom_call_target="tpu_custom_call" | custom-call | flops 4128768 | bytes 12386304 | tf_op jit(solution)/shard_map/take_half/pallas_call | solution.py:43
  10.6 7.7 %take_half.3 = (bf16[896,2304]{1,0:T(8,128)(2,1)}, f32[1,2304]{1,0:T(1,128)}) custom-call(s32[1]{0:T(128)} %bitcast.index, f32[896,4608]{1,0:T(8,128)} %x_ref.3), custom_call_target="tpu_custom_call" | custom-call | flops 4128768 | bytes 12386304 | tf_op jit(solution)/shard_map/take_half/pallas_call | solution.py:43
  30.3 81.2 %collective-permute-done.4 = f32[8,128]{1,0:T(8,128)S(1)} collective-permute-done((f32[8,128]{1,0:T(8,128)S(1)}, f32[8,128]{1,0:T(8,128)S(1)}, u32[]{:S(2)}, u32[]{:S(2)}) %collective-permute-start.4) | collective-permute-done | bytes 4128 | tf_op jit(solution)/shard_map/ppermute | solution.py:381
  119.6 19.0 %gram_blocks.5 = (bf16[3,448,896]{2,1,0:T(8,128)(2,1)}, bf16[3,448,896]{2,1,0:T(8,128)(2,1)}) custom-call(s32[4]{0:T(128)} %pad_add_fusion.flags, bf16[896,2304]{1,0:T(8,128)(2,1)} %get-tuple-element.124.refs_0_.refs_1_.refs_2_.refs_7_, bf16[896,2304]{1,0:T(8,128)(2,1)} %collective-permute-done.1.refs_1_.refs_2_.refs_3_.refs_8_), custom_call_target="tpu_custom_call" | custom-call | tf_op jit(solution)/shard_map/gram_blocks/pallas_call | solution.py:121
  141.8 20.5 %gram_blocks.6 = (bf16[3,448,896]{2,1,0:T(8,128)(2,1)}, bf16[3,448,896]{2,1,0:T(8,128)(2,1)}) custom-call(s32[4]{0:T(128)} %pad_add_fusion.flags, bf16[896,2304]{1,0:T(8,128)(2,1)} %collective-permute-done.refs_0_.refs_1_.refs_6_, bf16[896,2304]{1,0:T(8,128)(2,1)} %get-tuple-element.124.refs_0_.refs_1_.refs_2_.refs_7_, ...), custom_call_target="tpu_custom_call" | custom-call | tf_op jit(solution)/shard_map/gram_blocks/pallas_call | solution.py:121
  173.8 16.3 %gram_blocks.7.refs_3_.refs_2_ = f32[4,896,896]{2,1,0:T(8,128)} custom-call(s32[4]{0:T(128)} %pad_add_fusion.flags, bf16[896,1152]{1,0:T(8,128)(2,1)} %copy-done.9, bf16[896,2304]{1,0:T(8,128)(2,1)} %collective-permute-done.refs_0_.refs_1_.refs_6_, bf16[896,2304]{1,0:T(8,128)(2,1)} %get-tuple-element.124.refs_0_.refs_1_.refs_2_.refs_7_, ...), custom_call_target="tpu_custom_call" | custom-call | tf_op jit(solution)/shard_map/gram_blocks/pallas_call | solution.py:121
  202.5 9.2 %collective-permute-done.7.refs_0_ = bf16[896,1152]{1,0:T(8,128)(2,1)S(1)} collective-permute-done((bf16[896,1152]{1,0:T(8,128)(2,1)}, bf16[896,1152]{1,0:T(8,128)(2,1)S(1)}, u32[]{:S(2)}, u32[]{:S(2)}) %collective-permute-start.7) | collective-permute-done | bytes 2064416 | tf_op jit(solution)/shard_map/ppermute | solution.py:387
  215.2 10.4 %gram_blocks.9 = (bf16[2,448,896]{2,1,0:T(8,128)(2,1)}, bf16[2,448,896]{2,1,0:T(8,128)(2,1)}) custom-call(s32[4]{0:T(128)} %pad_add_fusion.flags, bf16[896,1152]{1,0:T(8,128)(2,1)} %copy-done.5, bf16[896,2304]{1,0:T(8,128)(2,1)} %collective-permute-done.refs_0_.refs_1_.refs_6_, f32[4,896,896]{2,1,0:T(8,128)} %gram_blocks.7.refs_3_.refs_2_), custom_call_target="tpu_custom_call" | custom-call | tf_op jit(solution)/shard_map/gram_blocks/pallas_call | solution.py:121
  225.6 10.9 %gram_blocks.8 = (bf16[2,448,896]{2,1,0:T(8,128)(2,1)}, bf16[2,448,896]{2,1,0:T(8,128)(2,1)}) custom-call(s32[4]{0:T(128)} %pad_add_fusion.flags, bf16[896,1152]{1,0:T(8,128)(2,1)} %copy-done.5, bf16[896,2304]{1,0:T(8,128)(2,1)} %get-tuple-element.124.refs_0_.refs_1_.refs_2_.refs_7_, ...), custom_call_target="tpu_custom_call" | custom-call | tf_op jit(solution)/shard_map/gram_blocks/pallas_call | solution.py:121
  253.3 15.3 %collective-permute-done.19 = bf16[2,224,896]{2,1,0:T(8,128)(2,1)S(1)} collective-permute-done((bf16[2,224,896]{2,1,0:T(8,128)(2,1)S(1)}, bf16[2,224,896]{2,1,0:T(8,128)(2,1)S(1)}, u32[]{:S(2)}, u32[]{:S(2)}) %collective-permute-start.19) | collective-permute-done | bytes 802848 | tf_op jit(solution)/shard_map/ppermute | solution.py:372
  270.7 14.8 %collective-permute-done.15 = bf16[2,224,896]{2,1,0:T(8,128)(2,1)S(1)} collective-permute-done((bf16[2,224,896]{2,1,0:T(8,128)(2,1)S(1)}, bf16[2,224,896]{2,1,0:T(8,128)(2,1)S(1)}, u32[]{:S(2)}, u32[]{:S(2)}) %collective-permute-start.15) | collective-permute-done | bytes 802848 | tf_op jit(solution)/shard_map/ppermute | solution.py:372
  299.4 16.4 %collective-permute-done.17.refs_2_ = bf16[3,224,896]{2,1,0:T(8,128)(2,1)S(1)} collective-permute-done((bf16[3,224,896]{2,1,0:T(8,128)(2,1)S(1)}, bf16[3,224,896]{2,1,0:T(8,128)(2,1)S(1)}, u32[]{:S(2)}, u32[]{:S(2)}) %collective-permute-start.17) | collective-permute-done | bytes 1204256 | tf_op jit(solution)/shard_map/ppermute | solution.py:372
  335.4 18.3 %collective-permute-done.23.refs_6_ = bf16[4,224,896]{2,1,0:T(8,128)(2,1)S(1)} collective-permute-done((bf16[4,224,896]{2,1,0:T(8,128)(2,1)S(1)}, bf16[4,224,896]{2,1,0:T(8,128)(2,1)S(1)}, u32[]{:S(2)}, u32[]{:S(2)}) %collective-permute-start.23) | collective-permute-done | bytes 1605664 | tf_op jit(solution)/shard_map/ppermute | solution.py:372
  361.5 19.7 %collective-permute-done.28.refs_10_ = bf16[3,224,896]{2,1,0:T(8,128)(2,1)S(1)} collective-permute-done((bf16[3,224,896]{2,1,0:T(8,128)(2,1)S(1)}, bf16[3,224,896]{2,1,0:T(8,128)(2,1)S(1)}, u32[]{:S(2)}, u32[]{:S(2)}) %collective-permute-start.28) | collective-permute-done | bytes 1204256 | tf_op jit(solution)/shard_map/ppermute | solution.py:372
  384.3 37.5 %poly_rows.1.own = bf16[896,3584]{1,0:T(8,128)(2,1)} custom-call(s32[4]{0:T(128)} %pad_add_fusion.flags, bf16[3,224,896]{2,1,0:T(8,128)(2,1)} %copy-done.14, bf16[3,224,896]{2,1,0:T(8,128)(2,1)} %collective-permute-done.16.refs_1_, bf16[3,224,896]{2,1,0:T(8,128)(2,1)} %copy-done.24, bf16[3,224,896]{2,1,0:T(8,128)(2,1)} %copy-done.26, ...), custom_call_target="tpu_custom_call" | custom-call | tf_op jit(solution)/shard_map/poly_rows/pallas_call | solution.py:200
  424.2 8.4 %collective-permute-done.32.pair = bf16[896,3584]{1,0:T(8,128)(2,1)} collective-permute-done((bf16[896,3584]{1,0:T(8,128)(2,1)}, bf16[896,3584]{1,0:T(8,128)(2,1)}, u32[]{:S(2)}, u32[]{:S(2)}) %collective-permute-start.32) | collective-permute-done | bytes 6422560 | tf_op jit(solution)/shard_map/ppermute | solution.py:369
  438.1 22.6 %product_far.3 = (bf16[896,1024]{1,0:T(8,128)(2,1)}, bf16[896,1024]{1,0:T(8,128)(2,1)}, f32[1,256]{1,0:T(1,128)}) custom-call(s32[4]{0:T(128)} %pad_add_fusion.flags, bf16[896,3584]{1,0:T(8,128)(2,1)} %poly_rows.1.own, bf16[896,3584]{1,0:T(8,128)(2,1)} %collective-permute-done.32.pair, f32[1]{0:T(128)} %bitcast.11.refs_0_.refs_4_, ...), custom_call_target="tpu_custom_call" | custom-call | tf_op jit(solution)/shard_map/product_far/pallas_call | solution.py:295
  463.6 15.1 %collective-permute-done.33.refs_0_ = bf16[224,3584]{1,0:T(8,128)(2,1)} collective-permute-done((bf16[224,3584]{1,0:T(8,128)(2,1)}, bf16[224,3584]{1,0:T(8,128)(2,1)}, u32[]{:S(2)}, u32[]{:S(2)}) %collective-permute-start.33) | collective-permute-done | bytes 1605664 | tf_op jit(solution)/shard_map/ppermute | solution.py:384
  479.2 19.0 %product_far.4 = (bf16[896,768]{1,0:T(8,128)(2,1)}, bf16[896,768]{1,0:T(8,128)(2,1)}, f32[1,256]{1,0:T(1,128)}) custom-call(s32[4]{0:T(128)} %pad_add_fusion.flags, bf16[896,3584]{1,0:T(8,128)(2,1)} %poly_rows.1.own, bf16[896,3584]{1,0:T(8,128)(2,1)} %collective-permute-done.32.pair, f32[1]{0:T(128)} %bitcast.11.refs_0_.refs_4_, ...), custom_call_target="tpu_custom_call" | custom-call | tf_op jit(solution)/shard_map/product_far/pallas_call | solution.py:295
  500.6 16.9 %collective-permute-done.37.refs_3_ = bf16[896,1024]{1,0:T(8,128)(2,1)} collective-permute-done((bf16[896,1024]{1,0:T(8,128)(2,1)}, bf16[896,1024]{1,0:T(8,128)(2,1)}, u32[]{:S(2)}, u32[]{:S(2)}) %collective-permute-start.37) | collective-permute-done | bytes 1835040 | tf_op jit(solution)/shard_map/ppermute | solution.py:384
  518.8 15.3 %product_far.5 = (bf16[896,512]{1,0:T(8,128)(2,1)}, bf16[896,512]{1,0:T(8,128)(2,1)}, f32[1,256]{1,0:T(1,128)}) custom-call(s32[4]{0:T(128)} %pad_add_fusion.flags, bf16[896,3584]{1,0:T(8,128)(2,1)} %poly_rows.1.own, bf16[896,3584]{1,0:T(8,128)(2,1)} %collective-permute-done.32.pair, f32[1]{0:T(128)} %bitcast.11.refs_0_.refs_4_, ...), custom_call_target="tpu_custom_call" | custom-call | tf_op jit(solution)/shard_map/product_far/pallas_call | solution.py:295
  537.4 24.8 %product_near.1 = (bf16[896,2304]{1,0:T(8,128)(2,1)}, f32[1,256]{1,0:T(1,128)}) custom-call(s32[4]{0:T(128)} %pad_add_fusion.flags, bf16[896,3584]{1,0:T(8,128)(2,1)} %poly_rows.1.own, bf16[896,3584]{1,0:T(8,128)(2,1)} %collective-permute-done.32.pair, bf16[224,3584]{1,0:T(8,128)(2,1)} %collective-permute-done.33.refs_0_, ...), custom_call_target="tpu_custom_call" | custom-call | tf_op jit(solution)/shard_map/product_near/pallas_call | solution.py:295
  569.2 14.1 %collective-permute-start.43 = (f32[8,128]{1,0:T(8,128)S(1)}, f32[8,128]{1,0:T(8,128)S(1)}, u32[]{:S(2)}, u32[]{:S(2)}) collective-permute-start(f32[8,128]{1,0:T(8,128)S(1)} %fusion.3), channel_id=1, source_target_pairs={{0,1},{1,0},{2,3},{3,2},{4,5},{5,4},{6,7},{7,6},{8,9},{9,8},{10,11... | collective-permute-start | bytes 12296 | tf_op jit(solution)/shard_map/ppermute | solution.py:381
  591.6 12.7 %finish.1 = f32[896,4608]{1,0:T(8,128)} custom-call(s32[4]{0:T(128)} %pad_add_fusion.flags, f32[1]{0:T(128)} %bitcast.12.factor, bf16[896,2304]{1,0:T(8,128)(2,1)} %get-tuple-element.156.near, bf16[896,1024]{1,0:T(8,128)(2,1)} %get-tuple-element.157.refs_0_, bf16[896,768]{1,0:T(8,128)(2,1)} %get-tuple-element.158.refs_1_, ...), custom_call_target="tpu_custom_call" | custom-call | tf_op jit(solution)/shard_map/finish/pallas_call | solution.py:340
  (198 shorter events, 144.5 us)
Async XLA Ops:
  7.9 103.6 %collective-permute-start = (bf16[896,2304]{1,0:T(8,128)(2,1)}, bf16[896,2304]{1,0:T(8,128)(2,1)}, u32[]{:S(2)}, u32[]{:S(2)}) collective-permute-start(bf16[896,2304]{1,0:T(8,128)(2,1)} %get-tuple-element.93.refs_3_), channel_id=1, source_target_pairs={{1,2},{2,1},{5,6},{6,5},{9,10},{10,9},{13,14},{14,13},{17,18},{18,... | collective-permute-start | bytes 12386312 | tf_op jit(solution)/shard_map/ppermute | solution.py:375
  18.3 96.9 %collective-permute-start.1 = (bf16[896,2304]{1,0:T(8,128)(2,1)}, bf16[896,2304]{1,0:T(8,128)(2,1)}, u32[]{:S(2)}, u32[]{:S(2)}) collective-permute-start(bf16[896,2304]{1,0:T(8,128)(2,1)} %get-tuple-element.124.refs_0_.refs_1_.refs_2_.refs_7_), channel_id=1, source_target_pairs={{0,1},{1,0},{2,3},{3,2},{4,5},{5,4},{6,7},{7,6},{8,9},{9,8},{10,11... | collective-permute-start | bytes 12386312 | tf_op jit(solution)/shard_map/ppermute | solution.py:381
  30.3 81.2 %collective-permute-start.4 = (f32[8,128]{1,0:T(8,128)S(1)}, f32[8,128]{1,0:T(8,128)S(1)}, u32[]{:S(2)}, u32[]{:S(2)}) collective-permute-start(f32[8,128]{1,0:T(8,128)S(1)} %fusion.4), channel_id=1, source_target_pairs={{0,1},{1,0},{2,3},{3,2},{4,5},{5,4},{6,7},{7,6},{8,9},{9,8},{10,11... | collective-permute-start | bytes 12296 | tf_op jit(solution)/shard_map/ppermute | solution.py:381
  115.3 47.5 %collective-permute-start.5 = (bf16[896,1152]{1,0:T(8,128)(2,1)}, bf16[896,1152]{1,0:T(8,128)(2,1)S(1)}, u32[]{:S(2)}, u32[]{:S(2)}) collective-permute-start(bf16[896,1152]{1,0:T(8,128)(2,1)} %slice_select_fusion), channel_id=1, source_target_pairs={{0,2},{3,1},{1,0},{2,3},{4,6},{7,5},{5,4},{6,7},{8,10},{11,9},{9,8... | collective-permute-start | bytes 6193160 | tf_op jit(solution)/shard_map/ppermute | solution.py:387
  117.9 44.4 %collective-permute-start.6 = (f32[8,128]{1,0:T(8,128)S(1)}, f32[8,128]{1,0:T(8,128)S(1)}, u32[]{:S(2)}, u32[]{:S(2)}) collective-permute-start(f32[8,128]{1,0:T(8,128)S(1)} %add.132), channel_id=1, source_target_pairs={{0,2},{2,0},{1,3},{3,1},{4,6},{6,4},{5,7},{7,5},{8,10},{10,8},{9,1... | collective-permute-start | bytes 12296 | tf_op jit(solution)/shard_map/ppermute | solution.py:378
  164.2 47.6 %collective-permute-start.7 = (bf16[896,1152]{1,0:T(8,128)(2,1)}, bf16[896,1152]{1,0:T(8,128)(2,1)S(1)}, u32[]{:S(2)}, u32[]{:S(2)}) collective-permute-start(bf16[896,1152]{1,0:T(8,128)(2,1)} %slice_select_fusion.1), channel_id=1, source_target_pairs={{0,2},{3,1},{1,0},{2,3},{4,6},{7,5},{5,4},{6,7},{8,10},{11,9},{9,8... | collective-permute-start | bytes 6193160 | tf_op jit(solution)/shard_map/ppermute | solution.py:387
  172.2 28.7 %collective-permute-start.9 = (bf16[3,224,896]{2,1,0:T(8,128)(2,1)S(1)}, bf16[3,224,896]{2,1,0:T(8,128)(2,1)}, u32[]{:S(2)}, u32[]{:S(2)}) collective-permute-start(bf16[3,224,896]{2,1,0:T(8,128)(2,1)S(1)} %constant_dynamic-slice_fusion.3), channel_id=1, source_target_pairs={{0,8},{4,12},{8,0},{12,4},{1,9},{5,13},{9,1},{13,5},{2,10},{6,14},... | collective-permute-start | bytes 3612680 | tf_op jit(solution)/shard_map/ppermute | solution.py:372
  214.4 28.5 %collective-permute-start.11 = (bf16[3,224,896]{2,1,0:T(8,128)(2,1)S(1)}, bf16[3,224,896]{2,1,0:T(8,128)(2,1)S(1)}, u32[]{:S(2)}, u32[]{:S(2)}) collective-permute-start(bf16[3,224,896]{2,1,0:T(8,128)(2,1)S(1)} %add_convert_fusion.5), channel_id=1, source_target_pairs={{1,2},{2,1},{5,6},{6,5},{9,10},{10,9},{13,14},{14,13},{17,18},{18,... | collective-permute-start | bytes 3612680 | tf_op jit(solution)/shard_map/ppermute | solution.py:375
  244.6 41.1 %collective-permute-start.13 = (bf16[3,224,896]{2,1,0:T(8,128)(2,1)S(1)}, bf16[3,224,896]{2,1,0:T(8,128)(2,1)S(1)}, u32[]{:S(2)}, u32[]{:S(2)}) collective-permute-start(bf16[3,224,896]{2,1,0:T(8,128)(2,1)S(1)} %add_convert_fusion.4), channel_id=1, source_target_pairs={{1,2},{2,1},{5,6},{6,5},{9,10},{10,9},{13,14},{14,13},{17,18},{18,... | collective-permute-start | bytes 3612680 | tf_op jit(solution)/shard_map/ppermute | solution.py:375
  251.4 34.1 %collective-permute-start.15 = (bf16[2,224,896]{2,1,0:T(8,128)(2,1)S(1)}, bf16[2,224,896]{2,1,0:T(8,128)(2,1)S(1)}, u32[]{:S(2)}, u32[]{:S(2)}) collective-permute-start(bf16[2,224,896]{2,1,0:T(8,128)(2,1)S(1)} %constant_dynamic-slice_fusion.1), channel_id=1, source_target_pairs={{0,8},{4,12},{8,0},{12,4},{1,9},{5,13},{9,1},{13,5},{2,10},{6,14},... | collective-permute-start | bytes 2408456 | tf_op jit(solution)/shard_map/ppermute | solution.py:372
  289.9 45.5 %collective-permute-start.24 = (bf16[896,1024]{1,0:T(8,128)(2,1)S(1)}, bf16[896,1024]{1,0:T(8,128)(2,1)S(1)}, u32[]{:S(2)}, u32[]{:S(2)}) collective-permute-start(bf16[896,1024]{1,0:T(8,128)(2,1)S(1)} %slice.139), channel_id=1, source_target_pairs={{0,1},{1,0},{2,3},{3,2},{4,5},{5,4},{6,7},{7,6},{8,9},{9,8},{10,11... | collective-permute-start | bytes 5505032 | tf_op jit(solution)/shard_map/ppermute | solution.py:381
  317.8 35.9 %collective-permute-start.23 = (bf16[4,224,896]{2,1,0:T(8,128)(2,1)S(1)}, bf16[4,224,896]{2,1,0:T(8,128)(2,1)S(1)}, u32[]{:S(2)}, u32[]{:S(2)}) collective-permute-start(bf16[4,224,896]{2,1,0:T(8,128)(2,1)S(1)} %fusion.refs_4_), channel_id=1, source_target_pairs={{0,8},{4,12},{8,0},{12,4},{1,9},{5,13},{9,1},{13,5},{2,10},{6,14},... | collective-permute-start | bytes 4816904 | tf_op jit(solution)/shard_map/ppermute | solution.py:372
  319.4 34.3 %collective-permute-start.22 = (bf16[4,224,896]{2,1,0:T(8,128)(2,1)S(1)}, bf16[4,224,896]{2,1,0:T(8,128)(2,1)S(1)}, u32[]{:S(2)}, u32[]{:S(2)}) collective-permute-start(bf16[4,224,896]{2,1,0:T(8,128)(2,1)S(1)} %fusion.refs_4_), channel_id=1, source_target_pairs={{0,4},{4,0},{8,12},{12,8},{1,5},{5,1},{9,13},{13,9},{2,6},{6,2},{1... | collective-permute-start | bytes 4816904 | tf_op jit(solution)/shard_map/ppermute | solution.py:369
  326.7 95.1 %collective-permute-start.31 = (bf16[2,896,1024]{2,1,0:T(8,128)(2,1)}, bf16[2,896,1024]{2,1,0:T(8,128)(2,1)}, u32[]{:S(2)}, u32[]{:S(2)}) collective-permute-start(bf16[2,896,1024]{2,1,0:T(8,128)(2,1)} %pad_maximum_fusion), channel_id=1, source_target_pairs={{1,2},{2,1},{5,6},{6,5},{9,10},{10,9},{13,14},{14,13},{17,18},{18,... | collective-permute-start | bytes 11010056 | tf_op jit(solution)/shard_map/ppermute | solution.py:375
  329.3 31.7 %collective-permute-start.21 = (bf16[3,224,896]{2,1,0:T(8,128)(2,1)S(1)}, bf16[3,224,896]{2,1,0:T(8,128)(2,1)S(1)}, u32[]{:S(2)}, u32[]{:S(2)}) collective-permute-start(bf16[3,224,896]{2,1,0:T(8,128)(2,1)S(1)} %copy-done.25), channel_id=1, source_target_pairs={{0,4},{4,0},{8,12},{12,8},{1,5},{5,1},{9,13},{13,9},{2,6},{6,2},{1... | collective-permute-start | bytes 3612680 | tf_op jit(solution)/shard_map/ppermute | solution.py:369
  356.6 65.2 %collective-permute-start.30 = (bf16[896,1280]{1,0:T(8,128)(2,1)S(1)}, bf16[896,1280]{1,0:T(8,128)(2,1)S(1)}, u32[]{:S(2)}, u32[]{:S(2)}) collective-permute-start(bf16[896,1280]{1,0:T(8,128)(2,1)S(1)} %slice.140), channel_id=1, source_target_pairs={{0,1},{1,0},{2,3},{3,2},{4,5},{5,4},{6,7},{7,6},{8,9},{9,8},{10,11... | collective-permute-start | bytes 6881288 | tf_op jit(solution)/shard_map/ppermute | solution.py:381
  422.0 41.5 %collective-permute-start.34 = (bf16[2,896,768]{2,1,0:T(8,128)(2,1)}, bf16[2,896,768]{2,1,0:T(8,128)(2,1)}, u32[]{:S(2)}, u32[]{:S(2)}) collective-permute-start(bf16[2,896,768]{2,1,0:T(8,128)(2,1)} %pad_maximum_fusion.1), channel_id=1, source_target_pairs={{1,2},{2,1},{5,6},{6,5},{9,10},{10,9},{13,14},{14,13},{17,18},{18,... | collective-permute-start | bytes 8257544 | tf_op jit(solution)/shard_map/ppermute | solution.py:375
  436.0 42.6 %collective-permute-start.33 = (bf16[224,3584]{1,0:T(8,128)(2,1)}, bf16[224,3584]{1,0:T(8,128)(2,1)}, u32[]{:S(2)}, u32[]{:S(2)}) collective-permute-start(bf16[224,3584]{1,0:T(8,128)(2,1)} %dynamic-slice_select_fusion), channel_id=1, source_target_pairs={{1,0},{2,3},{5,4},{6,7},{9,8},{10,11},{13,12},{14,15},{17,16},{18,... | collective-permute-start | bytes 4816904 | tf_op jit(solution)/shard_map/ppermute | solution.py:384
  437.3 63.2 %collective-permute-start.38 = (bf16[2,896,512]{2,1,0:T(8,128)(2,1)}, bf16[2,896,512]{2,1,0:T(8,128)(2,1)S(1)}, u32[]{:S(2)}, u32[]{:S(2)}) collective-permute-start(bf16[2,896,512]{2,1,0:T(8,128)(2,1)} %pad_maximum_fusion.2), channel_id=1, source_target_pairs={{1,2},{2,1},{5,6},{6,5},{9,10},{10,9},{13,14},{14,13},{17,18},{18,... | collective-permute-start | bytes 5505032 | tf_op jit(solution)/shard_map/ppermute | solution.py:375
  460.7 56.8 %collective-permute-start.37 = (bf16[896,1024]{1,0:T(8,128)(2,1)}, bf16[896,1024]{1,0:T(8,128)(2,1)}, u32[]{:S(2)}, u32[]{:S(2)}) collective-permute-start(bf16[896,1024]{1,0:T(8,128)(2,1)} %get-tuple-element.143), channel_id=1, source_target_pairs={{1,0},{2,3},{5,4},{6,7},{9,8},{10,11},{13,12},{14,15},{17,16},{18,... | collective-permute-start | bytes 5505032 | tf_op jit(solution)/shard_map/ppermute | solution.py:384
  478.6 38.8 %collective-permute-start.39 = (bf16[224,3584]{1,0:T(8,128)(2,1)}, bf16[224,3584]{1,0:T(8,128)(2,1)S(1)}, u32[]{:S(2)}, u32[]{:S(2)}) collective-permute-start(bf16[224,3584]{1,0:T(8,128)(2,1)} %collective-permute-done.33.refs_0_), channel_id=1, source_target_pairs={{0,8},{4,12},{8,0},{12,4},{1,9},{5,13},{9,1},{13,5},{2,10},{6,14},... | collective-permute-start | bytes 4816904 | tf_op jit(solution)/shard_map/ppermute | solution.py:372
  479.2 58.2 %collective-permute-start.36 = (bf16[224,3584]{1,0:T(8,128)(2,1)}, bf16[224,3584]{1,0:T(8,128)(2,1)}, u32[]{:S(2)}, u32[]{:S(2)}) collective-permute-start(bf16[224,3584]{1,0:T(8,128)(2,1)} %collective-permute-done.33.refs_0_), channel_id=1, source_target_pairs={{0,4},{4,0},{8,12},{12,8},{1,5},{5,1},{9,13},{13,9},{2,6},{6,2},{1... | collective-permute-start | bytes 4816904 | tf_op jit(solution)/shard_map/ppermute | solution.py:369
  517.5 46.0 %collective-permute-start.35 = (bf16[896,768]{1,0:T(8,128)(2,1)}, bf16[896,768]{1,0:T(8,128)(2,1)}, u32[]{:S(2)}, u32[]{:S(2)}) collective-permute-start(bf16[896,768]{1,0:T(8,128)(2,1)} %get-tuple-element.141), channel_id=1, source_target_pairs={{1,0},{2,3},{5,4},{6,7},{9,8},{10,11},{13,12},{14,15},{17,16},{18,... | collective-permute-start | bytes 4128776 | tf_op jit(solution)/shard_map/ppermute | solution.py:384
  534.1 56.6 %collective-permute-start.45 = (bf16[896,512]{1,0:T(8,128)(2,1)}, bf16[896,512]{1,0:T(8,128)(2,1)S(1)}, u32[]{:S(2)}, u32[]{:S(2)}) collective-permute-start(bf16[896,512]{1,0:T(8,128)(2,1)} %get-tuple-element.162), channel_id=1, source_target_pairs={{1,0},{2,3},{5,4},{6,7},{9,8},{10,11},{13,12},{14,15},{17,16},{18,... | collective-permute-start | bytes 2752520 | tf_op jit(solution)/shard_map/ppermute | solution.py:384
  (55 other events, 674.3 us)
